TPU v7x, 256 devices: a whole 4x4x8 slice. The times are simulated.
256 devices in a mesh: gx: 16 (over x, y), gy: 8 (over z), gz: 2 (over core).
Axes of the slice: x: 4, y: 4, z: 8, core: 2. Of those that a mesh axis runs over, the one named last changes fastest.
Arguments:
- displacement: float32 [3, 128, 64, 512], P(None, 'gx', 'gy', 'gz'), may hold values from -6 to 6
- physical: float32 [128, 64, 512], P('gx', 'gy', 'gz'), may hold values from 0.1 to 1
- design: float32 [128, 64, 512], P('gx', 'gy', 'gz'), may hold values from 0.05 to 0.95
- passive: int32 [128, 64, 512], P('gx', 'gy', 'gz'), may hold values 0 or 1
- supports: int32 [1024], replicated, may hold values from 0 to 4194303
Outputs:
- new_design: float32 [128, 64, 512], P('gx', 'gy', 'gz')
- new_physical: float32 [128, 64, 512], P('gx', 'gy', 'gz')
- node_blocks: float32 [6, 128, 64, 512], P(None, 'gx', 'gy', 'gz')
Inputs may be any that keep to these rules, and one draw needn't show every extreme that they name: `supports`: node number (i * 64 + j) * 512 + k for node (i, j, k); repeats may occur.
All inputs are finite; a program needn't handle non-finite values. No bound on the sum of `passive` on one device may be relied on, other than what follows from the above.
Results may differ from a plain program's by a relative error of at most 0.0003.
Values sent between devices are 32-bit elements; how exact they have to be, the bound alone decides.
No kernel may reach another device: no remote copies, remote signals or barrier semaphores. Data moves between devices by JAX's collectives and lax.ppermute only.
A program may use at most 64 MiB of HBM per device.

v0:
```python
import math

import jax
import jax.numpy as jnp
import numpy as np
from jax import lax
from jax.sharding import PartitionSpec as P

STEPS = 10


filter_radius = 2.5
penalty = 3.0
move_limit = 0.2
stiff_floor = 1e-09
volume_share = 0.5
log_lower = -20.0
log_upper = 20.0
poisson = 0.3


def from_behind(value, axis, steps):
    count = lax.axis_size(axis)
    initial, last = (max(0, -steps), min(count, count - steps))
    return lax.ppermute(value, axis, [(source, source + steps) for source in range(initial, last)])


def padded_2(shard, sides, width):
    for axis, dim in sides:
        devices, length = (lax.axis_size(axis), shard.shape[dim])
        up = [(i, (i + 1) % devices) for i in range(devices - 1)]
        down = [(j, i) for i, j in up]
        last = lax.slice_in_dim(shard, length - width, length, axis=dim)
        initial = lax.slice_in_dim(shard, 0, width, axis=dim)
        before = lax.ppermute(last, axis, up)
        after = lax.ppermute(initial, axis, down)
        shard = jnp.concatenate([before, shard, after], axis=dim)
    return shard


def corner_offsets():
    return [(q // 4, q // 2 % 2, q % 2) for q in range(8)]


def hex_stiffness():
    lame_first = poisson / ((1.0 + poisson) * (1.0 - 2.0 * poisson))
    shear_modulus = 0.5 / (1.0 + poisson)
    elastic = np.zeros((6, 6))
    elastic[:3, :3] = lame_first
    for d in range(3):
        elastic[d, d] += 2.0 * shear_modulus
        elastic[d + 3, d + 3] = shear_modulus
    corners = corner_offsets()
    points = [0.5 - 0.5 / math.sqrt(3.0), 0.5 + 0.5 / math.sqrt(3.0)]
    matrix = np.zeros((24, 24))
    for p in points:
        for q in points:
            for r in points:
                location = [p, q, r]
                gradients = np.zeros((8, 3))
                for n in range(8):
                    factors = [
                        location[e] if corners[n][e] == 1 else 1.0 - location[e] for e in range(3)
                    ]
                    for d in range(3):
                        sign_value = 1.0 if corners[n][d] == 1 else -1.0
                        gradients[n, d] = sign_value * factors[(d + 1) % 3] * factors[(d + 2) % 3]
                strain = np.zeros((6, 24))
                for n in range(8):
                    column = 3 * n
                    strain[0, column] = gradients[n, 0]
                    strain[1, column + 1] = gradients[n, 1]
                    strain[2, column + 2] = gradients[n, 2]
                    strain[3, column + 1] = gradients[n, 2]
                    strain[3, column + 2] = gradients[n, 1]
                    strain[4, column] = gradients[n, 2]
                    strain[4, column + 2] = gradients[n, 0]
                    strain[5, column] = gradients[n, 1]
                    strain[5, column + 1] = gradients[n, 0]
                matrix += strain.T @ elastic @ strain / 8.0
    return matrix


def corner_blocks():
    matrix = hex_stiffness()
    entry_pairs = [(0, 0), (1, 1), (2, 2), (1, 2), (0, 2), (0, 1)]
    block_table = np.zeros((8, 6))
    for n in range(8):
        for m, (i, j) in enumerate(entry_pairs):
            block_table[n, m] = matrix[3 * n + i, 3 * n + j]
    return block_table


def filter_taps():
    tap_list = []
    for a in range(-2, 3):
        for b in range(-2, 3):
            for c in range(-2, 3):
                weight = filter_radius - math.sqrt(a * a + b * b + c * c)
                if weight > 0.0:
                    tap_list.append((a, b, c, weight))
    return tap_list


def stencil(padded, offset, counts):
    accumulated = jnp.zeros(counts, jnp.float32)
    for a, b, c, weight in filter_taps():
        accumulated = (
            accumulated
            + weight
            * padded[
                offset + a : offset + a + counts[0],
                offset + b : offset + b + counts[1],
                offset + c : offset + c + counts[2],
            ]
        )
    return accumulated


def inside_line(first_cell, length, extent):
    coords = first_cell + jnp.arange(length, dtype=jnp.int32)
    return ((coords >= 0) & (coords < extent)).astype(jnp.float32)


def inside_block(firsts, lengths, extents):
    lines = [inside_line(firsts[d], lengths[d], extents[d]) for d in range(3)]
    return lines[0][:, None, None] * lines[1][None, :, None] * lines[2][None, None, :]


def weight_sums(firsts, lengths, extents):
    padded = inside_block([f - 2 for f in firsts], [n + 4 for n in lengths], extents)
    return stencil(padded, 2, tuple(lengths))


def element_energy(ghosted, plane_index, width_y, width_z, stiffness):
    node_slab = lax.dynamic_slice_in_dim(ghosted, plane_index, 2, 1)
    vectors = jnp.stack(
        [node_slab[:, a, b : b + width_y, c : c + width_z] for a, b, c in corner_offsets()]
    ).reshape(24, width_y * width_z)
    product = jnp.dot(
        stiffness, vectors, preferred_element_type=jnp.float32, precision=lax.Precision.HIGHEST
    )
    return jnp.sum(vectors * product, axis=0).reshape(width_y, width_z)


def import_upper(face_layer, stride):
    return from_behind(face_layer, ("gx", "gy", "gz"), -stride)


def extend_upper(nodal_field, along, stride, keep_factor):
    incoming = import_upper(lax.slice_in_dim(nodal_field, 0, 1, axis=along), stride) * keep_factor
    return jnp.concatenate([nodal_field, incoming], axis=along)


def export_lower(face_layer, stride):
    return from_behind(face_layer, ("gx", "gy", "gz"), stride)


def fold_lower(nodal_field, along, stride, keep_factor):
    top_index = nodal_field.shape[along] - 1
    incoming = (
        export_lower(lax.slice_in_dim(nodal_field, top_index, top_index + 1, axis=along), stride)
        * keep_factor
    )
    first_layer = lax.slice_in_dim(nodal_field, 0, 1, axis=along) + incoming
    return jnp.concatenate(
        [first_layer, lax.slice_in_dim(nodal_field, 1, top_index, axis=along)], axis=along
    )


def cube_scale(density):
    return stiff_floor + density * density * density * (1.0 - stiff_floor)


def body(displacement, physical, design, passive, supports):
    size_x, size_y, size_z = design.shape
    counts = (size_x, size_y, size_z)
    count_x = lax.axis_size("gx")
    count_y = lax.axis_size("gy")
    count_z = lax.axis_size("gz")
    place_x = lax.axis_index("gx")
    place_y = lax.axis_index("gy")
    place_z = lax.axis_index("gz")
    total_x = size_x * count_x
    total_y = size_y * count_y
    total_z = size_z * count_z
    extents = (total_x, total_y, total_z)
    firsts = (place_x * size_x, place_y * size_y, place_z * size_z)
    stride_x = count_y * count_z
    stiffness = jnp.asarray(hex_stiffness(), jnp.float32)
    blocks = jnp.asarray(corner_blocks(), jnp.float32)
    keep_high_y = (place_y < count_y - 1).astype(jnp.float32)
    keep_high_z = (place_z < count_z - 1).astype(jnp.float32)
    ghosted = extend_upper(displacement, 1, stride_x, 1.0)
    ghosted = extend_upper(ghosted, 2, count_z, keep_high_y)
    ghosted = extend_upper(ghosted, 3, 1, keep_high_z)
    energy = lax.map(
        lambda plane_index: element_energy(ghosted, plane_index, size_y, size_z, stiffness),
        jnp.arange(size_x, dtype=jnp.int32),
    )
    sensitivity = -penalty * (1.0 - stiff_floor) * physical * physical * energy
    wide_firsts = [f - 2 for f in firsts]
    wide_lengths = [n + 4 for n in counts]
    wide_sum = weight_sums(wide_firsts, wide_lengths, extents)
    weight_sum = wide_sum[2 : 2 + size_x, 2 : 2 + size_y, 2 : 2 + size_z]
    wide_inside = inside_block(wide_firsts, wide_lengths, extents)
    reciprocal = wide_inside / (wide_sum + (1.0 - wide_inside))
    volume_weight = stencil(reciprocal, 2, counts)
    rimmed = padded_2(sensitivity / weight_sum, (("gx", 0), ("gy", 1), ("gz", 2)), 2)
    filtered = stencil(rimmed, 2, counts)
    scaled_design = design * jnp.sqrt(-filtered / volume_weight)
    floor_bound = jnp.maximum(0.0, design - move_limit)
    ceiling = jnp.minimum(1.0, design + move_limit)
    solid_mask = passive == 1

    def candidate(log_mult):
        return jnp.where(
            solid_mask,
            1.0,
            jnp.clip(scaled_design * jnp.exp(-0.5 * log_mult), floor_bound, ceiling),
        )

    target = volume_share * (total_x * total_y * total_z)
    bracket_low = jnp.float32(log_lower)
    bracket_high = jnp.float32(log_upper)
    for t in range(STEPS):
        middle = 0.5 * (bracket_low + bracket_high)
        volume = lax.psum(jnp.sum(volume_weight * candidate(middle)), ("gx", "gy", "gz"))
        too_full = volume > target
        bracket_low = jnp.where(too_full, middle, bracket_low)
        bracket_high = jnp.where(too_full, bracket_high, middle)
    new_design = candidate(0.5 * (bracket_low + bracket_high))
    rimmed_design = padded_2(new_design, (("gx", 0), ("gy", 1), ("gz", 2)), 2)
    new_physical = stencil(rimmed_design, 2, counts) / weight_sum
    padded_scale = jnp.pad(cube_scale(new_physical), 1)
    partial_blocks = jnp.zeros((6, size_x + 1, size_y + 1, size_z + 1), jnp.float32)
    for n, (a, b, c) in enumerate(corner_offsets()):
        partial_blocks = (
            partial_blocks
            + blocks[n][:, None, None, None]
            * padded_scale[1 - a : 2 - a + size_x, 1 - b : 2 - b + size_y, 1 - c : 2 - c + size_z][
                None
            ]
        )
    keep_low_y = (place_y > 0).astype(jnp.float32)
    keep_low_z = (place_z > 0).astype(jnp.float32)
    assembled = fold_lower(partial_blocks, 1, stride_x, 1.0)
    assembled = fold_lower(assembled, 2, count_z, keep_low_y)
    assembled = fold_lower(assembled, 3, 1, keep_low_z)
    plane_nodes = total_y * total_z
    node_x = supports // plane_nodes - firsts[0]
    node_y = supports // total_z % total_y - firsts[1]
    node_z = supports % total_z - firsts[2]
    owned_here = (
        (node_x >= 0)
        & (node_x < size_x)
        & (node_y >= 0)
        & (node_y < size_y)
        & (node_z >= 0)
        & (node_z < size_z)
    )
    cell_count = size_x * size_y * size_z
    local_slot = jnp.where(owned_here, (node_x * size_y + node_y) * size_z + node_z, cell_count)
    support_marks = (
        jnp.zeros(cell_count, jnp.int32).at[local_slot].set(1, mode="drop").reshape(counts)
    )
    identity = jnp.array([1.0, 1.0, 1.0, 0.0, 0.0, 0.0], jnp.float32)
    node_blocks = jnp.where(support_marks[None] == 1, identity[:, None, None, None], assembled)
    return (new_design, new_physical, node_blocks)


def solution(mesh):
    in_specs = (
        P(None, "gx", "gy", "gz"),
        P("gx", "gy", "gz"),
        P("gx", "gy", "gz"),
        P("gx", "gy", "gz"),
        P(),
    )
    out_specs = (P("gx", "gy", "gz"), P("gx", "gy", "gz"), P(None, "gx", "gy", "gz"))
    return jax.shard_map(body, mesh=mesh, in_specs=in_specs, out_specs=out_specs, check_vma=False)
```

profile of v0, /device:TPU:1, one launch (start us, length us, event | category | flops | bytes accessed | tf_op | source)
XLA Modules:
  0.0 885.3 jit_solution(18128071156538247703)
XLA Ops:
  0.6 0.7 slice-done
  1.4 1.3 collective-permute-start
  2.7 0.9 constant_dynamic-update-slice_fusion.2
  3.9 2.7 collective-permute-done
  6.6 1.3 collective-permute-start.1
  8.0 3.6 collective-permute-done.1
  11.6 6.4 collective-permute-start.2
  18.1 5.7 multiply_divide_fusion
  24.5 26.8 %while.12 = (s32[]{:T(128)}, f32[8,8,256]{2,1,0:T(8,128)S(1)}, s32[8]{0:T(128)S(1)}, f32[3,9,9,257]{3,2,0,1:T(8,128)S(1)}, f32[24,24]{1,0:T(8,128)S(1)}) while((s32[]{:T(128)}, f32[8,8,256]{2,1,0:T(8,128)S(1)}, s32[8]{0:T(128)S(1)}, f32[3,9,9,257]{3,2,0,1:T(8,128)S(1)}, f32[24,24]{1,0:T(8,128)S(1)}) %tuple.59), condition=%wide.region_2.3_spmd.clone.clone, body=%wide.region_0.2_spmd.sunk.clone.sunk.clone | while | flops 14252039 | bytes 1026503 | solution.py:197
  51.5 1.3 collective-permute-start.4
  52.8 5.5 collective-permute-start.3
  58.3 0.8 collective-permute-done.3
  59.2 1.3 collective-permute-start.6
  60.5 4.0 collective-permute-start.5
  64.5 0.9 collective-permute-done.5
  65.5 1.3 collective-permute-start.7
  66.8 5.5 collective-permute-start.8
  72.4 0.8 collective-permute-done.8
  73.5 2.8 multiply_reduce_fusion.9
  76.3 85.2 %psum.70 = f32[]{:T(128)} all-reduce(f32[]{:T(128)} %get-tuple-element.65), channel_id=1, replica_groups=mesh['gx'=16,'gy'=8,'gz'=2] {'gx','gy','gz'}, use_global_device_ids=true, to_apply=%region_4.5 | all-reduce | flops 1 | bytes 8 | tf_op jit(solution)/shard_map/psum | solution.py:228
  162.2 0.6 multiply_reduce_fusion.8
  162.8 73.5 %psum.71 = f32[]{:T(128)} all-reduce(f32[]{:T(128)} %multiply_reduce_fusion.8), channel_id=1, replica_groups=mesh['gx'=16,'gy'=8,'gz'=2] {'gx','gy','gz'}, use_global_device_ids=true, to_apply=%region_6.7 | all-reduce | flops 1 | bytes 8 | tf_op jit(solution)/shard_map/psum | solution.py:228
  237.6 74.2 %psum.72 = f32[]{:T(128)} all-reduce(f32[]{:T(128)} %multiply_reduce_fusion.7), channel_id=1, replica_groups=mesh['gx'=16,'gy'=8,'gz'=2] {'gx','gy','gz'}, use_global_device_ids=true, to_apply=%region_8.9 | all-reduce | flops 1 | bytes 8 | tf_op jit(solution)/shard_map/psum | solution.py:228
  313.2 73.4 %psum.73 = f32[]{:T(128)} all-reduce(f32[]{:T(128)} %multiply_reduce_fusion.6), channel_id=1, replica_groups=mesh['gx'=16,'gy'=8,'gz'=2] {'gx','gy','gz'}, use_global_device_ids=true, to_apply=%region_10.11 | all-reduce | flops 1 | bytes 8 | tf_op jit(solution)/shard_map/psum | solution.py:228
  387.9 74.2 %psum.74 = f32[]{:T(128)} all-reduce(f32[]{:T(128)} %multiply_reduce_fusion.5), channel_id=1, replica_groups=mesh['gx'=16,'gy'=8,'gz'=2] {'gx','gy','gz'}, use_global_device_ids=true, to_apply=%region_12.13 | all-reduce | flops 1 | bytes 8 | tf_op jit(solution)/shard_map/psum | solution.py:228
  463.4 73.6 %psum.75 = f32[]{:T(128)} all-reduce(f32[]{:T(128)} %multiply_reduce_fusion.4), channel_id=1, replica_groups=mesh['gx'=16,'gy'=8,'gz'=2] {'gx','gy','gz'}, use_global_device_ids=true, to_apply=%region_14.15 | all-reduce | flops 1 | bytes 8 | tf_op jit(solution)/shard_map/psum | solution.py:228
  538.3 74.1 %psum.76 = f32[]{:T(128)} all-reduce(f32[]{:T(128)} %multiply_reduce_fusion.3), channel_id=1, replica_groups=mesh['gx'=16,'gy'=8,'gz'=2] {'gx','gy','gz'}, use_global_device_ids=true, to_apply=%region_16.17 | all-reduce | flops 1 | bytes 8 | tf_op jit(solution)/shard_map/psum | solution.py:228
  613.8 73.5 %psum.77 = f32[]{:T(128)} all-reduce(f32[]{:T(128)} %multiply_reduce_fusion.2), channel_id=1, replica_groups=mesh['gx'=16,'gy'=8,'gz'=2] {'gx','gy','gz'}, use_global_device_ids=true, to_apply=%region_18.19 | all-reduce | flops 1 | bytes 8 | tf_op jit(solution)/shard_map/psum | solution.py:228
  688.6 74.1 %psum.78 = f32[]{:T(128)} all-reduce(f32[]{:T(128)} %multiply_reduce_fusion.1), channel_id=1, replica_groups=mesh['gx'=16,'gy'=8,'gz'=2] {'gx','gy','gz'}, use_global_device_ids=true, to_apply=%region_20.21 | all-reduce | flops 1 | bytes 8 | tf_op jit(solution)/shard_map/psum | solution.py:228
  764.0 73.5 %psum.79 = f32[]{:T(128)} all-reduce(f32[]{:T(128)} %multiply_reduce_fusion), channel_id=1, replica_groups=mesh['gx'=16,'gy'=8,'gz'=2] {'gx','gy','gz'}, use_global_device_ids=true, to_apply=%region_22.23 | all-reduce | flops 1 | bytes 8 | tf_op jit(solution)/shard_map/psum | solution.py:228
  838.2 1.3 collective-permute-start.10
  839.5 4.0 collective-permute-start.9
  843.5 0.8 collective-permute-done.9
  844.4 1.3 collective-permute-start.12
  845.7 4.2 collective-permute-start.11
  849.9 0.9 collective-permute-done.11
  850.9 1.3 collective-permute-start.13
  852.2 4.7 collective-permute-start.14
  856.9 0.9 collective-permute-done.14
  858.0 1.6 fusion.186
  860.6 0.8 multiply_add_fusion
  861.4 3.9 collective-permute-start.15
  865.4 2.0 collective-permute-done.15
  867.5 3.9 collective-permute-start.16
  871.5 4.4 scatter_custom_fusion
  876.0 4.9 collective-permute-start.17
  881.2 3.0 collective-permute-done.17
  884.5 0.9 copy.40
  (189 shorter events, 19.6 us)
Async XLA Ops:
  0.6 0.7 slice-start
  1.4 5.2 collective-permute-start
  6.6 4.9 collective-permute-start.1
  11.6 12.2 %collective-permute-start.2 = (f32[3,9,9,1]{3,2,0,1:T(8,128)S(1)}, f32[3,9,9,1]{3,2,0,1:T(8,128)S(1)}, u32[]{:S(2)}, u32[]{:S(2)}) collective-permute-start(f32[3,9,9,1]{3,2,0,1:T(8,128)S(1)} %pad_maximum_fusion.3), channel_id=1, source_target_pairs={{1,0},{2,1},{3,2},{4,3},{5,4},{6,5},{7,6},{8,7},{9,8},{10,9},{11,1... | collective-permute-start | bytes 2924 | tf_op jit(solution)/shard_map/ppermute | solution.py:25
  23.8 0.7 copy-start.2
  24.5 26.9 %copy-start.4 = (f32[8,8,256]{2,1,0:T(8,128)S(1)}, f32[8,8,256]{2,1,0:T(8,128)}, u32[]{:S(2)}) copy-start(f32[8,8,256]{2,1,0:T(8,128)} %param.11) | copy-start | bytes 196612
  51.5 6.8 collective-permute-start.4
  52.8 6.4 collective-permute-start.3
  59.2 5.3 collective-permute-start.6
  60.5 4.9 collective-permute-start.5
  65.5 6.8 collective-permute-start.7
  66.8 6.4 collective-permute-start.8
  72.4 1.1 copy-start
  72.4 1.1 copy-start.3
  838.2 19.8 %copy-start.1 = (f32[8,8,256]{2,1,0:T(8,128)}, f32[8,8,256]{2,1,0:T(8,128)S(1)}, u32[]{:S(2)}) copy-start(f32[8,8,256]{2,1,0:T(8,128)S(1)} %minimum_select_fusion) | copy-start | bytes 196612
  838.2 5.3 collective-permute-start.10
  839.5 4.8 collective-permute-start.9
  844.4 5.5 collective-permute-start.12
  845.7 5.1 collective-permute-start.11
  850.9 6.0 collective-permute-start.13
  852.2 5.6 collective-permute-start.14
  859.7 0.7 copy-start.10
  859.9 0.7 copy-start.7
  859.9 0.7 copy-start.8
  859.9 0.7 copy-start.9
  861.4 6.0 collective-permute-start.15
  867.4 4.0 copy-start.5
  867.5 8.4 collective-permute-start.16
  876.0 8.2 collective-permute-start.17
  881.1 3.1 copy-start.6
where the time goes:
time: 900 us; the launch traced here: 885 us
  blocking collectives  749 us (83%)
  starting transfers between devices  57.3 us (6%)
  other arithmetic  18.1 us (2%)
  local copies, waits for them, and re-layouts  17.2 us (2%)
  waiting for transfers between devices  16.6 us (2%)
  loops' own time  16 us (2%)
    psum x10, blocking collectives, body(): lax.psum(jnp.sum(volume_weight * candidate(middle)), ('gx', 'gy', 'gz'))  749 us
    ppermute x6, starting transfers between devices, from_behind(): lax.ppermute(value, axis, [(source, source + steps) for source in range(i...  21.8 us
    ppermute x6, starting transfers between devices, padded_2(): before = lax.ppermute(last, axis, up)  20.2 us
  transfers between devices with their start and end apart: 18, of which 10 were waited for; matrix products, arithmetic and copies ran while one was open for 1% of the time, Pallas kernels for 0%

commit v1 on v0

v1 whole, which is shorter than its diff:
```python
import functools
import math

import jax
import jax.numpy as jnp
import numpy as np
from jax import lax
from jax.experimental import pallas as pl
from jax.experimental.pallas import tpu as pltpu
from jax.sharding import PartitionSpec as P

STEPS = 10

filter_radius = 2.5
penalty = 3.0
move_limit = 0.2
stiff_floor = 1e-09
volume_share = 0.5
log_lower = -20.0
log_upper = 20.0
poisson = 0.3

SX, SY, SZ = 8, 8, 256
ROWS, LANES, SIDE = 16, 384, 128
POINTS = 2**STEPS
F32 = jnp.float32


def corner_offsets():
    return [(q // 4, q // 2 % 2, q % 2) for q in range(8)]


def hex_stiffness():
    lame_first = poisson / ((1.0 + poisson) * (1.0 - 2.0 * poisson))
    shear_modulus = 0.5 / (1.0 + poisson)
    elastic = np.zeros((6, 6))
    elastic[:3, :3] = lame_first
    for d in range(3):
        elastic[d, d] += 2.0 * shear_modulus
        elastic[d + 3, d + 3] = shear_modulus
    corners = corner_offsets()
    points = [0.5 - 0.5 / math.sqrt(3.0), 0.5 + 0.5 / math.sqrt(3.0)]
    matrix = np.zeros((24, 24))
    for p in points:
        for q in points:
            for r in points:
                location = [p, q, r]
                gradients = np.zeros((8, 3))
                for n in range(8):
                    factors = [
                        location[e] if corners[n][e] == 1 else 1.0 - location[e] for e in range(3)
                    ]
                    for d in range(3):
                        sign_value = 1.0 if corners[n][d] == 1 else -1.0
                        gradients[n, d] = sign_value * factors[(d + 1) % 3] * factors[(d + 2) % 3]
                strain = np.zeros((6, 24))
                for n in range(8):
                    column = 3 * n
                    strain[0, column] = gradients[n, 0]
                    strain[1, column + 1] = gradients[n, 1]
                    strain[2, column + 2] = gradients[n, 2]
                    strain[3, column + 1] = gradients[n, 2]
                    strain[3, column + 2] = gradients[n, 1]
                    strain[4, column] = gradients[n, 2]
                    strain[4, column + 2] = gradients[n, 0]
                    strain[5, column] = gradients[n, 1]
                    strain[5, column + 1] = gradients[n, 0]
                matrix += strain.T @ elastic @ strain / 8.0
    return matrix


def energy_squares():
    corners = corner_offsets()
    modes = np.zeros((24, 24))
    for s in range(8):
        bits = (s // 4, s // 2 % 2, s % 2)
        for n in range(8):
            sign_value = 1.0
            for e in range(3):
                if bits[e] == 1 and corners[n][e] == 0:
                    sign_value = -sign_value
            for d in range(3):
                modes[3 * n + d, 3 * s + d] = sign_value
    form = modes.T @ hex_stiffness() @ modes / 64.0
    used = np.zeros((24, 24))
    squares = []
    for parity in range(8):
        members = [3 * (parity ^ (4, 2, 1)[d]) + d for d in range(3)]
        block = form[np.ix_(members, members)].copy()
        used[np.ix_(members, members)] = block
        for r in range(3):
            if block[r, r] < 1e-9:
                continue
            factors = block[r] / math.sqrt(block[r, r])
            block -= np.outer(factors, factors)
            squares.append([(members[c], factors[c]) for c in range(3) if abs(factors[c]) > 1e-9])
        assert np.abs(block).max() < 1e-9
    assert np.abs(used - form).max() < 1e-9
    return squares


def corner_factors():
    matrix = hex_stiffness()
    factors = (matrix[0, 0], matrix[1, 2], matrix[0, 2], matrix[0, 1])
    for n, corner in enumerate(corner_offsets()):
        sign = [1.0 if c == 1 else -1.0 for c in corner]
        block = matrix[3 * n : 3 * n + 3, 3 * n : 3 * n + 3]
        assert np.allclose(np.diag(block), factors[0])
        assert np.allclose(block[1, 2], factors[1] * sign[1] * sign[2])
        assert np.allclose(block[0, 2], factors[2] * sign[0] * sign[2])
        assert np.allclose(block[0, 1], factors[3] * sign[0] * sign[1])
    return factors


def tap(square):
    return max(0.0, filter_radius - math.sqrt(square))


def rolled(value, steps, dim):
    return pltpu.roll(value, (-steps) % value.shape[dim], dim)


def row_pairs(plane):
    return (
        rolled(plane, 1, 0) + rolled(plane, -1, 0),
        rolled(plane, 2, 0) + rolled(plane, -2, 0),
    )


def filtered_plane(plane_of, near_of, far_of, p):
    ring_0 = plane_of(p)
    ring_1 = near_of(p) + plane_of(p - 1) + plane_of(p + 1)
    ring_2 = near_of(p - 1) + near_of(p + 1)
    ring_4 = far_of(p) + plane_of(p - 2) + plane_of(p + 2)
    ring_5 = far_of(p - 1) + far_of(p + 1) + near_of(p - 2) + near_of(p + 2)
    layers = []
    for c in (0, 1, 2):
        total = None
        for square, ring in ((0, ring_0), (1, ring_1), (2, ring_2), (4, ring_4), (5, ring_5)):
            weight = tap(square + c * c)
            if weight > 0.0:
                total = weight * ring if total is None else total + weight * ring
        layers.append(total)
    middle, near, far = layers
    return middle + (rolled(near, 1, 1) + rolled(near, -1, 1)) + (rolled(far, 2, 1) + rolled(far, -2, 1))


def weights_kernel(place_ref, support_ref, inverse_ref, volume_ref, mark_ref, near_ref, far_ref, *, extents):
    total_x, total_y, total_z = extents
    first_x = place_ref[0] * SX
    first_y = place_ref[1] * SY
    first_z = place_ref[2] * SZ
    row = lax.broadcasted_iota(jnp.int32, (ROWS, LANES), 0)
    lane = lax.broadcasted_iota(jnp.int32, (ROWS, LANES), 1)
    y = first_y + jnp.where(row < 12, row, row - ROWS)
    z = first_z + jnp.where(lane < SZ + SIDE // 2, lane, lane - LANES)
    inside = jnp.where((y >= 0) & (y < total_y) & (z >= 0) & (z < total_z), 1.0, 0.0).astype(F32)
    near, far = row_pairs(inside)

    def present(p):
        x = first_x + p
        return jnp.where((x >= 0) & (x < total_x), 1.0, 0.0).astype(F32)

    for p in range(SX + 4):
        x = p - 2
        weight_sum = filtered_plane(
            lambda q: inside * present(q), lambda q: near * present(q), lambda q: far * present(q), x
        )
        here = inside * present(x)
        inverse = jnp.where(here > 0.0, 1.0 / jnp.where(here > 0.0, weight_sum, 1.0), 0.0)
        inverse_ref[p] = inverse
        inverse_near, inverse_far = row_pairs(inverse)
        near_ref[p] = inverse_near
        far_ref[p] = inverse_far
    for p in range(SX):
        volume = filtered_plane(
            lambda q: inverse_ref[q, 0:SY], lambda q: near_ref[q, 0:SY], lambda q: far_ref[q, 0:SY], p + 2
        )
        volume_ref[p] = volume[:, 0:SZ]
    node = support_ref[...]
    node_x = node // (total_y * total_z) - first_x
    node_y = node // total_z % total_y - first_y
    node_z = node % total_z - first_z
    owned = (node_x >= 0) & (node_x < SX) & (node_y >= 0) & (node_y < SY)
    line = jnp.where(owned, node_x * SY + node_y, -1)
    count = node.shape[1]
    lines = jnp.where(lax.broadcasted_iota(jnp.int32, (SX * SY, count), 0) == line, 1.0, 0.0)
    lanes = jnp.where(lax.broadcasted_iota(jnp.int32, (SZ, count), 0) == node_z, 1.0, 0.0)
    hits = lax.dot_general(
        lines.astype(jnp.bfloat16),
        lanes.astype(jnp.bfloat16),
        (((1,), (1,)), ((), ())),
        preferred_element_type=F32,
    )
    for p in range(SX):
        mark_ref[p] = hits[p * SY : (p + 1) * SY]


def side_mask(first_z_index, upper, lower):
    lane = lax.broadcasted_iota(jnp.int32, (ROWS, SIDE), 1)
    start = jnp.where(first_z_index == 0, 0, SIDE - lower)
    stop = jnp.where(first_z_index == 0, upper, SIDE)
    return (lane >= start) & (lane < stop)


def assemble(ext_ref, fields, low, high, up_rows, low_rows, own, x_low, x_high, y_low, y_high, side, keep):
    planes = low + SX + high
    for f in range(fields):
        for p in range(planes):
            if p < low:
                middle = x_low[f, p]
            elif p < low + SX:
                middle = own(f, p - low)
            else:
                middle = x_high[f, p - low - SX]
            ext_ref[f, p, 0:SY, 0:SZ] = middle
            filler = jnp.zeros((SY - up_rows - low_rows, SZ), F32)
            ext_ref[f, p, SY:ROWS, 0:SZ] = jnp.concatenate([y_high[f, p], filler, y_low[f, p]], axis=0)
            ext_ref[f, p, :, SZ:LANES] = jnp.where(keep, side[f, p], 0.0)


def design_kernel(
    place_ref, shift_ref, physical_ref, x_low, x_high, y_low, y_high, side, inverse_ref, volume_ref, design_ref,
    passive_ref, out_ref, up_ref, down_ref, ext_ref, sens_ref, near_ref, far_ref, *, squares
):
    keep = side_mask(place_ref[2], 3, 2)
    assemble(
        ext_ref, 4, 2, 3, 3, 2, lambda f, p: shift_ref[f, p] if f < 3 else physical_ref[p],
        x_low, x_high, y_low, y_high, side, keep,
    )
    scale = penalty * (1.0 - stiff_floor)

    @pl.loop(0, SX + 4)
    def _(p):
        modes = {}
        for d in range(3):
            here, above = ext_ref[d, p], ext_ref[d, p + 1]
            for a, along_x in enumerate((here + above, above - here)):
                beyond = rolled(along_x, 1, 0)
                for b, along_y in enumerate((along_x + beyond, beyond - along_x)):
                    next_lane = rolled(along_y, 1, 1)
                    for c, mode in enumerate((along_y + next_lane, next_lane - along_y)):
                        modes[3 * (4 * a + 2 * b + c) + d] = mode
        energy = None
        for terms in squares:
            line = None
            for mode, factor in terms:
                term = float(factor) * modes[mode]
                line = term if line is None else line + term
            energy = line * line if energy is None else energy + line * line
        density = ext_ref[3, p]
        sens = scale * density * density * energy * inverse_ref[p]
        sens_ref[p] = sens
        near, far = row_pairs(sens)
        near_ref[p] = near
        far_ref[p] = far

    for p in range(SX):
        filtered = filtered_plane(
            lambda q: sens_ref[q, 0:SY], lambda q: near_ref[q, 0:SY], lambda q: far_ref[q, 0:SY], p + 2
        )[:, 0:SZ]
        design = design_ref[p]
        solid = passive_ref[p] == 1
        scaled = design * jnp.sqrt(filtered / volume_ref[p])
        floor_bound = jnp.where(solid, 1.0, jnp.maximum(0.0, design - move_limit))
        ceiling = jnp.where(solid, 1.0, jnp.minimum(1.0, design + move_limit))
        for f, value in enumerate((scaled, floor_bound, ceiling)):
            out_ref[f, p] = value
            if p < 2:
                down_ref[f, p] = value
            if p >= SX - 3:
                up_ref[f, p - (SX - 3)] = value


def volumes_kernel(exp_ref, bounds_ref, volume_ref, out_ref, weighted_ref, sums_ref):
    for p in range(SX):
        weight = volume_ref[p]
        for f in range(3):
            weighted = weight * bounds_ref[f, p]
            for h in range(2):
                weighted_ref[f, 2 * p + h] = weighted[:, h * 128 : (h + 1) * 128]

    @pl.loop(0, POINTS // 8)
    def _(g):
        factors = [exp_ref[g * 8 + j] for j in range(8)]
        totals = [None] * 8
        for v in range(2 * SX):
            scaled, floor_bound, ceiling = weighted_ref[0, v], weighted_ref[1, v], weighted_ref[2, v]
            for j in range(8):
                value = jnp.minimum(jnp.maximum(scaled * factors[j], floor_bound), ceiling)
                totals[j] = value if totals[j] is None else totals[j] + value
        rows = [jnp.sum(total, axis=0, keepdims=True) for total in totals]
        sums_ref[pl.ds(pl.multiple_of(g * 8, 8), 8), :] = jnp.concatenate(rows, axis=0)

    copies = out_ref.shape[0]
    result = lax.dot_general(
        jnp.ones((copies, 128), F32),
        sums_ref[...],
        (((1,), (1,)), ((), ())),
        precision=lax.Precision.HIGHEST,
        preferred_element_type=F32,
    )
    for i in range(8):
        out_ref[:, i, :] = result[:, i * 128 : (i + 1) * 128]


def repeat_kernel(part_ref, out_ref):
    total = part_ref[0]
    for i in range(1, part_ref.shape[0]):
        total = total + part_ref[i]
    for i in range(out_ref.shape[0]):
        out_ref[i] = total


def final_kernel(
    place_ref, part_ref, own_ref, x_low, x_high, y_low, y_high, side, inverse_ref, mark_ref, new_design_ref,
    new_physical_ref, blocks_ref, ext_ref, near_ref, far_ref, stiff_ref, *, factors, target
):
    total = part_ref[0]
    for i in range(1, part_ref.shape[0]):
        total = total + part_ref[i]
    low_end = jnp.minimum(jnp.sum(jnp.where(total > target, 1.0, 0.0)), POINTS - 1.0)
    multiplier = log_lower + (log_upper - log_lower) / POINTS * (low_end + 0.5)
    factor = jnp.exp(jnp.broadcast_to(-0.5 * multiplier, (ROWS, LANES)))
    keep = side_mask(place_ref[2], 2, 3)
    assemble(ext_ref, 3, 3, 2, 2, 3, lambda f, p: own_ref[f, p], x_low, x_high, y_low, y_high, side, keep)
    planes = SX + 5
    for p in range(planes):
        chosen = jnp.minimum(jnp.maximum(ext_ref[0, p] * factor, ext_ref[1, p]), ext_ref[2, p])
        ext_ref[0, p] = chosen
        near, far = row_pairs(chosen)
        near_ref[p] = near
        far_ref[p] = far
        if 3 <= p < SX + 3:
            new_design_ref[p - 3] = chosen[0:SY, 0:SZ]
    for p in range(SX + 1):
        inverse = inverse_ref[p + 1]
        density = (
            filtered_plane(lambda q: ext_ref[0, q], lambda q: near_ref[q], lambda q: far_ref[q], p + 2) * inverse
        )
        if p >= 1:
            new_physical_ref[p - 1] = density[0:SY, 0:SZ]
        cube = stiff_floor + density * density * density * (1.0 - stiff_floor)
        stiff_ref[p] = jnp.where(inverse > 0.0, cube, 0.0)
    for p in range(SX):
        below, here = stiff_ref[p], stiff_ref[p + 1]
        x_sum, x_diff = here + below, below - here
        x_sum_back, x_diff_back = rolled(x_sum, -1, 0), rolled(x_diff, -1, 0)
        sum_sum = (x_sum + x_sum_back)[0:SY]
        sum_diff = (x_sum_back - x_sum)[0:SY]
        diff_sum = (x_diff + x_diff_back)[0:SY]
        diff_diff = (x_diff_back - x_diff)[0:SY]
        marked = mark_ref[p] > 0.5
        even = factors[0] * (sum_sum + rolled(sum_sum, -1, 1))[:, 0:SZ]
        even = jnp.where(marked, 1.0, even)
        blocks_ref[0, p] = even
        blocks_ref[1, p] = even
        blocks_ref[2, p] = even
        yz = factors[1] * (rolled(sum_diff, -1, 1) - sum_diff)[:, 0:SZ]
        xz = factors[2] * (rolled(diff_sum, -1, 1) - diff_sum)[:, 0:SZ]
        xy = factors[3] * (diff_diff + rolled(diff_diff, -1, 1))[:, 0:SZ]
        blocks_ref[3, p] = jnp.where(marked, 0.0, yz)
        blocks_ref[4, p] = jnp.where(marked, 0.0, xz)
        blocks_ref[5, p] = jnp.where(marked, 0.0, xy)


def call(kernel, smem, vmem, shapes, scratch, flops):
    specs = [pl.BlockSpec(memory_space=pltpu.SMEM)] * smem + [pl.BlockSpec(memory_space=pltpu.VMEM)] * vmem
    outs = [jax.ShapeDtypeStruct(shape, F32) for shape in shapes]
    return pl.pallas_call(
        kernel,
        out_shape=outs,
        in_specs=specs,
        out_specs=[pl.BlockSpec(memory_space=pltpu.VMEM)] * len(outs),
        scratch_shapes=[pltpu.VMEM(shape, F32) for shape in scratch],
        compiler_params=pltpu.CompilerParams(vmem_limit_bytes=32 * 2**20),
        cost_estimate=pl.CostEstimate(flops=flops, bytes_accessed=10**6, transcendentals=0),
    )


def exchange(up, down, axis):
    count = lax.axis_size(axis)
    low = lax.ppermute(up, axis, [(i, i + 1) for i in range(count - 1)])
    high = lax.ppermute(down, axis, [(i + 1, i) for i in range(count - 1)])
    return low, high


def side_lanes(ext, place_z):
    half = jnp.where(place_z == 0, ext[..., SZ - SIDE : SZ], ext[..., 0:SIDE])
    return lax.ppermute(half, "gz", [(0, 1), (1, 0)])


def body(displacement, physical, design, passive, supports):
    assert design.shape == (SX, SY, SZ) and lax.axis_size("gz") == 2
    sizes = [lax.axis_size(axis) for axis in ("gx", "gy", "gz")]
    extents = (SX * sizes[0], SY * sizes[1], SZ * sizes[2])
    place_z = lax.axis_index("gz")
    place = jnp.stack([lax.axis_index("gx"), lax.axis_index("gy"), place_z]).astype(jnp.int32)

    fields = jnp.concatenate([displacement, physical[None]], axis=0)
    x_low, x_high = exchange(fields[:, SX - 2 :], fields[:, 0:3], "gx")

    frame = (SX + 4, ROWS, LANES)
    inverse, volume_weight, marks = call(
        functools.partial(weights_kernel, extents=extents), 1, 1,
        [frame, (SX, SY, SZ), (SX, SY, SZ)], [frame, frame], 10**7,
    )(place, supports.reshape(1, -1))

    wide = jnp.concatenate([x_low, fields, x_high], axis=1)
    y_low, y_high = exchange(wide[:, :, SY - 2 :], wide[:, :, 0:3], "gy")
    filler = jnp.zeros((4, SX + 5, 3, SZ), F32)
    side = side_lanes(jnp.concatenate([wide, y_high, filler, y_low], axis=2), place_z)
    bounds, up, down = call(
        functools.partial(design_kernel, squares=energy_squares()), 1, 11,
        [(3, SX, SY, SZ), (3, 3, SY, SZ), (3, 2, SY, SZ)], [(4, SX + 5, ROWS, LANES), frame, frame, frame], 10**7,
    )(place, displacement, physical, x_low, x_high, y_low, y_high, side, inverse, volume_weight, design, passive)

    x_low, x_high = exchange(up, down, "gx")
    multipliers = log_lower + (log_upper - log_lower) / POINTS * np.arange(1, POINTS + 1)
    table = jnp.asarray(np.exp(-0.5 * multipliers), F32)
    inner, outer = sizes[1] * sizes[2], sizes[0]
    (part,) = call(
        volumes_kernel, 1, 2, [(inner, 8, 128)], [(3, 2 * SX, SY, 128), (POINTS, 128)], 10**8,
    )(table, bounds, volume_weight)
    part = lax.all_to_all(part, ("gy", "gz"), 0, 0, tiled=True)
    wide = jnp.concatenate([x_low, bounds, x_high], axis=1)
    y_low, y_high = exchange(wide[:, :, SY - 3 :], wide[:, :, 0:2], "gy")
    (part,) = call(repeat_kernel, 0, 1, [(outer, 8, 128)], [], 10**5)(part)
    part = lax.all_to_all(part, "gx", 0, 0, tiled=True)
    filler = jnp.zeros((3, SX + 5, 3, SZ), F32)
    side = side_lanes(jnp.concatenate([wide, y_high, filler, y_low], axis=2), place_z)

    ext = (SX + 5, ROWS, LANES)
    new_design, new_physical, node_blocks = call(
        functools.partial(
            final_kernel, factors=[float(f) for f in corner_factors()],
            target=volume_share * (extents[0] * extents[1] * extents[2]),
        ), 1, 9,
        [(SX, SY, SZ), (SX, SY, SZ), (6, SX, SY, SZ)], [(3,) + ext, ext, ext, (SX + 1, ROWS, LANES)], 10**7,
    )(place, part, bounds, x_low, x_high, y_low, y_high, side, inverse, marks)
    return (new_design, new_physical, node_blocks)


def solution(mesh):
    in_specs = (
        P(None, "gx", "gy", "gz"),
        P("gx", "gy", "gz"),
        P("gx", "gy", "gz"),
        P("gx", "gy", "gz"),
        P(),
    )
    out_specs = (P("gx", "gy", "gz"), P("gx", "gy", "gz"), P(None, "gx", "gy", "gz"))
    return jax.shard_map(body, mesh=mesh, in_specs=in_specs, out_specs=out_specs, check_vma=False)
```

time: 900 us -> 97 us (0.11); the launches traced: 885 us -> 96.6 us
  blocking collectives: 749 us -> 35.2 us
  starting transfers between devices: 57.3 us -> 29.7 us
  Pallas kernels: 0 us -> 18.2 us
  other arithmetic: 18.1 us -> 1.55 us
  local copies, waits for them, and re-layouts: 17.2 us -> 0.8 us
  loops' own time: 16 us -> 0 us
    psum x10 -> x0, blocking collectives: 749 us -> none  [body(): lax.psum(jnp.sum(volume_weight * candidate(middle)), ('gx', 'gy', 'gz'))]
    all_to_all x0 -> x2, blocking collectives: none -> 35.2 us  [the longest x1 19.2 us: body(): part = lax.all_to_all(part, 'gx', 0, 0, tiled=True)]
    ppermute x18 -> x10, starting transfers between devices: 57.3 us -> 29.7 us  [the longest x4 17 us: exchange(): low = lax.ppermute(up, axis, [(i, i + 1) for i in range(count - 1)])]
    pallas_call x0 -> x5, Pallas kernels: none -> 18.2 us  [the longest x1 11.6 us: body(): call(volumes_kernel, 1, 2, [(inner, 8, 128)], [(3, 2 * SX, SY, 128), (POI...]
    another operation x1 -> x0, loops' own time: 16 us -> none  [body(): lax.map(lambda plane_index: element_energy(ghosted, plane_index, size_y,...]
  transfers between devices with their start and end apart: 18 -> 10, of which waited for: 10 -> 5; matrix products, arithmetic and copies ran while one was open for 1% -> 0% of each run, Pallas kernels for 0% -> 13%
where the time goes in v1:
time: 97 us; the launch traced here: 96.6 us
  blocking collectives  35.2 us (36%)
  starting transfers between devices  29.7 us (31%)
  Pallas kernels  18.2 us (19%)
  waiting for transfers between devices  10.3 us (11%)
  other arithmetic  1.55 us (2%)
    all_to_all x1, blocking collectives, body(): part = lax.all_to_all(part, 'gx', 0, 0, tiled=True)  19.2 us
    ppermute x4, starting transfers between devices, exchange(): low = lax.ppermute(up, axis, [(i, i + 1) for i in range(count - 1)])  17 us
    all_to_all x1, blocking collectives, body(): part = lax.all_to_all(part, ('gy', 'gz'), 0, 0, tiled=True)  15.9 us
    pallas_call x1, Pallas kernels, body(): call(volumes_kernel, 1, 2, [(inner, 8, 128)], [(3, 2 * SX, SY, 128), (POI...  11.6 us
    ppermute x2, starting transfers between devices, side_lanes(): return lax.ppermute(half, 'gz', [(0, 1), (1, 0)])  7.55 us
    ppermute x4, waiting for transfers between devices, exchange(): high = lax.ppermute(down, axis, [(i + 1, i) for i in range(count - 1)])  7.02 us
    ppermute x4, starting transfers between devices, exchange(): high = lax.ppermute(down, axis, [(i + 1, i) for i in range(count - 1)])  5.16 us
    ppermute x4, waiting for transfers between devices, exchange(): low = lax.ppermute(up, axis, [(i, i + 1) for i in range(count - 1)])  3.27 us
  transfers between devices with their start and end apart: 10, of which 5 were waited for; matrix products, arithmetic and copies ran while one was open for 0% of the time, Pallas kernels for 13%

profile of v1, /device:TPU:1, one launch (start us, length us, event | category | flops | bytes accessed | tf_op | source)
XLA Modules:
  0.0 96.6 jit_solution(8704251168156003862)
XLA Ops:
  0.6 0.0 copy-start
  0.6 0.0 copy-start.1
  0.6 1.0 pad_maximum_fusion.6
  1.6 1.3 %collective-permute-start.1 = (f32[4,3,8,256]{3,2,1,0:T(8,128)S(1)}, f32[4,3,8,256]{3,2,1,0:T(8,128)S(1)}, u32[]{:S(2)}, u32[]{:S(2)}) collective-permute-start(f32[4,3,8,256]{3,2,1,0:T(8,128)S(1)} %pad_maximum_fusion.6), channel_id=1, source_target_pairs={{16,0},{32,16},{48,32},{64,48},{80,64},{96,80},{112,96},{128,112},... | collective-permute-start | bytes 294920 | tf_op jit(solution)/shard_map/ppermute | solution.py:384
  2.9 0.0 copy-done
  2.9 0.0 copy-done.1
  2.9 4.7 %collective-permute-start = (f32[4,2,8,256]{3,2,1,0:T(8,128)S(1)}, f32[4,2,8,256]{3,2,1,0:T(8,128)S(1)}, u32[]{:S(2)}, u32[]{:S(2)}) collective-permute-start(f32[4,2,8,256]{3,2,1,0:T(8,128)S(1)} %pad_maximum_fusion.7), channel_id=1, source_target_pairs={{0,16},{16,32},{32,48},{48,64},{64,80},{80,96},{96,112},{112,128},... | collective-permute-start | bytes 196616 | tf_op jit(solution)/shard_map/ppermute | solution.py:383
  7.6 1.3 %collective-permute-done.x_low = f32[4,2,8,256]{3,2,1,0:T(8,128)S(1)} collective-permute-done((f32[4,2,8,256]{3,2,1,0:T(8,128)S(1)}, f32[4,2,8,256]{3,2,1,0:T(8,128)S(1)}, u32[]{:S(2)}, u32[]{:S(2)}) %collective-permute-start) | collective-permute-done | bytes 65568 | tf_op jit(solution)/shard_map/ppermute | solution.py:383
  8.9 0.0 collective-permute-done.1.x_high
  8.9 1.3 %collective-permute-start.3 = (f32[4,13,3,256]{3,2,1,0:T(4,128)S(1)}, f32[4,13,3,256]{3,2,1,0:T(4,128)S(1)}, u32[]{:S(2)}, u32[]{:S(2)}) collective-permute-start(f32[4,13,3,256]{3,2,1,0:T(4,128)S(1)} %pad_maximum_fusion.2), channel_id=1, source_target_pairs={{2,0},{4,2},{6,4},{8,6},{10,8},{12,10},{14,12},{3,1},{5,3},{7,5},{... | collective-permute-start | bytes 479240 | tf_op jit(solution)/shard_map/ppermute | solution.py:384
  10.3 4.3 %collective-permute-start.2 = (f32[4,13,2,256]{3,2,1,0:T(2,128)S(1)}, f32[4,13,2,256]{3,2,1,0:T(2,128)S(1)}, u32[]{:S(2)}, u32[]{:S(2)}) collective-permute-start(f32[4,13,2,256]{3,2,1,0:T(2,128)S(1)} %pad_maximum_fusion.5), channel_id=1, source_target_pairs={{0,2},{2,4},{4,6},{6,8},{8,10},{10,12},{12,14},{1,3},{3,5},{5,7},{... | collective-permute-start | bytes 319496 | tf_op jit(solution)/shard_map/ppermute | solution.py:383
  14.7 0.1 fusion
  14.7 1.6 %collective-permute-done.2.y_low = f32[4,13,2,256]{3,2,1,0:T(2,128)S(1)} collective-permute-done((f32[4,13,2,256]{3,2,1,0:T(2,128)S(1)}, f32[4,13,2,256]{3,2,1,0:T(2,128)S(1)}, u32[]{:S(2)}, u32[]{:S(2)}) %collective-permute-start.2) | collective-permute-done | bytes 106528 | tf_op jit(solution)/shard_map/ppermute | solution.py:383
  16.3 0.0 collective-permute-done.3.y_high
  16.3 0.2 pad_maximum_fusion
  16.5 0.0 copy-start.2
  16.5 0.0 copy-start.3
  16.6 0.1 slice_select_fusion
  16.6 4.6 %collective-permute-start.4 = (f32[4,13,16,128]{3,2,1,0:T(8,128)S(1)}, f32[4,13,16,128]{3,2,1,0:T(8,128)S(1)}, u32[]{:S(2)}, u32[]{:S(2)}) collective-permute-start(f32[4,13,16,128]{3,2,1,0:T(8,128)S(1)} %slice_select_fusion), channel_id=1, source_target_pairs={{0,1},{1,0},{2,3},{3,2},{4,5},{5,4},{6,7},{7,6},{8,9},{9,8},{10,11... | collective-permute-start | bytes 1277960 | tf_op jit(solution)/shard_map/ppermute | solution.py:390
  21.2 0.0 copy-start.4
  21.2 0.1 pad_add_fusion.place_ref
  21.3 0.6 copy-done.4
  21.9 1.4 %shard_map.85 = (f32[12,16,384]{2,1,0:T(8,128)S(1)}, f32[8,8,256]{2,1,0:T(8,128)S(1)}, f32[8,8,256]{2,1,0:T(8,128)S(1)}) custom-call(s32[3]{0:T(128)S(1)} %pad_add_fusion.place_ref, s32[1,1024]{1,0:T(1,128)S(1)} %bitcast.10), custom_call_target="tpu_custom_call" | custom-call | flops 10000000 | bytes 1000000 | tf_op jit(solution)/shard_map/pallas_call | solution.py:404
  23.3 0.0 collective-permute-done.4.side
  23.3 0.0 copy-done.2
  23.3 0.0 copy-done.3
  23.3 3.1 %shard_map.86 = (f32[3,8,8,256]{3,2,1,0:T(8,128)S(1)}, f32[3,3,8,256]{3,2,1,0:T(8,128)S(1)}, f32[3,2,8,256]{3,2,1,0:T(8,128)S(1)}) custom-call(s32[3]{0:T(128)S(1)} %pad_add_fusion.place_ref, f32[3,8,8,256]{3,2,1,0:T(8,128)S(1)} %copy-done, f32[8,8,256]{2,1,0:T(8,128)S(1)} %copy-done.1, f32[4,2,8,256]{3,2,1,0:T(8,128)S(1)} %collective-permute-done.x_low, ...), custom_call_target="tpu_custom_call" | custom-call | flops 10000000 | bytes 1000000 | tf_op jit(solution)/shard_map/pallas_call | solution.py:413
  26.4 4.0 %collective-permute-start.5 = (f32[3,3,8,256]{3,2,1,0:T(8,128)S(1)}, f32[3,3,8,256]{3,2,1,0:T(8,128)S(1)}, u32[]{:S(2)}, u32[]{:S(2)}) collective-permute-start(f32[3,3,8,256]{3,2,1,0:T(8,128)S(1)} %get-tuple-element.12), channel_id=1, source_target_pairs={{0,16},{16,32},{32,48},{48,64},{64,80},{80,96},{96,112},{112,128},... | collective-permute-start | bytes 221192 | tf_op jit(solution)/shard_map/ppermute | solution.py:383
  30.4 1.3 %collective-permute-start.6 = (f32[3,2,8,256]{3,2,1,0:T(8,128)S(1)}, f32[3,2,8,256]{3,2,1,0:T(8,128)S(1)}, u32[]{:S(2)}, u32[]{:S(2)}) collective-permute-start(f32[3,2,8,256]{3,2,1,0:T(8,128)S(1)} %get-tuple-element.13), channel_id=1, source_target_pairs={{16,0},{32,16},{48,32},{64,48},{80,64},{96,80},{112,96},{128,112},... | collective-permute-start | bytes 147464 | tf_op jit(solution)/shard_map/ppermute | solution.py:384
  31.7 0.4 collective-permute-done.5.x_low
  32.1 3.1 %collective-permute-done.6.x_high = f32[3,2,8,256]{3,2,1,0:T(8,128)S(1)} collective-permute-done((f32[3,2,8,256]{3,2,1,0:T(8,128)S(1)}, f32[3,2,8,256]{3,2,1,0:T(8,128)S(1)}, u32[]{:S(2)}, u32[]{:S(2)}) %collective-permute-start.6) | collective-permute-done | bytes 49184 | tf_op jit(solution)/shard_map/ppermute | solution.py:384
  35.3 4.0 %collective-permute-start.7 = (f32[3,13,3,256]{3,2,1,0:T(4,128)S(1)}, f32[3,13,3,256]{3,2,1,0:T(4,128)S(1)}, u32[]{:S(2)}, u32[]{:S(2)}) collective-permute-start(f32[3,13,3,256]{3,2,1,0:T(4,128)S(1)} %slice.42), channel_id=1, source_target_pairs={{0,2},{2,4},{4,6},{6,8},{8,10},{10,12},{12,14},{1,3},{3,5},{5,7},{... | collective-permute-start | bytes 359432 | tf_op jit(solution)/shard_map/ppermute | solution.py:383
  39.4 1.3 %collective-permute-start.8 = (f32[3,13,2,256]{3,2,1,0:T(2,128)S(1)}, f32[3,13,2,256]{3,2,1,0:T(2,128)S(1)}, u32[]{:S(2)}, u32[]{:S(2)}) collective-permute-start(f32[3,13,2,256]{3,2,1,0:T(2,128)S(1)} %slice.43), channel_id=1, source_target_pairs={{2,0},{4,2},{6,4},{8,6},{10,8},{12,10},{14,12},{3,1},{5,3},{7,5},{... | collective-permute-start | bytes 239624 | tf_op jit(solution)/shard_map/ppermute | solution.py:384
  40.7 3.9 %collective-permute-done.8.y_high = f32[3,13,2,256]{3,2,1,0:T(2,128)S(1)} collective-permute-done((f32[3,13,2,256]{3,2,1,0:T(2,128)S(1)}, f32[3,13,2,256]{3,2,1,0:T(2,128)S(1)}, u32[]{:S(2)}, u32[]{:S(2)}) %collective-permute-start.8) | collective-permute-done | bytes 79904 | tf_op jit(solution)/shard_map/ppermute | solution.py:384
  44.5 0.0 collective-permute-done.7.y_low
  44.5 0.1 pad_maximum_fusion.1
  44.7 0.0 copy-start.5
  44.7 3.0 %collective-permute-start.9 = (f32[3,13,16,128]{3,2,1,0:T(8,128)S(1)}, f32[3,13,16,128]{3,2,1,0:T(8,128)S(1)}, u32[]{:S(2)}, u32[]{:S(2)}) collective-permute-start(f32[3,13,16,128]{3,2,1,0:T(8,128)S(1)} %slice_select_fusion.1), channel_id=1, source_target_pairs={{0,1},{1,0},{2,3},{3,2},{4,5},{5,4},{6,7},{7,6},{8,9},{9,8},{10,11... | collective-permute-start | bytes 958472 | tf_op jit(solution)/shard_map/ppermute | solution.py:390
  47.7 0.0 copy-done.5
  47.7 11.6 %shard_map.87 = f32[16,8,128]{2,1,0:T(8,128)S(1)} custom-call(f32[1024]{0:T(1024)S(1)} %copy-done.5, f32[3,8,8,256]{3,2,1,0:T(8,128)S(1)} %get-tuple-element.11.bounds_ref.own_ref, f32[8,8,256]{2,1,0:T(8,128)S(1)} %get-tuple-element.10.volume_ref), custom_call_target="tpu_custom_call" | custom-call | flops 100000000 | bytes 1000000 | tf_op jit(solution)/shard_map/pallas_call | solution.py:422
  59.3 15.9 %all_to_all.10.part_ref = f32[16,8,128]{2,1,0:T(8,128)S(1)} all-to-all(f32[16,8,128]{2,1,0:T(8,128)S(1)} %shard_map.87), channel_id=1, replica_groups=mesh['gx'=16,'gy'=8,'gz'=2] {'gy','gz'}, dimensions={0} | all-to-all | bytes 131072 | tf_op jit(solution)/shard_map/all_to_all | solution.py:425
  75.3 19.2 %all_to_all.11.part_ref = f32[16,8,128]{2,1,0:T(8,128)S(1)} all-to-all(f32[16,8,128]{2,1,0:T(8,128)S(1)} %shard_map.88), channel_id=1, replica_groups=mesh['gx'=16,'gy'=8,'gz'=2] {'gx'}, dimensions={0} | all-to-all | bytes 131072 | tf_op jit(solution)/shard_map/all_to_all | solution.py:429
  94.5 0.0 collective-permute-done.9.side
  94.5 2.1 %shard_map.89 = (f32[8,8,256]{2,1,0:T(8,128)}, f32[8,8,256]{2,1,0:T(8,128)}, f32[6,8,8,256]{3,2,1,0:T(8,128)}) custom-call(s32[3]{0:T(128)S(1)} %pad_add_fusion.place_ref, f32[16,8,128]{2,1,0:T(8,128)S(1)} %all_to_all.11.part_ref, f32[3,8,8,256]{3,2,1,0:T(8,128)S(1)} %get-tuple-element.11.bounds_ref.own_ref, ...), custom_call_target="tpu_custom_call" | custom-call | flops 10000000 | bytes 1000000 | tf_op jit(solution)/shard_map/pallas_call | solution.py:434
  (11 shorter events, 0.2 us)
Async XLA Ops:
  0.6 2.3 %copy-start = (f32[3,8,8,256]{3,2,1,0:T(8,128)S(1)}, f32[3,8,8,256]{3,2,1,0:T(8,128)}, u32[]{:S(2)}) copy-start(f32[3,8,8,256]{3,2,1,0:T(8,128)} %shift_ref.1) | copy-start | bytes 589828
  0.6 2.3 %copy-start.1 = (f32[8,8,256]{2,1,0:T(8,128)S(1)}, f32[8,8,256]{2,1,0:T(8,128)}, u32[]{:S(2)}) copy-start(f32[8,8,256]{2,1,0:T(8,128)} %physical_ref.1) | copy-start | bytes 196612
  1.6 7.3 %collective-permute-start.1 = (f32[4,3,8,256]{3,2,1,0:T(8,128)S(1)}, f32[4,3,8,256]{3,2,1,0:T(8,128)S(1)}, u32[]{:S(2)}, u32[]{:S(2)}) collective-permute-start(f32[4,3,8,256]{3,2,1,0:T(8,128)S(1)} %pad_maximum_fusion.6), channel_id=1, source_target_pairs={{16,0},{32,16},{48,32},{64,48},{80,64},{96,80},{112,96},{128,112},... | collective-permute-start | bytes 294920 | tf_op jit(solution)/shard_map/ppermute | solution.py:384
  2.9 6.0 %collective-permute-start = (f32[4,2,8,256]{3,2,1,0:T(8,128)S(1)}, f32[4,2,8,256]{3,2,1,0:T(8,128)S(1)}, u32[]{:S(2)}, u32[]{:S(2)}) collective-permute-start(f32[4,2,8,256]{3,2,1,0:T(8,128)S(1)} %pad_maximum_fusion.7), channel_id=1, source_target_pairs={{0,16},{16,32},{32,48},{48,64},{64,80},{80,96},{96,112},{112,128},... | collective-permute-start | bytes 196616 | tf_op jit(solution)/shard_map/ppermute | solution.py:383
  8.9 7.4 %collective-permute-start.3 = (f32[4,13,3,256]{3,2,1,0:T(4,128)S(1)}, f32[4,13,3,256]{3,2,1,0:T(4,128)S(1)}, u32[]{:S(2)}, u32[]{:S(2)}) collective-permute-start(f32[4,13,3,256]{3,2,1,0:T(4,128)S(1)} %pad_maximum_fusion.2), channel_id=1, source_target_pairs={{2,0},{4,2},{6,4},{8,6},{10,8},{12,10},{14,12},{3,1},{5,3},{7,5},{... | collective-permute-start | bytes 479240 | tf_op jit(solution)/shard_map/ppermute | solution.py:384
  10.3 6.0 %collective-permute-start.2 = (f32[4,13,2,256]{3,2,1,0:T(2,128)S(1)}, f32[4,13,2,256]{3,2,1,0:T(2,128)S(1)}, u32[]{:S(2)}, u32[]{:S(2)}) collective-permute-start(f32[4,13,2,256]{3,2,1,0:T(2,128)S(1)} %pad_maximum_fusion.5), channel_id=1, source_target_pairs={{0,2},{2,4},{4,6},{6,8},{8,10},{10,12},{12,14},{1,3},{3,5},{5,7},{... | collective-permute-start | bytes 319496 | tf_op jit(solution)/shard_map/ppermute | solution.py:383
  16.5 6.7 %copy-start.2 = (f32[8,8,256]{2,1,0:T(8,128)S(1)}, f32[8,8,256]{2,1,0:T(8,128)}, u32[]{:S(2)}) copy-start(f32[8,8,256]{2,1,0:T(8,128)} %design_ref.1) | copy-start | bytes 196612
  16.5 6.7 %copy-start.3 = (s32[8,8,256]{2,1,0:T(8,128)S(1)}, s32[8,8,256]{2,1,0:T(8,128)}, u32[]{:S(2)}) copy-start(s32[8,8,256]{2,1,0:T(8,128)} %passive_ref.1) | copy-start | bytes 196612
  16.6 6.6 %collective-permute-start.4 = (f32[4,13,16,128]{3,2,1,0:T(8,128)S(1)}, f32[4,13,16,128]{3,2,1,0:T(8,128)S(1)}, u32[]{:S(2)}, u32[]{:S(2)}) collective-permute-start(f32[4,13,16,128]{3,2,1,0:T(8,128)S(1)} %slice_select_fusion), channel_id=1, source_target_pairs={{0,1},{1,0},{2,3},{3,2},{4,5},{5,4},{6,7},{7,6},{8,9},{9,8},{10,11... | collective-permute-start | bytes 1277960 | tf_op jit(solution)/shard_map/ppermute | solution.py:390
  21.2 0.7 copy-start.4
  26.4 5.7 %collective-permute-start.5 = (f32[3,3,8,256]{3,2,1,0:T(8,128)S(1)}, f32[3,3,8,256]{3,2,1,0:T(8,128)S(1)}, u32[]{:S(2)}, u32[]{:S(2)}) collective-permute-start(f32[3,3,8,256]{3,2,1,0:T(8,128)S(1)} %get-tuple-element.12), channel_id=1, source_target_pairs={{0,16},{16,32},{32,48},{48,64},{64,80},{80,96},{96,112},{112,128},... | collective-permute-start | bytes 221192 | tf_op jit(solution)/shard_map/ppermute | solution.py:383
  30.4 4.8 %collective-permute-start.6 = (f32[3,2,8,256]{3,2,1,0:T(8,128)S(1)}, f32[3,2,8,256]{3,2,1,0:T(8,128)S(1)}, u32[]{:S(2)}, u32[]{:S(2)}) collective-permute-start(f32[3,2,8,256]{3,2,1,0:T(8,128)S(1)} %get-tuple-element.13), channel_id=1, source_target_pairs={{16,0},{32,16},{48,32},{64,48},{80,64},{96,80},{112,96},{128,112},... | collective-permute-start | bytes 147464 | tf_op jit(solution)/shard_map/ppermute | solution.py:384
  35.3 9.3 %collective-permute-start.7 = (f32[3,13,3,256]{3,2,1,0:T(4,128)S(1)}, f32[3,13,3,256]{3,2,1,0:T(4,128)S(1)}, u32[]{:S(2)}, u32[]{:S(2)}) collective-permute-start(f32[3,13,3,256]{3,2,1,0:T(4,128)S(1)} %slice.42), channel_id=1, source_target_pairs={{0,2},{2,4},{4,6},{6,8},{8,10},{10,12},{12,14},{1,3},{3,5},{5,7},{... | collective-permute-start | bytes 359432 | tf_op jit(solution)/shard_map/ppermute | solution.py:383
  39.4 5.2 %collective-permute-start.8 = (f32[3,13,2,256]{3,2,1,0:T(2,128)S(1)}, f32[3,13,2,256]{3,2,1,0:T(2,128)S(1)}, u32[]{:S(2)}, u32[]{:S(2)}) collective-permute-start(f32[3,13,2,256]{3,2,1,0:T(2,128)S(1)} %slice.43), channel_id=1, source_target_pairs={{2,0},{4,2},{6,4},{8,6},{10,8},{12,10},{14,12},{3,1},{5,3},{7,5},{... | collective-permute-start | bytes 239624 | tf_op jit(solution)/shard_map/ppermute | solution.py:384
  44.7 3.0 %copy-start.5 = (f32[1024]{0:T(1024)S(1)}, f32[1024]{0:T(1024)}, u32[]{:S(2)}) copy-start(f32[1024]{0:T(1024)} %constant.20.clone.exp_ref) | copy-start | bytes 12292
  44.7 49.8 %collective-permute-start.9 = (f32[3,13,16,128]{3,2,1,0:T(8,128)S(1)}, f32[3,13,16,128]{3,2,1,0:T(8,128)S(1)}, u32[]{:S(2)}, u32[]{:S(2)}) collective-permute-start(f32[3,13,16,128]{3,2,1,0:T(8,128)S(1)} %slice_select_fusion.1), channel_id=1, source_target_pairs={{0,1},{1,0},{2,3},{3,2},{4,5},{5,4},{6,7},{7,6},{8,9},{9,8},{10,11... | collective-permute-start | bytes 958472 | tf_op jit(solution)/shard_map/ppermute | solution.py:390

commit v2 on v1

--- a/solution.py
+++ b/solution.py
@@ -266,7 +266,7 @@
         ceiling = jnp.where(solid, 1.0, jnp.minimum(1.0, design + move_limit))
         for f, value in enumerate((scaled, floor_bound, ceiling)):
             out_ref[f, p] = value
-            if p < 2:
+            if p < 3:
                 down_ref[f, p] = value
             if p >= SX - 3:
                 up_ref[f, p - (SX - 3)] = value
@@ -378,11 +378,20 @@
     )
 
 
-def exchange(up, down, axis):
+def start_exchange(top, bottom, axis):
     count = lax.axis_size(axis)
-    low = lax.ppermute(up, axis, [(i, i + 1) for i in range(count - 1)])
-    high = lax.ppermute(down, axis, [(i + 1, i) for i in range(count - 1)])
-    return low, high
+    even = lax.axis_index(axis) % 2 == 0
+    results = []
+    for start, (first, second) in enumerate(((top, bottom), (bottom, top))):
+        pairs = [(i, i + 1) for i in range(start, count - 1, 2)]
+        moves = pairs + [(j, i) for i, j in pairs]
+        results.append(lax.ppermute(jnp.where(even, first, second), axis, moves))
+    return results
+
+
+def end_exchange(results, axis):
+    even = lax.axis_index(axis) % 2 == 0
+    return jnp.where(even, results[1], results[0]), jnp.where(even, results[0], results[1])
 
 
 def side_lanes(ext, place_z):
@@ -398,37 +407,47 @@
     place = jnp.stack([lax.axis_index("gx"), lax.axis_index("gy"), place_z]).astype(jnp.int32)
 
     fields = jnp.concatenate([displacement, physical[None]], axis=0)
-    x_low, x_high = exchange(fields[:, SX - 2 :], fields[:, 0:3], "gx")
+    swaps = start_exchange(fields[:, SX - 3 :], fields[:, 0:3], "gx")
 
     frame = (SX + 4, ROWS, LANES)
     inverse, volume_weight, marks = call(
         functools.partial(weights_kernel, extents=extents), 1, 1,
         [frame, (SX, SY, SZ), (SX, SY, SZ)], [frame, frame], 10**7,
     )(place, supports.reshape(1, -1))
-
+    swaps, inverse, volume_weight, marks = lax.optimization_barrier((swaps, inverse, volume_weight, marks))
+
+    x_low, x_high = end_exchange(swaps, "gx")
+    x_low = x_low[:, 1:]
     wide = jnp.concatenate([x_low, fields, x_high], axis=1)
-    y_low, y_high = exchange(wide[:, :, SY - 2 :], wide[:, :, 0:3], "gy")
+    y_low, y_high = end_exchange(start_exchange(wide[:, :, SY - 3 :], wide[:, :, 0:3], "gy"), "gy")
+    y_low = y_low[:, :, 1:]
     filler = jnp.zeros((4, SX + 5, 3, SZ), F32)
     side = side_lanes(jnp.concatenate([wide, y_high, filler, y_low], axis=2), place_z)
     bounds, up, down = call(
         functools.partial(design_kernel, squares=energy_squares()), 1, 11,
-        [(3, SX, SY, SZ), (3, 3, SY, SZ), (3, 2, SY, SZ)], [(4, SX + 5, ROWS, LANES), frame, frame, frame], 10**7,
+        [(3, SX, SY, SZ), (3, 3, SY, SZ), (3, 3, SY, SZ)], [(4, SX + 5, ROWS, LANES), frame, frame, frame], 10**7,
     )(place, displacement, physical, x_low, x_high, y_low, y_high, side, inverse, volume_weight, design, passive)
 
-    x_low, x_high = exchange(up, down, "gx")
+    swaps = start_exchange(up, down, "gx")
     multipliers = log_lower + (log_upper - log_lower) / POINTS * np.arange(1, POINTS + 1)
     table = jnp.asarray(np.exp(-0.5 * multipliers), F32)
     inner, outer = sizes[1] * sizes[2], sizes[0]
     (part,) = call(
         volumes_kernel, 1, 2, [(inner, 8, 128)], [(3, 2 * SX, SY, 128), (POINTS, 128)], 10**8,
     )(table, bounds, volume_weight)
+    swaps, part = lax.optimization_barrier((swaps, part))
+    x_low, x_high = end_exchange(swaps, "gx")
+    x_high = x_high[:, 0:2]
+    wide = jnp.concatenate([x_low, bounds, x_high], axis=1)
+    swaps = start_exchange(wide[:, :, SY - 3 :], wide[:, :, 0:3], "gy")
     part = lax.all_to_all(part, ("gy", "gz"), 0, 0, tiled=True)
-    wide = jnp.concatenate([x_low, bounds, x_high], axis=1)
-    y_low, y_high = exchange(wide[:, :, SY - 3 :], wide[:, :, 0:2], "gy")
+    swaps, part = lax.optimization_barrier((swaps, part))
+    y_low, y_high = end_exchange(swaps, "gy")
+    y_high = y_high[:, :, 0:2]
+    filler = jnp.zeros((3, SX + 5, 3, SZ), F32)
+    side = side_lanes(jnp.concatenate([wide, y_high, filler, y_low], axis=2), place_z)
     (part,) = call(repeat_kernel, 0, 1, [(outer, 8, 128)], [], 10**5)(part)
     part = lax.all_to_all(part, "gx", 0, 0, tiled=True)
-    filler = jnp.zeros((3, SX + 5, 3, SZ), F32)
-    side = side_lanes(jnp.concatenate([wide, y_high, filler, y_low], axis=2), place_z)
 
     ext = (SX + 5, ROWS, LANES)
     new_design, new_physical, node_blocks = call(

time: 97 us -> 79.4 us (0.82)
  blocking collectives: 35.2 us -> 14.6 us
  starting transfers between devices: 29.7 us -> 32.4 us
  waiting for transfers between devices: 10.3 us -> 8.44 us
    all_to_all x1 -> x0, blocking collectives: 15.9 us -> none  [body(): part = lax.all_to_all(part, ('gy', 'gz'), 0, 0, tiled=True)]
    all_to_all x0 -> x1, starting transfers between devices: none -> 8.71 us  [body(): part = lax.all_to_all(part, ('gy', 'gz'), 0, 0, tiled=True)]
    all_to_all x1, blocking collectives: 19.2 us -> 14.6 us  [body(): part = lax.all_to_all(part, 'gx', 0, 0, tiled=True)]
    ppermute x8, waiting for transfers between devices: 10.3 us -> 7.04 us  [start_exchange(): results.append(lax.ppermute(jnp.where(even, first, second), axis, moves))]
    ppermute x2, starting transfers between devices: 7.55 us -> 4.34 us  [side_lanes(): return lax.ppermute(half, 'gz', [(0, 1), (1, 0)])]
    ppermute x8, starting transfers between devices: 22.2 us -> 19.3 us  [start_exchange(): results.append(lax.ppermute(jnp.where(even, first, second), axis, moves))]
    select_n x0 -> x12, other arithmetic: none -> 1.41 us  [the longest x4 1.12 us: start_exchange(): results.append(lax.ppermute(jnp.where(even, first, second), axis, moves))]
    ppermute x2, waiting for transfers between devices: 0.01 us -> 1.4 us  [side_lanes(): return lax.ppermute(half, 'gz', [(0, 1), (1, 0)])]
  transfers between devices with their start and end apart: 10 -> 11, of which waited for: 5 -> 3; matrix products, arithmetic and copies ran while one was open for 0% -> 0% of each run, Pallas kernels for 13% -> 17%
where the time goes in v2:
time: 79.4 us; the launch traced here: 78.8 us
  starting transfers between devices  32.4 us (41%)
  Pallas kernels  18.9 us (24%)
  blocking collectives  14.6 us (18%)
  waiting for transfers between devices  8.44 us (11%)
  other arithmetic  1.97 us (2%)
  local copies, waits for them, and re-layouts  1.61 us (2%)
  between operations  0.87 us (1%)
    ppermute x8, starting transfers between devices, start_exchange(): results.append(lax.ppermute(jnp.where(even, first, second), axis, moves))  19.3 us
    all_to_all x1, blocking collectives, body(): part = lax.all_to_all(part, 'gx', 0, 0, tiled=True)  14.6 us
    pallas_call x1, Pallas kernels, body(): call(volumes_kernel, 1, 2, [(inner, 8, 128)], [(3, 2 * SX, SY, 128), (POI...  12.3 us
    all_to_all x1, starting transfers between devices, body(): part = lax.all_to_all(part, ('gy', 'gz'), 0, 0, tiled=True)  8.71 us
    ppermute x8, waiting for transfers between devices, start_exchange(): results.append(lax.ppermute(jnp.where(even, first, second), axis, moves))  7.04 us
    ppermute x2, starting transfers between devices, side_lanes(): return lax.ppermute(half, 'gz', [(0, 1), (1, 0)])  4.34 us
    pallas_call x1, Pallas kernels, body(): call(functools.partial(design_kernel, squares=energy_squares()), 1, 11, [...  3.1 us
    pallas_call x1, Pallas kernels, body(): call(functools.partial(final_kernel, factors=[float(f) for f in corner_fa...  2.08 us
  transfers between devices with their start and end apart: 11, of which 3 were waited for; matrix products, arithmetic and copies ran while one was open for 0% of the time, Pallas kernels for 17%

profile of v2, /device:TPU:1, one launch (start us, length us, event | category | flops | bytes accessed | tf_op | source)
XLA Modules:
  0.0 78.8 jit_solution(15982720051136171339)
XLA Ops:
  0.6 1.0 %broadcast_select_fusion.3 = (f32[4,3,8,256]{3,2,1,0:T(8,128)S(1)}, f32[4,3,8,256]{3,2,1,0:T(8,128)S(1)}) fusion(pred[]{:T(512)S(6)} %eq.26, f32[1,8,8,256]{3,2,1,0:T(8,128)} %bitcast.5, f32[3,8,8,256]{3,2,1,0:T(8,128)} %shift_ref.1), kind=kLoop, calls=%fused_computation.19 | loop fusion | flops 98304 | bytes 458753 | tf_op jit(solution)/shard_map/jit(_where)/select_n | solution.py:388
  1.6 0.7 collective-permute-start.1
  2.3 4.8 %collective-permute-start = (f32[4,3,8,256]{3,2,1,0:T(8,128)S(1)}, f32[4,3,8,256]{3,2,1,0:T(8,128)S(1)}, u32[]{:S(2)}, u32[]{:S(2)}) collective-permute-start(f32[4,3,8,256]{3,2,1,0:T(8,128)S(1)} %get-tuple-element.42), channel_id=1, source_target_pairs={{0,16},{32,48},{64,80},{96,112},{128,144},{160,176},{192,208},{224... | collective-permute-start | bytes 294920 | tf_op jit(solution)/shard_map/ppermute | solution.py:388
  7.1 0.1 pad_add_fusion.place_ref
  7.1 0.6 copy-done.4
  7.7 1.4 %shard_map.85 = (f32[12,16,384]{2,1,0:T(8,128)S(1)}, f32[8,8,256]{2,1,0:T(8,128)S(1)}, f32[8,8,256]{2,1,0:T(8,128)S(1)}) custom-call(s32[3]{0:T(128)S(1)} %pad_add_fusion.place_ref, s32[1,1024]{1,0:T(1,128)S(1)} %bitcast.8), custom_call_target="tpu_custom_call" | custom-call | flops 10000000 | bytes 1000000 | tf_op jit(solution)/shard_map/pallas_call | solution.py:413
  9.1 0.0 collective-permute-done.1
  9.1 0.0 collective-permute-done
  9.1 0.0 copy-start
  9.2 0.0 copy-start.1
  9.2 0.9 %copy-done = f32[3,8,8,256]{3,2,1,0:T(8,128)S(1)} copy-done((f32[3,8,8,256]{3,2,1,0:T(8,128)S(1)}, f32[3,8,8,256]{3,2,1,0:T(8,128)}, u32[]{:S(2)}) %copy-start) | copy-done | bytes 196632
  10.1 0.0 copy-done.1
  10.1 0.1 slice_select_fusion.3
  10.2 0.7 collective-permute-start.2
  10.9 4.6 %collective-permute-start.3 = (f32[4,13,3,256]{3,2,1,0:T(4,128)S(1)}, f32[4,13,3,256]{3,2,1,0:T(4,128)S(1)}, u32[]{:S(2)}, u32[]{:S(2)}) collective-permute-start(f32[4,13,3,256]{3,2,1,0:T(4,128)S(1)} %get-tuple-element.38), channel_id=1, source_target_pairs={{0,2},{4,6},{8,10},{12,14},{2,0},{6,4},{10,8},{14,12},{1,3},{5,7},... | collective-permute-start | bytes 479240 | tf_op jit(solution)/shard_map/ppermute | solution.py:388
  15.5 0.1 fusion
  15.5 0.0 collective-permute-done.2
  15.5 3.2 %collective-permute-done.3 = f32[4,13,3,256]{3,2,1,0:T(4,128)S(1)} collective-permute-done((f32[4,13,3,256]{3,2,1,0:T(4,128)S(1)}, f32[4,13,3,256]{3,2,1,0:T(4,128)S(1)}, u32[]{:S(2)}, u32[]{:S(2)}) %collective-permute-start.3) | collective-permute-done | bytes 159776 | tf_op jit(solution)/shard_map/ppermute | solution.py:388
  18.7 0.1 slice_select_fusion.6.y_low
  18.8 0.1 broadcast_select_fusion.y_high
  18.9 0.2 pad_maximum_fusion
  19.1 0.0 copy-start.2
  19.1 0.0 copy-start.3
  19.1 0.1 slice_select_fusion
  19.2 3.1 %collective-permute-start.4 = (f32[4,13,16,128]{3,2,1,0:T(8,128)S(1)}, f32[4,13,16,128]{3,2,1,0:T(8,128)S(1)}, u32[]{:S(2)}, u32[]{:S(2)}) collective-permute-start(f32[4,13,16,128]{3,2,1,0:T(8,128)S(1)} %slice_select_fusion), channel_id=1, source_target_pairs={{0,1},{1,0},{2,3},{3,2},{4,5},{5,4},{6,7},{7,6},{8,9},{9,8},{10,11... | collective-permute-start | bytes 1277960 | tf_op jit(solution)/shard_map/ppermute | solution.py:399
  22.2 1.4 %collective-permute-done.4.side = f32[4,13,16,128]{3,2,1,0:T(8,128)S(1)} collective-permute-done((f32[4,13,16,128]{3,2,1,0:T(8,128)S(1)}, f32[4,13,16,128]{3,2,1,0:T(8,128)S(1)}, u32[]{:S(2)}, u32[]{:S(2)}) %collective-permute-start.4) | collective-permute-done | bytes 426016 | tf_op jit(solution)/shard_map/ppermute | solution.py:399
  23.6 0.0 copy-done.2
  23.6 0.0 copy-done.3
  23.6 3.1 %shard_map.86 = (f32[3,8,8,256]{3,2,1,0:T(8,128)S(1)}, f32[3,3,8,256]{3,2,1,0:T(8,128)S(1)}, f32[3,3,8,256]{3,2,1,0:T(8,128)S(1)}) custom-call(s32[3]{0:T(128)S(1)} %pad_add_fusion.place_ref, f32[3,8,8,256]{3,2,1,0:T(8,128)S(1)} %copy-done, f32[8,8,256]{2,1,0:T(8,128)S(1)} %copy-done.1, f32[4,2,8,256]{3,2,1,0:T(8,128)S(1)} %slice_select_fusion.8.x_low, ...), custom_call_target="tpu_custom_call" | custom-call | flops 10000000 | bytes 1000000 | tf_op jit(solution)/shard_map/pallas_call | solution.py:426
  26.7 0.0 copy-start.5
  26.8 0.7 collective-permute-start.6
  27.4 3.4 %collective-permute-start.5 = (f32[3,3,8,256]{3,2,1,0:T(8,128)S(1)}, f32[3,3,8,256]{3,2,1,0:T(8,128)S(1)}, u32[]{:S(2)}, u32[]{:S(2)}) collective-permute-start(f32[3,3,8,256]{3,2,1,0:T(8,128)S(1)} %get-tuple-element.44), channel_id=1, source_target_pairs={{0,16},{32,48},{64,80},{96,112},{128,144},{160,176},{192,208},{224... | collective-permute-start | bytes 221192 | tf_op jit(solution)/shard_map/ppermute | solution.py:388
  30.9 12.3 %shard_map.87 = f32[16,8,128]{2,1,0:T(8,128)} custom-call(f32[1024]{0:T(1024)S(1)} %copy-done.5, f32[3,8,8,256]{3,2,1,0:T(8,128)S(1)} %get-tuple-element.29.bounds_ref.own_ref, f32[8,8,256]{2,1,0:T(8,128)S(1)} %get-tuple-element.26.volume_ref), custom_call_target="tpu_custom_call" | custom-call | flops 100000000 | bytes 1000000 | tf_op jit(solution)/shard_map/pallas_call | solution.py:435
  43.2 0.0 collective-permute-done.6
  43.2 0.0 collective-permute-done.5
  43.2 8.7 %all-to-all-start = ((f32[16,8,128]{2,1,0:T(8,128)}), f32[16,8,128]{2,1,0:T(8,128)S(1)}, u32[]{:S(2)}, u32[]{:S(2)}) async-start(f32[16,8,128]{2,1,0:T(8,128)} %shard_map.87), calls=%async_computation | async-start | bytes 131072 | tf_op jit(solution)/shard_map/all_to_all | solution.py:443
  51.9 0.1 slice_select_fusion.4
  52.0 0.7 collective-permute-start.8
  52.7 3.9 %collective-permute-start.7 = (f32[3,13,3,256]{3,2,1,0:T(4,128)S(1)}, f32[3,13,3,256]{3,2,1,0:T(4,128)S(1)}, u32[]{:S(2)}, u32[]{:S(2)}) collective-permute-start(f32[3,13,3,256]{3,2,1,0:T(4,128)S(1)} %get-tuple-element.40), channel_id=1, source_target_pairs={{0,2},{4,6},{8,10},{12,14},{2,0},{6,4},{10,8},{14,12},{1,3},{5,7},... | collective-permute-start | bytes 359432 | tf_op jit(solution)/shard_map/ppermute | solution.py:388
  56.6 0.0 collective-permute-done.8
  56.6 3.9 %collective-permute-done.7 = f32[3,13,3,256]{3,2,1,0:T(4,128)S(1)} collective-permute-done((f32[3,13,3,256]{3,2,1,0:T(4,128)S(1)}, f32[3,13,3,256]{3,2,1,0:T(4,128)S(1)}, u32[]{:S(2)}, u32[]{:S(2)}) %collective-permute-start.7) | collective-permute-done | bytes 119840 | tf_op jit(solution)/shard_map/ppermute | solution.py:388
  60.5 0.0 all-to-all-done.part_ref
  60.5 0.1 broadcast_select_fusion.1.y_low
  60.6 0.1 pad_maximum_fusion.1
  60.8 1.3 %collective-permute-start.9 = (f32[3,13,16,128]{3,2,1,0:T(8,128)S(1)}, f32[3,13,16,128]{3,2,1,0:T(8,128)S(1)}, u32[]{:S(2)}, u32[]{:S(2)}) collective-permute-start(f32[3,13,16,128]{3,2,1,0:T(8,128)S(1)} %slice_select_fusion.1), channel_id=1, source_target_pairs={{0,1},{1,0},{2,3},{3,2},{4,5},{5,4},{6,7},{7,6},{8,9},{9,8},{10,11... | collective-permute-start | bytes 958472 | tf_op jit(solution)/shard_map/ppermute | solution.py:399
  62.1 14.6 %all_to_all.10.part_ref = f32[16,8,128]{2,1,0:T(8,128)S(1)} all-to-all(f32[16,8,128]{2,1,0:T(8,128)S(1)} %shard_map.88), channel_id=1, replica_groups=mesh['gx'=16,'gy'=8,'gz'=2] {'gx'}, dimensions={0} | all-to-all | bytes 131072 | tf_op jit(solution)/shard_map/all_to_all | solution.py:450
  76.7 0.0 collective-permute-done.9.side
  76.7 2.1 %shard_map.89 = (f32[8,8,256]{2,1,0:T(8,128)}, f32[8,8,256]{2,1,0:T(8,128)}, f32[6,8,8,256]{3,2,1,0:T(8,128)}) custom-call(s32[3]{0:T(128)S(1)} %pad_add_fusion.place_ref, f32[16,8,128]{2,1,0:T(8,128)S(1)} %all_to_all.10.part_ref, f32[3,8,8,256]{3,2,1,0:T(8,128)S(1)} %get-tuple-element.29.bounds_ref.own_ref, ...), custom_call_target="tpu_custom_call" | custom-call | flops 10000000 | bytes 1000000 | tf_op jit(solution)/shard_map/pallas_call | solution.py:453
  (13 shorter events, 0.2 us)
Async XLA Ops:
  1.6 7.5 %collective-permute-start.1 = (f32[4,3,8,256]{3,2,1,0:T(8,128)S(1)}, f32[4,3,8,256]{3,2,1,0:T(8,128)S(1)}, u32[]{:S(2)}, u32[]{:S(2)}) collective-permute-start(f32[4,3,8,256]{3,2,1,0:T(8,128)S(1)} %get-tuple-element.41), channel_id=1, source_target_pairs={{16,32},{48,64},{80,96},{112,128},{144,160},{176,192},{208,224},{3... | collective-permute-start | bytes 294920 | tf_op jit(solution)/shard_map/ppermute | solution.py:388
  2.3 6.8 %collective-permute-start = (f32[4,3,8,256]{3,2,1,0:T(8,128)S(1)}, f32[4,3,8,256]{3,2,1,0:T(8,128)S(1)}, u32[]{:S(2)}, u32[]{:S(2)}) collective-permute-start(f32[4,3,8,256]{3,2,1,0:T(8,128)S(1)} %get-tuple-element.42), channel_id=1, source_target_pairs={{0,16},{32,48},{64,80},{96,112},{128,144},{160,176},{192,208},{224... | collective-permute-start | bytes 294920 | tf_op jit(solution)/shard_map/ppermute | solution.py:388
  7.0 0.7 copy-start.4
  9.1 0.9 %copy-start = (f32[3,8,8,256]{3,2,1,0:T(8,128)S(1)}, f32[3,8,8,256]{3,2,1,0:T(8,128)}, u32[]{:S(2)}) copy-start(f32[3,8,8,256]{3,2,1,0:T(8,128)} %shift_ref.1) | copy-start | bytes 589828
  9.2 0.9 %copy-start.1 = (f32[8,8,256]{2,1,0:T(8,128)S(1)}, f32[8,8,256]{2,1,0:T(8,128)}, u32[]{:S(2)}) copy-start(f32[8,8,256]{2,1,0:T(8,128)} %physical_ref.1) | copy-start | bytes 196612
  10.2 5.4 %collective-permute-start.2 = (f32[4,13,3,256]{3,2,1,0:T(4,128)S(1)}, f32[4,13,3,256]{3,2,1,0:T(4,128)S(1)}, u32[]{:S(2)}, u32[]{:S(2)}) collective-permute-start(f32[4,13,3,256]{3,2,1,0:T(4,128)S(1)} %get-tuple-element.37), channel_id=1, source_target_pairs={{2,4},{6,8},{10,12},{4,2},{8,6},{12,10},{3,5},{7,9},{11,13},{5,3},... | collective-permute-start | bytes 479240 | tf_op jit(solution)/shard_map/ppermute | solution.py:388
  10.9 7.8 %collective-permute-start.3 = (f32[4,13,3,256]{3,2,1,0:T(4,128)S(1)}, f32[4,13,3,256]{3,2,1,0:T(4,128)S(1)}, u32[]{:S(2)}, u32[]{:S(2)}) collective-permute-start(f32[4,13,3,256]{3,2,1,0:T(4,128)S(1)} %get-tuple-element.38), channel_id=1, source_target_pairs={{0,2},{4,6},{8,10},{12,14},{2,0},{6,4},{10,8},{14,12},{1,3},{5,7},... | collective-permute-start | bytes 479240 | tf_op jit(solution)/shard_map/ppermute | solution.py:388
  19.1 4.5 %copy-start.2 = (f32[8,8,256]{2,1,0:T(8,128)S(1)}, f32[8,8,256]{2,1,0:T(8,128)}, u32[]{:S(2)}) copy-start(f32[8,8,256]{2,1,0:T(8,128)} %design_ref.1) | copy-start | bytes 196612
  19.1 4.5 %copy-start.3 = (s32[8,8,256]{2,1,0:T(8,128)S(1)}, s32[8,8,256]{2,1,0:T(8,128)}, u32[]{:S(2)}) copy-start(s32[8,8,256]{2,1,0:T(8,128)} %passive_ref.1) | copy-start | bytes 196612
  19.2 4.5 %collective-permute-start.4 = (f32[4,13,16,128]{3,2,1,0:T(8,128)S(1)}, f32[4,13,16,128]{3,2,1,0:T(8,128)S(1)}, u32[]{:S(2)}, u32[]{:S(2)}) collective-permute-start(f32[4,13,16,128]{3,2,1,0:T(8,128)S(1)} %slice_select_fusion), channel_id=1, source_target_pairs={{0,1},{1,0},{2,3},{3,2},{4,5},{5,4},{6,7},{7,6},{8,9},{9,8},{10,11... | collective-permute-start | bytes 1277960 | tf_op jit(solution)/shard_map/ppermute | solution.py:399
  26.7 4.1 %copy-start.5 = (f32[1024]{0:T(1024)S(1)}, f32[1024]{0:T(1024)}, u32[]{:S(2)}) copy-start(f32[1024]{0:T(1024)} %constant.48.clone.exp_ref) | copy-start | bytes 12292
  26.8 16.4 %collective-permute-start.6 = (f32[3,3,8,256]{3,2,1,0:T(8,128)S(1)}, f32[3,3,8,256]{3,2,1,0:T(8,128)S(1)}, u32[]{:S(2)}, u32[]{:S(2)}) collective-permute-start(f32[3,3,8,256]{3,2,1,0:T(8,128)S(1)} %get-tuple-element.43), channel_id=1, source_target_pairs={{16,32},{48,64},{80,96},{112,128},{144,160},{176,192},{208,224},{3... | collective-permute-start | bytes 221192 | tf_op jit(solution)/shard_map/ppermute | solution.py:388
  27.4 15.7 %collective-permute-start.5 = (f32[3,3,8,256]{3,2,1,0:T(8,128)S(1)}, f32[3,3,8,256]{3,2,1,0:T(8,128)S(1)}, u32[]{:S(2)}, u32[]{:S(2)}) collective-permute-start(f32[3,3,8,256]{3,2,1,0:T(8,128)S(1)} %get-tuple-element.44), channel_id=1, source_target_pairs={{0,16},{32,48},{64,80},{96,112},{128,144},{160,176},{192,208},{224... | collective-permute-start | bytes 221192 | tf_op jit(solution)/shard_map/ppermute | solution.py:388
  43.2 17.3 %all-to-all-start = ((f32[16,8,128]{2,1,0:T(8,128)}), f32[16,8,128]{2,1,0:T(8,128)S(1)}, u32[]{:S(2)}, u32[]{:S(2)}) async-start(f32[16,8,128]{2,1,0:T(8,128)} %shard_map.87), calls=%async_computation | async-start | bytes 131072 | tf_op jit(solution)/shard_map/all_to_all | solution.py:443
  52.0 4.6 %collective-permute-start.8 = (f32[3,13,3,256]{3,2,1,0:T(4,128)S(1)}, f32[3,13,3,256]{3,2,1,0:T(4,128)S(1)}, u32[]{:S(2)}, u32[]{:S(2)}) collective-permute-start(f32[3,13,3,256]{3,2,1,0:T(4,128)S(1)} %get-tuple-element.39), channel_id=1, source_target_pairs={{2,4},{6,8},{10,12},{4,2},{8,6},{12,10},{3,5},{7,9},{11,13},{5,3},... | collective-permute-start | bytes 359432 | tf_op jit(solution)/shard_map/ppermute | solution.py:388
  52.7 7.8 %collective-permute-start.7 = (f32[3,13,3,256]{3,2,1,0:T(4,128)S(1)}, f32[3,13,3,256]{3,2,1,0:T(4,128)S(1)}, u32[]{:S(2)}, u32[]{:S(2)}) collective-permute-start(f32[3,13,3,256]{3,2,1,0:T(4,128)S(1)} %get-tuple-element.40), channel_id=1, source_target_pairs={{0,2},{4,6},{8,10},{12,14},{2,0},{6,4},{10,8},{14,12},{1,3},{5,7},... | collective-permute-start | bytes 359432 | tf_op jit(solution)/shard_map/ppermute | solution.py:388
  60.8 15.9 %collective-permute-start.9 = (f32[3,13,16,128]{3,2,1,0:T(8,128)S(1)}, f32[3,13,16,128]{3,2,1,0:T(8,128)S(1)}, u32[]{:S(2)}, u32[]{:S(2)}) collective-permute-start(f32[3,13,16,128]{3,2,1,0:T(8,128)S(1)} %slice_select_fusion.1), channel_id=1, source_target_pairs={{0,1},{1,0},{2,3},{3,2},{4,5},{5,4},{6,7},{7,6},{8,9},{9,8},{10,11... | collective-permute-start | bytes 958472 | tf_op jit(solution)/shard_map/ppermute | solution.py:399

commit v3 on v1

--- a/solution.py
+++ b/solution.py
@@ -22,6 +22,7 @@
 
 SX, SY, SZ = 8, 8, 256
 ROWS, LANES, SIDE = 16, 384, 128
+NODES, ELEMENTS, CHOSEN = SX + 10, SX + 9, SX + 5
 POINTS = 2**STEPS
 F32 = jnp.float32
 
@@ -161,8 +162,8 @@
         x = first_x + p
         return jnp.where((x >= 0) & (x < total_x), 1.0, 0.0).astype(F32)
 
-    for p in range(SX + 4):
-        x = p - 2
+    for p in range(ELEMENTS):
+        x = p - 5
         weight_sum = filtered_plane(
             lambda q: inside * present(q), lambda q: near * present(q), lambda q: far * present(q), x
         )
@@ -170,13 +171,12 @@
         inverse = jnp.where(here > 0.0, 1.0 / jnp.where(here > 0.0, weight_sum, 1.0), 0.0)
         inverse_ref[p] = inverse
         inverse_near, inverse_far = row_pairs(inverse)
-        near_ref[p] = inverse_near
-        far_ref[p] = inverse_far
-    for p in range(SX):
-        volume = filtered_plane(
-            lambda q: inverse_ref[q, 0:SY], lambda q: near_ref[q, 0:SY], lambda q: far_ref[q, 0:SY], p + 2
+        near_ref[p] = inverse_near[0:SY]
+        far_ref[p] = inverse_far[0:SY]
+    for p in range(CHOSEN):
+        volume_ref[p] = filtered_plane(
+            lambda q: inverse_ref[q, 0:SY], lambda q: near_ref[q], lambda q: far_ref[q], p + 2
         )
-        volume_ref[p] = volume[:, 0:SZ]
     node = support_ref[...]
     node_x = node // (total_y * total_z) - first_x
     node_y = node // total_z % total_y - first_y
@@ -196,41 +196,97 @@
         mark_ref[p] = hits[p * SY : (p + 1) * SY]
 
 
-def side_mask(first_z_index, upper, lower):
-    lane = lax.broadcasted_iota(jnp.int32, (ROWS, SIDE), 1)
-    start = jnp.where(first_z_index == 0, 0, SIDE - lower)
-    stop = jnp.where(first_z_index == 0, upper, SIDE)
-    return (lane >= start) & (lane < stop)
-
-
-def assemble(ext_ref, fields, low, high, up_rows, low_rows, own, x_low, x_high, y_low, y_high, side, keep):
-    planes = low + SX + high
-    for f in range(fields):
-        for p in range(planes):
-            if p < low:
-                middle = x_low[f, p]
-            elif p < low + SX:
-                middle = own(f, p - low)
-            else:
-                middle = x_high[f, p - low - SX]
-            ext_ref[f, p, 0:SY, 0:SZ] = middle
-            filler = jnp.zeros((SY - up_rows - low_rows, SZ), F32)
-            ext_ref[f, p, SY:ROWS, 0:SZ] = jnp.concatenate([y_high[f, p], filler, y_low[f, p]], axis=0)
-            ext_ref[f, p, :, SZ:LANES] = jnp.where(keep, side[f, p], 0.0)
+def is_even(place_ref, axis):
+    return place_ref[axis] % 2 == 0
+
+
+def place_pair(even, first_ref, second_ref, top, bottom, place):
+    first_ref[place] = jnp.where(even, top, bottom)
+    second_ref[place] = jnp.where(even, bottom, top)
+
+
+def low_high(even, first_ref, second_ref, place):
+    first, second = first_ref[place], second_ref[place]
+    return jnp.where(even, second, first), jnp.where(even, first, second)
+
+
+def row_tile(even, first_ref, second_ref, plane):
+    low, high = low_high(even, first_ref, second_ref, slice(3 * plane, 3 * plane + 3))
+    return jnp.concatenate([high, jnp.zeros((SY - 6, low.shape[1]), F32), low], axis=0)
+
+
+def faces_x_kernel(place_ref, shift_ref, physical_ref, design_ref, passive_ref, first_ref, second_ref):
+    even = is_even(place_ref, 0)
+    fields = [shift_ref.at[0], shift_ref.at[1], shift_ref.at[2], physical_ref]
+    for f, field in enumerate(fields):
+        place_pair(even, first_ref, second_ref, field[SX - 5 :], field[0:5], slice(5 * f, 5 * f + 5))
+    for f, field in enumerate((design_ref, passive_ref)):
+        top, bottom = field[SX - 3 :].astype(F32), field[0:3].astype(F32)
+        place_pair(even, first_ref, second_ref, top, bottom, slice(20 + 3 * f, 23 + 3 * f))
+
+
+def plane_reader(even, shift_ref, physical_ref, design_ref, passive_ref, x_first, x_second):
+    def read(index):
+        if index < 4 * NODES:
+            f, x, depth, base = index // NODES, index % NODES - 5, 5, 5 * (index // NODES)
+        else:
+            f, x = divmod(index - 4 * NODES, CHOSEN)
+            f, x, depth, base = f + 4, x - 3, 3, 20 + 3 * f
+        if 0 <= x < SX:
+            if f < 3:
+                return shift_ref[f, x]
+            return (physical_ref, design_ref, passive_ref)[f - 3][x].astype(F32)
+        low, high = low_high(even, x_first, x_second, base + (x + depth if x < 0 else x - SX))
+        return low if x < 0 else high
+
+    return read
+
+
+def faces_y_kernel(
+    place_ref, shift_ref, physical_ref, design_ref, passive_ref, x_first, x_second, first_ref, second_ref, side_ref
+):
+    even = is_even(place_ref, 1)
+    lower_core = place_ref[2] == 0
+    read = plane_reader(
+        is_even(place_ref, 0), shift_ref, physical_ref, design_ref, passive_ref, x_first, x_second
+    )
+    for index in range(4 * NODES + 2 * CHOSEN):
+        plane = read(index)
+        if index < 4 * NODES:
+            rows = slice(3 * index, 3 * index + 3)
+            place_pair(even, first_ref, second_ref, plane[SY - 3 :], plane[0:3], rows)
+        side_ref[index] = jnp.where(lower_core, plane[:, SZ - SIDE :], plane[:, 0:SIDE])
+
+
+def faces_z_kernel(place_ref, y_first, y_second, side_ref):
+    even = is_even(place_ref, 1)
+    lower_core = place_ref[2] == 0
+    for index in range(4 * NODES):
+        tile = row_tile(even, y_first, y_second, index)
+        side_ref[index] = jnp.where(lower_core, tile[:, SZ - SIDE :], tile[:, 0:SIDE])
 
 
 def design_kernel(
-    place_ref, shift_ref, physical_ref, x_low, x_high, y_low, y_high, side, inverse_ref, volume_ref, design_ref,
-    passive_ref, out_ref, up_ref, down_ref, ext_ref, sens_ref, near_ref, far_ref, *, squares
+    place_ref, shift_ref, physical_ref, design_ref, passive_ref, x_first, x_second, y_first, y_second, side,
+    y_side, inverse_ref, volume_ref, out_ref, first_ref, second_ref, ext_ref, sens_ref, near_ref, far_ref, *, squares
 ):
-    keep = side_mask(place_ref[2], 3, 2)
-    assemble(
-        ext_ref, 4, 2, 3, 3, 2, lambda f, p: shift_ref[f, p] if f < 3 else physical_ref[p],
-        x_low, x_high, y_low, y_high, side, keep,
-    )
+    lane = lax.broadcasted_iota(jnp.int32, (SY, SIDE), 1)
+    start = place_ref[2] * (SIDE // 2)
+    keep = (lane >= start) & (lane < start + SIDE // 2)
+    even = is_even(place_ref, 1)
+    read = plane_reader(
+        is_even(place_ref, 0), shift_ref, physical_ref, design_ref, passive_ref, x_first, x_second
+    )
+    for f in range(4):
+        for p in range(NODES):
+            index = NODES * f + p
+            ext_ref[f, p, 0:SY, 0:SZ] = read(index)
+            ext_ref[f, p, 0:SY, SZ:LANES] = jnp.where(keep, side[index], 0.0)
+            ext_ref[f, p, SY:ROWS, 0:SZ] = row_tile(even, y_first, y_second, index)
+            ext_ref[f, p, SY:ROWS, SZ:LANES] = jnp.where(keep, y_side[index], 0.0)
     scale = penalty * (1.0 - stiff_floor)
 
-    @pl.loop(0, SX + 4)
+    @pl.loop(0, ELEMENTS)
     def _(p):
         modes = {}
         for d in range(3):
@@ -250,58 +306,100 @@
             energy = line * line if energy is None else energy + line * line
         density = ext_ref[3, p]
         sens = scale * density * density * energy * inverse_ref[p]
-        sens_ref[p] = sens
+        sens_ref[p] = sens[0:SY]
         near, far = row_pairs(sens)
-        near_ref[p] = near
-        far_ref[p] = far
-
-    for p in range(SX):
-        filtered = filtered_plane(
-            lambda q: sens_ref[q, 0:SY], lambda q: near_ref[q, 0:SY], lambda q: far_ref[q, 0:SY], p + 2
-        )[:, 0:SZ]
-        design = design_ref[p]
-        solid = passive_ref[p] == 1
-        scaled = design * jnp.sqrt(filtered / volume_ref[p])
+        near_ref[p] = near[0:SY]
+        far_ref[p] = far[0:SY]
+
+    for p in range(CHOSEN):
+        filtered = filtered_plane(lambda q: sens_ref[q], lambda q: near_ref[q], lambda q: far_ref[q], p + 2)
+        index = 4 * NODES + p
+        design = jnp.concatenate([read(index), side[index]], axis=1)
+        solid = jnp.concatenate([read(index + CHOSEN), side[index + CHOSEN]], axis=1) > 0.5
+        inside = inverse_ref[p + 2, 0:SY] > 0.0
+        scaled = design * jnp.sqrt(filtered / jnp.where(inside, volume_ref[p], 1.0))
         floor_bound = jnp.where(solid, 1.0, jnp.maximum(0.0, design - move_limit))
         ceiling = jnp.where(solid, 1.0, jnp.minimum(1.0, design + move_limit))
         for f, value in enumerate((scaled, floor_bound, ceiling)):
+            value = jnp.where(inside, value, 0.0)
             out_ref[f, p] = value
-            if p < 2:
-                down_ref[f, p] = value
-            if p >= SX - 3:
-                up_ref[f, p - (SX - 3)] = value
-
-
-def volumes_kernel(exp_ref, bounds_ref, volume_ref, out_ref, weighted_ref, sums_ref):
-    for p in range(SX):
-        weight = volume_ref[p]
-        for f in range(3):
-            weighted = weight * bounds_ref[f, p]
-            for h in range(2):
-                weighted_ref[f, 2 * p + h] = weighted[:, h * 128 : (h + 1) * 128]
-
-    @pl.loop(0, POINTS // 8)
-    def _(g):
-        factors = [exp_ref[g * 8 + j] for j in range(8)]
-        totals = [None] * 8
-        for v in range(2 * SX):
-            scaled, floor_bound, ceiling = weighted_ref[0, v], weighted_ref[1, v], weighted_ref[2, v]
-            for j in range(8):
-                value = jnp.minimum(jnp.maximum(scaled * factors[j], floor_bound), ceiling)
-                totals[j] = value if totals[j] is None else totals[j] + value
-        rows = [jnp.sum(total, axis=0, keepdims=True) for total in totals]
-        sums_ref[pl.ds(pl.multiple_of(g * 8, 8), 8), :] = jnp.concatenate(rows, axis=0)
-
-    copies = out_ref.shape[0]
-    result = lax.dot_general(
-        jnp.ones((copies, 128), F32),
-        sums_ref[...],
-        (((1,), (1,)), ((), ())),
+            row = 3 * (CHOSEN * f + p)
+            place_pair(even, first_ref, second_ref, value[SY - 3 :], value[0:3], slice(row, row + 3))
+
+
+def three_parts(value):
+    first = value.astype(jnp.bfloat16).astype(F32)
+    second = (value - first).astype(jnp.bfloat16).astype(F32)
+    return first, second, value - first - second
+
+
+def volumes_kernel(bounds_ref, volume_ref, out_ref, high_ref, low_ref, value_ref):
+    step = (log_upper - log_lower) / POINTS
+    ceilings = jnp.zeros((SY, 128), F32)
+    for v in range(2 * SX):
+        place = (3 + v // 2, slice(None), slice(128 * (v % 2), 128 * (v % 2 + 1)))
+        weight = volume_ref[place]
+        scaled, floor_bound, ceiling = [bounds_ref[(f,) + place] for f in range(3)]
+        ceilings = ceilings + weight * ceiling
+        log_scaled = jnp.log(jnp.maximum(scaled, 1e-30))
+        for t, bound in enumerate((ceiling, floor_bound)):
+            reached = (2.0 * (log_scaled - jnp.log(jnp.maximum(bound, 1e-30))) - log_lower) / step
+            index = jnp.minimum(jnp.maximum(jnp.ceil(reached), 1.0), POINTS + 1.0) - 1.0
+            index = jnp.where(bound > 0.0, index, float(POINTS))
+            high = jnp.floor(index * (1.0 / 128.0))
+            high_ref[t, v] = high
+            low_ref[t, v] = index - 128.0 * high
+            sign = -1.0 if t == 0 else 1.0
+            parts = three_parts(sign * weight * bound) + three_parts(-sign * weight * scaled)
+            for n, part in enumerate(parts):
+                value_ref[t, n, v] = part
+
+    rows = lax.broadcasted_iota(jnp.int32, (8, 128), 0).astype(F32)
+    columns = lax.broadcasted_iota(jnp.int32, (128, 128), 0).astype(F32)
+
+    def add_group(v, total):
+        lefts, rights = [], []
+        for t in range(2):
+            for r in range(SY):
+                hit = rows == high_ref[t, v, r : r + 1, :]
+                left = [jnp.where(hit, value_ref[t, n, v, r : r + 1, :], 0.0) for n in range(6)]
+                lefts.append(jnp.concatenate(left, axis=0).astype(jnp.bfloat16))
+                right = jnp.where(columns == low_ref[t, v, r : r + 1, :], 1.0, 0.0)
+                rights.append(right.astype(jnp.bfloat16))
+        return total + lax.dot_general(
+            jnp.concatenate(lefts, axis=1),
+            jnp.concatenate(rights, axis=1),
+            (((1,), (1,)), ((), ())),
+            preferred_element_type=F32,
+        )
+
+    total = lax.fori_loop(0, 2 * SX, add_group, jnp.zeros((48, 128), F32))
+    constant = total[0:8] + total[8:16] + total[16:24]
+    slope = total[24:32] + total[32:40] + total[40:48]
+    upto = jnp.where(
+        lax.broadcasted_iota(jnp.int32, (128, 128), 0) <= lax.broadcasted_iota(jnp.int32, (128, 128), 1), 1.0, 0.0
+    )
+    running = lax.dot_general(
+        jnp.concatenate([constant, slope], axis=0),
+        upto,
+        (((1,), (0,)), ((), ())),
         precision=lax.Precision.HIGHEST,
         preferred_element_type=F32,
     )
-    for i in range(8):
-        out_ref[:, i, :] = result[:, i * 128 : (i + 1) * 128]
+    row = lax.broadcasted_iota(jnp.int32, (8, 128), 0)
+    lane = lax.broadcasted_iota(jnp.int32, (8, 128), 1)
+    cumulated = []
+    for part in (running[0:8], running[8:16]):
+        ends = jnp.broadcast_to(part[:, 127:128], (8, 128))
+        before = ends
+        for shift in (1, 2, 4):
+            before = before + jnp.where(row >= shift, rolled(before, -shift, 0), 0.0)
+        cumulated.append(part + (before - ends))
+    index = (row * 128 + lane + 1).astype(F32)
+    factor = jnp.exp(-0.5 * (log_lower + step * index))
+    result = jnp.sum(ceilings) + cumulated[0] + factor * cumulated[1]
+    for i in range(out_ref.shape[0]):
+        out_ref[i] = result
 
 
 def repeat_kernel(part_ref, out_ref):
@@ -313,30 +411,33 @@
 
 
 def final_kernel(
-    place_ref, part_ref, own_ref, x_low, x_high, y_low, y_high, side, inverse_ref, mark_ref, new_design_ref,
-    new_physical_ref, blocks_ref, ext_ref, near_ref, far_ref, stiff_ref, *, factors, target
+    place_ref, part_ref, own_ref, y_first, y_second, inverse_ref, mark_ref, new_design_ref, new_physical_ref,
+    blocks_ref, chosen_ref, near_ref, far_ref, stiff_ref, *, factors, target
 ):
     total = part_ref[0]
     for i in range(1, part_ref.shape[0]):
         total = total + part_ref[i]
     low_end = jnp.minimum(jnp.sum(jnp.where(total > target, 1.0, 0.0)), POINTS - 1.0)
     multiplier = log_lower + (log_upper - log_lower) / POINTS * (low_end + 0.5)
-    factor = jnp.exp(jnp.broadcast_to(-0.5 * multiplier, (ROWS, LANES)))
-    keep = side_mask(place_ref[2], 2, 3)
-    assemble(ext_ref, 3, 3, 2, 2, 3, lambda f, p: own_ref[f, p], x_low, x_high, y_low, y_high, side, keep)
-    planes = SX + 5
-    for p in range(planes):
-        chosen = jnp.minimum(jnp.maximum(ext_ref[0, p] * factor, ext_ref[1, p]), ext_ref[2, p])
-        ext_ref[0, p] = chosen
+    factor = jnp.exp(jnp.broadcast_to(-0.5 * multiplier, (SY, LANES)))
+    even = is_even(place_ref, 1)
+    for p in range(CHOSEN):
+        tiles = []
+        own = [own_ref[f, p] for f in range(3)]
+        beside = [row_tile(even, y_first, y_second, CHOSEN * f + p) for f in range(3)]
+        for scaled, floor_bound, ceiling in (own, beside):
+            tiles.append(jnp.minimum(jnp.maximum(scaled * factor, floor_bound), ceiling))
+        chosen = jnp.concatenate(tiles, axis=0)
+        chosen_ref[p] = chosen
         near, far = row_pairs(chosen)
         near_ref[p] = near
         far_ref[p] = far
         if 3 <= p < SX + 3:
-            new_design_ref[p - 3] = chosen[0:SY, 0:SZ]
+            new_design_ref[p - 3] = tiles[0][:, 0:SZ]
     for p in range(SX + 1):
-        inverse = inverse_ref[p + 1]
+        inverse = inverse_ref[p + 4]
         density = (
-            filtered_plane(lambda q: ext_ref[0, q], lambda q: near_ref[q], lambda q: far_ref[q], p + 2) * inverse
+            filtered_plane(lambda q: chosen_ref[q], lambda q: near_ref[q], lambda q: far_ref[q], p + 2) * inverse
         )
         if p >= 1:
             new_physical_ref[p - 1] = density[0:SY, 0:SZ]
@@ -378,66 +479,70 @@
     )
 
 
-def exchange(up, down, axis):
+def exchange(first, second, axis):
     count = lax.axis_size(axis)
-    low = lax.ppermute(up, axis, [(i, i + 1) for i in range(count - 1)])
-    high = lax.ppermute(down, axis, [(i + 1, i) for i in range(count - 1)])
-    return low, high
-
-
-def side_lanes(ext, place_z):
-    half = jnp.where(place_z == 0, ext[..., SZ - SIDE : SZ], ext[..., 0:SIDE])
-    return lax.ppermute(half, "gz", [(0, 1), (1, 0)])
+    results = []
+    for start, faces in enumerate((first, second)):
+        pairs = [(i, i + 1) for i in range(start, count - 1, 2)]
+        results.append(lax.ppermute(faces, axis, pairs + [(j, i) for i, j in pairs]))
+    return results
+
+
+def other_core(values):
+    return lax.ppermute(values, "gz", [(0, 1), (1, 0)])
 
 
 def body(displacement, physical, design, passive, supports):
     assert design.shape == (SX, SY, SZ) and lax.axis_size("gz") == 2
     sizes = [lax.axis_size(axis) for axis in ("gx", "gy", "gz")]
     extents = (SX * sizes[0], SY * sizes[1], SZ * sizes[2])
-    place_z = lax.axis_index("gz")
-    place = jnp.stack([lax.axis_index("gx"), lax.axis_index("gy"), place_z]).astype(jnp.int32)
-
-    fields = jnp.concatenate([displacement, physical[None]], axis=0)
-    x_low, x_high = exchange(fields[:, SX - 2 :], fields[:, 0:3], "gx")
-
-    frame = (SX + 4, ROWS, LANES)
+    place = jnp.stack([lax.axis_index(axis) for axis in ("gx", "gy", "gz")]).astype(jnp.int32)
+    own = (displacement, physical, design, passive)
+
+    x_faces = exchange(*call(faces_x_kernel, 1, 4, [(26, SY, SZ)] * 2, [], 10**6)(place, *own), "gx")
+    frame = (ELEMENTS, ROWS, LANES)
+    own_frame = (ELEMENTS, SY, LANES)
     inverse, volume_weight, marks = call(
         functools.partial(weights_kernel, extents=extents), 1, 1,
-        [frame, (SX, SY, SZ), (SX, SY, SZ)], [frame, frame], 10**7,
+        [frame, (CHOSEN, SY, LANES), (SX, SY, SZ)], [own_frame, own_frame], 10**7,
     )(place, supports.reshape(1, -1))
-
-    wide = jnp.concatenate([x_low, fields, x_high], axis=1)
-    y_low, y_high = exchange(wide[:, :, SY - 2 :], wide[:, :, 0:3], "gy")
-    filler = jnp.zeros((4, SX + 5, 3, SZ), F32)
-    side = side_lanes(jnp.concatenate([wide, y_high, filler, y_low], axis=2), place_z)
-    bounds, up, down = call(
-        functools.partial(design_kernel, squares=energy_squares()), 1, 11,
-        [(3, SX, SY, SZ), (3, 3, SY, SZ), (3, 2, SY, SZ)], [(4, SX + 5, ROWS, LANES), frame, frame, frame], 10**7,
-    )(place, displacement, physical, x_low, x_high, y_low, y_high, side, inverse, volume_weight, design, passive)
-
-    x_low, x_high = exchange(up, down, "gx")
-    multipliers = log_lower + (log_upper - log_lower) / POINTS * np.arange(1, POINTS + 1)
-    table = jnp.asarray(np.exp(-0.5 * multipliers), F32)
+    x_faces, inverse, volume_weight, marks = lax.optimization_barrier((x_faces, inverse, volume_weight, marks))
+
+    y_shape = (12 * NODES, SZ)
+    *y_faces, side = call(
+        faces_y_kernel, 1, 6, [y_shape, y_shape, (4 * NODES + 2 * CHOSEN, SY, SIDE)], [], 10**6
+    )(place, *own, *x_faces)
+    y_faces = exchange(*y_faces, "gy")
+    side = other_core(side)
+    (y_side,) = call(faces_z_kernel, 1, 2, [(4 * NODES, SY, SIDE)], [], 10**6)(place, *y_faces)
+    y_side = other_core(y_side)
+
+    y_shape = (9 * CHOSEN, LANES)
+    bounds, *y_bounds = call(
+        functools.partial(design_kernel, squares=energy_squares()), 1, 12,
+        [(3, CHOSEN, SY, LANES), y_shape, y_shape],
+        [(4, NODES, ROWS, LANES), own_frame, own_frame, own_frame], 10**7,
+    )(place, *own, *x_faces, *y_faces, side, y_side, inverse, volume_weight)
+
+    y_bounds = exchange(*y_bounds, "gy")
     inner, outer = sizes[1] * sizes[2], sizes[0]
+    elements = (2 * SX, SY, 128)
     (part,) = call(
-        volumes_kernel, 1, 2, [(inner, 8, 128)], [(3, 2 * SX, SY, 128), (POINTS, 128)], 10**8,
-    )(table, bounds, volume_weight)
+        volumes_kernel, 0, 2, [(inner, 8, 128)], [(2,) + elements, (2,) + elements, (2, 6) + elements], 10**8,
+    )(bounds, volume_weight)
     part = lax.all_to_all(part, ("gy", "gz"), 0, 0, tiled=True)
-    wide = jnp.concatenate([x_low, bounds, x_high], axis=1)
-    y_low, y_high = exchange(wide[:, :, SY - 3 :], wide[:, :, 0:2], "gy")
     (part,) = call(repeat_kernel, 0, 1, [(outer, 8, 128)], [], 10**5)(part)
+    y_bounds, part = lax.optimization_barrier((y_bounds, part))
     part = lax.all_to_all(part, "gx", 0, 0, tiled=True)
-    filler = jnp.zeros((3, SX + 5, 3, SZ), F32)
-    side = side_lanes(jnp.concatenate([wide, y_high, filler, y_low], axis=2), place_z)
-
-    ext = (SX + 5, ROWS, LANES)
+
+    chosen = (CHOSEN, ROWS, LANES)
     new_design, new_physical, node_blocks = call(
         functools.partial(
             final_kernel, factors=[float(f) for f in corner_factors()],
             target=volume_share * (extents[0] * extents[1] * extents[2]),
-        ), 1, 9,
-        [(SX, SY, SZ), (SX, SY, SZ), (6, SX, SY, SZ)], [(3,) + ext, ext, ext, (SX + 1, ROWS, LANES)], 10**7,
-    )(place, part, bounds, x_low, x_high, y_low, y_high, side, inverse, marks)
+        ), 1, 6,
+        [(SX, SY, SZ), (SX, SY, SZ), (6, SX, SY, SZ)], [chosen, chosen, chosen, (SX + 1, ROWS, LANES)], 10**7,
+    )(place, part, bounds, *y_bounds, inverse, marks)
     return (new_design, new_physical, node_blocks)
 
 

time: 97 us -> 75.2 us (0.78)
  starting transfers between devices: 29.7 us -> 17.3 us
  waiting for transfers between devices: 10.3 us -> 3.33 us
  Pallas kernels: 18.2 us -> 15.3 us
  local copies, waits for them, and re-layouts: 0.8 us -> 3.46 us
  other arithmetic: 1.55 us -> 0.08 us
    ppermute x10 -> x8, starting transfers between devices: 29.7 us -> 17.3 us  [the longest x6 12.2 us: exchange(): lax.ppermute(faces, axis, pairs + [(j, i) for i, j in pairs])]
    ppermute x10 -> x8, waiting for transfers between devices: 10.3 us -> 3.33 us  [the longest x6 2.12 us: exchange(): lax.ppermute(faces, axis, pairs + [(j, i) for i, j in pairs])]
    pallas_call x3 -> x6, Pallas kernels: 16.1 us -> 13.2 us  [the longest x1 5.17 us: body(): call(volumes_kernel, 0, 2, [(inner, 8, 128)], [(2,) + elements, (2,) + el...]
    unnamed x14 -> x12, local copies, waits for them, and re-layouts: 0.66 us -> 3.46 us
    all_to_all x1, blocking collectives: 19.2 us -> 17.3 us  [body(): part = lax.all_to_all(part, 'gx', 0, 0, tiled=True)]
    all_to_all x1, blocking collectives: 15.9 us -> 17.3 us  [body(): part = lax.all_to_all(part, ('gy', 'gz'), 0, 0, tiled=True)]
    concatenate x4 -> x0, other arithmetic: 1.32 us -> none  [the longest x1 0.95 us: body(): fields = jnp.concatenate([displacement, physical[None]], axis=0)]
  transfers between devices with their start and end apart: 10 -> 8, of which waited for: 5 -> 3; matrix products, arithmetic and copies ran while one was open for 0% -> 0% of each run, Pallas kernels for 13% -> 10%
where the time goes in v3:
time: 75.2 us; the launch traced here: 74.8 us
  blocking collectives  34.6 us (46%)
  starting transfers between devices  17.3 us (23%)
  Pallas kernels  15.3 us (20%)
  local copies, waits for them, and re-layouts  3.46 us (5%)
  waiting for transfers between devices  3.33 us (4%)
    all_to_all x1, blocking collectives, body(): part = lax.all_to_all(part, ('gy', 'gz'), 0, 0, tiled=True)  17.3 us
    all_to_all x1, blocking collectives, body(): part = lax.all_to_all(part, 'gx', 0, 0, tiled=True)  17.3 us
    ppermute x6, starting transfers between devices, exchange(): lax.ppermute(faces, axis, pairs + [(j, i) for i, j in pairs])  12.2 us
    pallas_call x1, Pallas kernels, body(): call(volumes_kernel, 0, 2, [(inner, 8, 128)], [(2,) + elements, (2,) + el...  5.17 us
    ppermute x2, starting transfers between devices, other_core(): return lax.ppermute(values, 'gz', [(0, 1), (1, 0)])  5.11 us
    pallas_call x1, Pallas kernels, body(): call(functools.partial(design_kernel, squares=energy_squares()), 1, 12, [...  4.35 us
    unnamed x12, local copies, waits for them, and re-layouts  3.46 us
    ppermute x6, waiting for transfers between devices, exchange(): lax.ppermute(faces, axis, pairs + [(j, i) for i, j in pairs])  2.12 us
  transfers between devices with their start and end apart: 8, of which 3 were waited for; matrix products, arithmetic and copies ran while one was open for 0% of the time, Pallas kernels for 10%

profile of v3, /device:TPU:1, one launch (start us, length us, event | category | flops | bytes accessed | tf_op | source)
XLA Modules:
  0.0 74.8 jit_solution(469769268332769609)
XLA Ops:
  0.6 0.1 pad_add_fusion.place_ref
  0.7 0.0 copy-start
  0.7 0.9 %copy-done = f32[3,8,8,256]{3,2,1,0:T(8,128)S(1)} copy-done((f32[3,8,8,256]{3,2,1,0:T(8,128)S(1)}, f32[3,8,8,256]{3,2,1,0:T(8,128)}, u32[]{:S(2)}) %copy-start) | copy-done | bytes 196632
  1.6 0.0 copy-start.2
  1.6 0.8 %copy-done.2 = f32[8,8,256]{2,1,0:T(8,128)S(1)} copy-done((f32[8,8,256]{2,1,0:T(8,128)S(1)}, f32[8,8,256]{2,1,0:T(8,128)}, u32[]{:S(2)}) %copy-start.2) | copy-done | bytes 65560
  2.5 0.0 copy-start.3
  2.5 0.8 %copy-done.3 = f32[8,8,256]{2,1,0:T(8,128)S(1)} copy-done((f32[8,8,256]{2,1,0:T(8,128)S(1)}, f32[8,8,256]{2,1,0:T(8,128)}, u32[]{:S(2)}) %copy-start.3) | copy-done | bytes 65560
  3.3 0.0 copy-start.4
  3.3 0.8 %copy-done.4 = s32[8,8,256]{2,1,0:T(8,128)S(1)} copy-done((s32[8,8,256]{2,1,0:T(8,128)S(1)}, s32[8,8,256]{2,1,0:T(8,128)}, u32[]{:S(2)}) %copy-start.4) | copy-done | bytes 65560
  4.2 0.0 copy-start.1
  4.2 0.6 shard_map.76
  4.7 0.0 copy-start.5
  4.8 2.2 %collective-permute-start = (f32[26,8,256]{2,1,0:T(8,128)S(1)}, f32[26,8,256]{2,1,0:T(8,128)S(1)}, u32[]{:S(2)}, u32[]{:S(2)}) collective-permute-start(f32[26,8,256]{2,1,0:T(8,128)S(1)} %get-tuple-element.22), channel_id=1, source_target_pairs={{0,16},{32,48},{64,80},{96,112},{128,144},{160,176},{192,208},{224... | collective-permute-start | bytes 638984 | tf_op jit(solution)/shard_map/ppermute | solution.py:487
  7.0 0.7 collective-permute-start.1
  7.6 0.0 copy-done.5
  7.7 1.7 %shard_map.77 = (f32[17,16,384]{2,1,0:T(8,128)S(1)}, f32[13,8,384]{2,1,0:T(8,128)S(1)}, f32[8,8,256]{2,1,0:T(8,128)S(1)}) custom-call(s32[3]{0:T(128)S(1)} %pad_add_fusion.place_ref, s32[1,1024]{1,0:T(1,128)S(1)} %bitcast.4), custom_call_target="tpu_custom_call" | custom-call | flops 10000000 | bytes 1000000 | tf_op jit(solution)/shard_map/pallas_call | solution.py:505
  9.3 1.4 %collective-permute-done.x_first = f32[26,8,256]{2,1,0:T(8,128)S(1)} collective-permute-done((f32[26,8,256]{2,1,0:T(8,128)S(1)}, f32[26,8,256]{2,1,0:T(8,128)S(1)}, u32[]{:S(2)}, u32[]{:S(2)}) %collective-permute-start) | collective-permute-done | bytes 213024 | tf_op jit(solution)/shard_map/ppermute | solution.py:487
  10.7 0.0 collective-permute-done.1.x_second
  10.7 0.0 copy-done.1
  10.7 0.7 shard_map.78
  11.4 2.8 %collective-permute-start.2 = (f32[216,256]{1,0:T(8,128)S(1)}, f32[216,256]{1,0:T(8,128)S(1)}, u32[]{:S(2)}, u32[]{:S(2)}) collective-permute-start(f32[216,256]{1,0:T(8,128)S(1)} %get-tuple-element.29), channel_id=1, source_target_pairs={{0,2},{4,6},{8,10},{12,14},{2,0},{6,4},{10,8},{14,12},{1,3},{5,7},... | collective-permute-start | bytes 663560 | tf_op jit(solution)/shard_map/ppermute | solution.py:487
  14.2 0.7 collective-permute-start.3
  14.9 1.9 %collective-permute-start.4 = (f32[98,8,128]{2,1,0:T(8,128)S(1)}, f32[98,8,128]{2,1,0:T(8,128)S(1)}, u32[]{:S(2)}, u32[]{:S(2)}) collective-permute-start(f32[98,8,128]{2,1,0:T(8,128)S(1)} %get-tuple-element.31), channel_id=1, source_target_pairs={{0,1},{1,0},{2,3},{3,2},{4,5},{5,4},{6,7},{7,6},{8,9},{9,8},{10,11... | collective-permute-start | bytes 1204232 | tf_op jit(solution)/shard_map/ppermute | solution.py:492
  16.8 0.7 collective-permute-done.2.y_first
  17.6 0.0 collective-permute-done.3.y_second
  17.6 0.7 shard_map.79
  18.3 3.2 %collective-permute-start.5 = (f32[72,8,128]{2,1,0:T(8,128)S(1)}, f32[72,8,128]{2,1,0:T(8,128)S(1)}, u32[]{:S(2)}, u32[]{:S(2)}) collective-permute-start(f32[72,8,128]{2,1,0:T(8,128)S(1)} %shard_map.79), channel_id=1, source_target_pairs={{0,1},{1,0},{2,3},{3,2},{4,5},{5,4},{6,7},{7,6},{8,9},{9,8},{10,11... | collective-permute-start | bytes 884744 | tf_op jit(solution)/shard_map/ppermute | solution.py:492
  21.5 0.0 collective-permute-done.4.side
  21.5 1.2 %collective-permute-done.5.y_side = f32[72,8,128]{2,1,0:T(8,128)S(1)} collective-permute-done((f32[72,8,128]{2,1,0:T(8,128)S(1)}, f32[72,8,128]{2,1,0:T(8,128)S(1)}, u32[]{:S(2)}, u32[]{:S(2)}) %collective-permute-start.5) | collective-permute-done | bytes 294944 | tf_op jit(solution)/shard_map/ppermute | solution.py:492
  22.7 4.4 %shard_map.80 = (f32[3,13,8,384]{3,2,1,0:T(8,128)S(1)}, f32[117,384]{1,0:T(8,128)S(1)}, f32[117,384]{1,0:T(8,128)S(1)}) custom-call(s32[3]{0:T(128)S(1)} %pad_add_fusion.place_ref, f32[3,8,8,256]{3,2,1,0:T(8,128)S(1)} %copy-done.1, f32[8,8,256]{2,1,0:T(8,128)S(1)} %copy-done.2, f32[8,8,256]{2,1,0:T(8,128)S(1)} %copy-done.3, s32[8,8,256]{2,1,0:T(8,128)S(1)} %copy-done.4, ...), custom_call_target="tpu_custom_call" | custom-call | flops 10000000 | bytes 1000000 | tf_op jit(solution)/shard_map/pallas_call | solution.py:521
  27.0 5.2 %collective-permute-start.6 = (f32[117,384]{1,0:T(8,128)S(1)}, f32[117,384]{1,0:T(8,128)S(1)}, u32[]{:S(2)}, u32[]{:S(2)}) collective-permute-start(f32[117,384]{1,0:T(8,128)S(1)} %get-tuple-element.34), channel_id=1, source_target_pairs={{0,2},{4,6},{8,10},{12,14},{2,0},{6,4},{10,8},{14,12},{1,3},{5,7},... | collective-permute-start | bytes 539144 | tf_op jit(solution)/shard_map/ppermute | solution.py:487
  32.2 0.7 collective-permute-start.7
  32.9 5.2 %shard_map.81 = f32[16,8,128]{2,1,0:T(8,128)S(1)} custom-call(f32[3,13,8,384]{3,2,1,0:T(8,128)S(1)} %get-tuple-element.36.bounds_ref.own_ref, f32[13,8,384]{2,1,0:T(8,128)S(1)} %get-tuple-element.33.volume_ref), custom_call_target="tpu_custom_call" | custom-call | flops 100000000 | bytes 1000000 | tf_op jit(solution)/shard_map/pallas_call | solution.py:530
  38.1 17.3 %all_to_all.10.part_ref = f32[16,8,128]{2,1,0:T(8,128)S(1)} all-to-all(f32[16,8,128]{2,1,0:T(8,128)S(1)} %shard_map.81), channel_id=1, replica_groups=mesh['gx'=16,'gy'=8,'gz'=2] {'gy','gz'}, dimensions={0} | all-to-all | bytes 131072 | tf_op jit(solution)/shard_map/all_to_all | solution.py:533
  55.4 0.0 collective-permute-done.6.y_first
  55.4 0.0 collective-permute-done.7.y_second
  55.4 17.3 %all_to_all.11.part_ref = f32[16,8,128]{2,1,0:T(8,128)S(1)} all-to-all(f32[16,8,128]{2,1,0:T(8,128)S(1)} %shard_map.82), channel_id=1, replica_groups=mesh['gx'=16,'gy'=8,'gz'=2] {'gx'}, dimensions={0} | all-to-all | bytes 131072 | tf_op jit(solution)/shard_map/all_to_all | solution.py:536
  72.7 2.1 %shard_map.83 = (f32[8,8,256]{2,1,0:T(8,128)}, f32[8,8,256]{2,1,0:T(8,128)}, f32[6,8,8,256]{3,2,1,0:T(8,128)}) custom-call(s32[3]{0:T(128)S(1)} %pad_add_fusion.place_ref, f32[16,8,128]{2,1,0:T(8,128)S(1)} %all_to_all.11.part_ref, f32[3,13,8,384]{3,2,1,0:T(8,128)S(1)} %get-tuple-element.36.bounds_ref.own_ref, f32[117,384]{1,0:T(8,128)S(1)} %collective-permute-done.6.y_first, ...), custom_call_target="tpu_custom_call" | custom-call | flops 10000000 | bytes 1000000 | tf_op jit(solution)/shard_map/pallas_call | solution.py:539
  (1 shorter events, 0.0 us)
Async XLA Ops:
  0.7 0.9 %copy-start = (f32[3,8,8,256]{3,2,1,0:T(8,128)S(1)}, f32[3,8,8,256]{3,2,1,0:T(8,128)}, u32[]{:S(2)}) copy-start(f32[3,8,8,256]{3,2,1,0:T(8,128)} %shift_ref.5) | copy-start | bytes 589828
  1.6 0.8 %copy-start.2 = (f32[8,8,256]{2,1,0:T(8,128)S(1)}, f32[8,8,256]{2,1,0:T(8,128)}, u32[]{:S(2)}) copy-start(f32[8,8,256]{2,1,0:T(8,128)} %physical_ref.5) | copy-start | bytes 196612
  2.5 0.8 %copy-start.3 = (f32[8,8,256]{2,1,0:T(8,128)S(1)}, f32[8,8,256]{2,1,0:T(8,128)}, u32[]{:S(2)}) copy-start(f32[8,8,256]{2,1,0:T(8,128)} %design_ref.5) | copy-start | bytes 196612
  3.3 0.8 %copy-start.4 = (s32[8,8,256]{2,1,0:T(8,128)S(1)}, s32[8,8,256]{2,1,0:T(8,128)}, u32[]{:S(2)}) copy-start(s32[8,8,256]{2,1,0:T(8,128)} %passive_ref.5) | copy-start | bytes 196612
  4.2 6.5 %copy-start.1 = (f32[3,8,8,256]{3,2,1,0:T(8,128)S(1)}, f32[3,8,8,256]{3,2,1,0:T(8,128)}, u32[]{:S(2)}) copy-start(f32[3,8,8,256]{3,2,1,0:T(8,128)} %shift_ref.5) | copy-start | bytes 589828
  4.7 2.9 %copy-start.5 = (s32[1024]{0:T(1024)S(1)}, s32[1024]{0:T(1024)}, u32[]{:S(2)}) copy-start(s32[1024]{0:T(1024)} %param.9) | copy-start | bytes 12292
  4.8 5.9 %collective-permute-start = (f32[26,8,256]{2,1,0:T(8,128)S(1)}, f32[26,8,256]{2,1,0:T(8,128)S(1)}, u32[]{:S(2)}, u32[]{:S(2)}) collective-permute-start(f32[26,8,256]{2,1,0:T(8,128)S(1)} %get-tuple-element.22), channel_id=1, source_target_pairs={{0,16},{32,48},{64,80},{96,112},{128,144},{160,176},{192,208},{224... | collective-permute-start | bytes 638984 | tf_op jit(solution)/shard_map/ppermute | solution.py:487
  7.0 3.7 %collective-permute-start.1 = (f32[26,8,256]{2,1,0:T(8,128)S(1)}, f32[26,8,256]{2,1,0:T(8,128)S(1)}, u32[]{:S(2)}, u32[]{:S(2)}) collective-permute-start(f32[26,8,256]{2,1,0:T(8,128)S(1)} %get-tuple-element.23), channel_id=1, source_target_pairs={{16,32},{48,64},{80,96},{112,128},{144,160},{176,192},{208,224},{3... | collective-permute-start | bytes 638984 | tf_op jit(solution)/shard_map/ppermute | solution.py:487
  11.4 6.1 %collective-permute-start.2 = (f32[216,256]{1,0:T(8,128)S(1)}, f32[216,256]{1,0:T(8,128)S(1)}, u32[]{:S(2)}, u32[]{:S(2)}) collective-permute-start(f32[216,256]{1,0:T(8,128)S(1)} %get-tuple-element.29), channel_id=1, source_target_pairs={{0,2},{4,6},{8,10},{12,14},{2,0},{6,4},{10,8},{14,12},{1,3},{5,7},... | collective-permute-start | bytes 663560 | tf_op jit(solution)/shard_map/ppermute | solution.py:487
  14.2 3.3 %collective-permute-start.3 = (f32[216,256]{1,0:T(8,128)S(1)}, f32[216,256]{1,0:T(8,128)S(1)}, u32[]{:S(2)}, u32[]{:S(2)}) collective-permute-start(f32[216,256]{1,0:T(8,128)S(1)} %get-tuple-element.30), channel_id=1, source_target_pairs={{2,4},{6,8},{10,12},{4,2},{8,6},{12,10},{3,5},{7,9},{11,13},{5,3},... | collective-permute-start | bytes 663560 | tf_op jit(solution)/shard_map/ppermute | solution.py:487
  14.9 6.6 %collective-permute-start.4 = (f32[98,8,128]{2,1,0:T(8,128)S(1)}, f32[98,8,128]{2,1,0:T(8,128)S(1)}, u32[]{:S(2)}, u32[]{:S(2)}) collective-permute-start(f32[98,8,128]{2,1,0:T(8,128)S(1)} %get-tuple-element.31), channel_id=1, source_target_pairs={{0,1},{1,0},{2,3},{3,2},{4,5},{5,4},{6,7},{7,6},{8,9},{9,8},{10,11... | collective-permute-start | bytes 1204232 | tf_op jit(solution)/shard_map/ppermute | solution.py:492
  18.3 4.4 %collective-permute-start.5 = (f32[72,8,128]{2,1,0:T(8,128)S(1)}, f32[72,8,128]{2,1,0:T(8,128)S(1)}, u32[]{:S(2)}, u32[]{:S(2)}) collective-permute-start(f32[72,8,128]{2,1,0:T(8,128)S(1)} %shard_map.79), channel_id=1, source_target_pairs={{0,1},{1,0},{2,3},{3,2},{4,5},{5,4},{6,7},{7,6},{8,9},{9,8},{10,11... | collective-permute-start | bytes 884744 | tf_op jit(solution)/shard_map/ppermute | solution.py:492
  27.0 28.4 %collective-permute-start.6 = (f32[117,384]{1,0:T(8,128)S(1)}, f32[117,384]{1,0:T(8,128)S(1)}, u32[]{:S(2)}, u32[]{:S(2)}) collective-permute-start(f32[117,384]{1,0:T(8,128)S(1)} %get-tuple-element.34), channel_id=1, source_target_pairs={{0,2},{4,6},{8,10},{12,14},{2,0},{6,4},{10,8},{14,12},{1,3},{5,7},... | collective-permute-start | bytes 539144 | tf_op jit(solution)/shard_map/ppermute | solution.py:487
  32.2 23.2 %collective-permute-start.7 = (f32[117,384]{1,0:T(8,128)S(1)}, f32[117,384]{1,0:T(8,128)S(1)}, u32[]{:S(2)}, u32[]{:S(2)}) collective-permute-start(f32[117,384]{1,0:T(8,128)S(1)} %get-tuple-element.35), channel_id=1, source_target_pairs={{2,4},{6,8},{10,12},{4,2},{8,6},{12,10},{3,5},{7,9},{11,13},{5,3},... | collective-permute-start | bytes 539144 | tf_op jit(solution)/shard_map/ppermute | solution.py:487

commit v4 on v3

--- a/solution.py
+++ b/solution.py
@@ -146,11 +146,11 @@
     return middle + (rolled(near, 1, 1) + rolled(near, -1, 1)) + (rolled(far, 2, 1) + rolled(far, -2, 1))
 
 
-def weights_kernel(place_ref, support_ref, inverse_ref, volume_ref, mark_ref, near_ref, far_ref, *, extents):
+def weights_kernel(support_ref, inverse_ref, volume_ref, mark_ref, near_ref, far_ref, *, extents):
     total_x, total_y, total_z = extents
-    first_x = place_ref[0] * SX
-    first_y = place_ref[1] * SY
-    first_z = place_ref[2] * SZ
+    first_x = lax.axis_index("gx") * SX
+    first_y = lax.axis_index("gy") * SY
+    first_z = lax.axis_index("gz") * SZ
     row = lax.broadcasted_iota(jnp.int32, (ROWS, LANES), 0)
     lane = lax.broadcasted_iota(jnp.int32, (ROWS, LANES), 1)
     y = first_y + jnp.where(row < 12, row, row - ROWS)
@@ -196,8 +196,8 @@
         mark_ref[p] = hits[p * SY : (p + 1) * SY]
 
 
-def is_even(place_ref, axis):
-    return place_ref[axis] % 2 == 0
+def is_even(axis):
+    return lax.axis_index(axis) % 2 == 0
 
 
 def place_pair(even, first_ref, second_ref, top, bottom, place):
@@ -215,27 +215,46 @@
     return jnp.concatenate([high, jnp.zeros((SY - 6, low.shape[1]), F32), low], axis=0)
 
 
-def faces_x_kernel(place_ref, shift_ref, physical_ref, design_ref, passive_ref, first_ref, second_ref):
-    even = is_even(place_ref, 0)
-    fields = [shift_ref.at[0], shift_ref.at[1], shift_ref.at[2], physical_ref]
-    for f, field in enumerate(fields):
-        place_pair(even, first_ref, second_ref, field[SX - 5 :], field[0:5], slice(5 * f, 5 * f + 5))
-    for f, field in enumerate((design_ref, passive_ref)):
-        top, bottom = field[SX - 3 :].astype(F32), field[0:3].astype(F32)
-        place_pair(even, first_ref, second_ref, top, bottom, slice(20 + 3 * f, 23 + 3 * f))
-
-
-def plane_reader(even, shift_ref, physical_ref, design_ref, passive_ref, x_first, x_second):
+def faces_x_kernel(
+    shift_ref, physical_ref, design_ref, passive_ref, own_ref, first_ref, second_ref, passive_own, semaphores
+):
+    copies = [
+        pltpu.make_async_copy(source, target, semaphores.at[n])
+        for n, (source, target) in enumerate(
+            (
+                (shift_ref, own_ref.at[0:3]),
+                (physical_ref, own_ref.at[3]),
+                (design_ref, own_ref.at[4]),
+                (passive_ref, passive_own),
+            )
+        )
+    ]
+    for copy in copies:
+        copy.start()
+    for copy in copies:
+        copy.wait()
+    own_ref[5] = passive_own[...].astype(F32)
+    even = is_even("gx")
+    for f in range(6):
+        depth = 5 if f < 4 else 3
+        row = 5 * f if f < 4 else 8 + 3 * f
+        place_pair(
+            even, first_ref, second_ref, own_ref[f, SX - depth :], own_ref[f, 0:depth], slice(row, row + depth)
+        )
+
+
+def plane_reader(own_ref, x_first, x_second):
+    even = is_even("gx")
+
     def read(index):
         if index < 4 * NODES:
-            f, x, depth, base = index // NODES, index % NODES - 5, 5, 5 * (index // NODES)
+            f, x = index // NODES, index % NODES - 5
+            depth, base = 5, 5 * f
         else:
-            f, x = divmod(index - 4 * NODES, CHOSEN)
-            f, x, depth, base = f + 4, x - 3, 3, 20 + 3 * f
+            f, x = 4 + (index - 4 * NODES) // CHOSEN, (index - 4 * NODES) % CHOSEN - 3
+            depth, base = 3, 8 + 3 * f
         if 0 <= x < SX:
-            if f < 3:
-                return shift_ref[f, x]
-            return (physical_ref, design_ref, passive_ref)[f - 3][x].astype(F32)
+            return own_ref[f, x]
         low, high = low_high(even, x_first, x_second, base + (x + depth if x < 0 else x - SX))
         return low if x < 0 else high
 
@@ -243,13 +262,11 @@
 
 
 def faces_y_kernel(
-    place_ref, shift_ref, physical_ref, design_ref, passive_ref, x_first, x_second, first_ref, second_ref, side_ref
+    own_ref, x_first, x_second, first_ref, second_ref, side_ref
 ):
-    even = is_even(place_ref, 1)
-    lower_core = place_ref[2] == 0
-    read = plane_reader(
-        is_even(place_ref, 0), shift_ref, physical_ref, design_ref, passive_ref, x_first, x_second
-    )
+    even = is_even("gy")
+    lower_core = lax.axis_index("gz") == 0
+    read = plane_reader(own_ref, x_first, x_second)
     for index in range(4 * NODES + 2 * CHOSEN):
         plane = read(index)
         if index < 4 * NODES:
@@ -258,25 +275,23 @@
         side_ref[index] = jnp.where(lower_core, plane[:, SZ - SIDE :], plane[:, 0:SIDE])
 
 
-def faces_z_kernel(place_ref, y_first, y_second, side_ref):
-    even = is_even(place_ref, 1)
-    lower_core = place_ref[2] == 0
+def faces_z_kernel(y_first, y_second, side_ref):
+    even = is_even("gy")
+    lower_core = lax.axis_index("gz") == 0
     for index in range(4 * NODES):
         tile = row_tile(even, y_first, y_second, index)
         side_ref[index] = jnp.where(lower_core, tile[:, SZ - SIDE :], tile[:, 0:SIDE])
 
 
 def design_kernel(
-    place_ref, shift_ref, physical_ref, design_ref, passive_ref, x_first, x_second, y_first, y_second, side,
-    y_side, inverse_ref, volume_ref, out_ref, first_ref, second_ref, ext_ref, sens_ref, near_ref, far_ref, *, squares
+    own_ref, x_first, x_second, y_first, y_second, side, y_side, inverse_ref, volume_ref, out_ref, first_ref,
+    second_ref, ext_ref, sens_ref, near_ref, far_ref, *, squares
 ):
     lane = lax.broadcasted_iota(jnp.int32, (SY, SIDE), 1)
-    start = place_ref[2] * (SIDE // 2)
+    start = lax.axis_index("gz") * (SIDE // 2)
     keep = (lane >= start) & (lane < start + SIDE // 2)
-    even = is_even(place_ref, 1)
-    read = plane_reader(
-        is_even(place_ref, 0), shift_ref, physical_ref, design_ref, passive_ref, x_first, x_second
-    )
+    even = is_even("gy")
+    read = plane_reader(own_ref, x_first, x_second)
     for f in range(4):
         for p in range(NODES):
             index = NODES * f + p
@@ -355,7 +370,7 @@
                 value_ref[t, n, v] = part
 
     rows = lax.broadcasted_iota(jnp.int32, (8, 128), 0).astype(F32)
-    columns = lax.broadcasted_iota(jnp.int32, (128, 128), 0).astype(F32)
+    columns = lax.broadcasted_iota(jnp.int32, (128, 128), 0).astype(F32).astype(jnp.bfloat16)
 
     def add_group(v, total):
         lefts, rights = [], []
@@ -364,16 +379,17 @@
                 hit = rows == high_ref[t, v, r : r + 1, :]
                 left = [jnp.where(hit, value_ref[t, n, v, r : r + 1, :], 0.0) for n in range(6)]
                 lefts.append(jnp.concatenate(left, axis=0).astype(jnp.bfloat16))
-                right = jnp.where(columns == low_ref[t, v, r : r + 1, :], 1.0, 0.0)
-                rights.append(right.astype(jnp.bfloat16))
+                low = jnp.broadcast_to(low_ref[t, v, r : r + 1, :], (16, 128)).astype(jnp.bfloat16)
+                low = jnp.concatenate([low] * 8, axis=0)
+                rights.append(jnp.where(columns == low, jnp.bfloat16(1.0), jnp.bfloat16(0.0)))
         return total + lax.dot_general(
+            jnp.concatenate(rights, axis=1),
             jnp.concatenate(lefts, axis=1),
-            jnp.concatenate(rights, axis=1),
             (((1,), (1,)), ((), ())),
             preferred_element_type=F32,
         )
 
-    total = lax.fori_loop(0, 2 * SX, add_group, jnp.zeros((48, 128), F32))
+    total = lax.fori_loop(0, 2 * SX, add_group, jnp.zeros((128, 48), F32), unroll=4).T
     constant = total[0:8] + total[8:16] + total[16:24]
     slope = total[24:32] + total[32:40] + total[40:48]
     upto = jnp.where(
@@ -411,7 +427,7 @@
 
 
 def final_kernel(
-    place_ref, part_ref, own_ref, y_first, y_second, inverse_ref, mark_ref, new_design_ref, new_physical_ref,
+    part_ref, own_ref, y_first, y_second, inverse_ref, mark_ref, new_design_ref, new_physical_ref,
     blocks_ref, chosen_ref, near_ref, far_ref, stiff_ref, *, factors, target
 ):
     total = part_ref[0]
@@ -420,7 +436,7 @@
     low_end = jnp.minimum(jnp.sum(jnp.where(total > target, 1.0, 0.0)), POINTS - 1.0)
     multiplier = log_lower + (log_upper - log_lower) / POINTS * (low_end + 0.5)
     factor = jnp.exp(jnp.broadcast_to(-0.5 * multiplier, (SY, LANES)))
-    even = is_even(place_ref, 1)
+    even = is_even("gy")
     for p in range(CHOSEN):
         tiles = []
         own = [own_ref[f, p] for f in range(3)]
@@ -465,18 +481,17 @@
         blocks_ref[5, p] = jnp.where(marked, 0.0, xy)
 
 
-def call(kernel, smem, vmem, shapes, scratch, flops):
-    specs = [pl.BlockSpec(memory_space=pltpu.SMEM)] * smem + [pl.BlockSpec(memory_space=pltpu.VMEM)] * vmem
+def call(kernel, inputs, shapes, scratch, flops, space=pltpu.VMEM, grant=32):
     outs = [jax.ShapeDtypeStruct(shape, F32) for shape in shapes]
     return pl.pallas_call(
         kernel,
         out_shape=outs,
-        in_specs=specs,
+        in_specs=[pl.BlockSpec(memory_space=space)] * len(inputs),
         out_specs=[pl.BlockSpec(memory_space=pltpu.VMEM)] * len(outs),
-        scratch_shapes=[pltpu.VMEM(shape, F32) for shape in scratch],
-        compiler_params=pltpu.CompilerParams(vmem_limit_bytes=32 * 2**20),
+        scratch_shapes=[pltpu.VMEM(shape, F32) if isinstance(shape, tuple) else shape for shape in scratch],
+        compiler_params=pltpu.CompilerParams(vmem_limit_bytes=grant * 2**20),
         cost_estimate=pl.CostEstimate(flops=flops, bytes_accessed=10**6, transcendentals=0),
-    )
+    )(*inputs)
 
 
 def exchange(first, second, axis):
@@ -496,53 +511,57 @@
     assert design.shape == (SX, SY, SZ) and lax.axis_size("gz") == 2
     sizes = [lax.axis_size(axis) for axis in ("gx", "gy", "gz")]
     extents = (SX * sizes[0], SY * sizes[1], SZ * sizes[2])
-    place = jnp.stack([lax.axis_index(axis) for axis in ("gx", "gy", "gz")]).astype(jnp.int32)
-    own = (displacement, physical, design, passive)
-
-    x_faces = exchange(*call(faces_x_kernel, 1, 4, [(26, SY, SZ)] * 2, [], 10**6)(place, *own), "gx")
+    block = (SX, SY, SZ)
+    faces = (26, SY, SZ)
+    own, *x_faces = call(
+        faces_x_kernel, (displacement, physical, design, passive), [(6,) + block, faces, faces],
+        [pltpu.VMEM(block, jnp.int32), pltpu.SemaphoreType.DMA((4,))], 10**6, pltpu.HBM, 62,
+    )
+    x_faces = exchange(*x_faces, "gx")
     frame = (ELEMENTS, ROWS, LANES)
     own_frame = (ELEMENTS, SY, LANES)
     inverse, volume_weight, marks = call(
-        functools.partial(weights_kernel, extents=extents), 1, 1,
-        [frame, (CHOSEN, SY, LANES), (SX, SY, SZ)], [own_frame, own_frame], 10**7,
-    )(place, supports.reshape(1, -1))
+        functools.partial(weights_kernel, extents=extents), (supports.reshape(1, -1),),
+        [frame, (CHOSEN, SY, LANES), block], [own_frame, own_frame], 10**7,
+    )
     x_faces, inverse, volume_weight, marks = lax.optimization_barrier((x_faces, inverse, volume_weight, marks))
 
-    y_shape = (12 * NODES, SZ)
+    faces = (12 * NODES, SZ)
     *y_faces, side = call(
-        faces_y_kernel, 1, 6, [y_shape, y_shape, (4 * NODES + 2 * CHOSEN, SY, SIDE)], [], 10**6
-    )(place, *own, *x_faces)
+        faces_y_kernel, (own, *x_faces), [faces, faces, (4 * NODES + 2 * CHOSEN, SY, SIDE)], [], 10**6
+    )
     y_faces = exchange(*y_faces, "gy")
     side = other_core(side)
-    (y_side,) = call(faces_z_kernel, 1, 2, [(4 * NODES, SY, SIDE)], [], 10**6)(place, *y_faces)
+    (y_side,) = call(faces_z_kernel, y_faces, [(4 * NODES, SY, SIDE)], [], 10**6)
     y_side = other_core(y_side)
 
-    y_shape = (9 * CHOSEN, LANES)
+    faces = (9 * CHOSEN, LANES)
     bounds, *y_bounds = call(
-        functools.partial(design_kernel, squares=energy_squares()), 1, 12,
-        [(3, CHOSEN, SY, LANES), y_shape, y_shape],
+        functools.partial(design_kernel, squares=energy_squares()),
+        (own, *x_faces, *y_faces, side, y_side, inverse, volume_weight),
+        [(3, CHOSEN, SY, LANES), faces, faces],
         [(4, NODES, ROWS, LANES), own_frame, own_frame, own_frame], 10**7,
-    )(place, *own, *x_faces, *y_faces, side, y_side, inverse, volume_weight)
+    )
 
     y_bounds = exchange(*y_bounds, "gy")
     inner, outer = sizes[1] * sizes[2], sizes[0]
     elements = (2 * SX, SY, 128)
     (part,) = call(
-        volumes_kernel, 0, 2, [(inner, 8, 128)], [(2,) + elements, (2,) + elements, (2, 6) + elements], 10**8,
-    )(bounds, volume_weight)
+        volumes_kernel, (bounds, volume_weight), [(inner, 8, 128)],
+        [(2,) + elements, (2,) + elements, (2, 6) + elements], 10**8,
+    )
     part = lax.all_to_all(part, ("gy", "gz"), 0, 0, tiled=True)
-    (part,) = call(repeat_kernel, 0, 1, [(outer, 8, 128)], [], 10**5)(part)
+    (part,) = call(repeat_kernel, (part,), [(outer, 8, 128)], [], 10**5)
     y_bounds, part = lax.optimization_barrier((y_bounds, part))
     part = lax.all_to_all(part, "gx", 0, 0, tiled=True)
 
     chosen = (CHOSEN, ROWS, LANES)
+    target = volume_share * (extents[0] * extents[1] * extents[2])
     new_design, new_physical, node_blocks = call(
-        functools.partial(
-            final_kernel, factors=[float(f) for f in corner_factors()],
-            target=volume_share * (extents[0] * extents[1] * extents[2]),
-        ), 1, 6,
-        [(SX, SY, SZ), (SX, SY, SZ), (6, SX, SY, SZ)], [chosen, chosen, chosen, (SX + 1, ROWS, LANES)], 10**7,
-    )(place, part, bounds, *y_bounds, inverse, marks)
+        functools.partial(final_kernel, factors=[float(f) for f in corner_factors()], target=target),
+        (part, bounds, *y_bounds, inverse, marks), [block, block, (6,) + block],
+        [chosen, chosen, chosen, (SX + 1, ROWS, LANES)], 10**7,
+    )
     return (new_design, new_physical, node_blocks)
 
 

time: 75.2 us -> 70 us (0.931)
  Pallas kernels: 15.3 us -> 12 us
  local copies, waits for them, and re-layouts: 3.46 us -> 1.01 us
  waiting for transfers between devices: 3.33 us -> 4.19 us
    pallas_call x8, Pallas kernels: 15.3 us -> 12 us  [call(): pl.pallas_call(kernel, out_shape=outs, in_specs=[pl.BlockSpec(memory_spac...]
    unnamed x12 -> x6, local copies, waits for them, and re-layouts: 3.46 us -> 1.01 us
    ppermute x6, waiting for transfers between devices: 2.12 us -> 2.98 us  [exchange(): lax.ppermute(faces, axis, pairs + [(j, i) for i, j in pairs])]
  transfers between devices with their start and end apart: 8 -> 8, of which waited for: 3 -> 3; matrix products, arithmetic and copies ran while one was open for 0% -> 0% of each run, Pallas kernels for 10% -> 6%
where the time goes in v4:
time: 70 us; the launch traced here: 69.7 us
  blocking collectives  34.6 us (49%)
  starting transfers between devices  17.2 us (25%)
  Pallas kernels  12 us (17%)
  waiting for transfers between devices  4.19 us (6%)
  local copies, waits for them, and re-layouts  1.01 us (1%)
  between operations  0.74 us (1%)
    all_to_all x1, blocking collectives, body(): part = lax.all_to_all(part, ('gy', 'gz'), 0, 0, tiled=True)  17.3 us
    all_to_all x1, blocking collectives, body(): part = lax.all_to_all(part, 'gx', 0, 0, tiled=True)  17.3 us
    ppermute x6, starting transfers between devices, exchange(): lax.ppermute(faces, axis, pairs + [(j, i) for i, j in pairs])  12.1 us
    pallas_call x8, Pallas kernels, call(): pl.pallas_call(kernel, out_shape=outs, in_specs=[pl.BlockSpec(memory_spac...  12 us
    ppermute x2, starting transfers between devices, other_core(): return lax.ppermute(values, 'gz', [(0, 1), (1, 0)])  5.11 us
    ppermute x6, waiting for transfers between devices, exchange(): lax.ppermute(faces, axis, pairs + [(j, i) for i, j in pairs])  2.98 us
  transfers between devices with their start and end apart: 8, of which 3 were waited for; matrix products, arithmetic and copies ran while one was open for 0% of the time, Pallas kernels for 6%

profile of v4, /device:TPU:1, one launch (start us, length us, event | category | flops | bytes accessed | tf_op | source)
XLA Modules:
  0.0 69.7 jit_solution(7366272581663888451)
XLA Ops:
  0.6 2.0 %shard_map.76 = (f32[6,8,8,256]{3,2,1,0:T(8,128)}, f32[26,8,256]{2,1,0:T(8,128)}, f32[26,8,256]{2,1,0:T(8,128)}) custom-call(f32[3,8,8,256]{3,2,1,0:T(8,128)} %shift_ref.1, f32[8,8,256]{2,1,0:T(8,128)} %physical_ref.1, f32[8,8,256]{2,1,0:T(8,128)} %design_ref.1, s32[8,8,256]{2,1,0:T(8,128)} %passive_ref.1), custom_call_target="tpu_custom_call" | custom-call | flops 1000000 | bytes 1000000 | tf_op jit(solution)/shard_map/pallas_call | solution.py:486
  2.6 0.0 copy-start.2
  2.6 2.2 %collective-permute-start = (f32[26,8,256]{2,1,0:T(8,128)}, f32[26,8,256]{2,1,0:T(8,128)S(1)}, u32[]{:S(2)}, u32[]{:S(2)}) collective-permute-start(f32[26,8,256]{2,1,0:T(8,128)} %get-tuple-element.24), channel_id=1, source_target_pairs={{0,16},{32,48},{64,80},{96,112},{128,144},{160,176},{192,208},{224... | collective-permute-start | bytes 638984 | tf_op jit(solution)/shard_map/ppermute | solution.py:502
  4.8 0.7 collective-permute-start.1
  5.5 0.0 copy-done.2
  5.5 1.1 %shard_map.77 = (f32[17,16,384]{2,1,0:T(8,128)S(1)}, f32[13,8,384]{2,1,0:T(8,128)S(1)}, f32[8,8,256]{2,1,0:T(8,128)S(1)}) custom-call(s32[1,1024]{1,0:T(1,128)S(1)} %bitcast.1), custom_call_target="tpu_custom_call" | custom-call | flops 10000000 | bytes 1000000 | tf_op jit(solution)/shard_map/pallas_call | solution.py:486
  6.6 2.2 %collective-permute-done.x_first = f32[26,8,256]{2,1,0:T(8,128)S(1)} collective-permute-done((f32[26,8,256]{2,1,0:T(8,128)}, f32[26,8,256]{2,1,0:T(8,128)S(1)}, u32[]{:S(2)}, u32[]{:S(2)}) %collective-permute-start) | collective-permute-done | bytes 213024 | tf_op jit(solution)/shard_map/ppermute | solution.py:502
  8.9 0.0 collective-permute-done.1.x_second
  8.9 0.0 copy-start
  8.9 1.0 %copy-done = f32[6,8,8,256]{3,2,1,0:T(8,128)S(1)} copy-done((f32[6,8,8,256]{3,2,1,0:T(8,128)S(1)}, f32[6,8,8,256]{3,2,1,0:T(8,128)}, u32[]{:S(2)}) %copy-start) | copy-done | bytes 393240
  9.9 0.2 shard_map.78
  10.0 0.0 copy-start.1
  10.0 2.7 %collective-permute-start.2 = (f32[216,256]{1,0:T(8,128)S(1)}, f32[216,256]{1,0:T(8,128)S(1)}, u32[]{:S(2)}, u32[]{:S(2)}) collective-permute-start(f32[216,256]{1,0:T(8,128)S(1)} %get-tuple-element.31), channel_id=1, source_target_pairs={{0,2},{4,6},{8,10},{12,14},{2,0},{6,4},{10,8},{14,12},{1,3},{5,7},... | collective-permute-start | bytes 663560 | tf_op jit(solution)/shard_map/ppermute | solution.py:502
  12.7 0.7 collective-permute-start.3
  13.4 1.9 %collective-permute-start.4 = (f32[98,8,128]{2,1,0:T(8,128)S(1)}, f32[98,8,128]{2,1,0:T(8,128)S(1)}, u32[]{:S(2)}, u32[]{:S(2)}) collective-permute-start(f32[98,8,128]{2,1,0:T(8,128)S(1)} %get-tuple-element.33), channel_id=1, source_target_pairs={{0,1},{1,0},{2,3},{3,2},{4,5},{5,4},{6,7},{7,6},{8,9},{9,8},{10,11... | collective-permute-start | bytes 1204232 | tf_op jit(solution)/shard_map/ppermute | solution.py:507
  15.3 0.7 %collective-permute-done.2.y_first = f32[216,256]{1,0:T(8,128)S(1)} collective-permute-done((f32[216,256]{1,0:T(8,128)S(1)}, f32[216,256]{1,0:T(8,128)S(1)}, u32[]{:S(2)}, u32[]{:S(2)}) %collective-permute-start.2) | collective-permute-done | bytes 221216 | tf_op jit(solution)/shard_map/ppermute | solution.py:502
  16.1 0.0 collective-permute-done.3.y_second
  16.1 0.2 shard_map.79
  16.2 3.2 %collective-permute-start.5 = (f32[72,8,128]{2,1,0:T(8,128)S(1)}, f32[72,8,128]{2,1,0:T(8,128)S(1)}, u32[]{:S(2)}, u32[]{:S(2)}) collective-permute-start(f32[72,8,128]{2,1,0:T(8,128)S(1)} %shard_map.79), channel_id=1, source_target_pairs={{0,1},{1,0},{2,3},{3,2},{4,5},{5,4},{6,7},{7,6},{8,9},{9,8},{10,11... | collective-permute-start | bytes 884744 | tf_op jit(solution)/shard_map/ppermute | solution.py:507
  19.4 0.0 collective-permute-done.4.side
  19.4 1.2 %collective-permute-done.5.y_side = f32[72,8,128]{2,1,0:T(8,128)S(1)} collective-permute-done((f32[72,8,128]{2,1,0:T(8,128)S(1)}, f32[72,8,128]{2,1,0:T(8,128)S(1)}, u32[]{:S(2)}, u32[]{:S(2)}) %collective-permute-start.5) | collective-permute-done | bytes 294944 | tf_op jit(solution)/shard_map/ppermute | solution.py:507
  20.6 0.0 copy-done.1
  20.6 3.8 %shard_map.80 = (f32[3,13,8,384]{3,2,1,0:T(8,128)S(1)}, f32[117,384]{1,0:T(8,128)S(1)}, f32[117,384]{1,0:T(8,128)S(1)}) custom-call(f32[6,8,8,256]{3,2,1,0:T(8,128)S(1)} %copy-done.1, f32[26,8,256]{2,1,0:T(8,128)S(1)} %collective-permute-done.x_first, f32[26,8,256]{2,1,0:T(8,128)S(1)} %collective-permute-done.1.x_second, ...), custom_call_target="tpu_custom_call" | custom-call | flops 10000000 | bytes 1000000 | tf_op jit(solution)/shard_map/pallas_call | solution.py:486
  24.5 5.2 %collective-permute-start.6 = (f32[117,384]{1,0:T(8,128)S(1)}, f32[117,384]{1,0:T(8,128)S(1)}, u32[]{:S(2)}, u32[]{:S(2)}) collective-permute-start(f32[117,384]{1,0:T(8,128)S(1)} %get-tuple-element.36), channel_id=1, source_target_pairs={{0,2},{4,6},{8,10},{12,14},{2,0},{6,4},{10,8},{14,12},{1,3},{5,7},... | collective-permute-start | bytes 539144 | tf_op jit(solution)/shard_map/ppermute | solution.py:502
  29.7 0.7 collective-permute-start.7
  30.3 3.2 %shard_map.81 = f32[16,8,128]{2,1,0:T(8,128)S(1)} custom-call(f32[3,13,8,384]{3,2,1,0:T(8,128)S(1)} %get-tuple-element.38.bounds_ref.own_ref, f32[13,8,384]{2,1,0:T(8,128)S(1)} %get-tuple-element.35.volume_ref), custom_call_target="tpu_custom_call" | custom-call | flops 100000000 | bytes 1000000 | tf_op jit(solution)/shard_map/pallas_call | solution.py:486
  33.5 17.3 %all_to_all.10.part_ref = f32[16,8,128]{2,1,0:T(8,128)S(1)} all-to-all(f32[16,8,128]{2,1,0:T(8,128)S(1)} %shard_map.81), channel_id=1, replica_groups=mesh['gx'=16,'gy'=8,'gz'=2] {'gy','gz'}, dimensions={0} | all-to-all | bytes 131072 | tf_op jit(solution)/shard_map/all_to_all | solution.py:553
  50.9 0.0 collective-permute-done.6.y_first
  50.9 0.0 collective-permute-done.7.y_second
  50.9 17.3 %all_to_all.11.part_ref = f32[16,8,128]{2,1,0:T(8,128)S(1)} all-to-all(f32[16,8,128]{2,1,0:T(8,128)S(1)} %shard_map.82), channel_id=1, replica_groups=mesh['gx'=16,'gy'=8,'gz'=2] {'gx'}, dimensions={0} | all-to-all | bytes 131072 | tf_op jit(solution)/shard_map/all_to_all | solution.py:556
  68.1 1.6 %shard_map.83 = (f32[8,8,256]{2,1,0:T(8,128)}, f32[8,8,256]{2,1,0:T(8,128)}, f32[6,8,8,256]{3,2,1,0:T(8,128)}) custom-call(f32[16,8,128]{2,1,0:T(8,128)S(1)} %all_to_all.11.part_ref, f32[3,13,8,384]{3,2,1,0:T(8,128)S(1)} %get-tuple-element.38.bounds_ref.own_ref, f32[117,384]{1,0:T(8,128)S(1)} %collective-permute-done.6.y_first, ...), custom_call_target="tpu_custom_call" | custom-call | flops 10000000 | bytes 1000000 | tf_op jit(solution)/shard_map/pallas_call | solution.py:486
  (1 shorter events, 0.0 us)
Async XLA Ops:
  2.6 2.9 %copy-start.2 = (s32[1024]{0:T(1024)S(1)}, s32[1024]{0:T(1024)}, u32[]{:S(2)}) copy-start(s32[1024]{0:T(1024)} %param.9) | copy-start | bytes 12292
  2.6 6.3 %collective-permute-start = (f32[26,8,256]{2,1,0:T(8,128)}, f32[26,8,256]{2,1,0:T(8,128)S(1)}, u32[]{:S(2)}, u32[]{:S(2)}) collective-permute-start(f32[26,8,256]{2,1,0:T(8,128)} %get-tuple-element.24), channel_id=1, source_target_pairs={{0,16},{32,48},{64,80},{96,112},{128,144},{160,176},{192,208},{224... | collective-permute-start | bytes 638984 | tf_op jit(solution)/shard_map/ppermute | solution.py:502
  4.8 4.1 %collective-permute-start.1 = (f32[26,8,256]{2,1,0:T(8,128)}, f32[26,8,256]{2,1,0:T(8,128)S(1)}, u32[]{:S(2)}, u32[]{:S(2)}) collective-permute-start(f32[26,8,256]{2,1,0:T(8,128)} %get-tuple-element.25), channel_id=1, source_target_pairs={{16,32},{48,64},{80,96},{112,128},{144,160},{176,192},{208,224},{3... | collective-permute-start | bytes 638984 | tf_op jit(solution)/shard_map/ppermute | solution.py:502
  8.9 1.0 %copy-start = (f32[6,8,8,256]{3,2,1,0:T(8,128)S(1)}, f32[6,8,8,256]{3,2,1,0:T(8,128)}, u32[]{:S(2)}) copy-start(f32[6,8,8,256]{3,2,1,0:T(8,128)} %get-tuple-element.23.own_ref) | copy-start | bytes 1179652
  10.0 10.6 %copy-start.1 = (f32[6,8,8,256]{3,2,1,0:T(8,128)S(1)}, f32[6,8,8,256]{3,2,1,0:T(8,128)}, u32[]{:S(2)}) copy-start(f32[6,8,8,256]{3,2,1,0:T(8,128)} %get-tuple-element.23.own_ref) | copy-start | bytes 1179652
  10.0 6.0 %collective-permute-start.2 = (f32[216,256]{1,0:T(8,128)S(1)}, f32[216,256]{1,0:T(8,128)S(1)}, u32[]{:S(2)}, u32[]{:S(2)}) collective-permute-start(f32[216,256]{1,0:T(8,128)S(1)} %get-tuple-element.31), channel_id=1, source_target_pairs={{0,2},{4,6},{8,10},{12,14},{2,0},{6,4},{10,8},{14,12},{1,3},{5,7},... | collective-permute-start | bytes 663560 | tf_op jit(solution)/shard_map/ppermute | solution.py:502
  12.7 3.3 %collective-permute-start.3 = (f32[216,256]{1,0:T(8,128)S(1)}, f32[216,256]{1,0:T(8,128)S(1)}, u32[]{:S(2)}, u32[]{:S(2)}) collective-permute-start(f32[216,256]{1,0:T(8,128)S(1)} %get-tuple-element.32), channel_id=1, source_target_pairs={{2,4},{6,8},{10,12},{4,2},{8,6},{12,10},{3,5},{7,9},{11,13},{5,3},... | collective-permute-start | bytes 663560 | tf_op jit(solution)/shard_map/ppermute | solution.py:502
  13.4 6.0 %collective-permute-start.4 = (f32[98,8,128]{2,1,0:T(8,128)S(1)}, f32[98,8,128]{2,1,0:T(8,128)S(1)}, u32[]{:S(2)}, u32[]{:S(2)}) collective-permute-start(f32[98,8,128]{2,1,0:T(8,128)S(1)} %get-tuple-element.33), channel_id=1, source_target_pairs={{0,1},{1,0},{2,3},{3,2},{4,5},{5,4},{6,7},{7,6},{8,9},{9,8},{10,11... | collective-permute-start | bytes 1204232 | tf_op jit(solution)/shard_map/ppermute | solution.py:507
  16.2 4.4 %collective-permute-start.5 = (f32[72,8,128]{2,1,0:T(8,128)S(1)}, f32[72,8,128]{2,1,0:T(8,128)S(1)}, u32[]{:S(2)}, u32[]{:S(2)}) collective-permute-start(f32[72,8,128]{2,1,0:T(8,128)S(1)} %shard_map.79), channel_id=1, source_target_pairs={{0,1},{1,0},{2,3},{3,2},{4,5},{5,4},{6,7},{7,6},{8,9},{9,8},{10,11... | collective-permute-start | bytes 884744 | tf_op jit(solution)/shard_map/ppermute | solution.py:507
  24.5 26.4 %collective-permute-start.6 = (f32[117,384]{1,0:T(8,128)S(1)}, f32[117,384]{1,0:T(8,128)S(1)}, u32[]{:S(2)}, u32[]{:S(2)}) collective-permute-start(f32[117,384]{1,0:T(8,128)S(1)} %get-tuple-element.36), channel_id=1, source_target_pairs={{0,2},{4,6},{8,10},{12,14},{2,0},{6,4},{10,8},{14,12},{1,3},{5,7},... | collective-permute-start | bytes 539144 | tf_op jit(solution)/shard_map/ppermute | solution.py:502
  29.7 21.2 %collective-permute-start.7 = (f32[117,384]{1,0:T(8,128)S(1)}, f32[117,384]{1,0:T(8,128)S(1)}, u32[]{:S(2)}, u32[]{:S(2)}) collective-permute-start(f32[117,384]{1,0:T(8,128)S(1)} %get-tuple-element.37), channel_id=1, source_target_pairs={{2,4},{6,8},{10,12},{4,2},{8,6},{12,10},{3,5},{7,9},{11,13},{5,3},... | collective-permute-start | bytes 539144 | tf_op jit(solution)/shard_map/ppermute | solution.py:502

commit v5 on v4

--- a/solution.py
+++ b/solution.py
@@ -70,7 +70,7 @@
     return matrix
 
 
-def energy_squares():
+def energy_groups():
     corners = corner_offsets()
     modes = np.zeros((24, 24))
     for s in range(8):
@@ -83,21 +83,33 @@
             for d in range(3):
                 modes[3 * n + d, 3 * s + d] = sign_value
     form = modes.T @ hex_stiffness() @ modes / 64.0
-    used = np.zeros((24, 24))
-    squares = []
+    groups = []
+
+    def add(coefficient, members):
+        if abs(coefficient) < 1e-9:
+            return
+        for group in groups:
+            if abs(group[0] - coefficient) < 1e-9:
+                group[1].append(members)
+                return
+        groups.append((coefficient, [members]))
+
     for parity in range(8):
-        members = [3 * (parity ^ (4, 2, 1)[d]) + d for d in range(3)]
-        block = form[np.ix_(members, members)].copy()
-        used[np.ix_(members, members)] = block
-        for r in range(3):
-            if block[r, r] < 1e-9:
-                continue
-            factors = block[r] / math.sqrt(block[r, r])
-            block -= np.outer(factors, factors)
-            squares.append([(members[c], factors[c]) for c in range(3) if abs(factors[c]) > 1e-9])
-        assert np.abs(block).max() < 1e-9
-    assert np.abs(used - form).max() < 1e-9
-    return squares
+        left = [3 * (parity ^ (4, 2, 1)[d]) + d for d in range(3)]
+        while left:
+            first = left[0]
+            block = [m for m in left if m == first or abs(form[first, m]) > 1e-9]
+            left = [m for m in left if m not in block]
+            beside = form[block[0], block[1]] if len(block) > 1 else 0.0
+            add(beside, block)
+            for m in block:
+                add(form[m, m] - beside, [m])
+    rebuilt = np.zeros((24, 24))
+    for coefficient, sums in groups:
+        for members in sums:
+            rebuilt[np.ix_(members, members)] += coefficient
+    assert np.abs(rebuilt - form).max() < 1e-9
+    return groups
 
 
 def corner_factors():
@@ -146,7 +158,11 @@
     return middle + (rolled(near, 1, 1) + rolled(near, -1, 1)) + (rolled(far, 2, 1) + rolled(far, -2, 1))
 
 
-def weights_kernel(support_ref, inverse_ref, volume_ref, mark_ref, near_ref, far_ref, *, extents):
+def weights_kernel(
+    own_ref, support_ref, own_copy, inverse_ref, volume_ref, mark_ref, near_ref, far_ref, semaphore, *, extents
+):
+    copy = pltpu.make_async_copy(own_ref, own_copy, semaphore)
+    copy.start()
     total_x, total_y, total_z = extents
     first_x = lax.axis_index("gx") * SX
     first_y = lax.axis_index("gy") * SY
@@ -194,6 +210,7 @@
     )
     for p in range(SX):
         mark_ref[p] = hits[p * SY : (p + 1) * SY]
+    copy.wait()
 
 
 def is_even(axis):
@@ -218,17 +235,13 @@
 def faces_x_kernel(
     shift_ref, physical_ref, design_ref, passive_ref, own_ref, first_ref, second_ref, passive_own, semaphores
 ):
-    copies = [
-        pltpu.make_async_copy(source, target, semaphores.at[n])
-        for n, (source, target) in enumerate(
-            (
-                (shift_ref, own_ref.at[0:3]),
-                (physical_ref, own_ref.at[3]),
-                (design_ref, own_ref.at[4]),
-                (passive_ref, passive_own),
-            )
-        )
-    ]
+    pairs = (
+        (shift_ref, own_ref.at[0:3]),
+        (physical_ref, own_ref.at[3]),
+        (design_ref, own_ref.at[4]),
+        (passive_ref, passive_own),
+    )
+    copies = [pltpu.make_async_copy(*pair, semaphores.at[n]) for n, pair in enumerate(pairs)]
     for copy in copies:
         copy.start()
     for copy in copies:
@@ -285,7 +298,7 @@
 
 def design_kernel(
     own_ref, x_first, x_second, y_first, y_second, side, y_side, inverse_ref, volume_ref, out_ref, first_ref,
-    second_ref, ext_ref, sens_ref, near_ref, far_ref, *, squares
+    second_ref, part_ref, ext_ref, sens_ref, near_ref, far_ref, high_ref, low_ref, value_ref, *, groups
 ):
     lane = lax.broadcasted_iota(jnp.int32, (SY, SIDE), 1)
     start = lax.axis_index("gz") * (SIDE // 2)
@@ -313,12 +326,13 @@
                     for c, mode in enumerate((along_y + next_lane, next_lane - along_y)):
                         modes[3 * (4 * a + 2 * b + c) + d] = mode
         energy = None
-        for terms in squares:
-            line = None
-            for mode, factor in terms:
-                term = float(factor) * modes[mode]
-                line = term if line is None else line + term
-            energy = line * line if energy is None else energy + line * line
+        for coefficient, sums in groups:
+            squares = None
+            for members in sums:
+                value = functools.reduce(lambda left, right: left + right, [modes[m] for m in members])
+                squares = value * value if squares is None else squares + value * value
+            squares = float(coefficient) * squares
+            energy = squares if energy is None else energy + squares
         density = ext_ref[3, p]
         sens = scale * density * density * energy * inverse_ref[p]
         sens_ref[p] = sens[0:SY]
@@ -340,6 +354,7 @@
             out_ref[f, p] = value
             row = 3 * (CHOSEN * f + p)
             place_pair(even, first_ref, second_ref, value[SY - 3 :], value[0:3], slice(row, row + 3))
+    add_volumes(out_ref, volume_ref, part_ref, high_ref, low_ref, value_ref)
 
 
 def three_parts(value):
@@ -348,7 +363,7 @@
     return first, second, value - first - second
 
 
-def volumes_kernel(bounds_ref, volume_ref, out_ref, high_ref, low_ref, value_ref):
+def add_volumes(bounds_ref, volume_ref, out_ref, high_ref, low_ref, value_ref):
     step = (log_upper - log_lower) / POINTS
     ceilings = jnp.zeros((SY, 128), F32)
     for v in range(2 * SX):
@@ -481,12 +496,12 @@
         blocks_ref[5, p] = jnp.where(marked, 0.0, xy)
 
 
-def call(kernel, inputs, shapes, scratch, flops, space=pltpu.VMEM, grant=32):
+def call(kernel, inputs, shapes, scratch, flops, spaces=None, grant=32):
     outs = [jax.ShapeDtypeStruct(shape, F32) for shape in shapes]
     return pl.pallas_call(
         kernel,
         out_shape=outs,
-        in_specs=[pl.BlockSpec(memory_space=space)] * len(inputs),
+        in_specs=[pl.BlockSpec(memory_space=space) for space in spaces or [pltpu.VMEM] * len(inputs)],
         out_specs=[pl.BlockSpec(memory_space=pltpu.VMEM)] * len(outs),
         scratch_shapes=[pltpu.VMEM(shape, F32) if isinstance(shape, tuple) else shape for shape in scratch],
         compiler_params=pltpu.CompilerParams(vmem_limit_bytes=grant * 2**20),
@@ -515,16 +530,17 @@
     faces = (26, SY, SZ)
     own, *x_faces = call(
         faces_x_kernel, (displacement, physical, design, passive), [(6,) + block, faces, faces],
-        [pltpu.VMEM(block, jnp.int32), pltpu.SemaphoreType.DMA((4,))], 10**6, pltpu.HBM, 62,
+        [pltpu.VMEM(block, jnp.int32), pltpu.SemaphoreType.DMA((4,))], 10**6, [pltpu.HBM] * 4, 62,
     )
     x_faces = exchange(*x_faces, "gx")
     frame = (ELEMENTS, ROWS, LANES)
     own_frame = (ELEMENTS, SY, LANES)
-    inverse, volume_weight, marks = call(
-        functools.partial(weights_kernel, extents=extents), (supports.reshape(1, -1),),
-        [frame, (CHOSEN, SY, LANES), block], [own_frame, own_frame], 10**7,
-    )
-    x_faces, inverse, volume_weight, marks = lax.optimization_barrier((x_faces, inverse, volume_weight, marks))
+    weights = call(
+        functools.partial(weights_kernel, extents=extents), (own, supports.reshape(1, -1)),
+        [(6,) + block, frame, (CHOSEN, SY, LANES), block],
+        [own_frame, own_frame, pltpu.SemaphoreType.DMA(())], 10**7, [pltpu.HBM, pltpu.VMEM],
+    )
+    x_faces, (own, inverse, volume_weight, marks) = lax.optimization_barrier((x_faces, weights))
 
     faces = (12 * NODES, SZ)
     *y_faces, side = call(
@@ -536,23 +552,20 @@
     y_side = other_core(y_side)
 
     faces = (9 * CHOSEN, LANES)
-    bounds, *y_bounds = call(
-        functools.partial(design_kernel, squares=energy_squares()),
-        (own, *x_faces, *y_faces, side, y_side, inverse, volume_weight),
-        [(3, CHOSEN, SY, LANES), faces, faces],
-        [(4, NODES, ROWS, LANES), own_frame, own_frame, own_frame], 10**7,
-    )
-
-    y_bounds = exchange(*y_bounds, "gy")
     inner, outer = sizes[1] * sizes[2], sizes[0]
     elements = (2 * SX, SY, 128)
-    (part,) = call(
-        volumes_kernel, (bounds, volume_weight), [(inner, 8, 128)],
-        [(2,) + elements, (2,) + elements, (2, 6) + elements], 10**8,
-    )
+    bounds, *y_bounds, part = call(
+        functools.partial(design_kernel, groups=energy_groups()),
+        (own, *x_faces, *y_faces, side, y_side, inverse, volume_weight),
+        [(3, CHOSEN, SY, LANES), faces, faces, (inner, 8, 128)],
+        [(4, NODES, ROWS, LANES), own_frame, own_frame, own_frame]
+        + [(2,) + elements, (2,) + elements, (2, 6) + elements], 10**7,
+    )
+
     part = lax.all_to_all(part, ("gy", "gz"), 0, 0, tiled=True)
+    y_bounds, part = lax.optimization_barrier((y_bounds, part))
+    y_bounds = exchange(*y_bounds, "gy")
     (part,) = call(repeat_kernel, (part,), [(outer, 8, 128)], [], 10**5)
-    y_bounds, part = lax.optimization_barrier((y_bounds, part))
     part = lax.all_to_all(part, "gx", 0, 0, tiled=True)
 
     chosen = (CHOSEN, ROWS, LANES)

time: 70 us -> 68 us (0.971)
  the two profiles are of different devices: /device:TPU:1 before, /device:TPU:64 now
where the time goes in v5:
time: 68 us; the launch traced here: 67.7 us
  blocking collectives  32.7 us (48%)
  Pallas kernels  12.1 us (18%)
  starting transfers between devices  11.1 us (16%)
  waiting for transfers between devices  10 us (15%)
  local copies, waits for them, and re-layouts  1 us (1%)
  between operations  0.74 us (1%)
    all_to_all x1, blocking collectives, body(): part = lax.all_to_all(part, 'gx', 0, 0, tiled=True)  18.7 us
    all_to_all x1, blocking collectives, body(): part = lax.all_to_all(part, ('gy', 'gz'), 0, 0, tiled=True)  14 us
    pallas_call x7, Pallas kernels, call(): pl.pallas_call(kernel, out_shape=outs, in_specs=[pl.BlockSpec(memory_spac...  12.1 us
    ppermute x6, starting transfers between devices, exchange(): lax.ppermute(faces, axis, pairs + [(j, i) for i, j in pairs])  10.9 us
    ppermute x6, waiting for transfers between devices, exchange(): lax.ppermute(faces, axis, pairs + [(j, i) for i, j in pairs])  8.49 us
    ppermute x2, waiting for transfers between devices, other_core(): return lax.ppermute(values, 'gz', [(0, 1), (1, 0)])  1.56 us
  transfers between devices with their start and end apart: 8, of which 4 were waited for; matrix products, arithmetic and copies ran while one was open for 0% of the time, Pallas kernels for 2%

profile of v5, /device:TPU:64, one launch (start us, length us, event | category | flops | bytes accessed | tf_op | source)
XLA Modules:
  0.0 67.7 jit_solution(6263512778361657130)
XLA Ops:
  0.6 1.9 %shard_map.76 = (f32[6,8,8,256]{3,2,1,0:T(8,128)}, f32[26,8,256]{2,1,0:T(8,128)}, f32[26,8,256]{2,1,0:T(8,128)}) custom-call(f32[3,8,8,256]{3,2,1,0:T(8,128)} %shift_ref.1, f32[8,8,256]{2,1,0:T(8,128)} %physical_ref.1, f32[8,8,256]{2,1,0:T(8,128)} %design_ref.1, s32[8,8,256]{2,1,0:T(8,128)} %passive_ref.1), custom_call_target="tpu_custom_call" | custom-call | flops 1000000 | bytes 1000000 | tf_op jit(solution)/shard_map/pallas_call | solution.py:501
  2.6 0.0 copy-start.1
  2.6 1.7 %collective-permute-start = (f32[26,8,256]{2,1,0:T(8,128)}, f32[26,8,256]{2,1,0:T(8,128)S(1)}, u32[]{:S(2)}, u32[]{:S(2)}) collective-permute-start(f32[26,8,256]{2,1,0:T(8,128)} %get-tuple-element.26), channel_id=1, source_target_pairs={{0,16},{32,48},{64,80},{96,112},{128,144},{160,176},{192,208},{224... | collective-permute-start | bytes 638984 | tf_op jit(solution)/shard_map/ppermute | solution.py:517
  4.3 0.7 collective-permute-start.1
  4.9 0.0 copy-done.1
  4.9 0.0 copy-start
  4.9 1.0 %copy-done = f32[6,8,8,256]{3,2,1,0:T(8,128)S(1)} copy-done((f32[6,8,8,256]{3,2,1,0:T(8,128)S(1)}, f32[6,8,8,256]{3,2,1,0:T(8,128)}, u32[]{:S(2)}) %copy-start) | copy-done | bytes 393240
  5.9 1.3 %shard_map.77 = (f32[6,8,8,256]{3,2,1,0:T(8,128)S(1)}, f32[17,16,384]{2,1,0:T(8,128)S(1)}, f32[13,8,384]{2,1,0:T(8,128)S(1)}, f32[8,8,256]{2,1,0:T(8,128)S(1)}) custom-call(f32[6,8,8,256]{3,2,1,0:T(8,128)S(1)} %copy-done, s32[1,1024]{1,0:T(1,128)S(1)} %bitcast.1), custom_call_target="tpu_custom_call" | custom-call | flops 10000000 | bytes 1000000 | tf_op jit(solution)/shard_map/pallas_call | solution.py:501
  7.3 2.6 %collective-permute-done.x_first = f32[26,8,256]{2,1,0:T(8,128)S(1)} collective-permute-done((f32[26,8,256]{2,1,0:T(8,128)}, f32[26,8,256]{2,1,0:T(8,128)S(1)}, u32[]{:S(2)}, u32[]{:S(2)}) %collective-permute-start) | collective-permute-done | bytes 213024 | tf_op jit(solution)/shard_map/ppermute | solution.py:517
  9.9 0.0 collective-permute-done.1.x_second
  9.9 0.2 shard_map.78
  10.1 2.0 %collective-permute-start.2 = (f32[216,256]{1,0:T(8,128)S(1)}, f32[216,256]{1,0:T(8,128)S(1)}, u32[]{:S(2)}, u32[]{:S(2)}) collective-permute-start(f32[216,256]{1,0:T(8,128)S(1)} %get-tuple-element.36), channel_id=1, source_target_pairs={{0,2},{4,6},{8,10},{12,14},{2,0},{6,4},{10,8},{14,12},{1,3},{5,7},... | collective-permute-start | bytes 663560 | tf_op jit(solution)/shard_map/ppermute | solution.py:517
  12.1 1.9 %collective-permute-start.3 = (f32[216,256]{1,0:T(8,128)S(1)}, f32[216,256]{1,0:T(8,128)S(1)}, u32[]{:S(2)}, u32[]{:S(2)}) collective-permute-start(f32[216,256]{1,0:T(8,128)S(1)} %get-tuple-element.37), channel_id=1, source_target_pairs={{2,4},{6,8},{10,12},{4,2},{8,6},{12,10},{3,5},{7,9},{11,13},{5,3},... | collective-permute-start | bytes 663560 | tf_op jit(solution)/shard_map/ppermute | solution.py:517
  14.0 0.1 collective-permute-start.4
  14.1 2.5 %collective-permute-done.2.y_first = f32[216,256]{1,0:T(8,128)S(1)} collective-permute-done((f32[216,256]{1,0:T(8,128)S(1)}, f32[216,256]{1,0:T(8,128)S(1)}, u32[]{:S(2)}, u32[]{:S(2)}) %collective-permute-start.2) | collective-permute-done | bytes 221216 | tf_op jit(solution)/shard_map/ppermute | solution.py:517
  16.6 3.3 %collective-permute-done.3.y_second = f32[216,256]{1,0:T(8,128)S(1)} collective-permute-done((f32[216,256]{1,0:T(8,128)S(1)}, f32[216,256]{1,0:T(8,128)S(1)}, u32[]{:S(2)}, u32[]{:S(2)}) %collective-permute-start.3) | collective-permute-done | bytes 221216 | tf_op jit(solution)/shard_map/ppermute | solution.py:517
  20.0 0.2 shard_map.79
  20.1 0.1 collective-permute-start.5
  20.2 0.0 collective-permute-done.4.side
  20.2 1.6 %collective-permute-done.5.y_side = f32[72,8,128]{2,1,0:T(8,128)S(1)} collective-permute-done((f32[72,8,128]{2,1,0:T(8,128)S(1)}, f32[72,8,128]{2,1,0:T(8,128)S(1)}, u32[]{:S(2)}, u32[]{:S(2)}) %collective-permute-start.5) | collective-permute-done | bytes 294944 | tf_op jit(solution)/shard_map/ppermute | solution.py:522
  21.8 6.9 %shard_map.80 = (f32[3,13,8,384]{3,2,1,0:T(8,128)S(1)}, f32[117,384]{1,0:T(8,128)S(1)}, f32[117,384]{1,0:T(8,128)S(1)}, f32[16,8,128]{2,1,0:T(8,128)S(1)}) custom-call(f32[6,8,8,256]{3,2,1,0:T(8,128)S(1)} %get-tuple-element.33.own_ref, f32[26,8,256]{2,1,0:T(8,128)S(1)} %collective-permute-done.x_first, f32[26,8,256]{2,1,0:T(8,128)S(1)} %collective-permute-done.1.x_second, ...), custom_call_target="tpu_custom_call" | custom-call | flops 10000000 | bytes 1000000 | tf_op jit(solution)/shard_map/pallas_call | solution.py:501
  28.7 14.0 %all_to_all.10.part_ref = f32[16,8,128]{2,1,0:T(8,128)S(1)} all-to-all(f32[16,8,128]{2,1,0:T(8,128)S(1)} %get-tuple-element.43), channel_id=1, replica_groups=mesh['gx'=16,'gy'=8,'gz'=2] {'gy','gz'}, dimensions={0} | all-to-all | bytes 131072 | tf_op jit(solution)/shard_map/all_to_all | solution.py:565
  42.7 0.7 collective-permute-start.6
  43.4 4.0 %collective-permute-start.7 = (f32[117,384]{1,0:T(8,128)S(1)}, f32[117,384]{1,0:T(8,128)S(1)}, u32[]{:S(2)}, u32[]{:S(2)}) collective-permute-start(f32[117,384]{1,0:T(8,128)S(1)} %get-tuple-element.47), channel_id=1, source_target_pairs={{2,4},{6,8},{10,12},{4,2},{8,6},{12,10},{3,5},{7,9},{11,13},{5,3},... | collective-permute-start | bytes 539144 | tf_op jit(solution)/shard_map/ppermute | solution.py:517
  47.4 18.7 %all_to_all.11.part_ref = f32[16,8,128]{2,1,0:T(8,128)S(1)} all-to-all(f32[16,8,128]{2,1,0:T(8,128)S(1)} %shard_map.81), channel_id=1, replica_groups=mesh['gx'=16,'gy'=8,'gz'=2] {'gx'}, dimensions={0} | all-to-all | bytes 131072 | tf_op jit(solution)/shard_map/all_to_all | solution.py:569
  66.1 0.0 collective-permute-done.6.y_first
  66.1 0.0 collective-permute-done.7.y_second
  66.1 1.6 %shard_map.82 = (f32[8,8,256]{2,1,0:T(8,128)}, f32[8,8,256]{2,1,0:T(8,128)}, f32[6,8,8,256]{3,2,1,0:T(8,128)}) custom-call(f32[16,8,128]{2,1,0:T(8,128)S(1)} %all_to_all.11.part_ref, f32[3,13,8,384]{3,2,1,0:T(8,128)S(1)} %get-tuple-element.45.own_ref, f32[117,384]{1,0:T(8,128)S(1)} %collective-permute-done.6.y_first, ...), custom_call_target="tpu_custom_call" | custom-call | flops 10000000 | bytes 1000000 | tf_op jit(solution)/shard_map/pallas_call | solution.py:501
  (1 shorter events, 0.0 us)
Async XLA Ops:
  2.6 2.3 %copy-start.1 = (s32[1024]{0:T(1024)S(1)}, s32[1024]{0:T(1024)}, u32[]{:S(2)}) copy-start(s32[1024]{0:T(1024)} %param.9) | copy-start | bytes 12292
  2.6 7.3 %collective-permute-start = (f32[26,8,256]{2,1,0:T(8,128)}, f32[26,8,256]{2,1,0:T(8,128)S(1)}, u32[]{:S(2)}, u32[]{:S(2)}) collective-permute-start(f32[26,8,256]{2,1,0:T(8,128)} %get-tuple-element.26), channel_id=1, source_target_pairs={{0,16},{32,48},{64,80},{96,112},{128,144},{160,176},{192,208},{224... | collective-permute-start | bytes 638984 | tf_op jit(solution)/shard_map/ppermute | solution.py:517
  4.3 5.6 %collective-permute-start.1 = (f32[26,8,256]{2,1,0:T(8,128)}, f32[26,8,256]{2,1,0:T(8,128)S(1)}, u32[]{:S(2)}, u32[]{:S(2)}) collective-permute-start(f32[26,8,256]{2,1,0:T(8,128)} %get-tuple-element.27), channel_id=1, source_target_pairs={{16,32},{48,64},{80,96},{112,128},{144,160},{176,192},{208,224},{3... | collective-permute-start | bytes 638984 | tf_op jit(solution)/shard_map/ppermute | solution.py:517
  4.9 1.0 %copy-start = (f32[6,8,8,256]{3,2,1,0:T(8,128)S(1)}, f32[6,8,8,256]{3,2,1,0:T(8,128)}, u32[]{:S(2)}) copy-start(f32[6,8,8,256]{3,2,1,0:T(8,128)} %get-tuple-element.28.own_ref) | copy-start | bytes 1179652
  10.1 6.6 %collective-permute-start.2 = (f32[216,256]{1,0:T(8,128)S(1)}, f32[216,256]{1,0:T(8,128)S(1)}, u32[]{:S(2)}, u32[]{:S(2)}) collective-permute-start(f32[216,256]{1,0:T(8,128)S(1)} %get-tuple-element.36), channel_id=1, source_target_pairs={{0,2},{4,6},{8,10},{12,14},{2,0},{6,4},{10,8},{14,12},{1,3},{5,7},... | collective-permute-start | bytes 663560 | tf_op jit(solution)/shard_map/ppermute | solution.py:517
  12.1 7.9 %collective-permute-start.3 = (f32[216,256]{1,0:T(8,128)S(1)}, f32[216,256]{1,0:T(8,128)S(1)}, u32[]{:S(2)}, u32[]{:S(2)}) collective-permute-start(f32[216,256]{1,0:T(8,128)S(1)} %get-tuple-element.37), channel_id=1, source_target_pairs={{2,4},{6,8},{10,12},{4,2},{8,6},{12,10},{3,5},{7,9},{11,13},{5,3},... | collective-permute-start | bytes 663560 | tf_op jit(solution)/shard_map/ppermute | solution.py:517
  14.0 6.2 %collective-permute-start.4 = (f32[98,8,128]{2,1,0:T(8,128)S(1)}, f32[98,8,128]{2,1,0:T(8,128)S(1)}, u32[]{:S(2)}, u32[]{:S(2)}) collective-permute-start(f32[98,8,128]{2,1,0:T(8,128)S(1)} %get-tuple-element.38), channel_id=1, source_target_pairs={{0,1},{1,0},{2,3},{3,2},{4,5},{5,4},{6,7},{7,6},{8,9},{9,8},{10,11... | collective-permute-start | bytes 1204232 | tf_op jit(solution)/shard_map/ppermute | solution.py:522
  20.1 1.7 %collective-permute-start.5 = (f32[72,8,128]{2,1,0:T(8,128)S(1)}, f32[72,8,128]{2,1,0:T(8,128)S(1)}, u32[]{:S(2)}, u32[]{:S(2)}) collective-permute-start(f32[72,8,128]{2,1,0:T(8,128)S(1)} %shard_map.79), channel_id=1, source_target_pairs={{0,1},{1,0},{2,3},{3,2},{4,5},{5,4},{6,7},{7,6},{8,9},{9,8},{10,11... | collective-permute-start | bytes 884744 | tf_op jit(solution)/shard_map/ppermute | solution.py:522
  42.7 23.4 %collective-permute-start.6 = (f32[117,384]{1,0:T(8,128)S(1)}, f32[117,384]{1,0:T(8,128)S(1)}, u32[]{:S(2)}, u32[]{:S(2)}) collective-permute-start(f32[117,384]{1,0:T(8,128)S(1)} %get-tuple-element.46), channel_id=1, source_target_pairs={{0,2},{4,6},{8,10},{12,14},{2,0},{6,4},{10,8},{14,12},{1,3},{5,7},... | collective-permute-start | bytes 539144 | tf_op jit(solution)/shard_map/ppermute | solution.py:517
  43.4 22.7 %collective-permute-start.7 = (f32[117,384]{1,0:T(8,128)S(1)}, f32[117,384]{1,0:T(8,128)S(1)}, u32[]{:S(2)}, u32[]{:S(2)}) collective-permute-start(f32[117,384]{1,0:T(8,128)S(1)} %get-tuple-element.47), channel_id=1, source_target_pairs={{2,4},{6,8},{10,12},{4,2},{8,6},{12,10},{3,5},{7,9},{11,13},{5,3},... | collective-permute-start | bytes 539144 | tf_op jit(solution)/shard_map/ppermute | solution.py:517

commit v6 on v5

--- a/solution.py
+++ b/solution.py
@@ -214,7 +214,7 @@
 
 
 def is_even(axis):
-    return lax.axis_index(axis) % 2 == 0
+    return (lax.axis_index(axis) + lax.axis_index("gz")) % 2 == 0
 
 
 def place_pair(even, first_ref, second_ref, top, bottom, place):
@@ -227,9 +227,16 @@
     return jnp.where(even, second, first), jnp.where(even, first, second)
 
 
-def row_tile(even, first_ref, second_ref, plane):
-    low, high = low_high(even, first_ref, second_ref, slice(3 * plane, 3 * plane + 3))
-    return jnp.concatenate([high, jnp.zeros((SY - 6, low.shape[1]), F32), low], axis=0)
+def row_place(index):
+    if index < 3 * NODES:
+        return slice(3 * index, 3 * index + 3)
+    return slice(2 * index + 3 * NODES, 2 * index + 3 * NODES + 2)
+
+
+def row_tile(even, first_ref, second_ref, place):
+    low, high = low_high(even, first_ref, second_ref, place)
+    filler = jnp.zeros((SY - 2 * low.shape[0], low.shape[1]), F32)
+    return jnp.concatenate([high, filler, low], axis=0)
 
 
 def faces_x_kernel(
@@ -283,8 +290,9 @@
     for index in range(4 * NODES + 2 * CHOSEN):
         plane = read(index)
         if index < 4 * NODES:
-            rows = slice(3 * index, 3 * index + 3)
-            place_pair(even, first_ref, second_ref, plane[SY - 3 :], plane[0:3], rows)
+            rows = row_place(index)
+            depth = rows.stop - rows.start
+            place_pair(even, first_ref, second_ref, plane[SY - depth :], plane[0:depth], rows)
         side_ref[index] = jnp.where(lower_core, plane[:, SZ - SIDE :], plane[:, 0:SIDE])
 
 
@@ -292,7 +300,7 @@
     even = is_even("gy")
     lower_core = lax.axis_index("gz") == 0
     for index in range(4 * NODES):
-        tile = row_tile(even, y_first, y_second, index)
+        tile = row_tile(even, y_first, y_second, row_place(index))
         side_ref[index] = jnp.where(lower_core, tile[:, SZ - SIDE :], tile[:, 0:SIDE])
 
 
@@ -310,7 +318,7 @@
             index = NODES * f + p
             ext_ref[f, p, 0:SY, 0:SZ] = read(index)
             ext_ref[f, p, 0:SY, SZ:LANES] = jnp.where(keep, side[index], 0.0)
-            ext_ref[f, p, SY:ROWS, 0:SZ] = row_tile(even, y_first, y_second, index)
+            ext_ref[f, p, SY:ROWS, 0:SZ] = row_tile(even, y_first, y_second, row_place(index))
             ext_ref[f, p, SY:ROWS, SZ:LANES] = jnp.where(keep, y_side[index], 0.0)
     scale = penalty * (1.0 - stiff_floor)
 
@@ -455,7 +463,10 @@
     for p in range(CHOSEN):
         tiles = []
         own = [own_ref[f, p] for f in range(3)]
-        beside = [row_tile(even, y_first, y_second, CHOSEN * f + p) for f in range(3)]
+        beside = []
+        for f in range(3):
+            row = 3 * (CHOSEN * f + p)
+            beside.append(row_tile(even, y_first, y_second, slice(row, row + 3)))
         for scaled, floor_bound, ceiling in (own, beside):
             tiles.append(jnp.minimum(jnp.maximum(scaled * factor, floor_bound), ceiling))
         chosen = jnp.concatenate(tiles, axis=0)
@@ -512,9 +523,12 @@
 def exchange(first, second, axis):
     count = lax.axis_size(axis)
     results = []
-    for start, faces in enumerate((first, second)):
-        pairs = [(i, i + 1) for i in range(start, count - 1, 2)]
-        results.append(lax.ppermute(faces, axis, pairs + [(j, i) for i, j in pairs]))
+    for turn, faces in enumerate((first, second)):
+        moves = []
+        for core in range(2):
+            for i in range((turn + core) % 2, count - 1, 2):
+                moves += [(2 * i + core, 2 * i + 2 + core), (2 * i + 2 + core, 2 * i + core)]
+        results.append(lax.ppermute(faces, (axis, "gz"), moves))
     return results
 
 
@@ -542,7 +556,7 @@
     )
     x_faces, (own, inverse, volume_weight, marks) = lax.optimization_barrier((x_faces, weights))
 
-    faces = (12 * NODES, SZ)
+    faces = (11 * NODES, SZ)
     *y_faces, side = call(
         faces_y_kernel, (own, *x_faces), [faces, faces, (4 * NODES + 2 * CHOSEN, SY, SIDE)], [], 10**6
     )

time: 68 us -> 72.9 us (1.072)
  the two profiles are of different devices: /device:TPU:64 before, /device:TPU:1 now
where the time goes in v6:
time: 72.9 us; the launch traced here: 72.5 us
  blocking collectives  32.6 us (45%)
  starting transfers between devices  17 us (23%)
  Pallas kernels  12.1 us (17%)
  waiting for transfers between devices  9.02 us (12%)
  local copies, waits for them, and re-layouts  1 us (1%)
  between operations  0.78 us (1%)
    all_to_all x1, blocking collectives, body(): part = lax.all_to_all(part, 'gx', 0, 0, tiled=True)  17.3 us
    ppermute x6, starting transfers between devices, exchange(): results.append(lax.ppermute(faces, (axis, 'gz'), moves))  16.8 us
    all_to_all x1, blocking collectives, body(): part = lax.all_to_all(part, ('gy', 'gz'), 0, 0, tiled=True)  15.3 us
    pallas_call x7, Pallas kernels, call(): pl.pallas_call(kernel, out_shape=outs, in_specs=[pl.BlockSpec(memory_spac...  12.1 us
    ppermute x6, waiting for transfers between devices, exchange(): results.append(lax.ppermute(faces, (axis, 'gz'), moves))  7.46 us
    ppermute x2, waiting for transfers between devices, other_core(): return lax.ppermute(values, 'gz', [(0, 1), (1, 0)])  1.56 us
  transfers between devices with their start and end apart: 8, of which 3 were waited for; matrix products, arithmetic and copies ran while one was open for 0% of the time, Pallas kernels for 2%

profile of v6, /device:TPU:1, one launch (start us, length us, event | category | flops | bytes accessed | tf_op | source)
XLA Modules:
  0.0 72.5 jit_solution(17162732102369073146)
XLA Ops:
  0.6 1.9 %shard_map.76 = (f32[6,8,8,256]{3,2,1,0:T(8,128)}, f32[26,8,256]{2,1,0:T(8,128)}, f32[26,8,256]{2,1,0:T(8,128)}) custom-call(f32[3,8,8,256]{3,2,1,0:T(8,128)} %shift_ref.1, f32[8,8,256]{2,1,0:T(8,128)} %physical_ref.1, f32[8,8,256]{2,1,0:T(8,128)} %design_ref.1, s32[8,8,256]{2,1,0:T(8,128)} %passive_ref.1), custom_call_target="tpu_custom_call" | custom-call | flops 1000000 | bytes 1000000 | tf_op jit(solution)/shard_map/pallas_call | solution.py:512
  2.6 0.0 copy-start.1
  2.6 0.7 collective-permute-start
  3.3 6.6 %collective-permute-start.1 = (f32[26,8,256]{2,1,0:T(8,128)}, f32[26,8,256]{2,1,0:T(8,128)S(1)}, u32[]{:S(2)}, u32[]{:S(2)}) collective-permute-start(f32[26,8,256]{2,1,0:T(8,128)} %get-tuple-element.27), channel_id=1, source_target_pairs={{16,32},{32,16},{48,64},{64,48},{80,96},{96,80},{112,128},{128,112... | collective-permute-start | bytes 638984 | tf_op jit(solution)/shard_map/ppermute | solution.py:531
  9.8 0.0 copy-done.1
  9.9 0.0 copy-start
  9.9 1.0 %copy-done = f32[6,8,8,256]{3,2,1,0:T(8,128)S(1)} copy-done((f32[6,8,8,256]{3,2,1,0:T(8,128)S(1)}, f32[6,8,8,256]{3,2,1,0:T(8,128)}, u32[]{:S(2)}) %copy-start) | copy-done | bytes 393240
  10.9 1.3 %shard_map.77 = (f32[6,8,8,256]{3,2,1,0:T(8,128)S(1)}, f32[17,16,384]{2,1,0:T(8,128)S(1)}, f32[13,8,384]{2,1,0:T(8,128)S(1)}, f32[8,8,256]{2,1,0:T(8,128)S(1)}) custom-call(f32[6,8,8,256]{3,2,1,0:T(8,128)S(1)} %copy-done, s32[1,1024]{1,0:T(1,128)S(1)} %bitcast.1), custom_call_target="tpu_custom_call" | custom-call | flops 10000000 | bytes 1000000 | tf_op jit(solution)/shard_map/pallas_call | solution.py:512
  12.2 0.0 collective-permute-done.x_first
  12.2 3.3 %collective-permute-done.1.x_second = f32[26,8,256]{2,1,0:T(8,128)S(1)} collective-permute-done((f32[26,8,256]{2,1,0:T(8,128)}, f32[26,8,256]{2,1,0:T(8,128)S(1)}, u32[]{:S(2)}, u32[]{:S(2)}) %collective-permute-start.1) | collective-permute-done | bytes 213024 | tf_op jit(solution)/shard_map/ppermute | solution.py:531
  15.5 0.2 shard_map.78
  15.6 0.7 collective-permute-start.2
  16.3 4.6 %collective-permute-start.3 = (f32[198,256]{1,0:T(8,128)S(1)}, f32[198,256]{1,0:T(8,128)S(1)}, u32[]{:S(2)}, u32[]{:S(2)}) collective-permute-start(f32[198,256]{1,0:T(8,128)S(1)} %get-tuple-element.37), channel_id=1, source_target_pairs={{2,4},{4,2},{6,8},{8,6},{10,12},{12,10},{1,3},{3,1},{5,7},{7,5},{9... | collective-permute-start | bytes 608264 | tf_op jit(solution)/shard_map/ppermute | solution.py:531
  20.9 0.1 collective-permute-start.4
  21.0 0.0 collective-permute-done.2.y_first
  21.0 4.2 %collective-permute-done.3.y_second = f32[198,256]{1,0:T(8,128)S(1)} collective-permute-done((f32[198,256]{1,0:T(8,128)S(1)}, f32[198,256]{1,0:T(8,128)S(1)}, u32[]{:S(2)}, u32[]{:S(2)}) %collective-permute-start.3) | collective-permute-done | bytes 202784 | tf_op jit(solution)/shard_map/ppermute | solution.py:531
  25.2 0.2 shard_map.79
  25.4 0.1 collective-permute-start.5
  25.5 0.0 collective-permute-done.4.side
  25.5 1.6 %collective-permute-done.5.y_side = f32[72,8,128]{2,1,0:T(8,128)S(1)} collective-permute-done((f32[72,8,128]{2,1,0:T(8,128)S(1)}, f32[72,8,128]{2,1,0:T(8,128)S(1)}, u32[]{:S(2)}, u32[]{:S(2)}) %collective-permute-start.5) | collective-permute-done | bytes 294944 | tf_op jit(solution)/shard_map/ppermute | solution.py:536
  27.0 6.9 %shard_map.80 = (f32[3,13,8,384]{3,2,1,0:T(8,128)S(1)}, f32[117,384]{1,0:T(8,128)S(1)}, f32[117,384]{1,0:T(8,128)S(1)}, f32[16,8,128]{2,1,0:T(8,128)S(1)}) custom-call(f32[6,8,8,256]{3,2,1,0:T(8,128)S(1)} %get-tuple-element.33.own_ref, f32[26,8,256]{2,1,0:T(8,128)S(1)} %collective-permute-done.x_first, f32[26,8,256]{2,1,0:T(8,128)S(1)} %collective-permute-done.1.x_second, ...), custom_call_target="tpu_custom_call" | custom-call | flops 10000000 | bytes 1000000 | tf_op jit(solution)/shard_map/pallas_call | solution.py:512
  33.9 15.3 %all_to_all.10.part_ref = f32[16,8,128]{2,1,0:T(8,128)S(1)} all-to-all(f32[16,8,128]{2,1,0:T(8,128)S(1)} %get-tuple-element.43), channel_id=1, replica_groups=mesh['gx'=16,'gy'=8,'gz'=2] {'gy','gz'}, dimensions={0} | all-to-all | bytes 131072 | tf_op jit(solution)/shard_map/all_to_all | solution.py:579
  49.2 0.7 collective-permute-start.6
  49.9 3.7 %collective-permute-start.7 = (f32[117,384]{1,0:T(8,128)S(1)}, f32[117,384]{1,0:T(8,128)S(1)}, u32[]{:S(2)}, u32[]{:S(2)}) collective-permute-start(f32[117,384]{1,0:T(8,128)S(1)} %get-tuple-element.47), channel_id=1, source_target_pairs={{2,4},{4,2},{6,8},{8,6},{10,12},{12,10},{1,3},{3,1},{5,7},{7,5},{9... | collective-permute-start | bytes 539144 | tf_op jit(solution)/shard_map/ppermute | solution.py:531
  53.6 17.3 %all_to_all.11.part_ref = f32[16,8,128]{2,1,0:T(8,128)S(1)} all-to-all(f32[16,8,128]{2,1,0:T(8,128)S(1)} %shard_map.81), channel_id=1, replica_groups=mesh['gx'=16,'gy'=8,'gz'=2] {'gx'}, dimensions={0} | all-to-all | bytes 131072 | tf_op jit(solution)/shard_map/all_to_all | solution.py:583
  70.9 0.0 collective-permute-done.6.y_first
  70.9 0.0 collective-permute-done.7.y_second
  70.9 1.6 %shard_map.82 = (f32[8,8,256]{2,1,0:T(8,128)}, f32[8,8,256]{2,1,0:T(8,128)}, f32[6,8,8,256]{3,2,1,0:T(8,128)}) custom-call(f32[16,8,128]{2,1,0:T(8,128)S(1)} %all_to_all.11.part_ref, f32[3,13,8,384]{3,2,1,0:T(8,128)S(1)} %get-tuple-element.45.own_ref, f32[117,384]{1,0:T(8,128)S(1)} %collective-permute-done.6.y_first, ...), custom_call_target="tpu_custom_call" | custom-call | flops 10000000 | bytes 1000000 | tf_op jit(solution)/shard_map/pallas_call | solution.py:512
  (1 shorter events, 0.0 us)
Async XLA Ops:
  2.6 7.3 %copy-start.1 = (s32[1024]{0:T(1024)S(1)}, s32[1024]{0:T(1024)}, u32[]{:S(2)}) copy-start(s32[1024]{0:T(1024)} %param.9) | copy-start | bytes 12292
  2.6 9.6 %collective-permute-start = (f32[26,8,256]{2,1,0:T(8,128)}, f32[26,8,256]{2,1,0:T(8,128)S(1)}, u32[]{:S(2)}, u32[]{:S(2)}) collective-permute-start(f32[26,8,256]{2,1,0:T(8,128)} %get-tuple-element.26), channel_id=1, source_target_pairs={{0,16},{16,0},{32,48},{48,32},{64,80},{80,64},{96,112},{112,96},{1... | collective-permute-start | bytes 638984 | tf_op jit(solution)/shard_map/ppermute | solution.py:531
  3.3 12.2 %collective-permute-start.1 = (f32[26,8,256]{2,1,0:T(8,128)}, f32[26,8,256]{2,1,0:T(8,128)S(1)}, u32[]{:S(2)}, u32[]{:S(2)}) collective-permute-start(f32[26,8,256]{2,1,0:T(8,128)} %get-tuple-element.27), channel_id=1, source_target_pairs={{16,32},{32,16},{48,64},{64,48},{80,96},{96,80},{112,128},{128,112... | collective-permute-start | bytes 638984 | tf_op jit(solution)/shard_map/ppermute | solution.py:531
  9.9 1.0 %copy-start = (f32[6,8,8,256]{3,2,1,0:T(8,128)S(1)}, f32[6,8,8,256]{3,2,1,0:T(8,128)}, u32[]{:S(2)}) copy-start(f32[6,8,8,256]{3,2,1,0:T(8,128)} %get-tuple-element.28.own_ref) | copy-start | bytes 1179652
  15.6 5.4 %collective-permute-start.2 = (f32[198,256]{1,0:T(8,128)S(1)}, f32[198,256]{1,0:T(8,128)S(1)}, u32[]{:S(2)}, u32[]{:S(2)}) collective-permute-start(f32[198,256]{1,0:T(8,128)S(1)} %get-tuple-element.36), channel_id=1, source_target_pairs={{0,2},{2,0},{4,6},{6,4},{8,10},{10,8},{12,14},{14,12},{3,5},{5,3},... | collective-permute-start | bytes 608264 | tf_op jit(solution)/shard_map/ppermute | solution.py:531
  16.3 8.9 %collective-permute-start.3 = (f32[198,256]{1,0:T(8,128)S(1)}, f32[198,256]{1,0:T(8,128)S(1)}, u32[]{:S(2)}, u32[]{:S(2)}) collective-permute-start(f32[198,256]{1,0:T(8,128)S(1)} %get-tuple-element.37), channel_id=1, source_target_pairs={{2,4},{4,2},{6,8},{8,6},{10,12},{12,10},{1,3},{3,1},{5,7},{7,5},{9... | collective-permute-start | bytes 608264 | tf_op jit(solution)/shard_map/ppermute | solution.py:531
  20.9 4.6 %collective-permute-start.4 = (f32[98,8,128]{2,1,0:T(8,128)S(1)}, f32[98,8,128]{2,1,0:T(8,128)S(1)}, u32[]{:S(2)}, u32[]{:S(2)}) collective-permute-start(f32[98,8,128]{2,1,0:T(8,128)S(1)} %get-tuple-element.38), channel_id=1, source_target_pairs={{0,1},{1,0},{2,3},{3,2},{4,5},{5,4},{6,7},{7,6},{8,9},{9,8},{10,11... | collective-permute-start | bytes 1204232 | tf_op jit(solution)/shard_map/ppermute | solution.py:536
  25.4 1.7 %collective-permute-start.5 = (f32[72,8,128]{2,1,0:T(8,128)S(1)}, f32[72,8,128]{2,1,0:T(8,128)S(1)}, u32[]{:S(2)}, u32[]{:S(2)}) collective-permute-start(f32[72,8,128]{2,1,0:T(8,128)S(1)} %shard_map.79), channel_id=1, source_target_pairs={{0,1},{1,0},{2,3},{3,2},{4,5},{5,4},{6,7},{7,6},{8,9},{9,8},{10,11... | collective-permute-start | bytes 884744 | tf_op jit(solution)/shard_map/ppermute | solution.py:536
  49.2 21.7 %collective-permute-start.6 = (f32[117,384]{1,0:T(8,128)S(1)}, f32[117,384]{1,0:T(8,128)S(1)}, u32[]{:S(2)}, u32[]{:S(2)}) collective-permute-start(f32[117,384]{1,0:T(8,128)S(1)} %get-tuple-element.46), channel_id=1, source_target_pairs={{0,2},{2,0},{4,6},{6,4},{8,10},{10,8},{12,14},{14,12},{3,5},{5,3},... | collective-permute-start | bytes 539144 | tf_op jit(solution)/shard_map/ppermute | solution.py:531
  49.9 21.1 %collective-permute-start.7 = (f32[117,384]{1,0:T(8,128)S(1)}, f32[117,384]{1,0:T(8,128)S(1)}, u32[]{:S(2)}, u32[]{:S(2)}) collective-permute-start(f32[117,384]{1,0:T(8,128)S(1)} %get-tuple-element.47), channel_id=1, source_target_pairs={{2,4},{4,2},{6,8},{8,6},{10,12},{12,10},{1,3},{3,1},{5,7},{7,5},{9... | collective-permute-start | bytes 539144 | tf_op jit(solution)/shard_map/ppermute | solution.py:531

commit v7 on v6

--- a/solution.py
+++ b/solution.py
@@ -214,7 +214,7 @@
 
 
 def is_even(axis):
-    return (lax.axis_index(axis) + lax.axis_index("gz")) % 2 == 0
+    return lax.axis_index(axis) % 2 == 0
 
 
 def place_pair(even, first_ref, second_ref, top, bottom, place):
@@ -222,9 +222,12 @@
     second_ref[place] = jnp.where(even, bottom, top)
 
 
-def low_high(even, first_ref, second_ref, place):
+def low_high(axis, first_ref, second_ref, place):
+    index = lax.axis_index(axis)
     first, second = first_ref[place], second_ref[place]
-    return jnp.where(even, second, first), jnp.where(even, first, second)
+    low = jnp.where(index == 0, 0.0, jnp.where(index % 2 == 0, second, first))
+    high = jnp.where(index == lax.axis_size(axis) - 1, 0.0, jnp.where(index % 2 == 0, first, second))
+    return low, high
 
 
 def row_place(index):
@@ -233,8 +236,8 @@
     return slice(2 * index + 3 * NODES, 2 * index + 3 * NODES + 2)
 
 
-def row_tile(even, first_ref, second_ref, place):
-    low, high = low_high(even, first_ref, second_ref, place)
+def row_tile(first_ref, second_ref, place):
+    low, high = low_high("gy", first_ref, second_ref, place)
     filler = jnp.zeros((SY - 2 * low.shape[0], low.shape[1]), F32)
     return jnp.concatenate([high, filler, low], axis=0)
 
@@ -264,8 +267,6 @@
 
 
 def plane_reader(own_ref, x_first, x_second):
-    even = is_even("gx")
-
     def read(index):
         if index < 4 * NODES:
             f, x = index // NODES, index % NODES - 5
@@ -275,7 +276,7 @@
             depth, base = 3, 8 + 3 * f
         if 0 <= x < SX:
             return own_ref[f, x]
-        low, high = low_high(even, x_first, x_second, base + (x + depth if x < 0 else x - SX))
+        low, high = low_high("gx", x_first, x_second, base + (x + depth if x < 0 else x - SX))
         return low if x < 0 else high
 
     return read
@@ -297,10 +298,9 @@
 
 
 def faces_z_kernel(y_first, y_second, side_ref):
-    even = is_even("gy")
     lower_core = lax.axis_index("gz") == 0
     for index in range(4 * NODES):
-        tile = row_tile(even, y_first, y_second, row_place(index))
+        tile = row_tile(y_first, y_second, row_place(index))
         side_ref[index] = jnp.where(lower_core, tile[:, SZ - SIDE :], tile[:, 0:SIDE])
 
 
@@ -318,7 +318,7 @@
             index = NODES * f + p
             ext_ref[f, p, 0:SY, 0:SZ] = read(index)
             ext_ref[f, p, 0:SY, SZ:LANES] = jnp.where(keep, side[index], 0.0)
-            ext_ref[f, p, SY:ROWS, 0:SZ] = row_tile(even, y_first, y_second, row_place(index))
+            ext_ref[f, p, SY:ROWS, 0:SZ] = row_tile(y_first, y_second, row_place(index))
             ext_ref[f, p, SY:ROWS, SZ:LANES] = jnp.where(keep, y_side[index], 0.0)
     scale = penalty * (1.0 - stiff_floor)
 
@@ -459,14 +459,13 @@
     low_end = jnp.minimum(jnp.sum(jnp.where(total > target, 1.0, 0.0)), POINTS - 1.0)
     multiplier = log_lower + (log_upper - log_lower) / POINTS * (low_end + 0.5)
     factor = jnp.exp(jnp.broadcast_to(-0.5 * multiplier, (SY, LANES)))
-    even = is_even("gy")
     for p in range(CHOSEN):
         tiles = []
         own = [own_ref[f, p] for f in range(3)]
         beside = []
         for f in range(3):
             row = 3 * (CHOSEN * f + p)
-            beside.append(row_tile(even, y_first, y_second, slice(row, row + 3)))
+            beside.append(row_tile(y_first, y_second, slice(row, row + 3)))
         for scaled, floor_bound, ceiling in (own, beside):
             tiles.append(jnp.minimum(jnp.maximum(scaled * factor, floor_bound), ceiling))
         chosen = jnp.concatenate(tiles, axis=0)
@@ -523,12 +522,9 @@
 def exchange(first, second, axis):
     count = lax.axis_size(axis)
     results = []
-    for turn, faces in enumerate((first, second)):
-        moves = []
-        for core in range(2):
-            for i in range((turn + core) % 2, count - 1, 2):
-                moves += [(2 * i + core, 2 * i + 2 + core), (2 * i + 2 + core, 2 * i + core)]
-        results.append(lax.ppermute(faces, (axis, "gz"), moves))
+    for start, faces in enumerate((first, second)):
+        pairs = [(i, (i + 1) % count) for i in range(start, count, 2)]
+        results.append(lax.ppermute(faces, axis, pairs + [(j, i) for i, j in pairs]))
     return results
 
 

time: 72.9 us -> 63.4 us (0.87)
  blocking collectives: 32.6 us -> 25.6 us
  waiting for transfers between devices: 9.02 us -> 4.54 us
  starting transfers between devices: 17 us -> 19.1 us
    all_to_all x1, blocking collectives: 17.3 us -> 11.8 us  [body(): part = lax.all_to_all(part, 'gx', 0, 0, tiled=True)]
    ppermute x2, starting transfers between devices: 0.19 us -> 5.53 us  [other_core(): return lax.ppermute(values, 'gz', [(0, 1), (1, 0)])]
    ppermute x6, waiting for transfers between devices: 7.46 us -> 3.33 us  [exchange(): lax.ppermute(faces, axis, pairs + [(j, i) for i, j in pairs])]
    ppermute x6, starting transfers between devices: 16.8 us -> 13.5 us  [exchange(): lax.ppermute(faces, axis, pairs + [(j, i) for i, j in pairs])]
    all_to_all x1, blocking collectives: 15.3 us -> 13.8 us  [body(): part = lax.all_to_all(part, ('gy', 'gz'), 0, 0, tiled=True)]
where the time goes in v7:
time: 63.4 us; the launch traced here: 63.1 us
  blocking collectives  25.6 us (40%)
  starting transfers between devices  19.1 us (30%)
  Pallas kernels  12.2 us (19%)
  waiting for transfers between devices  4.54 us (7%)
  local copies, waits for them, and re-layouts  1 us (2%)
  between operations  0.69 us (1%)
    all_to_all x1, blocking collectives, body(): part = lax.all_to_all(part, ('gy', 'gz'), 0, 0, tiled=True)  13.8 us
    ppermute x6, starting transfers between devices, exchange(): lax.ppermute(faces, axis, pairs + [(j, i) for i, j in pairs])  13.5 us
    pallas_call x7, Pallas kernels, call(): pl.pallas_call(kernel, out_shape=outs, in_specs=[pl.BlockSpec(memory_spac...  12.2 us
    all_to_all x1, blocking collectives, body(): part = lax.all_to_all(part, 'gx', 0, 0, tiled=True)  11.8 us
    ppermute x2, starting transfers between devices, other_core(): return lax.ppermute(values, 'gz', [(0, 1), (1, 0)])  5.53 us
    ppermute x6, waiting for transfers between devices, exchange(): lax.ppermute(faces, axis, pairs + [(j, i) for i, j in pairs])  3.33 us
  transfers between devices with their start and end apart: 8, of which 3 were waited for; matrix products, arithmetic and copies ran while one was open for 0% of the time, Pallas kernels for 2%

profile of v7, /device:TPU:1, one launch (start us, length us, event | category | flops | bytes accessed | tf_op | source)
XLA Modules:
  0.0 63.1 jit_solution(17327561355934448323)
XLA Ops:
  0.6 1.9 %shard_map.76 = (f32[6,8,8,256]{3,2,1,0:T(8,128)}, f32[26,8,256]{2,1,0:T(8,128)}, f32[26,8,256]{2,1,0:T(8,128)}) custom-call(f32[3,8,8,256]{3,2,1,0:T(8,128)} %shift_ref.1, f32[8,8,256]{2,1,0:T(8,128)} %physical_ref.1, f32[8,8,256]{2,1,0:T(8,128)} %design_ref.1, s32[8,8,256]{2,1,0:T(8,128)} %passive_ref.1), custom_call_target="tpu_custom_call" | custom-call | flops 1000000 | bytes 1000000 | tf_op jit(solution)/shard_map/pallas_call | solution.py:511
  2.6 0.0 copy-start.1
  2.6 2.2 %collective-permute-start = (f32[26,8,256]{2,1,0:T(8,128)}, f32[26,8,256]{2,1,0:T(8,128)S(1)}, u32[]{:S(2)}, u32[]{:S(2)}) collective-permute-start(f32[26,8,256]{2,1,0:T(8,128)} %get-tuple-element.26), channel_id=1, source_target_pairs={{0,16},{32,48},{64,80},{96,112},{128,144},{160,176},{192,208},{224... | collective-permute-start | bytes 638984 | tf_op jit(solution)/shard_map/ppermute | solution.py:527
  4.8 4.1 %collective-permute-start.1 = (f32[26,8,256]{2,1,0:T(8,128)}, f32[26,8,256]{2,1,0:T(8,128)S(1)}, u32[]{:S(2)}, u32[]{:S(2)}) collective-permute-start(f32[26,8,256]{2,1,0:T(8,128)} %get-tuple-element.27), channel_id=1, source_target_pairs={{16,32},{48,64},{80,96},{112,128},{144,160},{176,192},{208,224},{2... | collective-permute-start | bytes 638984 | tf_op jit(solution)/shard_map/ppermute | solution.py:527
  8.9 0.0 copy-done.1
  8.9 0.0 copy-start
  8.9 1.0 %copy-done = f32[6,8,8,256]{3,2,1,0:T(8,128)S(1)} copy-done((f32[6,8,8,256]{3,2,1,0:T(8,128)S(1)}, f32[6,8,8,256]{3,2,1,0:T(8,128)}, u32[]{:S(2)}) %copy-start) | copy-done | bytes 393240
  9.9 1.3 %shard_map.77 = (f32[6,8,8,256]{3,2,1,0:T(8,128)S(1)}, f32[17,16,384]{2,1,0:T(8,128)S(1)}, f32[13,8,384]{2,1,0:T(8,128)S(1)}, f32[8,8,256]{2,1,0:T(8,128)S(1)}) custom-call(f32[6,8,8,256]{3,2,1,0:T(8,128)S(1)} %copy-done, s32[1,1024]{1,0:T(1,128)S(1)} %bitcast.1), custom_call_target="tpu_custom_call" | custom-call | flops 10000000 | bytes 1000000 | tf_op jit(solution)/shard_map/pallas_call | solution.py:511
  11.2 0.0 collective-permute-done.x_first
  11.3 2.6 %collective-permute-done.1.x_second = f32[26,8,256]{2,1,0:T(8,128)S(1)} collective-permute-done((f32[26,8,256]{2,1,0:T(8,128)}, f32[26,8,256]{2,1,0:T(8,128)S(1)}, u32[]{:S(2)}, u32[]{:S(2)}) %collective-permute-start.1) | collective-permute-done | bytes 213024 | tf_op jit(solution)/shard_map/ppermute | solution.py:527
  13.9 0.2 shard_map.78
  14.0 2.0 %collective-permute-start.2 = (f32[198,256]{1,0:T(8,128)S(1)}, f32[198,256]{1,0:T(8,128)S(1)}, u32[]{:S(2)}, u32[]{:S(2)}) collective-permute-start(f32[198,256]{1,0:T(8,128)S(1)} %get-tuple-element.36), channel_id=1, source_target_pairs={{0,2},{4,6},{8,10},{12,14},{2,0},{6,4},{10,8},{14,12},{1,3},{5,7},... | collective-permute-start | bytes 608264 | tf_op jit(solution)/shard_map/ppermute | solution.py:527
  16.0 4.7 %collective-permute-start.3 = (f32[198,256]{1,0:T(8,128)S(1)}, f32[198,256]{1,0:T(8,128)S(1)}, u32[]{:S(2)}, u32[]{:S(2)}) collective-permute-start(f32[198,256]{1,0:T(8,128)S(1)} %get-tuple-element.37), channel_id=1, source_target_pairs={{2,4},{6,8},{10,12},{14,0},{4,2},{8,6},{12,10},{0,14},{3,5},{7,9},... | collective-permute-start | bytes 608264 | tf_op jit(solution)/shard_map/ppermute | solution.py:527
  20.7 2.4 %collective-permute-start.4 = (f32[98,8,128]{2,1,0:T(8,128)S(1)}, f32[98,8,128]{2,1,0:T(8,128)S(1)}, u32[]{:S(2)}, u32[]{:S(2)}) collective-permute-start(f32[98,8,128]{2,1,0:T(8,128)S(1)} %get-tuple-element.38), channel_id=1, source_target_pairs={{0,1},{1,0},{2,3},{3,2},{4,5},{5,4},{6,7},{7,6},{8,9},{9,8},{10,11... | collective-permute-start | bytes 1204232 | tf_op jit(solution)/shard_map/ppermute | solution.py:532
  23.1 0.0 collective-permute-done.2.y_first
  23.1 0.7 %collective-permute-done.3.y_second = f32[198,256]{1,0:T(8,128)S(1)} collective-permute-done((f32[198,256]{1,0:T(8,128)S(1)}, f32[198,256]{1,0:T(8,128)S(1)}, u32[]{:S(2)}, u32[]{:S(2)}) %collective-permute-start.3) | collective-permute-done | bytes 202784 | tf_op jit(solution)/shard_map/ppermute | solution.py:527
  23.9 0.2 shard_map.79
  24.1 3.1 %collective-permute-start.5 = (f32[72,8,128]{2,1,0:T(8,128)S(1)}, f32[72,8,128]{2,1,0:T(8,128)S(1)}, u32[]{:S(2)}, u32[]{:S(2)}) collective-permute-start(f32[72,8,128]{2,1,0:T(8,128)S(1)} %shard_map.79), channel_id=1, source_target_pairs={{0,1},{1,0},{2,3},{3,2},{4,5},{5,4},{6,7},{7,6},{8,9},{9,8},{10,11... | collective-permute-start | bytes 884744 | tf_op jit(solution)/shard_map/ppermute | solution.py:532
  27.2 0.0 collective-permute-done.4.side
  27.2 1.2 %collective-permute-done.5.y_side = f32[72,8,128]{2,1,0:T(8,128)S(1)} collective-permute-done((f32[72,8,128]{2,1,0:T(8,128)S(1)}, f32[72,8,128]{2,1,0:T(8,128)S(1)}, u32[]{:S(2)}, u32[]{:S(2)}) %collective-permute-start.5) | collective-permute-done | bytes 294944 | tf_op jit(solution)/shard_map/ppermute | solution.py:532
  28.4 6.9 %shard_map.80 = (f32[3,13,8,384]{3,2,1,0:T(8,128)S(1)}, f32[117,384]{1,0:T(8,128)S(1)}, f32[117,384]{1,0:T(8,128)S(1)}, f32[16,8,128]{2,1,0:T(8,128)S(1)}) custom-call(f32[6,8,8,256]{3,2,1,0:T(8,128)S(1)} %get-tuple-element.33.own_ref, f32[26,8,256]{2,1,0:T(8,128)S(1)} %collective-permute-done.x_first, f32[26,8,256]{2,1,0:T(8,128)S(1)} %collective-permute-done.1.x_second, ...), custom_call_target="tpu_custom_call" | custom-call | flops 10000000 | bytes 1000000 | tf_op jit(solution)/shard_map/pallas_call | solution.py:511
  35.3 13.8 %all_to_all.10.part_ref = f32[16,8,128]{2,1,0:T(8,128)S(1)} all-to-all(f32[16,8,128]{2,1,0:T(8,128)S(1)} %get-tuple-element.43), channel_id=1, replica_groups=mesh['gx'=16,'gy'=8,'gz'=2] {'gy','gz'}, dimensions={0} | all-to-all | bytes 131072 | tf_op jit(solution)/shard_map/all_to_all | solution.py:575
  49.2 0.2 collective-permute-start.6
  49.4 0.4 collective-permute-start.7
  49.7 11.8 %all_to_all.11.part_ref = f32[16,8,128]{2,1,0:T(8,128)S(1)} all-to-all(f32[16,8,128]{2,1,0:T(8,128)S(1)} %shard_map.81), channel_id=1, replica_groups=mesh['gx'=16,'gy'=8,'gz'=2] {'gx'}, dimensions={0} | all-to-all | bytes 131072 | tf_op jit(solution)/shard_map/all_to_all | solution.py:579
  61.5 0.0 collective-permute-done.6.y_first
  61.5 0.0 collective-permute-done.7.y_second
  61.5 1.6 %shard_map.82 = (f32[8,8,256]{2,1,0:T(8,128)}, f32[8,8,256]{2,1,0:T(8,128)}, f32[6,8,8,256]{3,2,1,0:T(8,128)}) custom-call(f32[16,8,128]{2,1,0:T(8,128)S(1)} %all_to_all.11.part_ref, f32[3,13,8,384]{3,2,1,0:T(8,128)S(1)} %get-tuple-element.45.own_ref, f32[117,384]{1,0:T(8,128)S(1)} %collective-permute-done.6.y_first, ...), custom_call_target="tpu_custom_call" | custom-call | flops 10000000 | bytes 1000000 | tf_op jit(solution)/shard_map/pallas_call | solution.py:511
  (1 shorter events, 0.0 us)
Async XLA Ops:
  2.6 6.3 %copy-start.1 = (s32[1024]{0:T(1024)S(1)}, s32[1024]{0:T(1024)}, u32[]{:S(2)}) copy-start(s32[1024]{0:T(1024)} %param.9) | copy-start | bytes 12292
  2.6 8.7 %collective-permute-start = (f32[26,8,256]{2,1,0:T(8,128)}, f32[26,8,256]{2,1,0:T(8,128)S(1)}, u32[]{:S(2)}, u32[]{:S(2)}) collective-permute-start(f32[26,8,256]{2,1,0:T(8,128)} %get-tuple-element.26), channel_id=1, source_target_pairs={{0,16},{32,48},{64,80},{96,112},{128,144},{160,176},{192,208},{224... | collective-permute-start | bytes 638984 | tf_op jit(solution)/shard_map/ppermute | solution.py:527
  4.8 9.1 %collective-permute-start.1 = (f32[26,8,256]{2,1,0:T(8,128)}, f32[26,8,256]{2,1,0:T(8,128)S(1)}, u32[]{:S(2)}, u32[]{:S(2)}) collective-permute-start(f32[26,8,256]{2,1,0:T(8,128)} %get-tuple-element.27), channel_id=1, source_target_pairs={{16,32},{48,64},{80,96},{112,128},{144,160},{176,192},{208,224},{2... | collective-permute-start | bytes 638984 | tf_op jit(solution)/shard_map/ppermute | solution.py:527
  8.9 1.0 %copy-start = (f32[6,8,8,256]{3,2,1,0:T(8,128)S(1)}, f32[6,8,8,256]{3,2,1,0:T(8,128)}, u32[]{:S(2)}) copy-start(f32[6,8,8,256]{3,2,1,0:T(8,128)} %get-tuple-element.28.own_ref) | copy-start | bytes 1179652
  14.0 9.1 %collective-permute-start.2 = (f32[198,256]{1,0:T(8,128)S(1)}, f32[198,256]{1,0:T(8,128)S(1)}, u32[]{:S(2)}, u32[]{:S(2)}) collective-permute-start(f32[198,256]{1,0:T(8,128)S(1)} %get-tuple-element.36), channel_id=1, source_target_pairs={{0,2},{4,6},{8,10},{12,14},{2,0},{6,4},{10,8},{14,12},{1,3},{5,7},... | collective-permute-start | bytes 608264 | tf_op jit(solution)/shard_map/ppermute | solution.py:527
  16.0 7.8 %collective-permute-start.3 = (f32[198,256]{1,0:T(8,128)S(1)}, f32[198,256]{1,0:T(8,128)S(1)}, u32[]{:S(2)}, u32[]{:S(2)}) collective-permute-start(f32[198,256]{1,0:T(8,128)S(1)} %get-tuple-element.37), channel_id=1, source_target_pairs={{2,4},{6,8},{10,12},{14,0},{4,2},{8,6},{12,10},{0,14},{3,5},{7,9},... | collective-permute-start | bytes 608264 | tf_op jit(solution)/shard_map/ppermute | solution.py:527
  20.7 6.4 %collective-permute-start.4 = (f32[98,8,128]{2,1,0:T(8,128)S(1)}, f32[98,8,128]{2,1,0:T(8,128)S(1)}, u32[]{:S(2)}, u32[]{:S(2)}) collective-permute-start(f32[98,8,128]{2,1,0:T(8,128)S(1)} %get-tuple-element.38), channel_id=1, source_target_pairs={{0,1},{1,0},{2,3},{3,2},{4,5},{5,4},{6,7},{7,6},{8,9},{9,8},{10,11... | collective-permute-start | bytes 1204232 | tf_op jit(solution)/shard_map/ppermute | solution.py:532
  24.1 4.3 %collective-permute-start.5 = (f32[72,8,128]{2,1,0:T(8,128)S(1)}, f32[72,8,128]{2,1,0:T(8,128)S(1)}, u32[]{:S(2)}, u32[]{:S(2)}) collective-permute-start(f32[72,8,128]{2,1,0:T(8,128)S(1)} %shard_map.79), channel_id=1, source_target_pairs={{0,1},{1,0},{2,3},{3,2},{4,5},{5,4},{6,7},{7,6},{8,9},{9,8},{10,11... | collective-permute-start | bytes 884744 | tf_op jit(solution)/shard_map/ppermute | solution.py:532
  49.2 12.4 %collective-permute-start.6 = (f32[117,384]{1,0:T(8,128)S(1)}, f32[117,384]{1,0:T(8,128)S(1)}, u32[]{:S(2)}, u32[]{:S(2)}) collective-permute-start(f32[117,384]{1,0:T(8,128)S(1)} %get-tuple-element.46), channel_id=1, source_target_pairs={{0,2},{4,6},{8,10},{12,14},{2,0},{6,4},{10,8},{14,12},{1,3},{5,7},... | collective-permute-start | bytes 539144 | tf_op jit(solution)/shard_map/ppermute | solution.py:527
  49.4 12.2 %collective-permute-start.7 = (f32[117,384]{1,0:T(8,128)S(1)}, f32[117,384]{1,0:T(8,128)S(1)}, u32[]{:S(2)}, u32[]{:S(2)}) collective-permute-start(f32[117,384]{1,0:T(8,128)S(1)} %get-tuple-element.47), channel_id=1, source_target_pairs={{2,4},{6,8},{10,12},{14,0},{4,2},{8,6},{12,10},{0,14},{3,5},{7,9},... | collective-permute-start | bytes 539144 | tf_op jit(solution)/shard_map/ppermute | solution.py:527

commit v8 on v7

--- a/solution.py
+++ b/solution.py
@@ -158,11 +158,7 @@
     return middle + (rolled(near, 1, 1) + rolled(near, -1, 1)) + (rolled(far, 2, 1) + rolled(far, -2, 1))
 
 
-def weights_kernel(
-    own_ref, support_ref, own_copy, inverse_ref, volume_ref, mark_ref, near_ref, far_ref, semaphore, *, extents
-):
-    copy = pltpu.make_async_copy(own_ref, own_copy, semaphore)
-    copy.start()
+def weights_kernel(support_ref, inverse_ref, volume_ref, mark_ref, near_ref, far_ref, *, extents):
     total_x, total_y, total_z = extents
     first_x = lax.axis_index("gx") * SX
     first_y = lax.axis_index("gy") * SY
@@ -210,7 +206,6 @@
     )
     for p in range(SX):
         mark_ref[p] = hits[p * SY : (p + 1) * SY]
-    copy.wait()
 
 
 def is_even(axis):
@@ -242,77 +237,60 @@
     return jnp.concatenate([high, filler, low], axis=0)
 
 
-def faces_x_kernel(
-    shift_ref, physical_ref, design_ref, passive_ref, own_ref, first_ref, second_ref, passive_own, semaphores
-):
-    pairs = (
-        (shift_ref, own_ref.at[0:3]),
-        (physical_ref, own_ref.at[3]),
-        (design_ref, own_ref.at[4]),
-        (passive_ref, passive_own),
-    )
-    copies = [pltpu.make_async_copy(*pair, semaphores.at[n]) for n, pair in enumerate(pairs)]
-    for copy in copies:
-        copy.start()
-    for copy in copies:
-        copy.wait()
-    own_ref[5] = passive_own[...].astype(F32)
-    even = is_even("gx")
-    for f in range(6):
-        depth = 5 if f < 4 else 3
-        row = 5 * f if f < 4 else 8 + 3 * f
-        place_pair(
-            even, first_ref, second_ref, own_ref[f, SX - depth :], own_ref[f, 0:depth], slice(row, row + depth)
-        )
-
-
-def plane_reader(own_ref, x_first, x_second):
+def plane_reader(shift_ref, physical_ref, x_first, x_second):
     def read(index):
-        if index < 4 * NODES:
-            f, x = index // NODES, index % NODES - 5
-            depth, base = 5, 5 * f
-        else:
-            f, x = 4 + (index - 4 * NODES) // CHOSEN, (index - 4 * NODES) % CHOSEN - 3
-            depth, base = 3, 8 + 3 * f
+        f, x = index // NODES, index % NODES - 5
         if 0 <= x < SX:
-            return own_ref[f, x]
-        low, high = low_high("gx", x_first, x_second, base + (x + depth if x < 0 else x - SX))
+            return shift_ref[f, x] if f < 3 else physical_ref[x]
+        low, high = low_high("gx", x_first, x_second, (f, x + 5 if x < 0 else x - SX))
         return low if x < 0 else high
 
     return read
 
 
-def faces_y_kernel(
-    own_ref, x_first, x_second, first_ref, second_ref, side_ref
-):
+def design_reader(design_ref, passive_ref, x_first, x_second):
+    def read(index):
+        f, x = index // CHOSEN, index % CHOSEN - 3
+        if 0 <= x < SX:
+            return design_ref[x] if f == 0 else passive_ref[x].astype(F32)
+        low, high = low_high("gx", x_first, x_second, (f, x + 3 if x < 0 else x - SX))
+        return low if x < 0 else high
+
+    return read
+
+
+def near_half(plane):
+    return jnp.where(lax.axis_index("gz") == 0, plane[:, SZ - SIDE :], plane[:, 0:SIDE])
+
+
+def faces_y_kernel(shift_ref, physical_ref, x_first, x_second, first_ref, second_ref, side_ref):
     even = is_even("gy")
-    lower_core = lax.axis_index("gz") == 0
-    read = plane_reader(own_ref, x_first, x_second)
-    for index in range(4 * NODES + 2 * CHOSEN):
+    read = plane_reader(shift_ref, physical_ref, x_first, x_second)
+    for index in range(4 * NODES):
         plane = read(index)
-        if index < 4 * NODES:
-            rows = row_place(index)
-            depth = rows.stop - rows.start
-            place_pair(even, first_ref, second_ref, plane[SY - depth :], plane[0:depth], rows)
-        side_ref[index] = jnp.where(lower_core, plane[:, SZ - SIDE :], plane[:, 0:SIDE])
-
-
-def faces_z_kernel(y_first, y_second, side_ref):
-    lower_core = lax.axis_index("gz") == 0
+        rows = row_place(index)
+        depth = rows.stop - rows.start
+        place_pair(even, first_ref, second_ref, plane[SY - depth :], plane[0:depth], rows)
+        side_ref[index] = near_half(plane)
+
+
+def faces_z_kernel(y_first, y_second, design_ref, passive_ref, d_first, d_second, side_ref):
     for index in range(4 * NODES):
-        tile = row_tile(y_first, y_second, row_place(index))
-        side_ref[index] = jnp.where(lower_core, tile[:, SZ - SIDE :], tile[:, 0:SIDE])
+        side_ref[index] = near_half(row_tile(y_first, y_second, row_place(index)))
+    read = design_reader(design_ref, passive_ref, d_first, d_second)
+    for index in range(2 * CHOSEN):
+        side_ref[4 * NODES + index] = near_half(read(index))
 
 
 def design_kernel(
-    own_ref, x_first, x_second, y_first, y_second, side, y_side, inverse_ref, volume_ref, out_ref, first_ref,
-    second_ref, part_ref, ext_ref, sens_ref, near_ref, far_ref, high_ref, low_ref, value_ref, *, groups
+    shift_ref, physical_ref, design_ref, passive_ref, x_first, x_second, y_first, y_second, d_first, d_second,
+    side, y_side, inverse_ref, volume_ref, out_ref, first_ref, second_ref, part_ref, ext_ref, sens_ref, near_ref, far_ref, high_ref, low_ref, value_ref, *, groups
 ):
     lane = lax.broadcasted_iota(jnp.int32, (SY, SIDE), 1)
     start = lax.axis_index("gz") * (SIDE // 2)
     keep = (lane >= start) & (lane < start + SIDE // 2)
     even = is_even("gy")
-    read = plane_reader(own_ref, x_first, x_second)
+    read = plane_reader(shift_ref, physical_ref, x_first, x_second)
     for f in range(4):
         for p in range(NODES):
             index = NODES * f + p
@@ -348,11 +326,12 @@
         near_ref[p] = near[0:SY]
         far_ref[p] = far[0:SY]
 
+    read_design = design_reader(design_ref, passive_ref, d_first, d_second)
     for p in range(CHOSEN):
         filtered = filtered_plane(lambda q: sens_ref[q], lambda q: near_ref[q], lambda q: far_ref[q], p + 2)
         index = 4 * NODES + p
-        design = jnp.concatenate([read(index), side[index]], axis=1)
-        solid = jnp.concatenate([read(index + CHOSEN), side[index + CHOSEN]], axis=1) > 0.5
+        design = jnp.concatenate([read_design(p), y_side[index]], axis=1)
+        solid = jnp.concatenate([read_design(p + CHOSEN), y_side[index + CHOSEN]], axis=1) > 0.5
         inside = inverse_ref[p + 2, 0:SY] > 0.0
         scaled = design * jnp.sqrt(filtered / jnp.where(inside, volume_ref[p], 1.0))
         floor_bound = jnp.where(solid, 1.0, jnp.maximum(0.0, design - move_limit))
@@ -537,28 +516,35 @@
     sizes = [lax.axis_size(axis) for axis in ("gx", "gy", "gz")]
     extents = (SX * sizes[0], SY * sizes[1], SZ * sizes[2])
     block = (SX, SY, SZ)
-    faces = (26, SY, SZ)
-    own, *x_faces = call(
-        faces_x_kernel, (displacement, physical, design, passive), [(6,) + block, faces, faces],
-        [pltpu.VMEM(block, jnp.int32), pltpu.SemaphoreType.DMA((4,))], 10**6, [pltpu.HBM] * 4, 62,
-    )
-    x_faces = exchange(*x_faces, "gx")
+    even = lax.axis_index("gx") % 2 == 0
+
+    def swaps(fields, depth):
+        top, bottom = fields[:, SX - depth :], fields[:, 0:depth]
+        return jnp.where(even, top, bottom), jnp.where(even, bottom, top)
+
+    x_faces = exchange(*swaps(jnp.concatenate([displacement, physical[None]], axis=0), 5), "gx")
     frame = (ELEMENTS, ROWS, LANES)
     own_frame = (ELEMENTS, SY, LANES)
     weights = call(
-        functools.partial(weights_kernel, extents=extents), (own, supports.reshape(1, -1)),
-        [(6,) + block, frame, (CHOSEN, SY, LANES), block],
-        [own_frame, own_frame, pltpu.SemaphoreType.DMA(())], 10**7, [pltpu.HBM, pltpu.VMEM],
-    )
-    x_faces, (own, inverse, volume_weight, marks) = lax.optimization_barrier((x_faces, weights))
+        functools.partial(weights_kernel, extents=extents), (supports.reshape(1, -1),),
+        [frame, (CHOSEN, SY, LANES), block], [own_frame, own_frame], 10**7,
+    )
+    design_faces = swaps(jnp.stack([design, passive.astype(F32)]), 3)
+    x_faces, design_faces, (inverse, volume_weight, marks) = lax.optimization_barrier(
+        (x_faces, design_faces, weights)
+    )
 
     faces = (11 * NODES, SZ)
     *y_faces, side = call(
-        faces_y_kernel, (own, *x_faces), [faces, faces, (4 * NODES + 2 * CHOSEN, SY, SIDE)], [], 10**6
-    )
+        faces_y_kernel, (displacement, physical, *x_faces), [faces, faces, (4 * NODES, SY, SIDE)], [], 10**6
+    )
+    y_faces, side, design_faces = lax.optimization_barrier((y_faces, side, design_faces))
     y_faces = exchange(*y_faces, "gy")
-    side = other_core(side)
-    (y_side,) = call(faces_z_kernel, y_faces, [(4 * NODES, SY, SIDE)], [], 10**6)
+    design_faces = exchange(*design_faces, "gx")
+    y_faces, side = lax.optimization_barrier((y_faces, other_core(side)))
+    (y_side,) = call(
+        faces_z_kernel, (*y_faces, design, passive, *design_faces), [(4 * NODES + 2 * CHOSEN, SY, SIDE)], [], 10**6
+    )
     y_side = other_core(y_side)
 
     faces = (9 * CHOSEN, LANES)
@@ -566,7 +552,8 @@
     elements = (2 * SX, SY, 128)
     bounds, *y_bounds, part = call(
         functools.partial(design_kernel, groups=energy_groups()),
-        (own, *x_faces, *y_faces, side, y_side, inverse, volume_weight),
+        (displacement, physical, design, passive, *x_faces, *y_faces, *design_faces, side, y_side, inverse,
+         volume_weight),
         [(3, CHOSEN, SY, LANES), faces, faces, (inner, 8, 128)],
         [(4, NODES, ROWS, LANES), own_frame, own_frame, own_frame]
         + [(2,) + elements, (2,) + elements, (2, 6) + elements], 10**7,

time: 63.4 us -> 62.5 us (0.986)
  blocking collectives: 25.6 us -> 22.3 us
  waiting for transfers between devices: 4.54 us -> 7.2 us
  Pallas kernels: 12.2 us -> 10.1 us
  other arithmetic: 0 us -> 1.18 us
  starting transfers between devices: 19.1 us -> 20.2 us
    all_to_all x1, blocking collectives: 13.8 us -> 11.3 us  [body(): part = lax.all_to_all(part, ('gy', 'gz'), 0, 0, tiled=True)]
    ppermute x6 -> x8, starting transfers between devices: 13.5 us -> 16.1 us  [exchange(): lax.ppermute(faces, axis, pairs + [(j, i) for i, j in pairs])]
    ppermute x6 -> x8, waiting for transfers between devices: 3.33 us -> 5.83 us  [exchange(): lax.ppermute(faces, axis, pairs + [(j, i) for i, j in pairs])]
    pallas_call x7 -> x6, Pallas kernels: 12.2 us -> 10.1 us  [call(): pl.pallas_call(kernel, out_shape=outs, in_specs=[pl.BlockSpec(memory_spac...]
    ppermute x2, starting transfers between devices: 5.53 us -> 4.11 us  [other_core(): return lax.ppermute(values, 'gz', [(0, 1), (1, 0)])]
    select_n x0 -> x2, other arithmetic: none -> 1.17 us  [swaps(): return (jnp.where(even, top, bottom), jnp.where(even, bottom, top))]
    all_to_all x1, blocking collectives: 11.8 us -> 11 us  [body(): part = lax.all_to_all(part, 'gx', 0, 0, tiled=True)]
  transfers between devices with their start and end apart: 8 -> 10, of which waited for: 3 -> 5; matrix products, arithmetic and copies ran while one was open for 0% -> 0% of each run, Pallas kernels for 2% -> 2%
where the time goes in v8:
time: 62.5 us; the launch traced here: 62.3 us
  blocking collectives  22.3 us (36%)
  starting transfers between devices  20.2 us (32%)
  Pallas kernels  10.1 us (16%)
  waiting for transfers between devices  7.2 us (12%)
  other arithmetic  1.18 us (2%)
  between operations  0.73 us (1%)
  local copies, waits for them, and re-layouts  0.67 us (1%)
    ppermute x8, starting transfers between devices, exchange(): lax.ppermute(faces, axis, pairs + [(j, i) for i, j in pairs])  16.1 us
    all_to_all x1, blocking collectives, body(): part = lax.all_to_all(part, ('gy', 'gz'), 0, 0, tiled=True)  11.3 us
    all_to_all x1, blocking collectives, body(): part = lax.all_to_all(part, 'gx', 0, 0, tiled=True)  11 us
    pallas_call x6, Pallas kernels, call(): pl.pallas_call(kernel, out_shape=outs, in_specs=[pl.BlockSpec(memory_spac...  10.1 us
    ppermute x8, waiting for transfers between devices, exchange(): lax.ppermute(faces, axis, pairs + [(j, i) for i, j in pairs])  5.83 us
    ppermute x2, starting transfers between devices, other_core(): return lax.ppermute(values, 'gz', [(0, 1), (1, 0)])  4.11 us
    ppermute x2, waiting for transfers between devices, other_core(): return lax.ppermute(values, 'gz', [(0, 1), (1, 0)])  1.36 us
  transfers between devices with their start and end apart: 10, of which 5 were waited for; matrix products, arithmetic and copies ran while one was open for 0% of the time, Pallas kernels for 2%

profile of v8, /device:TPU:1, one launch (start us, length us, event | category | flops | bytes accessed | tf_op | source)
XLA Modules:
  0.0 62.3 jit_solution(12279298747434731731)
XLA Ops:
  0.6 0.0 copy-start.2
  0.7 1.2 %fusion.2 = (f32[4,5,8,256]{3,2,1,0:T(8,128)S(1)}, f32[4,5,8,256]{3,2,1,0:T(8,128)S(1)}) fusion(f32[1,8,8,256]{3,2,1,0:T(8,128)} %bitcast.6, f32[3,8,8,256]{3,2,1,0:T(8,128)} %shift_ref.3, pred[]{:T(512)S(6)} %eq.5), kind=kLoop, calls=%fused_computation.5 | loop fusion | flops 204800 | bytes 589825 | tf_op jit(solution)/shard_map/jit(_where)/select_n | solution.py:523
  1.8 5.8 %collective-permute-start.1 = (f32[4,5,8,256]{3,2,1,0:T(8,128)S(1)}, f32[4,5,8,256]{3,2,1,0:T(8,128)S(1)}, u32[]{:S(2)}, u32[]{:S(2)}) collective-permute-start(f32[4,5,8,256]{3,2,1,0:T(8,128)S(1)} %get-tuple-element.59), channel_id=1, source_target_pairs={{16,32},{48,64},{80,96},{112,128},{144,160},{176,192},{208,224},{2... | collective-permute-start | bytes 491528 | tf_op jit(solution)/shard_map/ppermute | solution.py:506
  7.7 0.0 copy-start.4
  7.7 0.0 copy-start.1
  7.7 0.0 copy-start
  7.7 0.0 collective-permute-start
  7.7 0.0 copy-done.2
  7.7 0.6 %copy-done.4 = s32[1024]{0:T(1024)S(1)} copy-done((s32[1024]{0:T(1024)S(1)}, s32[1024]{0:T(1024)}, u32[]{:S(2)}) %copy-start.4) | copy-done | bytes 4120
  8.3 1.1 %shard_map.76 = (f32[17,16,384]{2,1,0:T(8,128)S(1)}, f32[13,8,384]{2,1,0:T(8,128)S(1)}, f32[8,8,256]{2,1,0:T(8,128)S(1)}) custom-call(s32[1,1024]{1,0:T(1,128)S(1)} %bitcast.7), custom_call_target="tpu_custom_call" | custom-call | flops 10000000 | bytes 1000000 | tf_op jit(solution)/shard_map/pallas_call | solution.py:490
  9.5 0.0 copy-done.1
  9.5 0.0 copy-start.3
  9.5 1.0 %collective-permute-done.1.x_second = f32[4,5,8,256]{3,2,1,0:T(8,128)S(1)} collective-permute-done((f32[4,5,8,256]{3,2,1,0:T(8,128)S(1)}, f32[4,5,8,256]{3,2,1,0:T(8,128)S(1)}, u32[]{:S(2)}, u32[]{:S(2)}) %collective-permute-start.1) | collective-permute-done | bytes 163872 | tf_op jit(solution)/shard_map/ppermute | solution.py:506
  10.5 1.9 %collective-permute-done.x_first = f32[4,5,8,256]{3,2,1,0:T(8,128)S(1)} collective-permute-done((f32[4,5,8,256]{3,2,1,0:T(8,128)S(1)}, f32[4,5,8,256]{3,2,1,0:T(8,128)S(1)}, u32[]{:S(2)}, u32[]{:S(2)}) %collective-permute-start) | collective-permute-done | bytes 163872 | tf_op jit(solution)/shard_map/ppermute | solution.py:506
  12.4 0.0 copy-done
  12.4 0.0 copy-done.3
  12.4 0.2 shard_map.77
  12.6 2.0 %collective-permute-start.4 = (f32[72,8,128]{2,1,0:T(8,128)S(1)}, f32[72,8,128]{2,1,0:T(8,128)S(1)}, u32[]{:S(2)}, u32[]{:S(2)}) collective-permute-start(f32[72,8,128]{2,1,0:T(8,128)S(1)} %get-tuple-element.43), channel_id=1, source_target_pairs={{0,1},{1,0},{2,3},{3,2},{4,5},{5,4},{6,7},{7,6},{8,9},{9,8},{10,11... | collective-permute-start | bytes 884744 | tf_op jit(solution)/shard_map/ppermute | solution.py:511
  14.5 1.7 %collective-permute-start.2 = (f32[198,256]{1,0:T(8,128)S(1)}, f32[198,256]{1,0:T(8,128)S(1)}, u32[]{:S(2)}, u32[]{:S(2)}) collective-permute-start(f32[198,256]{1,0:T(8,128)S(1)} %get-tuple-element.41), channel_id=1, source_target_pairs={{0,2},{4,6},{8,10},{12,14},{2,0},{6,4},{10,8},{14,12},{1,3},{5,7},... | collective-permute-start | bytes 608264 | tf_op jit(solution)/shard_map/ppermute | solution.py:506
  16.2 4.7 %collective-permute-start.3 = (f32[198,256]{1,0:T(8,128)S(1)}, f32[198,256]{1,0:T(8,128)S(1)}, u32[]{:S(2)}, u32[]{:S(2)}) collective-permute-start(f32[198,256]{1,0:T(8,128)S(1)} %get-tuple-element.42), channel_id=1, source_target_pairs={{2,4},{6,8},{10,12},{14,0},{4,2},{8,6},{12,10},{0,14},{3,5},{7,9},... | collective-permute-start | bytes 608264 | tf_op jit(solution)/shard_map/ppermute | solution.py:506
  20.9 0.0 collective-permute-start.5
  20.9 3.3 %collective-permute-start.6 = (f32[2,3,8,256]{3,2,1,0:T(8,128)S(1)}, f32[2,3,8,256]{3,2,1,0:T(8,128)S(1)}, u32[]{:S(2)}, u32[]{:S(2)}) collective-permute-start(f32[2,3,8,256]{3,2,1,0:T(8,128)S(1)} %get-tuple-element.47), channel_id=1, source_target_pairs={{16,32},{48,64},{80,96},{112,128},{144,160},{176,192},{208,224},{2... | collective-permute-start | bytes 147464 | tf_op jit(solution)/shard_map/ppermute | solution.py:506
  24.2 0.0 collective-permute-done.2.y_first
  24.2 1.8 %collective-permute-done.3.y_second = f32[198,256]{1,0:T(8,128)S(1)} collective-permute-done((f32[198,256]{1,0:T(8,128)S(1)}, f32[198,256]{1,0:T(8,128)S(1)}, u32[]{:S(2)}, u32[]{:S(2)}) %collective-permute-start.3) | collective-permute-done | bytes 202784 | tf_op jit(solution)/shard_map/ppermute | solution.py:506
  26.0 0.0 collective-permute-done.4.side
  26.0 0.0 collective-permute-done.5.d_first
  26.0 1.1 %collective-permute-done.6.d_second = f32[2,3,8,256]{3,2,1,0:T(8,128)S(1)} collective-permute-done((f32[2,3,8,256]{3,2,1,0:T(8,128)S(1)}, f32[2,3,8,256]{3,2,1,0:T(8,128)S(1)}, u32[]{:S(2)}, u32[]{:S(2)}) %collective-permute-start.6) | collective-permute-done | bytes 49184 | tf_op jit(solution)/shard_map/ppermute | solution.py:506
  27.1 0.2 shard_map.78
  27.3 2.2 %collective-permute-start.7 = (f32[98,8,128]{2,1,0:T(8,128)S(1)}, f32[98,8,128]{2,1,0:T(8,128)S(1)}, u32[]{:S(2)}, u32[]{:S(2)}) collective-permute-start(f32[98,8,128]{2,1,0:T(8,128)S(1)} %shard_map.78), channel_id=1, source_target_pairs={{0,1},{1,0},{2,3},{3,2},{4,5},{5,4},{6,7},{7,6},{8,9},{9,8},{10,11... | collective-permute-start | bytes 1204232 | tf_op jit(solution)/shard_map/ppermute | solution.py:511
  29.5 1.4 %collective-permute-done.7.y_side = f32[98,8,128]{2,1,0:T(8,128)S(1)} collective-permute-done((f32[98,8,128]{2,1,0:T(8,128)S(1)}, f32[98,8,128]{2,1,0:T(8,128)S(1)}, u32[]{:S(2)}, u32[]{:S(2)}) %collective-permute-start.7) | collective-permute-done | bytes 401440 | tf_op jit(solution)/shard_map/ppermute | solution.py:511
  30.9 7.0 %shard_map.79 = (f32[3,13,8,384]{3,2,1,0:T(8,128)S(1)}, f32[117,384]{1,0:T(8,128)S(1)}, f32[117,384]{1,0:T(8,128)S(1)}, f32[16,8,128]{2,1,0:T(8,128)S(1)}) custom-call(f32[3,8,8,256]{3,2,1,0:T(8,128)S(1)} %copy-done, f32[8,8,256]{2,1,0:T(8,128)S(1)} %copy-done.3, f32[8,8,256]{2,1,0:T(8,128)S(1)} %copy-done.1, s32[8,8,256]{2,1,0:T(8,128)S(1)} %copy-done.2, ...), custom_call_target="tpu_custom_call" | custom-call | flops 10000000 | bytes 1000000 | tf_op jit(solution)/shard_map/pallas_call | solution.py:490
  37.8 11.3 %all_to_all.10.part_ref = f32[16,8,128]{2,1,0:T(8,128)S(1)} all-to-all(f32[16,8,128]{2,1,0:T(8,128)S(1)} %get-tuple-element.53), channel_id=1, replica_groups=mesh['gx'=16,'gy'=8,'gz'=2] {'gy','gz'}, dimensions={0} | all-to-all | bytes 131072 | tf_op jit(solution)/shard_map/all_to_all | solution.py:562
  49.1 0.2 collective-permute-start.8
  49.3 0.4 collective-permute-start.9
  49.7 11.0 %all_to_all.11.part_ref = f32[16,8,128]{2,1,0:T(8,128)S(1)} all-to-all(f32[16,8,128]{2,1,0:T(8,128)S(1)} %shard_map.80), channel_id=1, replica_groups=mesh['gx'=16,'gy'=8,'gz'=2] {'gx'}, dimensions={0} | all-to-all | bytes 131072 | tf_op jit(solution)/shard_map/all_to_all | solution.py:566
  60.7 0.0 collective-permute-done.8.y_first
  60.7 0.0 collective-permute-done.9.y_second
  60.7 1.6 %shard_map.81 = (f32[8,8,256]{2,1,0:T(8,128)}, f32[8,8,256]{2,1,0:T(8,128)}, f32[6,8,8,256]{3,2,1,0:T(8,128)}) custom-call(f32[16,8,128]{2,1,0:T(8,128)S(1)} %all_to_all.11.part_ref, f32[3,13,8,384]{3,2,1,0:T(8,128)S(1)} %get-tuple-element.55.own_ref, f32[117,384]{1,0:T(8,128)S(1)} %collective-permute-done.8.y_first, ...), custom_call_target="tpu_custom_call" | custom-call | flops 10000000 | bytes 1000000 | tf_op jit(solution)/shard_map/pallas_call | solution.py:490
  (3 shorter events, 0.0 us)
Async XLA Ops:
  0.6 7.0 %copy-start.2 = (s32[8,8,256]{2,1,0:T(8,128)S(1)}, s32[8,8,256]{2,1,0:T(8,128)}, u32[]{:S(2)}) copy-start(s32[8,8,256]{2,1,0:T(8,128)} %passive_ref.3) | copy-start | bytes 196612
  1.8 8.7 %collective-permute-start.1 = (f32[4,5,8,256]{3,2,1,0:T(8,128)S(1)}, f32[4,5,8,256]{3,2,1,0:T(8,128)S(1)}, u32[]{:S(2)}, u32[]{:S(2)}) collective-permute-start(f32[4,5,8,256]{3,2,1,0:T(8,128)S(1)} %get-tuple-element.59), channel_id=1, source_target_pairs={{16,32},{48,64},{80,96},{112,128},{144,160},{176,192},{208,224},{2... | collective-permute-start | bytes 491528 | tf_op jit(solution)/shard_map/ppermute | solution.py:506
  7.7 0.7 %copy-start.4 = (s32[1024]{0:T(1024)S(1)}, s32[1024]{0:T(1024)}, u32[]{:S(2)}) copy-start(s32[1024]{0:T(1024)} %param.9) | copy-start | bytes 12292
  7.7 1.8 %copy-start.1 = (f32[8,8,256]{2,1,0:T(8,128)S(1)}, f32[8,8,256]{2,1,0:T(8,128)}, u32[]{:S(2)}) copy-start(f32[8,8,256]{2,1,0:T(8,128)} %design_ref.3) | copy-start | bytes 196612
  7.7 4.8 %copy-start = (f32[3,8,8,256]{3,2,1,0:T(8,128)S(1)}, f32[3,8,8,256]{3,2,1,0:T(8,128)}, u32[]{:S(2)}) copy-start(f32[3,8,8,256]{3,2,1,0:T(8,128)} %shift_ref.3) | copy-start | bytes 589828
  7.7 4.7 %collective-permute-start = (f32[4,5,8,256]{3,2,1,0:T(8,128)S(1)}, f32[4,5,8,256]{3,2,1,0:T(8,128)S(1)}, u32[]{:S(2)}, u32[]{:S(2)}) collective-permute-start(f32[4,5,8,256]{3,2,1,0:T(8,128)S(1)} %get-tuple-element.60), channel_id=1, source_target_pairs={{0,16},{32,48},{64,80},{96,112},{128,144},{160,176},{192,208},{224... | collective-permute-start | bytes 491528 | tf_op jit(solution)/shard_map/ppermute | solution.py:506
  9.5 2.9 %copy-start.3 = (f32[8,8,256]{2,1,0:T(8,128)S(1)}, f32[8,8,256]{2,1,0:T(8,128)}, u32[]{:S(2)}) copy-start(f32[8,8,256]{2,1,0:T(8,128)} %physical_ref.3) | copy-start | bytes 196612
  12.6 13.4 %collective-permute-start.4 = (f32[72,8,128]{2,1,0:T(8,128)S(1)}, f32[72,8,128]{2,1,0:T(8,128)S(1)}, u32[]{:S(2)}, u32[]{:S(2)}) collective-permute-start(f32[72,8,128]{2,1,0:T(8,128)S(1)} %get-tuple-element.43), channel_id=1, source_target_pairs={{0,1},{1,0},{2,3},{3,2},{4,5},{5,4},{6,7},{7,6},{8,9},{9,8},{10,11... | collective-permute-start | bytes 884744 | tf_op jit(solution)/shard_map/ppermute | solution.py:511
  14.5 9.7 %collective-permute-start.2 = (f32[198,256]{1,0:T(8,128)S(1)}, f32[198,256]{1,0:T(8,128)S(1)}, u32[]{:S(2)}, u32[]{:S(2)}) collective-permute-start(f32[198,256]{1,0:T(8,128)S(1)} %get-tuple-element.41), channel_id=1, source_target_pairs={{0,2},{4,6},{8,10},{12,14},{2,0},{6,4},{10,8},{14,12},{1,3},{5,7},... | collective-permute-start | bytes 608264 | tf_op jit(solution)/shard_map/ppermute | solution.py:506
  16.2 9.8 %collective-permute-start.3 = (f32[198,256]{1,0:T(8,128)S(1)}, f32[198,256]{1,0:T(8,128)S(1)}, u32[]{:S(2)}, u32[]{:S(2)}) collective-permute-start(f32[198,256]{1,0:T(8,128)S(1)} %get-tuple-element.42), channel_id=1, source_target_pairs={{2,4},{6,8},{10,12},{14,0},{4,2},{8,6},{12,10},{0,14},{3,5},{7,9},... | collective-permute-start | bytes 608264 | tf_op jit(solution)/shard_map/ppermute | solution.py:506
  20.9 5.2 %collective-permute-start.5 = (f32[2,3,8,256]{3,2,1,0:T(8,128)S(1)}, f32[2,3,8,256]{3,2,1,0:T(8,128)S(1)}, u32[]{:S(2)}, u32[]{:S(2)}) collective-permute-start(f32[2,3,8,256]{3,2,1,0:T(8,128)S(1)} %get-tuple-element.46), channel_id=1, source_target_pairs={{0,16},{32,48},{64,80},{96,112},{128,144},{160,176},{192,208},{224... | collective-permute-start | bytes 147464 | tf_op jit(solution)/shard_map/ppermute | solution.py:506
  20.9 6.3 %collective-permute-start.6 = (f32[2,3,8,256]{3,2,1,0:T(8,128)S(1)}, f32[2,3,8,256]{3,2,1,0:T(8,128)S(1)}, u32[]{:S(2)}, u32[]{:S(2)}) collective-permute-start(f32[2,3,8,256]{3,2,1,0:T(8,128)S(1)} %get-tuple-element.47), channel_id=1, source_target_pairs={{16,32},{48,64},{80,96},{112,128},{144,160},{176,192},{208,224},{2... | collective-permute-start | bytes 147464 | tf_op jit(solution)/shard_map/ppermute | solution.py:506
  27.3 3.5 %collective-permute-start.7 = (f32[98,8,128]{2,1,0:T(8,128)S(1)}, f32[98,8,128]{2,1,0:T(8,128)S(1)}, u32[]{:S(2)}, u32[]{:S(2)}) collective-permute-start(f32[98,8,128]{2,1,0:T(8,128)S(1)} %shard_map.78), channel_id=1, source_target_pairs={{0,1},{1,0},{2,3},{3,2},{4,5},{5,4},{6,7},{7,6},{8,9},{9,8},{10,11... | collective-permute-start | bytes 1204232 | tf_op jit(solution)/shard_map/ppermute | solution.py:511
  49.1 11.6 %collective-permute-start.8 = (f32[117,384]{1,0:T(8,128)S(1)}, f32[117,384]{1,0:T(8,128)S(1)}, u32[]{:S(2)}, u32[]{:S(2)}) collective-permute-start(f32[117,384]{1,0:T(8,128)S(1)} %get-tuple-element.56), channel_id=1, source_target_pairs={{0,2},{4,6},{8,10},{12,14},{2,0},{6,4},{10,8},{14,12},{1,3},{5,7},... | collective-permute-start | bytes 539144 | tf_op jit(solution)/shard_map/ppermute | solution.py:506
  49.3 11.4 %collective-permute-start.9 = (f32[117,384]{1,0:T(8,128)S(1)}, f32[117,384]{1,0:T(8,128)S(1)}, u32[]{:S(2)}, u32[]{:S(2)}) collective-permute-start(f32[117,384]{1,0:T(8,128)S(1)} %get-tuple-element.57), channel_id=1, source_target_pairs={{2,4},{6,8},{10,12},{14,0},{4,2},{8,6},{12,10},{0,14},{3,5},{7,9},... | collective-permute-start | bytes 539144 | tf_op jit(solution)/shard_map/ppermute | solution.py:506

commit v9 on v8

--- a/solution.py
+++ b/solution.py
@@ -158,7 +158,7 @@
     return middle + (rolled(near, 1, 1) + rolled(near, -1, 1)) + (rolled(far, 2, 1) + rolled(far, -2, 1))
 
 
-def weights_kernel(support_ref, inverse_ref, volume_ref, mark_ref, near_ref, far_ref, *, extents):
+def weights_kernel(support_ref, inverse_ref, edge_ref, volume_ref, mark_ref, near_ref, far_ref, *, extents):
     total_x, total_y, total_z = extents
     first_x = lax.axis_index("gx") * SX
     first_y = lax.axis_index("gy") * SY
@@ -182,6 +182,7 @@
         here = inside * present(x)
         inverse = jnp.where(here > 0.0, 1.0 / jnp.where(here > 0.0, weight_sum, 1.0), 0.0)
         inverse_ref[p] = inverse
+        edge_ref[p] = jnp.concatenate([inverse[7:11], inverse[14:16], inverse[0:2]], axis=0)
         inverse_near, inverse_far = row_pairs(inverse)
         near_ref[p] = inverse_near[0:SY]
         far_ref[p] = inverse_far[0:SY]
@@ -263,7 +264,13 @@
     return jnp.where(lax.axis_index("gz") == 0, plane[:, SZ - SIDE :], plane[:, 0:SIDE])
 
 
-def faces_y_kernel(shift_ref, physical_ref, x_first, x_second, first_ref, second_ref, side_ref):
+def edge_tile(plane, low, high):
+    missing = 3 - high.shape[0]
+    filler = [jnp.zeros((missing, SZ), F32)] if missing else []
+    return jnp.concatenate([plane[7:8], high, *filler, low[low.shape[0] - 2 :], plane[0:2]], axis=0)
+
+
+def faces_y_kernel(shift_ref, physical_ref, x_first, x_second, first_ref, second_ref):
     even = is_even("gy")
     read = plane_reader(shift_ref, physical_ref, x_first, x_second)
     for index in range(4 * NODES):
@@ -271,33 +278,38 @@
         rows = row_place(index)
         depth = rows.stop - rows.start
         place_pair(even, first_ref, second_ref, plane[SY - depth :], plane[0:depth], rows)
-        side_ref[index] = near_half(plane)
-
-
-def faces_z_kernel(y_first, y_second, design_ref, passive_ref, d_first, d_second, side_ref):
+
+
+def faces_side_kernel(shift_ref, physical_ref, x_first, x_second, side_ref):
+    read = plane_reader(shift_ref, physical_ref, x_first, x_second)
     for index in range(4 * NODES):
-        side_ref[index] = near_half(row_tile(y_first, y_second, row_place(index)))
+        side_ref[index] = near_half(read(index))
+
+
+def faces_edge_kernel(
+    shift_ref, physical_ref, x_first, x_second, y_first, y_second, design_ref, passive_ref, d_first, d_second,
+    edge_ref, side_ref
+):
+    read = plane_reader(shift_ref, physical_ref, x_first, x_second)
+    for index in range(4 * NODES):
+        low, high = low_high("gy", y_first, y_second, row_place(index))
+        tile = edge_tile(read(index), low, high)
+        edge_ref[index] = tile
+        side_ref[index] = near_half(tile)
     read = design_reader(design_ref, passive_ref, d_first, d_second)
     for index in range(2 * CHOSEN):
         side_ref[4 * NODES + index] = near_half(read(index))
 
 
-def design_kernel(
-    shift_ref, physical_ref, design_ref, passive_ref, x_first, x_second, y_first, y_second, d_first, d_second,
-    side, y_side, inverse_ref, volume_ref, out_ref, first_ref, second_ref, part_ref, ext_ref, sens_ref, near_ref, far_ref, high_ref, low_ref, value_ref, *, groups
-):
+def scaled_energy(ext_ref, read, side, inverse_of, out_ref, groups):
     lane = lax.broadcasted_iota(jnp.int32, (SY, SIDE), 1)
     start = lax.axis_index("gz") * (SIDE // 2)
     keep = (lane >= start) & (lane < start + SIDE // 2)
-    even = is_even("gy")
-    read = plane_reader(shift_ref, physical_ref, x_first, x_second)
     for f in range(4):
         for p in range(NODES):
             index = NODES * f + p
-            ext_ref[f, p, 0:SY, 0:SZ] = read(index)
-            ext_ref[f, p, 0:SY, SZ:LANES] = jnp.where(keep, side[index], 0.0)
-            ext_ref[f, p, SY:ROWS, 0:SZ] = row_tile(y_first, y_second, row_place(index))
-            ext_ref[f, p, SY:ROWS, SZ:LANES] = jnp.where(keep, y_side[index], 0.0)
+            ext_ref[f, p, :, 0:SZ] = read(index)
+            ext_ref[f, p, :, SZ:LANES] = jnp.where(keep, side[index], 0.0)
     scale = penalty * (1.0 - stiff_floor)
 
     @pl.loop(0, ELEMENTS)
@@ -320,9 +332,30 @@
             squares = float(coefficient) * squares
             energy = squares if energy is None else energy + squares
         density = ext_ref[3, p]
-        sens = scale * density * density * energy * inverse_ref[p]
-        sens_ref[p] = sens[0:SY]
-        near, far = row_pairs(sens)
+        out_ref[p] = scale * density * density * energy * inverse_of(p)
+
+
+def inner_kernel(shift_ref, physical_ref, x_first, x_second, side, inverse_ref, out_ref, ext_ref, *, groups):
+    read = plane_reader(shift_ref, physical_ref, x_first, x_second)
+    scaled_energy(ext_ref, read, side, lambda p: inverse_ref[p, 0:SY], out_ref, groups)
+
+
+def design_kernel(
+    design_ref, passive_ref, d_first, d_second, inner_ref, edge_tiles, edge_side, inverse_ref, edge_ref, volume_ref,
+    out_ref, first_ref, second_ref, part_ref, ext_ref, outer_ref, sens_ref, near_ref, far_ref, high_ref, low_ref,
+    value_ref, *, groups
+):
+    even = is_even("gy")
+    scaled_energy(
+        ext_ref, lambda index: edge_tiles[index], edge_side, lambda p: edge_ref[p], outer_ref, groups
+    )
+    row = lax.broadcasted_iota(jnp.int32, (SY, LANES), 0)
+    for p in range(ELEMENTS):
+        outer = outer_ref[p]
+        own = jnp.where(row == 7, rolled(outer, -7, 0), inner_ref[p])
+        beyond = jnp.where(row < 4, rolled(outer, 1, 0), rolled(outer, -2, 0))
+        sens_ref[p] = own
+        near, far = row_pairs(jnp.concatenate([own, beyond], axis=0))
         near_ref[p] = near[0:SY]
         far_ref[p] = far[0:SY]
 
@@ -330,8 +363,8 @@
     for p in range(CHOSEN):
         filtered = filtered_plane(lambda q: sens_ref[q], lambda q: near_ref[q], lambda q: far_ref[q], p + 2)
         index = 4 * NODES + p
-        design = jnp.concatenate([read_design(p), y_side[index]], axis=1)
-        solid = jnp.concatenate([read_design(p + CHOSEN), y_side[index + CHOSEN]], axis=1) > 0.5
+        design = jnp.concatenate([read_design(p), edge_side[index]], axis=1)
+        solid = jnp.concatenate([read_design(p + CHOSEN), edge_side[index + CHOSEN]], axis=1) > 0.5
         inside = inverse_ref[p + 2, 0:SY] > 0.0
         scaled = design * jnp.sqrt(filtered / jnp.where(inside, volume_ref[p], 1.0))
         floor_bound = jnp.where(solid, 1.0, jnp.maximum(0.0, design - move_limit))
@@ -494,7 +527,7 @@
         out_specs=[pl.BlockSpec(memory_space=pltpu.VMEM)] * len(outs),
         scratch_shapes=[pltpu.VMEM(shape, F32) if isinstance(shape, tuple) else shape for shape in scratch],
         compiler_params=pltpu.CompilerParams(vmem_limit_bytes=grant * 2**20),
-        cost_estimate=pl.CostEstimate(flops=flops, bytes_accessed=10**6, transcendentals=0),
+        cost_estimate=pl.CostEstimate(flops=flops, bytes_accessed=min(flops, 10**6), transcendentals=0),
     )(*inputs)
 
 
@@ -527,35 +560,41 @@
     own_frame = (ELEMENTS, SY, LANES)
     weights = call(
         functools.partial(weights_kernel, extents=extents), (supports.reshape(1, -1),),
-        [frame, (CHOSEN, SY, LANES), block], [own_frame, own_frame], 10**7,
+        [frame, own_frame, (CHOSEN, SY, LANES), block], [own_frame, own_frame], 10**7,
     )
     design_faces = swaps(jnp.stack([design, passive.astype(F32)]), 3)
-    x_faces, design_faces, (inverse, volume_weight, marks) = lax.optimization_barrier(
+    x_faces, design_faces, (inverse, edge, volume_weight, marks) = lax.optimization_barrier(
         (x_faces, design_faces, weights)
     )
 
+    groups = energy_groups()
     faces = (11 * NODES, SZ)
-    *y_faces, side = call(
-        faces_y_kernel, (displacement, physical, *x_faces), [faces, faces, (4 * NODES, SY, SIDE)], [], 10**6
-    )
-    y_faces, side, design_faces = lax.optimization_barrier((y_faces, side, design_faces))
+    tiles = (4 * NODES, SY, SZ)
+    ext = (4, NODES, SY, LANES)
+    y_faces = call(faces_y_kernel, (displacement, physical, *x_faces), [faces, faces], [], 10**6)
+    y_faces, x_faces, design_faces = lax.optimization_barrier((y_faces, x_faces, design_faces))
     y_faces = exchange(*y_faces, "gy")
     design_faces = exchange(*design_faces, "gx")
-    y_faces, side = lax.optimization_barrier((y_faces, other_core(side)))
-    (y_side,) = call(
-        faces_z_kernel, (*y_faces, design, passive, *design_faces), [(4 * NODES + 2 * CHOSEN, SY, SIDE)], [], 10**6
-    )
-    y_side = other_core(y_side)
+    (side,) = call(faces_side_kernel, (displacement, physical, *x_faces), [(4 * NODES, SY, SIDE)], [], 1)
+    (inner_part,) = call(
+        functools.partial(inner_kernel, groups=groups),
+        (displacement, physical, *x_faces, other_core(side), inverse), [own_frame], [ext], 1,
+    )
+    y_faces, inner_part = lax.optimization_barrier((y_faces, inner_part))
+    edge_tiles, side = call(
+        faces_edge_kernel, (displacement, physical, *x_faces, *y_faces, design, passive, *design_faces),
+        [tiles, (4 * NODES + 2 * CHOSEN, SY, SIDE)], [], 10**6,
+    )
+    side = other_core(side)
 
     faces = (9 * CHOSEN, LANES)
     inner, outer = sizes[1] * sizes[2], sizes[0]
     elements = (2 * SX, SY, 128)
     bounds, *y_bounds, part = call(
-        functools.partial(design_kernel, groups=energy_groups()),
-        (displacement, physical, design, passive, *x_faces, *y_faces, *design_faces, side, y_side, inverse,
-         volume_weight),
+        functools.partial(design_kernel, groups=groups),
+        (design, passive, *design_faces, inner_part, edge_tiles, side, inverse, edge, volume_weight),
         [(3, CHOSEN, SY, LANES), faces, faces, (inner, 8, 128)],
-        [(4, NODES, ROWS, LANES), own_frame, own_frame, own_frame]
+        [ext, own_frame, own_frame, own_frame, own_frame]
         + [(2,) + elements, (2,) + elements, (2, 6) + elements], 10**7,
     )
 

time: 62.5 us -> 61.6 us (0.986)
  waiting for transfers between devices: 7.2 us -> 4.98 us
  Pallas kernels: 10.1 us -> 11.4 us
    ppermute x8, waiting for transfers between devices: 5.83 us -> 3.61 us  [exchange(): lax.ppermute(faces, axis, pairs + [(j, i) for i, j in pairs])]
    pallas_call x6 -> x8, Pallas kernels: 10.1 us -> 11.4 us  [call(): pl.pallas_call(kernel, out_shape=outs, in_specs=[pl.BlockSpec(memory_spac...]
  transfers between devices with their start and end apart: 10 -> 10, of which waited for: 5 -> 4; matrix products, arithmetic and copies ran while one was open for 0% -> 0% of each run, Pallas kernels for 2% -> 5%
where the time goes in v9:
time: 61.6 us; the launch traced here: 61.4 us
  blocking collectives  22.3 us (36%)
  starting transfers between devices  20.2 us (33%)
  Pallas kernels  11.4 us (19%)
  waiting for transfers between devices  4.98 us (8%)
  other arithmetic  1.18 us (2%)
  between operations  0.77 us (1%)
  local copies, waits for them, and re-layouts  0.67 us (1%)
    ppermute x8, starting transfers between devices, exchange(): lax.ppermute(faces, axis, pairs + [(j, i) for i, j in pairs])  16.1 us
    pallas_call x8, Pallas kernels, call(): pl.pallas_call(kernel, out_shape=outs, in_specs=[pl.BlockSpec(memory_spac...  11.4 us
    all_to_all x1, blocking collectives, body(): part = lax.all_to_all(part, ('gy', 'gz'), 0, 0, tiled=True)  11.3 us
    all_to_all x1, blocking collectives, body(): part = lax.all_to_all(part, 'gx', 0, 0, tiled=True)  11 us
    ppermute x2, starting transfers between devices, other_core(): return lax.ppermute(values, 'gz', [(0, 1), (1, 0)])  4.11 us
    ppermute x8, waiting for transfers between devices, exchange(): lax.ppermute(faces, axis, pairs + [(j, i) for i, j in pairs])  3.61 us
    ppermute x2, waiting for transfers between devices, other_core(): return lax.ppermute(values, 'gz', [(0, 1), (1, 0)])  1.36 us
  transfers between devices with their start and end apart: 10, of which 4 were waited for; matrix products, arithmetic and copies ran while one was open for 0% of the time, Pallas kernels for 5%

profile of v9, /device:TPU:1, one launch (start us, length us, event | category | flops | bytes accessed | tf_op | source)
XLA Modules:
  0.0 61.4 jit_solution(10107752827701779222)
XLA Ops:
  0.6 0.0 copy-start.3
  0.7 1.2 %fusion.2 = (f32[4,5,8,256]{3,2,1,0:T(8,128)S(1)}, f32[4,5,8,256]{3,2,1,0:T(8,128)S(1)}) fusion(f32[1,8,8,256]{3,2,1,0:T(8,128)} %bitcast.5, f32[3,8,8,256]{3,2,1,0:T(8,128)} %shift_ref.7, pred[]{:T(512)S(6)} %eq.5), kind=kLoop, calls=%fused_computation.5 | loop fusion | flops 204800 | bytes 589825 | tf_op jit(solution)/shard_map/jit(_where)/select_n | solution.py:556
  1.8 5.8 %collective-permute-start.1 = (f32[4,5,8,256]{3,2,1,0:T(8,128)S(1)}, f32[4,5,8,256]{3,2,1,0:T(8,128)S(1)}, u32[]{:S(2)}, u32[]{:S(2)}) collective-permute-start(f32[4,5,8,256]{3,2,1,0:T(8,128)S(1)} %get-tuple-element.67), channel_id=1, source_target_pairs={{16,32},{48,64},{80,96},{112,128},{144,160},{176,192},{208,224},{2... | collective-permute-start | bytes 491528 | tf_op jit(solution)/shard_map/ppermute | solution.py:539
  7.7 0.0 copy-start.4
  7.7 0.0 copy-start.2
  7.7 0.0 copy-start
  7.7 0.0 collective-permute-start
  7.7 0.0 copy-done.3
  7.7 0.6 %copy-done.4 = s32[1024]{0:T(1024)S(1)} copy-done((s32[1024]{0:T(1024)S(1)}, s32[1024]{0:T(1024)}, u32[]{:S(2)}) %copy-start.4) | copy-done | bytes 4120
  8.3 1.2 %shard_map.76 = (f32[17,16,384]{2,1,0:T(8,128)S(1)}, f32[17,8,384]{2,1,0:T(8,128)S(1)}, f32[13,8,384]{2,1,0:T(8,128)S(1)}, f32[8,8,256]{2,1,0:T(8,128)S(1)}) custom-call(s32[1,1024]{1,0:T(1,128)S(1)} %bitcast.7), custom_call_target="tpu_custom_call" | custom-call | flops 10000000 | bytes 1000000 | tf_op jit(solution)/shard_map/pallas_call | solution.py:523
  9.5 0.0 copy-done.2
  9.5 0.0 copy-start.1
  9.5 1.0 %collective-permute-done.1.x_second = f32[4,5,8,256]{3,2,1,0:T(8,128)S(1)} collective-permute-done((f32[4,5,8,256]{3,2,1,0:T(8,128)S(1)}, f32[4,5,8,256]{3,2,1,0:T(8,128)S(1)}, u32[]{:S(2)}, u32[]{:S(2)}) %collective-permute-start.1) | collective-permute-done | bytes 163872 | tf_op jit(solution)/shard_map/ppermute | solution.py:539
  10.5 1.9 %collective-permute-done.x_first = f32[4,5,8,256]{3,2,1,0:T(8,128)S(1)} collective-permute-done((f32[4,5,8,256]{3,2,1,0:T(8,128)S(1)}, f32[4,5,8,256]{3,2,1,0:T(8,128)S(1)}, u32[]{:S(2)}, u32[]{:S(2)}) %collective-permute-start) | collective-permute-done | bytes 163872 | tf_op jit(solution)/shard_map/ppermute | solution.py:539
  12.4 0.0 copy-done
  12.4 0.0 copy-done.1
  12.4 0.2 shard_map.77
  12.6 0.1 shard_map.78
  12.6 2.0 %collective-permute-start.6 = (f32[72,8,128]{2,1,0:T(8,128)S(1)}, f32[72,8,128]{2,1,0:T(8,128)S(1)}, u32[]{:S(2)}, u32[]{:S(2)}) collective-permute-start(f32[72,8,128]{2,1,0:T(8,128)S(1)} %shard_map.78), channel_id=1, source_target_pairs={{0,1},{1,0},{2,3},{3,2},{4,5},{5,4},{6,7},{7,6},{8,9},{9,8},{10,11... | collective-permute-start | bytes 884744 | tf_op jit(solution)/shard_map/ppermute | solution.py:544
  14.6 1.7 %collective-permute-start.4 = (f32[198,256]{1,0:T(8,128)S(1)}, f32[198,256]{1,0:T(8,128)S(1)}, u32[]{:S(2)}, u32[]{:S(2)}) collective-permute-start(f32[198,256]{1,0:T(8,128)S(1)} %get-tuple-element.47), channel_id=1, source_target_pairs={{0,2},{4,6},{8,10},{12,14},{2,0},{6,4},{10,8},{14,12},{1,3},{5,7},... | collective-permute-start | bytes 608264 | tf_op jit(solution)/shard_map/ppermute | solution.py:539
  16.3 4.7 %collective-permute-start.5 = (f32[198,256]{1,0:T(8,128)S(1)}, f32[198,256]{1,0:T(8,128)S(1)}, u32[]{:S(2)}, u32[]{:S(2)}) collective-permute-start(f32[198,256]{1,0:T(8,128)S(1)} %get-tuple-element.48), channel_id=1, source_target_pairs={{2,4},{6,8},{10,12},{14,0},{4,2},{8,6},{12,10},{0,14},{3,5},{7,9},... | collective-permute-start | bytes 608264 | tf_op jit(solution)/shard_map/ppermute | solution.py:539
  20.9 0.0 collective-permute-start.2
  20.9 3.3 %collective-permute-start.3 = (f32[2,3,8,256]{3,2,1,0:T(8,128)S(1)}, f32[2,3,8,256]{3,2,1,0:T(8,128)S(1)}, u32[]{:S(2)}, u32[]{:S(2)}) collective-permute-start(f32[2,3,8,256]{3,2,1,0:T(8,128)S(1)} %get-tuple-element.46), channel_id=1, source_target_pairs={{16,32},{48,64},{80,96},{112,128},{144,160},{176,192},{208,224},{2... | collective-permute-start | bytes 147464 | tf_op jit(solution)/shard_map/ppermute | solution.py:539
  24.2 0.0 collective-permute-done.6.side
  24.2 2.2 %shard_map.79.inner_ref = f32[17,8,384]{2,1,0:T(8,128)S(1)} custom-call(f32[3,8,8,256]{3,2,1,0:T(8,128)S(1)} %copy-done, f32[8,8,256]{2,1,0:T(8,128)S(1)} %copy-done.1, f32[4,5,8,256]{3,2,1,0:T(8,128)S(1)} %collective-permute-done.x_first, f32[4,5,8,256]{3,2,1,0:T(8,128)S(1)} %collective-permute-done.1.x_second, ...), custom_call_target="tpu_custom_call" | custom-call | flops 1 | bytes 1 | tf_op jit(solution)/shard_map/pallas_call | solution.py:523
  26.4 0.0 collective-permute-done.4.y_first
  26.4 0.0 collective-permute-done.5.y_second
  26.4 0.0 collective-permute-done.2.d_first
  26.5 0.7 %collective-permute-done.3.d_second = f32[2,3,8,256]{3,2,1,0:T(8,128)S(1)} collective-permute-done((f32[2,3,8,256]{3,2,1,0:T(8,128)S(1)}, f32[2,3,8,256]{3,2,1,0:T(8,128)S(1)}, u32[]{:S(2)}, u32[]{:S(2)}) %collective-permute-start.3) | collective-permute-done | bytes 49184 | tf_op jit(solution)/shard_map/ppermute | solution.py:539
  27.2 0.3 shard_map.80
  27.5 2.2 %collective-permute-start.7 = (f32[98,8,128]{2,1,0:T(8,128)S(1)}, f32[98,8,128]{2,1,0:T(8,128)S(1)}, u32[]{:S(2)}, u32[]{:S(2)}) collective-permute-start(f32[98,8,128]{2,1,0:T(8,128)S(1)} %get-tuple-element.56), channel_id=1, source_target_pairs={{0,1},{1,0},{2,3},{3,2},{4,5},{5,4},{6,7},{7,6},{8,9},{9,8},{10,11... | collective-permute-start | bytes 1204232 | tf_op jit(solution)/shard_map/ppermute | solution.py:544
  29.6 1.4 %collective-permute-done.7.edge_side = f32[98,8,128]{2,1,0:T(8,128)S(1)} collective-permute-done((f32[98,8,128]{2,1,0:T(8,128)S(1)}, f32[98,8,128]{2,1,0:T(8,128)S(1)}, u32[]{:S(2)}, u32[]{:S(2)}) %collective-permute-start.7) | collective-permute-done | bytes 401440 | tf_op jit(solution)/shard_map/ppermute | solution.py:544
  31.0 5.9 %shard_map.81 = (f32[3,13,8,384]{3,2,1,0:T(8,128)S(1)}, f32[117,384]{1,0:T(8,128)S(1)}, f32[117,384]{1,0:T(8,128)S(1)}, f32[16,8,128]{2,1,0:T(8,128)S(1)}) custom-call(f32[8,8,256]{2,1,0:T(8,128)S(1)} %copy-done.2, s32[8,8,256]{2,1,0:T(8,128)S(1)} %copy-done.3, f32[2,3,8,256]{3,2,1,0:T(8,128)S(1)} %collective-permute-done.2.d_first, ...), custom_call_target="tpu_custom_call" | custom-call | flops 10000000 | bytes 1000000 | tf_op jit(solution)/shard_map/pallas_call | solution.py:523
  36.9 11.3 %all_to_all.10.part_ref = f32[16,8,128]{2,1,0:T(8,128)S(1)} all-to-all(f32[16,8,128]{2,1,0:T(8,128)S(1)} %get-tuple-element.61), channel_id=1, replica_groups=mesh['gx'=16,'gy'=8,'gz'=2] {'gy','gz'}, dimensions={0} | all-to-all | bytes 131072 | tf_op jit(solution)/shard_map/all_to_all | solution.py:601
  48.2 0.2 collective-permute-start.8
  48.4 0.4 collective-permute-start.9
  48.8 11.0 %all_to_all.11.part_ref = f32[16,8,128]{2,1,0:T(8,128)S(1)} all-to-all(f32[16,8,128]{2,1,0:T(8,128)S(1)} %shard_map.82), channel_id=1, replica_groups=mesh['gx'=16,'gy'=8,'gz'=2] {'gx'}, dimensions={0} | all-to-all | bytes 131072 | tf_op jit(solution)/shard_map/all_to_all | solution.py:605
  59.8 0.0 collective-permute-done.8.y_first
  59.8 0.0 collective-permute-done.9.y_second
  59.8 1.6 %shard_map.83 = (f32[8,8,256]{2,1,0:T(8,128)}, f32[8,8,256]{2,1,0:T(8,128)}, f32[6,8,8,256]{3,2,1,0:T(8,128)}) custom-call(f32[16,8,128]{2,1,0:T(8,128)S(1)} %all_to_all.11.part_ref, f32[3,13,8,384]{3,2,1,0:T(8,128)S(1)} %get-tuple-element.63.own_ref, f32[117,384]{1,0:T(8,128)S(1)} %collective-permute-done.8.y_first, ...), custom_call_target="tpu_custom_call" | custom-call | flops 10000000 | bytes 1000000 | tf_op jit(solution)/shard_map/pallas_call | solution.py:523
  (3 shorter events, 0.0 us)
Async XLA Ops:
  0.6 7.0 %copy-start.3 = (s32[8,8,256]{2,1,0:T(8,128)S(1)}, s32[8,8,256]{2,1,0:T(8,128)}, u32[]{:S(2)}) copy-start(s32[8,8,256]{2,1,0:T(8,128)} %passive_ref.3) | copy-start | bytes 196612
  1.8 8.7 %collective-permute-start.1 = (f32[4,5,8,256]{3,2,1,0:T(8,128)S(1)}, f32[4,5,8,256]{3,2,1,0:T(8,128)S(1)}, u32[]{:S(2)}, u32[]{:S(2)}) collective-permute-start(f32[4,5,8,256]{3,2,1,0:T(8,128)S(1)} %get-tuple-element.67), channel_id=1, source_target_pairs={{16,32},{48,64},{80,96},{112,128},{144,160},{176,192},{208,224},{2... | collective-permute-start | bytes 491528 | tf_op jit(solution)/shard_map/ppermute | solution.py:539
  7.7 0.7 %copy-start.4 = (s32[1024]{0:T(1024)S(1)}, s32[1024]{0:T(1024)}, u32[]{:S(2)}) copy-start(s32[1024]{0:T(1024)} %param.9) | copy-start | bytes 12292
  7.7 1.8 %copy-start.2 = (f32[8,8,256]{2,1,0:T(8,128)S(1)}, f32[8,8,256]{2,1,0:T(8,128)}, u32[]{:S(2)}) copy-start(f32[8,8,256]{2,1,0:T(8,128)} %design_ref.3) | copy-start | bytes 196612
  7.7 4.8 %copy-start = (f32[3,8,8,256]{3,2,1,0:T(8,128)S(1)}, f32[3,8,8,256]{3,2,1,0:T(8,128)}, u32[]{:S(2)}) copy-start(f32[3,8,8,256]{3,2,1,0:T(8,128)} %shift_ref.7) | copy-start | bytes 589828
  7.7 4.7 %collective-permute-start = (f32[4,5,8,256]{3,2,1,0:T(8,128)S(1)}, f32[4,5,8,256]{3,2,1,0:T(8,128)S(1)}, u32[]{:S(2)}, u32[]{:S(2)}) collective-permute-start(f32[4,5,8,256]{3,2,1,0:T(8,128)S(1)} %get-tuple-element.68), channel_id=1, source_target_pairs={{0,16},{32,48},{64,80},{96,112},{128,144},{160,176},{192,208},{224... | collective-permute-start | bytes 491528 | tf_op jit(solution)/shard_map/ppermute | solution.py:539
  9.5 2.9 %copy-start.1 = (f32[8,8,256]{2,1,0:T(8,128)S(1)}, f32[8,8,256]{2,1,0:T(8,128)}, u32[]{:S(2)}) copy-start(f32[8,8,256]{2,1,0:T(8,128)} %physical_ref.7) | copy-start | bytes 196612
  12.6 11.6 %collective-permute-start.6 = (f32[72,8,128]{2,1,0:T(8,128)S(1)}, f32[72,8,128]{2,1,0:T(8,128)S(1)}, u32[]{:S(2)}, u32[]{:S(2)}) collective-permute-start(f32[72,8,128]{2,1,0:T(8,128)S(1)} %shard_map.78), channel_id=1, source_target_pairs={{0,1},{1,0},{2,3},{3,2},{4,5},{5,4},{6,7},{7,6},{8,9},{9,8},{10,11... | collective-permute-start | bytes 884744 | tf_op jit(solution)/shard_map/ppermute | solution.py:544
  14.6 11.8 %collective-permute-start.4 = (f32[198,256]{1,0:T(8,128)S(1)}, f32[198,256]{1,0:T(8,128)S(1)}, u32[]{:S(2)}, u32[]{:S(2)}) collective-permute-start(f32[198,256]{1,0:T(8,128)S(1)} %get-tuple-element.47), channel_id=1, source_target_pairs={{0,2},{4,6},{8,10},{12,14},{2,0},{6,4},{10,8},{14,12},{1,3},{5,7},... | collective-permute-start | bytes 608264 | tf_op jit(solution)/shard_map/ppermute | solution.py:539
  16.3 10.2 %collective-permute-start.5 = (f32[198,256]{1,0:T(8,128)S(1)}, f32[198,256]{1,0:T(8,128)S(1)}, u32[]{:S(2)}, u32[]{:S(2)}) collective-permute-start(f32[198,256]{1,0:T(8,128)S(1)} %get-tuple-element.48), channel_id=1, source_target_pairs={{2,4},{6,8},{10,12},{14,0},{4,2},{8,6},{12,10},{0,14},{3,5},{7,9},... | collective-permute-start | bytes 608264 | tf_op jit(solution)/shard_map/ppermute | solution.py:539
  20.9 5.5 %collective-permute-start.2 = (f32[2,3,8,256]{3,2,1,0:T(8,128)S(1)}, f32[2,3,8,256]{3,2,1,0:T(8,128)S(1)}, u32[]{:S(2)}, u32[]{:S(2)}) collective-permute-start(f32[2,3,8,256]{3,2,1,0:T(8,128)S(1)} %get-tuple-element.45), channel_id=1, source_target_pairs={{0,16},{32,48},{64,80},{96,112},{128,144},{160,176},{192,208},{224... | collective-permute-start | bytes 147464 | tf_op jit(solution)/shard_map/ppermute | solution.py:539
  20.9 6.3 %collective-permute-start.3 = (f32[2,3,8,256]{3,2,1,0:T(8,128)S(1)}, f32[2,3,8,256]{3,2,1,0:T(8,128)S(1)}, u32[]{:S(2)}, u32[]{:S(2)}) collective-permute-start(f32[2,3,8,256]{3,2,1,0:T(8,128)S(1)} %get-tuple-element.46), channel_id=1, source_target_pairs={{16,32},{48,64},{80,96},{112,128},{144,160},{176,192},{208,224},{2... | collective-permute-start | bytes 147464 | tf_op jit(solution)/shard_map/ppermute | solution.py:539
  27.5 3.5 %collective-permute-start.7 = (f32[98,8,128]{2,1,0:T(8,128)S(1)}, f32[98,8,128]{2,1,0:T(8,128)S(1)}, u32[]{:S(2)}, u32[]{:S(2)}) collective-permute-start(f32[98,8,128]{2,1,0:T(8,128)S(1)} %get-tuple-element.56), channel_id=1, source_target_pairs={{0,1},{1,0},{2,3},{3,2},{4,5},{5,4},{6,7},{7,6},{8,9},{9,8},{10,11... | collective-permute-start | bytes 1204232 | tf_op jit(solution)/shard_map/ppermute | solution.py:544
  48.2 11.6 %collective-permute-start.8 = (f32[117,384]{1,0:T(8,128)S(1)}, f32[117,384]{1,0:T(8,128)S(1)}, u32[]{:S(2)}, u32[]{:S(2)}) collective-permute-start(f32[117,384]{1,0:T(8,128)S(1)} %get-tuple-element.64), channel_id=1, source_target_pairs={{0,2},{4,6},{8,10},{12,14},{2,0},{6,4},{10,8},{14,12},{1,3},{5,7},... | collective-permute-start | bytes 539144 | tf_op jit(solution)/shard_map/ppermute | solution.py:539
  48.4 11.4 %collective-permute-start.9 = (f32[117,384]{1,0:T(8,128)S(1)}, f32[117,384]{1,0:T(8,128)S(1)}, u32[]{:S(2)}, u32[]{:S(2)}) collective-permute-start(f32[117,384]{1,0:T(8,128)S(1)} %get-tuple-element.65), channel_id=1, source_target_pairs={{2,4},{6,8},{10,12},{14,0},{4,2},{8,6},{12,10},{0,14},{3,5},{7,9},... | collective-permute-start | bytes 539144 | tf_op jit(solution)/shard_map/ppermute | solution.py:539

commit v10 on v9

--- a/solution.py
+++ b/solution.py
@@ -312,7 +312,7 @@
             ext_ref[f, p, :, SZ:LANES] = jnp.where(keep, side[index], 0.0)
     scale = penalty * (1.0 - stiff_floor)
 
-    @pl.loop(0, ELEMENTS)
+    @pl.loop(0, ELEMENTS, unroll=True)
     def _(p):
         modes = {}
         for d in range(3):
@@ -424,7 +424,7 @@
             preferred_element_type=F32,
         )
 
-    total = lax.fori_loop(0, 2 * SX, add_group, jnp.zeros((128, 48), F32), unroll=4).T
+    total = lax.fori_loop(0, 2 * SX, add_group, jnp.zeros((128, 48), F32), unroll=8).T
     constant = total[0:8] + total[8:16] + total[16:24]
     slope = total[24:32] + total[32:40] + total[40:48]
     upto = jnp.where(

time: 61.6 us -> 60.1 us (0.976)
  Pallas kernels: 11.4 us -> 8.65 us
  waiting for transfers between devices: 4.98 us -> 6.18 us
    pallas_call x8, Pallas kernels: 11.4 us -> 8.65 us  [call(): pl.pallas_call(kernel, out_shape=outs, in_specs=[pl.BlockSpec(memory_spac...]
    ppermute x8, waiting for transfers between devices: 3.61 us -> 4.82 us  [exchange(): lax.ppermute(faces, axis, pairs + [(j, i) for i, j in pairs])]
  transfers between devices with their start and end apart: 10 -> 10, of which waited for: 4 -> 5; matrix products, arithmetic and copies ran while one was open for 0% -> 0% of each run, Pallas kernels for 5% -> 4%
where the time goes in v10:
time: 60.1 us; the launch traced here: 59.9 us
  blocking collectives  22.3 us (37%)
  starting transfers between devices  20.2 us (34%)
  Pallas kernels  8.65 us (14%)
  waiting for transfers between devices  6.18 us (10%)
  other arithmetic  1.18 us (2%)
  between operations  0.75 us (1%)
  local copies, waits for them, and re-layouts  0.67 us (1%)
    ppermute x8, starting transfers between devices, exchange(): lax.ppermute(faces, axis, pairs + [(j, i) for i, j in pairs])  16.1 us
    all_to_all x1, blocking collectives, body(): part = lax.all_to_all(part, ('gy', 'gz'), 0, 0, tiled=True)  11.3 us
    all_to_all x1, blocking collectives, body(): part = lax.all_to_all(part, 'gx', 0, 0, tiled=True)  11 us
    pallas_call x8, Pallas kernels, call(): pl.pallas_call(kernel, out_shape=outs, in_specs=[pl.BlockSpec(memory_spac...  8.65 us
    ppermute x8, waiting for transfers between devices, exchange(): lax.ppermute(faces, axis, pairs + [(j, i) for i, j in pairs])  4.82 us
    ppermute x2, starting transfers between devices, other_core(): return lax.ppermute(values, 'gz', [(0, 1), (1, 0)])  4.11 us
    ppermute x2, waiting for transfers between devices, other_core(): return lax.ppermute(values, 'gz', [(0, 1), (1, 0)])  1.36 us
  transfers between devices with their start and end apart: 10, of which 5 were waited for; matrix products, arithmetic and copies ran while one was open for 0% of the time, Pallas kernels for 4%

profile of v10, /device:TPU:1, one launch (start us, length us, event | category | flops | bytes accessed | tf_op | source)
XLA Modules:
  0.0 59.9 jit_solution(11031839432174855964)
XLA Ops:
  0.6 0.0 copy-start.3
  0.7 1.2 %fusion.2 = (f32[4,5,8,256]{3,2,1,0:T(8,128)S(1)}, f32[4,5,8,256]{3,2,1,0:T(8,128)S(1)}) fusion(f32[1,8,8,256]{3,2,1,0:T(8,128)} %bitcast.5, f32[3,8,8,256]{3,2,1,0:T(8,128)} %shift_ref.7, pred[]{:T(512)S(6)} %eq.5), kind=kLoop, calls=%fused_computation.5 | loop fusion | flops 204800 | bytes 589825 | tf_op jit(solution)/shard_map/jit(_where)/select_n | solution.py:556
  1.8 5.8 %collective-permute-start.1 = (f32[4,5,8,256]{3,2,1,0:T(8,128)S(1)}, f32[4,5,8,256]{3,2,1,0:T(8,128)S(1)}, u32[]{:S(2)}, u32[]{:S(2)}) collective-permute-start(f32[4,5,8,256]{3,2,1,0:T(8,128)S(1)} %get-tuple-element.67), channel_id=1, source_target_pairs={{16,32},{48,64},{80,96},{112,128},{144,160},{176,192},{208,224},{2... | collective-permute-start | bytes 491528 | tf_op jit(solution)/shard_map/ppermute | solution.py:539
  7.7 0.0 copy-start.4
  7.7 0.0 copy-start.2
  7.7 0.0 copy-start
  7.7 0.0 collective-permute-start
  7.7 0.0 copy-done.3
  7.7 0.6 %copy-done.4 = s32[1024]{0:T(1024)S(1)} copy-done((s32[1024]{0:T(1024)S(1)}, s32[1024]{0:T(1024)}, u32[]{:S(2)}) %copy-start.4) | copy-done | bytes 4120
  8.3 1.2 %shard_map.76 = (f32[17,16,384]{2,1,0:T(8,128)S(1)}, f32[17,8,384]{2,1,0:T(8,128)S(1)}, f32[13,8,384]{2,1,0:T(8,128)S(1)}, f32[8,8,256]{2,1,0:T(8,128)S(1)}) custom-call(s32[1,1024]{1,0:T(1,128)S(1)} %bitcast.7), custom_call_target="tpu_custom_call" | custom-call | flops 10000000 | bytes 1000000 | tf_op jit(solution)/shard_map/pallas_call | solution.py:523
  9.5 0.0 copy-done.2
  9.5 0.0 copy-start.1
  9.5 1.0 %collective-permute-done.1.x_second = f32[4,5,8,256]{3,2,1,0:T(8,128)S(1)} collective-permute-done((f32[4,5,8,256]{3,2,1,0:T(8,128)S(1)}, f32[4,5,8,256]{3,2,1,0:T(8,128)S(1)}, u32[]{:S(2)}, u32[]{:S(2)}) %collective-permute-start.1) | collective-permute-done | bytes 163872 | tf_op jit(solution)/shard_map/ppermute | solution.py:539
  10.5 1.9 %collective-permute-done.x_first = f32[4,5,8,256]{3,2,1,0:T(8,128)S(1)} collective-permute-done((f32[4,5,8,256]{3,2,1,0:T(8,128)S(1)}, f32[4,5,8,256]{3,2,1,0:T(8,128)S(1)}, u32[]{:S(2)}, u32[]{:S(2)}) %collective-permute-start) | collective-permute-done | bytes 163872 | tf_op jit(solution)/shard_map/ppermute | solution.py:539
  12.4 0.0 copy-done
  12.4 0.0 copy-done.1
  12.4 0.2 shard_map.77
  12.6 0.1 shard_map.78
  12.6 2.0 %collective-permute-start.6 = (f32[72,8,128]{2,1,0:T(8,128)S(1)}, f32[72,8,128]{2,1,0:T(8,128)S(1)}, u32[]{:S(2)}, u32[]{:S(2)}) collective-permute-start(f32[72,8,128]{2,1,0:T(8,128)S(1)} %shard_map.78), channel_id=1, source_target_pairs={{0,1},{1,0},{2,3},{3,2},{4,5},{5,4},{6,7},{7,6},{8,9},{9,8},{10,11... | collective-permute-start | bytes 884744 | tf_op jit(solution)/shard_map/ppermute | solution.py:544
  14.6 1.7 %collective-permute-start.4 = (f32[198,256]{1,0:T(8,128)S(1)}, f32[198,256]{1,0:T(8,128)S(1)}, u32[]{:S(2)}, u32[]{:S(2)}) collective-permute-start(f32[198,256]{1,0:T(8,128)S(1)} %get-tuple-element.47), channel_id=1, source_target_pairs={{0,2},{4,6},{8,10},{12,14},{2,0},{6,4},{10,8},{14,12},{1,3},{5,7},... | collective-permute-start | bytes 608264 | tf_op jit(solution)/shard_map/ppermute | solution.py:539
  16.3 4.7 %collective-permute-start.5 = (f32[198,256]{1,0:T(8,128)S(1)}, f32[198,256]{1,0:T(8,128)S(1)}, u32[]{:S(2)}, u32[]{:S(2)}) collective-permute-start(f32[198,256]{1,0:T(8,128)S(1)} %get-tuple-element.48), channel_id=1, source_target_pairs={{2,4},{6,8},{10,12},{14,0},{4,2},{8,6},{12,10},{0,14},{3,5},{7,9},... | collective-permute-start | bytes 608264 | tf_op jit(solution)/shard_map/ppermute | solution.py:539
  20.9 0.0 collective-permute-start.2
  20.9 3.3 %collective-permute-start.3 = (f32[2,3,8,256]{3,2,1,0:T(8,128)S(1)}, f32[2,3,8,256]{3,2,1,0:T(8,128)S(1)}, u32[]{:S(2)}, u32[]{:S(2)}) collective-permute-start(f32[2,3,8,256]{3,2,1,0:T(8,128)S(1)} %get-tuple-element.46), channel_id=1, source_target_pairs={{16,32},{48,64},{80,96},{112,128},{144,160},{176,192},{208,224},{2... | collective-permute-start | bytes 147464 | tf_op jit(solution)/shard_map/ppermute | solution.py:539
  24.2 0.0 collective-permute-done.6.side
  24.2 1.0 %shard_map.79.inner_ref = f32[17,8,384]{2,1,0:T(8,128)S(1)} custom-call(f32[3,8,8,256]{3,2,1,0:T(8,128)S(1)} %copy-done, f32[8,8,256]{2,1,0:T(8,128)S(1)} %copy-done.1, f32[4,5,8,256]{3,2,1,0:T(8,128)S(1)} %collective-permute-done.x_first, f32[4,5,8,256]{3,2,1,0:T(8,128)S(1)} %collective-permute-done.1.x_second, ...), custom_call_target="tpu_custom_call" | custom-call | flops 1 | bytes 1 | tf_op jit(solution)/shard_map/pallas_call | solution.py:523
  25.2 0.0 collective-permute-done.4.y_first
  25.2 0.8 %collective-permute-done.5.y_second = f32[198,256]{1,0:T(8,128)S(1)} collective-permute-done((f32[198,256]{1,0:T(8,128)S(1)}, f32[198,256]{1,0:T(8,128)S(1)}, u32[]{:S(2)}, u32[]{:S(2)}) %collective-permute-start.5) | collective-permute-done | bytes 202784 | tf_op jit(solution)/shard_map/ppermute | solution.py:539
  26.1 0.0 collective-permute-done.2.d_first
  26.1 1.1 %collective-permute-done.3.d_second = f32[2,3,8,256]{3,2,1,0:T(8,128)S(1)} collective-permute-done((f32[2,3,8,256]{3,2,1,0:T(8,128)S(1)}, f32[2,3,8,256]{3,2,1,0:T(8,128)S(1)}, u32[]{:S(2)}, u32[]{:S(2)}) %collective-permute-start.3) | collective-permute-done | bytes 49184 | tf_op jit(solution)/shard_map/ppermute | solution.py:539
  27.2 0.3 shard_map.80
  27.5 2.2 %collective-permute-start.7 = (f32[98,8,128]{2,1,0:T(8,128)S(1)}, f32[98,8,128]{2,1,0:T(8,128)S(1)}, u32[]{:S(2)}, u32[]{:S(2)}) collective-permute-start(f32[98,8,128]{2,1,0:T(8,128)S(1)} %get-tuple-element.56), channel_id=1, source_target_pairs={{0,1},{1,0},{2,3},{3,2},{4,5},{5,4},{6,7},{7,6},{8,9},{9,8},{10,11... | collective-permute-start | bytes 1204232 | tf_op jit(solution)/shard_map/ppermute | solution.py:544
  29.6 1.4 %collective-permute-done.7.edge_side = f32[98,8,128]{2,1,0:T(8,128)S(1)} collective-permute-done((f32[98,8,128]{2,1,0:T(8,128)S(1)}, f32[98,8,128]{2,1,0:T(8,128)S(1)}, u32[]{:S(2)}, u32[]{:S(2)}) %collective-permute-start.7) | collective-permute-done | bytes 401440 | tf_op jit(solution)/shard_map/ppermute | solution.py:544
  31.0 4.4 %shard_map.81 = (f32[3,13,8,384]{3,2,1,0:T(8,128)S(1)}, f32[117,384]{1,0:T(8,128)S(1)}, f32[117,384]{1,0:T(8,128)S(1)}, f32[16,8,128]{2,1,0:T(8,128)S(1)}) custom-call(f32[8,8,256]{2,1,0:T(8,128)S(1)} %copy-done.2, s32[8,8,256]{2,1,0:T(8,128)S(1)} %copy-done.3, f32[2,3,8,256]{3,2,1,0:T(8,128)S(1)} %collective-permute-done.2.d_first, ...), custom_call_target="tpu_custom_call" | custom-call | flops 10000000 | bytes 1000000 | tf_op jit(solution)/shard_map/pallas_call | solution.py:523
  35.4 11.3 %all_to_all.10.part_ref = f32[16,8,128]{2,1,0:T(8,128)S(1)} all-to-all(f32[16,8,128]{2,1,0:T(8,128)S(1)} %get-tuple-element.61), channel_id=1, replica_groups=mesh['gx'=16,'gy'=8,'gz'=2] {'gy','gz'}, dimensions={0} | all-to-all | bytes 131072 | tf_op jit(solution)/shard_map/all_to_all | solution.py:601
  46.7 0.2 collective-permute-start.8
  46.9 0.4 collective-permute-start.9
  47.3 11.0 %all_to_all.11.part_ref = f32[16,8,128]{2,1,0:T(8,128)S(1)} all-to-all(f32[16,8,128]{2,1,0:T(8,128)S(1)} %shard_map.82), channel_id=1, replica_groups=mesh['gx'=16,'gy'=8,'gz'=2] {'gx'}, dimensions={0} | all-to-all | bytes 131072 | tf_op jit(solution)/shard_map/all_to_all | solution.py:605
  58.3 0.0 collective-permute-done.8.y_first
  58.3 0.0 collective-permute-done.9.y_second
  58.3 1.6 %shard_map.83 = (f32[8,8,256]{2,1,0:T(8,128)}, f32[8,8,256]{2,1,0:T(8,128)}, f32[6,8,8,256]{3,2,1,0:T(8,128)}) custom-call(f32[16,8,128]{2,1,0:T(8,128)S(1)} %all_to_all.11.part_ref, f32[3,13,8,384]{3,2,1,0:T(8,128)S(1)} %get-tuple-element.63.own_ref, f32[117,384]{1,0:T(8,128)S(1)} %collective-permute-done.8.y_first, ...), custom_call_target="tpu_custom_call" | custom-call | flops 10000000 | bytes 1000000 | tf_op jit(solution)/shard_map/pallas_call | solution.py:523
  (3 shorter events, 0.0 us)
Async XLA Ops:
  0.6 7.0 %copy-start.3 = (s32[8,8,256]{2,1,0:T(8,128)S(1)}, s32[8,8,256]{2,1,0:T(8,128)}, u32[]{:S(2)}) copy-start(s32[8,8,256]{2,1,0:T(8,128)} %passive_ref.3) | copy-start | bytes 196612
  1.8 8.7 %collective-permute-start.1 = (f32[4,5,8,256]{3,2,1,0:T(8,128)S(1)}, f32[4,5,8,256]{3,2,1,0:T(8,128)S(1)}, u32[]{:S(2)}, u32[]{:S(2)}) collective-permute-start(f32[4,5,8,256]{3,2,1,0:T(8,128)S(1)} %get-tuple-element.67), channel_id=1, source_target_pairs={{16,32},{48,64},{80,96},{112,128},{144,160},{176,192},{208,224},{2... | collective-permute-start | bytes 491528 | tf_op jit(solution)/shard_map/ppermute | solution.py:539
  7.7 0.7 %copy-start.4 = (s32[1024]{0:T(1024)S(1)}, s32[1024]{0:T(1024)}, u32[]{:S(2)}) copy-start(s32[1024]{0:T(1024)} %param.9) | copy-start | bytes 12292
  7.7 1.8 %copy-start.2 = (f32[8,8,256]{2,1,0:T(8,128)S(1)}, f32[8,8,256]{2,1,0:T(8,128)}, u32[]{:S(2)}) copy-start(f32[8,8,256]{2,1,0:T(8,128)} %design_ref.3) | copy-start | bytes 196612
  7.7 4.8 %copy-start = (f32[3,8,8,256]{3,2,1,0:T(8,128)S(1)}, f32[3,8,8,256]{3,2,1,0:T(8,128)}, u32[]{:S(2)}) copy-start(f32[3,8,8,256]{3,2,1,0:T(8,128)} %shift_ref.7) | copy-start | bytes 589828
  7.7 4.7 %collective-permute-start = (f32[4,5,8,256]{3,2,1,0:T(8,128)S(1)}, f32[4,5,8,256]{3,2,1,0:T(8,128)S(1)}, u32[]{:S(2)}, u32[]{:S(2)}) collective-permute-start(f32[4,5,8,256]{3,2,1,0:T(8,128)S(1)} %get-tuple-element.68), channel_id=1, source_target_pairs={{0,16},{32,48},{64,80},{96,112},{128,144},{160,176},{192,208},{224... | collective-permute-start | bytes 491528 | tf_op jit(solution)/shard_map/ppermute | solution.py:539
  9.5 2.9 %copy-start.1 = (f32[8,8,256]{2,1,0:T(8,128)S(1)}, f32[8,8,256]{2,1,0:T(8,128)}, u32[]{:S(2)}) copy-start(f32[8,8,256]{2,1,0:T(8,128)} %physical_ref.7) | copy-start | bytes 196612
  12.6 11.6 %collective-permute-start.6 = (f32[72,8,128]{2,1,0:T(8,128)S(1)}, f32[72,8,128]{2,1,0:T(8,128)S(1)}, u32[]{:S(2)}, u32[]{:S(2)}) collective-permute-start(f32[72,8,128]{2,1,0:T(8,128)S(1)} %shard_map.78), channel_id=1, source_target_pairs={{0,1},{1,0},{2,3},{3,2},{4,5},{5,4},{6,7},{7,6},{8,9},{9,8},{10,11... | collective-permute-start | bytes 884744 | tf_op jit(solution)/shard_map/ppermute | solution.py:544
  14.6 10.6 %collective-permute-start.4 = (f32[198,256]{1,0:T(8,128)S(1)}, f32[198,256]{1,0:T(8,128)S(1)}, u32[]{:S(2)}, u32[]{:S(2)}) collective-permute-start(f32[198,256]{1,0:T(8,128)S(1)} %get-tuple-element.47), channel_id=1, source_target_pairs={{0,2},{4,6},{8,10},{12,14},{2,0},{6,4},{10,8},{14,12},{1,3},{5,7},... | collective-permute-start | bytes 608264 | tf_op jit(solution)/shard_map/ppermute | solution.py:539
  16.3 9.8 %collective-permute-start.5 = (f32[198,256]{1,0:T(8,128)S(1)}, f32[198,256]{1,0:T(8,128)S(1)}, u32[]{:S(2)}, u32[]{:S(2)}) collective-permute-start(f32[198,256]{1,0:T(8,128)S(1)} %get-tuple-element.48), channel_id=1, source_target_pairs={{2,4},{6,8},{10,12},{14,0},{4,2},{8,6},{12,10},{0,14},{3,5},{7,9},... | collective-permute-start | bytes 608264 | tf_op jit(solution)/shard_map/ppermute | solution.py:539
  20.9 5.2 %collective-permute-start.2 = (f32[2,3,8,256]{3,2,1,0:T(8,128)S(1)}, f32[2,3,8,256]{3,2,1,0:T(8,128)S(1)}, u32[]{:S(2)}, u32[]{:S(2)}) collective-permute-start(f32[2,3,8,256]{3,2,1,0:T(8,128)S(1)} %get-tuple-element.45), channel_id=1, source_target_pairs={{0,16},{32,48},{64,80},{96,112},{128,144},{160,176},{192,208},{224... | collective-permute-start | bytes 147464 | tf_op jit(solution)/shard_map/ppermute | solution.py:539
  20.9 6.3 %collective-permute-start.3 = (f32[2,3,8,256]{3,2,1,0:T(8,128)S(1)}, f32[2,3,8,256]{3,2,1,0:T(8,128)S(1)}, u32[]{:S(2)}, u32[]{:S(2)}) collective-permute-start(f32[2,3,8,256]{3,2,1,0:T(8,128)S(1)} %get-tuple-element.46), channel_id=1, source_target_pairs={{16,32},{48,64},{80,96},{112,128},{144,160},{176,192},{208,224},{2... | collective-permute-start | bytes 147464 | tf_op jit(solution)/shard_map/ppermute | solution.py:539
  27.5 3.5 %collective-permute-start.7 = (f32[98,8,128]{2,1,0:T(8,128)S(1)}, f32[98,8,128]{2,1,0:T(8,128)S(1)}, u32[]{:S(2)}, u32[]{:S(2)}) collective-permute-start(f32[98,8,128]{2,1,0:T(8,128)S(1)} %get-tuple-element.56), channel_id=1, source_target_pairs={{0,1},{1,0},{2,3},{3,2},{4,5},{5,4},{6,7},{7,6},{8,9},{9,8},{10,11... | collective-permute-start | bytes 1204232 | tf_op jit(solution)/shard_map/ppermute | solution.py:544
  46.7 11.6 %collective-permute-start.8 = (f32[117,384]{1,0:T(8,128)S(1)}, f32[117,384]{1,0:T(8,128)S(1)}, u32[]{:S(2)}, u32[]{:S(2)}) collective-permute-start(f32[117,384]{1,0:T(8,128)S(1)} %get-tuple-element.64), channel_id=1, source_target_pairs={{0,2},{4,6},{8,10},{12,14},{2,0},{6,4},{10,8},{14,12},{1,3},{5,7},... | collective-permute-start | bytes 539144 | tf_op jit(solution)/shard_map/ppermute | solution.py:539
  46.9 11.4 %collective-permute-start.9 = (f32[117,384]{1,0:T(8,128)S(1)}, f32[117,384]{1,0:T(8,128)S(1)}, u32[]{:S(2)}, u32[]{:S(2)}) collective-permute-start(f32[117,384]{1,0:T(8,128)S(1)} %get-tuple-element.65), channel_id=1, source_target_pairs={{2,4},{6,8},{10,12},{14,0},{4,2},{8,6},{12,10},{0,14},{3,5},{7,9},... | collective-permute-start | bytes 539144 | tf_op jit(solution)/shard_map/ppermute | solution.py:539

commit v11 on v10

--- a/solution.py
+++ b/solution.py
@@ -209,8 +209,8 @@
         mark_ref[p] = hits[p * SY : (p + 1) * SY]
 
 
-def is_even(axis):
-    return lax.axis_index(axis) % 2 == 0
+def is_first(axis):
+    return (lax.axis_index(axis) + (axis == "gy")) % 2 == 0
 
 
 def place_pair(even, first_ref, second_ref, top, bottom, place):
@@ -219,10 +219,10 @@
 
 
 def low_high(axis, first_ref, second_ref, place):
-    index = lax.axis_index(axis)
+    index, leads = lax.axis_index(axis), is_first(axis)
     first, second = first_ref[place], second_ref[place]
-    low = jnp.where(index == 0, 0.0, jnp.where(index % 2 == 0, second, first))
-    high = jnp.where(index == lax.axis_size(axis) - 1, 0.0, jnp.where(index % 2 == 0, first, second))
+    low = jnp.where(index == 0, 0.0, jnp.where(leads, second, first))
+    high = jnp.where(index == lax.axis_size(axis) - 1, 0.0, jnp.where(leads, first, second))
     return low, high
 
 
@@ -271,7 +271,7 @@
 
 
 def faces_y_kernel(shift_ref, physical_ref, x_first, x_second, first_ref, second_ref):
-    even = is_even("gy")
+    even = is_first("gy")
     read = plane_reader(shift_ref, physical_ref, x_first, x_second)
     for index in range(4 * NODES):
         plane = read(index)
@@ -345,7 +345,7 @@
     out_ref, first_ref, second_ref, part_ref, ext_ref, outer_ref, sens_ref, near_ref, far_ref, high_ref, low_ref,
     value_ref, *, groups
 ):
-    even = is_even("gy")
+    even = is_first("gy")
     scaled_energy(
         ext_ref, lambda index: edge_tiles[index], edge_side, lambda p: edge_ref[p], outer_ref, groups
     )
@@ -535,7 +535,7 @@
     count = lax.axis_size(axis)
     results = []
     for start, faces in enumerate((first, second)):
-        pairs = [(i, (i + 1) % count) for i in range(start, count, 2)]
+        pairs = [(i, (i + 1) % count) for i in range((start + (axis == "gy")) % 2, count, 2)]
         results.append(lax.ppermute(faces, axis, pairs + [(j, i) for i, j in pairs]))
     return results
 
@@ -549,7 +549,7 @@
     sizes = [lax.axis_size(axis) for axis in ("gx", "gy", "gz")]
     extents = (SX * sizes[0], SY * sizes[1], SZ * sizes[2])
     block = (SX, SY, SZ)
-    even = lax.axis_index("gx") % 2 == 0
+    even = is_first("gx")
 
     def swaps(fields, depth):
         top, bottom = fields[:, SX - depth :], fields[:, 0:depth]

time: 60.1 us -> 60.3 us (level)
  blocking collectives: 22.3 us -> 23.4 us
  starting transfers between devices: 20.2 us -> 19.1 us
    all_to_all x1, blocking collectives: 11.3 us -> 12.6 us  [body(): part = lax.all_to_all(part, ('gy', 'gz'), 0, 0, tiled=True)]
    ppermute x8, starting transfers between devices: 16.1 us -> 15.3 us  [exchange(): lax.ppermute(faces, axis, pairs + [(j, i) for i, j in pairs])]
where the time goes in v11:
time: 60.3 us; the launch traced here: 59.9 us
  blocking collectives  23.4 us (39%)
  starting transfers between devices  19.1 us (32%)
  Pallas kernels  8.65 us (14%)
  waiting for transfers between devices  6.23 us (10%)
  other arithmetic  1.18 us (2%)
  between operations  0.75 us (1%)
  local copies, waits for them, and re-layouts  0.67 us (1%)
    ppermute x8, starting transfers between devices, exchange(): lax.ppermute(faces, axis, pairs + [(j, i) for i, j in pairs])  15.3 us
    all_to_all x1, blocking collectives, body(): part = lax.all_to_all(part, ('gy', 'gz'), 0, 0, tiled=True)  12.6 us
    all_to_all x1, blocking collectives, body(): part = lax.all_to_all(part, 'gx', 0, 0, tiled=True)  10.7 us
    pallas_call x8, Pallas kernels, call(): pl.pallas_call(kernel, out_shape=outs, in_specs=[pl.BlockSpec(memory_spac...  8.65 us
    ppermute x8, waiting for transfers between devices, exchange(): lax.ppermute(faces, axis, pairs + [(j, i) for i, j in pairs])  4.87 us
    ppermute x2, starting transfers between devices, other_core(): return lax.ppermute(values, 'gz', [(0, 1), (1, 0)])  3.78 us
    ppermute x2, waiting for transfers between devices, other_core(): return lax.ppermute(values, 'gz', [(0, 1), (1, 0)])  1.36 us
  transfers between devices with their start and end apart: 10, of which 5 were waited for; matrix products, arithmetic and copies ran while one was open for 0% of the time, Pallas kernels for 4%

profile of v11, /device:TPU:1, one launch (start us, length us, event | category | flops | bytes accessed | tf_op | source)
XLA Modules:
  0.0 59.9 jit_solution(12232256764695636241)
XLA Ops:
  0.6 0.0 copy-start.3
  0.7 1.2 %fusion.2 = (f32[4,5,8,256]{3,2,1,0:T(8,128)S(1)}, f32[4,5,8,256]{3,2,1,0:T(8,128)S(1)}) fusion(f32[1,8,8,256]{3,2,1,0:T(8,128)} %bitcast.5, f32[3,8,8,256]{3,2,1,0:T(8,128)} %shift_ref.7, pred[]{:T(512)S(6)} %eq.5), kind=kLoop, calls=%fused_computation.5 | loop fusion | flops 204800 | bytes 589825 | tf_op jit(solution)/shard_map/jit(_where)/select_n | solution.py:556
  1.8 5.8 %collective-permute-start.1 = (f32[4,5,8,256]{3,2,1,0:T(8,128)S(1)}, f32[4,5,8,256]{3,2,1,0:T(8,128)S(1)}, u32[]{:S(2)}, u32[]{:S(2)}) collective-permute-start(f32[4,5,8,256]{3,2,1,0:T(8,128)S(1)} %get-tuple-element.67), channel_id=1, source_target_pairs={{16,32},{48,64},{80,96},{112,128},{144,160},{176,192},{208,224},{2... | collective-permute-start | bytes 491528 | tf_op jit(solution)/shard_map/ppermute | solution.py:539
  7.7 0.0 copy-start.4
  7.7 0.0 copy-start.2
  7.7 0.0 copy-start
  7.7 0.0 collective-permute-start
  7.7 0.0 copy-done.3
  7.7 0.6 %copy-done.4 = s32[1024]{0:T(1024)S(1)} copy-done((s32[1024]{0:T(1024)S(1)}, s32[1024]{0:T(1024)}, u32[]{:S(2)}) %copy-start.4) | copy-done | bytes 4120
  8.3 1.2 %shard_map.76 = (f32[17,16,384]{2,1,0:T(8,128)S(1)}, f32[17,8,384]{2,1,0:T(8,128)S(1)}, f32[13,8,384]{2,1,0:T(8,128)S(1)}, f32[8,8,256]{2,1,0:T(8,128)S(1)}) custom-call(s32[1,1024]{1,0:T(1,128)S(1)} %bitcast.7), custom_call_target="tpu_custom_call" | custom-call | flops 10000000 | bytes 1000000 | tf_op jit(solution)/shard_map/pallas_call | solution.py:523
  9.5 0.0 copy-done.2
  9.5 0.0 copy-start.1
  9.5 1.0 %collective-permute-done.1.x_second = f32[4,5,8,256]{3,2,1,0:T(8,128)S(1)} collective-permute-done((f32[4,5,8,256]{3,2,1,0:T(8,128)S(1)}, f32[4,5,8,256]{3,2,1,0:T(8,128)S(1)}, u32[]{:S(2)}, u32[]{:S(2)}) %collective-permute-start.1) | collective-permute-done | bytes 163872 | tf_op jit(solution)/shard_map/ppermute | solution.py:539
  10.5 1.9 %collective-permute-done.x_first = f32[4,5,8,256]{3,2,1,0:T(8,128)S(1)} collective-permute-done((f32[4,5,8,256]{3,2,1,0:T(8,128)S(1)}, f32[4,5,8,256]{3,2,1,0:T(8,128)S(1)}, u32[]{:S(2)}, u32[]{:S(2)}) %collective-permute-start) | collective-permute-done | bytes 163872 | tf_op jit(solution)/shard_map/ppermute | solution.py:539
  12.4 0.0 copy-done
  12.4 0.0 copy-done.1
  12.4 0.2 shard_map.77
  12.6 0.1 shard_map.78
  12.6 2.0 %collective-permute-start.6 = (f32[72,8,128]{2,1,0:T(8,128)S(1)}, f32[72,8,128]{2,1,0:T(8,128)S(1)}, u32[]{:S(2)}, u32[]{:S(2)}) collective-permute-start(f32[72,8,128]{2,1,0:T(8,128)S(1)} %shard_map.78), channel_id=1, source_target_pairs={{0,1},{1,0},{2,3},{3,2},{4,5},{5,4},{6,7},{7,6},{8,9},{9,8},{10,11... | collective-permute-start | bytes 884744 | tf_op jit(solution)/shard_map/ppermute | solution.py:544
  14.6 5.6 %collective-permute-start.4 = (f32[198,256]{1,0:T(8,128)S(1)}, f32[198,256]{1,0:T(8,128)S(1)}, u32[]{:S(2)}, u32[]{:S(2)}) collective-permute-start(f32[198,256]{1,0:T(8,128)S(1)} %get-tuple-element.47), channel_id=1, source_target_pairs={{2,4},{6,8},{10,12},{14,0},{4,2},{8,6},{12,10},{0,14},{3,5},{7,9},... | collective-permute-start | bytes 608264 | tf_op jit(solution)/shard_map/ppermute | solution.py:539
  20.2 0.0 collective-permute-start.5
  20.2 0.0 collective-permute-start.2
  20.2 3.3 %collective-permute-start.3 = (f32[2,3,8,256]{3,2,1,0:T(8,128)S(1)}, f32[2,3,8,256]{3,2,1,0:T(8,128)S(1)}, u32[]{:S(2)}, u32[]{:S(2)}) collective-permute-start(f32[2,3,8,256]{3,2,1,0:T(8,128)S(1)} %get-tuple-element.46), channel_id=1, source_target_pairs={{16,32},{48,64},{80,96},{112,128},{144,160},{176,192},{208,224},{2... | collective-permute-start | bytes 147464 | tf_op jit(solution)/shard_map/ppermute | solution.py:539
  23.5 0.0 collective-permute-done.6.side
  23.5 1.0 %shard_map.79.inner_ref = f32[17,8,384]{2,1,0:T(8,128)S(1)} custom-call(f32[3,8,8,256]{3,2,1,0:T(8,128)S(1)} %copy-done, f32[8,8,256]{2,1,0:T(8,128)S(1)} %copy-done.1, f32[4,5,8,256]{3,2,1,0:T(8,128)S(1)} %collective-permute-done.x_first, f32[4,5,8,256]{3,2,1,0:T(8,128)S(1)} %collective-permute-done.1.x_second, ...), custom_call_target="tpu_custom_call" | custom-call | flops 1 | bytes 1 | tf_op jit(solution)/shard_map/pallas_call | solution.py:523
  24.5 1.0 %collective-permute-done.4.y_first = f32[198,256]{1,0:T(8,128)S(1)} collective-permute-done((f32[198,256]{1,0:T(8,128)S(1)}, f32[198,256]{1,0:T(8,128)S(1)}, u32[]{:S(2)}, u32[]{:S(2)}) %collective-permute-start.4) | collective-permute-done | bytes 202784 | tf_op jit(solution)/shard_map/ppermute | solution.py:539
  25.5 1.0 %collective-permute-done.5.y_second = f32[198,256]{1,0:T(8,128)S(1)} collective-permute-done((f32[198,256]{1,0:T(8,128)S(1)}, f32[198,256]{1,0:T(8,128)S(1)}, u32[]{:S(2)}, u32[]{:S(2)}) %collective-permute-start.5) | collective-permute-done | bytes 202784 | tf_op jit(solution)/shard_map/ppermute | solution.py:539
  26.5 0.0 collective-permute-done.2.d_first
  26.5 0.0 collective-permute-done.3.d_second
  26.5 0.3 shard_map.80
  26.8 1.8 %collective-permute-start.7 = (f32[98,8,128]{2,1,0:T(8,128)S(1)}, f32[98,8,128]{2,1,0:T(8,128)S(1)}, u32[]{:S(2)}, u32[]{:S(2)}) collective-permute-start(f32[98,8,128]{2,1,0:T(8,128)S(1)} %get-tuple-element.56), channel_id=1, source_target_pairs={{0,1},{1,0},{2,3},{3,2},{4,5},{5,4},{6,7},{7,6},{8,9},{9,8},{10,11... | collective-permute-start | bytes 1204232 | tf_op jit(solution)/shard_map/ppermute | solution.py:544
  28.6 1.4 %collective-permute-done.7.edge_side = f32[98,8,128]{2,1,0:T(8,128)S(1)} collective-permute-done((f32[98,8,128]{2,1,0:T(8,128)S(1)}, f32[98,8,128]{2,1,0:T(8,128)S(1)}, u32[]{:S(2)}, u32[]{:S(2)}) %collective-permute-start.7) | collective-permute-done | bytes 401440 | tf_op jit(solution)/shard_map/ppermute | solution.py:544
  30.0 4.4 %shard_map.81 = (f32[3,13,8,384]{3,2,1,0:T(8,128)S(1)}, f32[117,384]{1,0:T(8,128)S(1)}, f32[117,384]{1,0:T(8,128)S(1)}, f32[16,8,128]{2,1,0:T(8,128)S(1)}) custom-call(f32[8,8,256]{2,1,0:T(8,128)S(1)} %copy-done.2, s32[8,8,256]{2,1,0:T(8,128)S(1)} %copy-done.3, f32[2,3,8,256]{3,2,1,0:T(8,128)S(1)} %collective-permute-done.2.d_first, ...), custom_call_target="tpu_custom_call" | custom-call | flops 10000000 | bytes 1000000 | tf_op jit(solution)/shard_map/pallas_call | solution.py:523
  34.4 12.6 %all_to_all.10.part_ref = f32[16,8,128]{2,1,0:T(8,128)S(1)} all-to-all(f32[16,8,128]{2,1,0:T(8,128)S(1)} %get-tuple-element.61), channel_id=1, replica_groups=mesh['gx'=16,'gy'=8,'gz'=2] {'gy','gz'}, dimensions={0} | all-to-all | bytes 131072 | tf_op jit(solution)/shard_map/all_to_all | solution.py:601
  47.0 0.1 collective-permute-start.8
  47.1 0.4 collective-permute-start.9
  47.6 10.7 %all_to_all.11.part_ref = f32[16,8,128]{2,1,0:T(8,128)S(1)} all-to-all(f32[16,8,128]{2,1,0:T(8,128)S(1)} %shard_map.82), channel_id=1, replica_groups=mesh['gx'=16,'gy'=8,'gz'=2] {'gx'}, dimensions={0} | all-to-all | bytes 131072 | tf_op jit(solution)/shard_map/all_to_all | solution.py:605
  58.3 0.0 collective-permute-done.8.y_first
  58.3 0.0 collective-permute-done.9.y_second
  58.3 1.6 %shard_map.83 = (f32[8,8,256]{2,1,0:T(8,128)}, f32[8,8,256]{2,1,0:T(8,128)}, f32[6,8,8,256]{3,2,1,0:T(8,128)}) custom-call(f32[16,8,128]{2,1,0:T(8,128)S(1)} %all_to_all.11.part_ref, f32[3,13,8,384]{3,2,1,0:T(8,128)S(1)} %get-tuple-element.63.own_ref, f32[117,384]{1,0:T(8,128)S(1)} %collective-permute-done.8.y_first, ...), custom_call_target="tpu_custom_call" | custom-call | flops 10000000 | bytes 1000000 | tf_op jit(solution)/shard_map/pallas_call | solution.py:523
  (3 shorter events, 0.0 us)
Async XLA Ops:
  0.6 7.0 %copy-start.3 = (s32[8,8,256]{2,1,0:T(8,128)S(1)}, s32[8,8,256]{2,1,0:T(8,128)}, u32[]{:S(2)}) copy-start(s32[8,8,256]{2,1,0:T(8,128)} %passive_ref.3) | copy-start | bytes 196612
  1.8 8.7 %collective-permute-start.1 = (f32[4,5,8,256]{3,2,1,0:T(8,128)S(1)}, f32[4,5,8,256]{3,2,1,0:T(8,128)S(1)}, u32[]{:S(2)}, u32[]{:S(2)}) collective-permute-start(f32[4,5,8,256]{3,2,1,0:T(8,128)S(1)} %get-tuple-element.67), channel_id=1, source_target_pairs={{16,32},{48,64},{80,96},{112,128},{144,160},{176,192},{208,224},{2... | collective-permute-start | bytes 491528 | tf_op jit(solution)/shard_map/ppermute | solution.py:539
  7.7 0.7 %copy-start.4 = (s32[1024]{0:T(1024)S(1)}, s32[1024]{0:T(1024)}, u32[]{:S(2)}) copy-start(s32[1024]{0:T(1024)} %param.9) | copy-start | bytes 12292
  7.7 1.8 %copy-start.2 = (f32[8,8,256]{2,1,0:T(8,128)S(1)}, f32[8,8,256]{2,1,0:T(8,128)}, u32[]{:S(2)}) copy-start(f32[8,8,256]{2,1,0:T(8,128)} %design_ref.3) | copy-start | bytes 196612
  7.7 4.8 %copy-start = (f32[3,8,8,256]{3,2,1,0:T(8,128)S(1)}, f32[3,8,8,256]{3,2,1,0:T(8,128)}, u32[]{:S(2)}) copy-start(f32[3,8,8,256]{3,2,1,0:T(8,128)} %shift_ref.7) | copy-start | bytes 589828
  7.7 4.7 %collective-permute-start = (f32[4,5,8,256]{3,2,1,0:T(8,128)S(1)}, f32[4,5,8,256]{3,2,1,0:T(8,128)S(1)}, u32[]{:S(2)}, u32[]{:S(2)}) collective-permute-start(f32[4,5,8,256]{3,2,1,0:T(8,128)S(1)} %get-tuple-element.68), channel_id=1, source_target_pairs={{0,16},{32,48},{64,80},{96,112},{128,144},{160,176},{192,208},{224... | collective-permute-start | bytes 491528 | tf_op jit(solution)/shard_map/ppermute | solution.py:539
  9.5 2.9 %copy-start.1 = (f32[8,8,256]{2,1,0:T(8,128)S(1)}, f32[8,8,256]{2,1,0:T(8,128)}, u32[]{:S(2)}) copy-start(f32[8,8,256]{2,1,0:T(8,128)} %physical_ref.7) | copy-start | bytes 196612
  12.6 10.9 %collective-permute-start.6 = (f32[72,8,128]{2,1,0:T(8,128)S(1)}, f32[72,8,128]{2,1,0:T(8,128)S(1)}, u32[]{:S(2)}, u32[]{:S(2)}) collective-permute-start(f32[72,8,128]{2,1,0:T(8,128)S(1)} %shard_map.78), channel_id=1, source_target_pairs={{0,1},{1,0},{2,3},{3,2},{4,5},{5,4},{6,7},{7,6},{8,9},{9,8},{10,11... | collective-permute-start | bytes 884744 | tf_op jit(solution)/shard_map/ppermute | solution.py:544
  14.6 10.9 %collective-permute-start.4 = (f32[198,256]{1,0:T(8,128)S(1)}, f32[198,256]{1,0:T(8,128)S(1)}, u32[]{:S(2)}, u32[]{:S(2)}) collective-permute-start(f32[198,256]{1,0:T(8,128)S(1)} %get-tuple-element.47), channel_id=1, source_target_pairs={{2,4},{6,8},{10,12},{14,0},{4,2},{8,6},{12,10},{0,14},{3,5},{7,9},... | collective-permute-start | bytes 608264 | tf_op jit(solution)/shard_map/ppermute | solution.py:539
  20.2 6.3 %collective-permute-start.5 = (f32[198,256]{1,0:T(8,128)S(1)}, f32[198,256]{1,0:T(8,128)S(1)}, u32[]{:S(2)}, u32[]{:S(2)}) collective-permute-start(f32[198,256]{1,0:T(8,128)S(1)} %get-tuple-element.48), channel_id=1, source_target_pairs={{0,2},{4,6},{8,10},{12,14},{2,0},{6,4},{10,8},{14,12},{1,3},{5,7},... | collective-permute-start | bytes 608264 | tf_op jit(solution)/shard_map/ppermute | solution.py:539
  20.2 6.3 %collective-permute-start.2 = (f32[2,3,8,256]{3,2,1,0:T(8,128)S(1)}, f32[2,3,8,256]{3,2,1,0:T(8,128)S(1)}, u32[]{:S(2)}, u32[]{:S(2)}) collective-permute-start(f32[2,3,8,256]{3,2,1,0:T(8,128)S(1)} %get-tuple-element.45), channel_id=1, source_target_pairs={{0,16},{32,48},{64,80},{96,112},{128,144},{160,176},{192,208},{224... | collective-permute-start | bytes 147464 | tf_op jit(solution)/shard_map/ppermute | solution.py:539
  20.2 6.3 %collective-permute-start.3 = (f32[2,3,8,256]{3,2,1,0:T(8,128)S(1)}, f32[2,3,8,256]{3,2,1,0:T(8,128)S(1)}, u32[]{:S(2)}, u32[]{:S(2)}) collective-permute-start(f32[2,3,8,256]{3,2,1,0:T(8,128)S(1)} %get-tuple-element.46), channel_id=1, source_target_pairs={{16,32},{48,64},{80,96},{112,128},{144,160},{176,192},{208,224},{2... | collective-permute-start | bytes 147464 | tf_op jit(solution)/shard_map/ppermute | solution.py:539
  26.8 3.2 %collective-permute-start.7 = (f32[98,8,128]{2,1,0:T(8,128)S(1)}, f32[98,8,128]{2,1,0:T(8,128)S(1)}, u32[]{:S(2)}, u32[]{:S(2)}) collective-permute-start(f32[98,8,128]{2,1,0:T(8,128)S(1)} %get-tuple-element.56), channel_id=1, source_target_pairs={{0,1},{1,0},{2,3},{3,2},{4,5},{5,4},{6,7},{7,6},{8,9},{9,8},{10,11... | collective-permute-start | bytes 1204232 | tf_op jit(solution)/shard_map/ppermute | solution.py:544
  47.0 11.3 %collective-permute-start.8 = (f32[117,384]{1,0:T(8,128)S(1)}, f32[117,384]{1,0:T(8,128)S(1)}, u32[]{:S(2)}, u32[]{:S(2)}) collective-permute-start(f32[117,384]{1,0:T(8,128)S(1)} %get-tuple-element.64), channel_id=1, source_target_pairs={{2,4},{6,8},{10,12},{14,0},{4,2},{8,6},{12,10},{0,14},{3,5},{7,9},... | collective-permute-start | bytes 539144 | tf_op jit(solution)/shard_map/ppermute | solution.py:539
  47.1 11.2 %collective-permute-start.9 = (f32[117,384]{1,0:T(8,128)S(1)}, f32[117,384]{1,0:T(8,128)S(1)}, u32[]{:S(2)}, u32[]{:S(2)}) collective-permute-start(f32[117,384]{1,0:T(8,128)S(1)} %get-tuple-element.65), channel_id=1, source_target_pairs={{0,2},{4,6},{8,10},{12,14},{2,0},{6,4},{10,8},{14,12},{1,3},{5,7},... | collective-permute-start | bytes 539144 | tf_op jit(solution)/shard_map/ppermute | solution.py:539

commit v12 on v10

--- a/solution.py
+++ b/solution.py
@@ -409,14 +409,16 @@
 
     def add_group(v, total):
         lefts, rights = [], []
-        for t in range(2):
-            for r in range(SY):
+        for r in range(SY):
+            left, right = [], []
+            for t in range(2):
                 hit = rows == high_ref[t, v, r : r + 1, :]
-                left = [jnp.where(hit, value_ref[t, n, v, r : r + 1, :], 0.0) for n in range(6)]
-                lefts.append(jnp.concatenate(left, axis=0).astype(jnp.bfloat16))
+                left += [jnp.where(hit, value_ref[t, n, v, r : r + 1, :], 0.0) for n in range(6)]
                 low = jnp.broadcast_to(low_ref[t, v, r : r + 1, :], (16, 128)).astype(jnp.bfloat16)
                 low = jnp.concatenate([low] * 8, axis=0)
-                rights.append(jnp.where(columns == low, jnp.bfloat16(1.0), jnp.bfloat16(0.0)))
+                right.append(jnp.where(columns == low, jnp.bfloat16(1.0), jnp.bfloat16(0.0)))
+            lefts.append(jnp.concatenate(left, axis=0).astype(jnp.bfloat16))
+            rights.append(jnp.concatenate(right, axis=0))
         return total + lax.dot_general(
             jnp.concatenate(rights, axis=1),
             jnp.concatenate(lefts, axis=1),
@@ -424,7 +426,8 @@
             preferred_element_type=F32,
         )
 
-    total = lax.fori_loop(0, 2 * SX, add_group, jnp.zeros((128, 48), F32), unroll=8).T
+    total = lax.fori_loop(0, 2 * SX, add_group, jnp.zeros((256, 96), F32), unroll=8)
+    total = (total[0:128, 0:48] + total[128:256, 48:96]).T
     constant = total[0:8] + total[8:16] + total[16:24]
     slope = total[24:32] + total[32:40] + total[40:48]
     upto = jnp.where(

time: 60.1 us -> 60.2 us (level)
  no operation moved by 1% of the time
where the time goes in v12:
time: 60.2 us; the launch traced here: 60 us
  blocking collectives  22.3 us (37%)
  starting transfers between devices  20.2 us (34%)
  Pallas kernels  8.74 us (15%)
  waiting for transfers between devices  6.18 us (10%)
  other arithmetic  1.18 us (2%)
  between operations  0.75 us (1%)
  local copies, waits for them, and re-layouts  0.67 us (1%)
    ppermute x8, starting transfers between devices, exchange(): lax.ppermute(faces, axis, pairs + [(j, i) for i, j in pairs])  16.1 us
    all_to_all x1, blocking collectives, body(): part = lax.all_to_all(part, ('gy', 'gz'), 0, 0, tiled=True)  11.3 us
    all_to_all x1, blocking collectives, body(): part = lax.all_to_all(part, 'gx', 0, 0, tiled=True)  11 us
    pallas_call x8, Pallas kernels, call(): pl.pallas_call(kernel, out_shape=outs, in_specs=[pl.BlockSpec(memory_spac...  8.74 us
    ppermute x8, waiting for transfers between devices, exchange(): lax.ppermute(faces, axis, pairs + [(j, i) for i, j in pairs])  4.82 us
    ppermute x2, starting transfers between devices, other_core(): return lax.ppermute(values, 'gz', [(0, 1), (1, 0)])  4.11 us
    ppermute x2, waiting for transfers between devices, other_core(): return lax.ppermute(values, 'gz', [(0, 1), (1, 0)])  1.36 us
  transfers between devices with their start and end apart: 10, of which 5 were waited for; matrix products, arithmetic and copies ran while one was open for 0% of the time, Pallas kernels for 4%

profile of v12, /device:TPU:1, one launch (start us, length us, event | category | flops | bytes accessed | tf_op | source)
XLA Modules:
  0.0 60.0 jit_solution(8700578934437678435)
XLA Ops:
  0.6 0.0 copy-start.3
  0.7 1.2 %fusion.2 = (f32[4,5,8,256]{3,2,1,0:T(8,128)S(1)}, f32[4,5,8,256]{3,2,1,0:T(8,128)S(1)}) fusion(f32[1,8,8,256]{3,2,1,0:T(8,128)} %bitcast.5, f32[3,8,8,256]{3,2,1,0:T(8,128)} %shift_ref.7, pred[]{:T(512)S(6)} %eq.5), kind=kLoop, calls=%fused_computation.5 | loop fusion | flops 204800 | bytes 589825 | tf_op jit(solution)/shard_map/jit(_where)/select_n | solution.py:559
  1.8 5.8 %collective-permute-start.1 = (f32[4,5,8,256]{3,2,1,0:T(8,128)S(1)}, f32[4,5,8,256]{3,2,1,0:T(8,128)S(1)}, u32[]{:S(2)}, u32[]{:S(2)}) collective-permute-start(f32[4,5,8,256]{3,2,1,0:T(8,128)S(1)} %get-tuple-element.67), channel_id=1, source_target_pairs={{16,32},{48,64},{80,96},{112,128},{144,160},{176,192},{208,224},{2... | collective-permute-start | bytes 491528 | tf_op jit(solution)/shard_map/ppermute | solution.py:542
  7.7 0.0 copy-start.4
  7.7 0.0 copy-start.2
  7.7 0.0 copy-start
  7.7 0.0 collective-permute-start
  7.7 0.0 copy-done.3
  7.7 0.6 %copy-done.4 = s32[1024]{0:T(1024)S(1)} copy-done((s32[1024]{0:T(1024)S(1)}, s32[1024]{0:T(1024)}, u32[]{:S(2)}) %copy-start.4) | copy-done | bytes 4120
  8.3 1.2 %shard_map.76 = (f32[17,16,384]{2,1,0:T(8,128)S(1)}, f32[17,8,384]{2,1,0:T(8,128)S(1)}, f32[13,8,384]{2,1,0:T(8,128)S(1)}, f32[8,8,256]{2,1,0:T(8,128)S(1)}) custom-call(s32[1,1024]{1,0:T(1,128)S(1)} %bitcast.7), custom_call_target="tpu_custom_call" | custom-call | flops 10000000 | bytes 1000000 | tf_op jit(solution)/shard_map/pallas_call | solution.py:526
  9.5 0.0 copy-done.2
  9.5 0.0 copy-start.1
  9.5 1.0 %collective-permute-done.1.x_second = f32[4,5,8,256]{3,2,1,0:T(8,128)S(1)} collective-permute-done((f32[4,5,8,256]{3,2,1,0:T(8,128)S(1)}, f32[4,5,8,256]{3,2,1,0:T(8,128)S(1)}, u32[]{:S(2)}, u32[]{:S(2)}) %collective-permute-start.1) | collective-permute-done | bytes 163872 | tf_op jit(solution)/shard_map/ppermute | solution.py:542
  10.5 1.9 %collective-permute-done.x_first = f32[4,5,8,256]{3,2,1,0:T(8,128)S(1)} collective-permute-done((f32[4,5,8,256]{3,2,1,0:T(8,128)S(1)}, f32[4,5,8,256]{3,2,1,0:T(8,128)S(1)}, u32[]{:S(2)}, u32[]{:S(2)}) %collective-permute-start) | collective-permute-done | bytes 163872 | tf_op jit(solution)/shard_map/ppermute | solution.py:542
  12.4 0.0 copy-done
  12.4 0.0 copy-done.1
  12.4 0.2 shard_map.77
  12.6 0.1 shard_map.78
  12.6 2.0 %collective-permute-start.6 = (f32[72,8,128]{2,1,0:T(8,128)S(1)}, f32[72,8,128]{2,1,0:T(8,128)S(1)}, u32[]{:S(2)}, u32[]{:S(2)}) collective-permute-start(f32[72,8,128]{2,1,0:T(8,128)S(1)} %shard_map.78), channel_id=1, source_target_pairs={{0,1},{1,0},{2,3},{3,2},{4,5},{5,4},{6,7},{7,6},{8,9},{9,8},{10,11... | collective-permute-start | bytes 884744 | tf_op jit(solution)/shard_map/ppermute | solution.py:547
  14.6 1.7 %collective-permute-start.4 = (f32[198,256]{1,0:T(8,128)S(1)}, f32[198,256]{1,0:T(8,128)S(1)}, u32[]{:S(2)}, u32[]{:S(2)}) collective-permute-start(f32[198,256]{1,0:T(8,128)S(1)} %get-tuple-element.47), channel_id=1, source_target_pairs={{0,2},{4,6},{8,10},{12,14},{2,0},{6,4},{10,8},{14,12},{1,3},{5,7},... | collective-permute-start | bytes 608264 | tf_op jit(solution)/shard_map/ppermute | solution.py:542
  16.3 4.7 %collective-permute-start.5 = (f32[198,256]{1,0:T(8,128)S(1)}, f32[198,256]{1,0:T(8,128)S(1)}, u32[]{:S(2)}, u32[]{:S(2)}) collective-permute-start(f32[198,256]{1,0:T(8,128)S(1)} %get-tuple-element.48), channel_id=1, source_target_pairs={{2,4},{6,8},{10,12},{14,0},{4,2},{8,6},{12,10},{0,14},{3,5},{7,9},... | collective-permute-start | bytes 608264 | tf_op jit(solution)/shard_map/ppermute | solution.py:542
  20.9 0.0 collective-permute-start.2
  20.9 3.3 %collective-permute-start.3 = (f32[2,3,8,256]{3,2,1,0:T(8,128)S(1)}, f32[2,3,8,256]{3,2,1,0:T(8,128)S(1)}, u32[]{:S(2)}, u32[]{:S(2)}) collective-permute-start(f32[2,3,8,256]{3,2,1,0:T(8,128)S(1)} %get-tuple-element.46), channel_id=1, source_target_pairs={{16,32},{48,64},{80,96},{112,128},{144,160},{176,192},{208,224},{2... | collective-permute-start | bytes 147464 | tf_op jit(solution)/shard_map/ppermute | solution.py:542
  24.2 0.0 collective-permute-done.6.side
  24.2 1.0 %shard_map.79.inner_ref = f32[17,8,384]{2,1,0:T(8,128)S(1)} custom-call(f32[3,8,8,256]{3,2,1,0:T(8,128)S(1)} %copy-done, f32[8,8,256]{2,1,0:T(8,128)S(1)} %copy-done.1, f32[4,5,8,256]{3,2,1,0:T(8,128)S(1)} %collective-permute-done.x_first, f32[4,5,8,256]{3,2,1,0:T(8,128)S(1)} %collective-permute-done.1.x_second, ...), custom_call_target="tpu_custom_call" | custom-call | flops 1 | bytes 1 | tf_op jit(solution)/shard_map/pallas_call | solution.py:526
  25.2 0.0 collective-permute-done.4.y_first
  25.2 0.8 %collective-permute-done.5.y_second = f32[198,256]{1,0:T(8,128)S(1)} collective-permute-done((f32[198,256]{1,0:T(8,128)S(1)}, f32[198,256]{1,0:T(8,128)S(1)}, u32[]{:S(2)}, u32[]{:S(2)}) %collective-permute-start.5) | collective-permute-done | bytes 202784 | tf_op jit(solution)/shard_map/ppermute | solution.py:542
  26.1 0.0 collective-permute-done.2.d_first
  26.1 1.1 %collective-permute-done.3.d_second = f32[2,3,8,256]{3,2,1,0:T(8,128)S(1)} collective-permute-done((f32[2,3,8,256]{3,2,1,0:T(8,128)S(1)}, f32[2,3,8,256]{3,2,1,0:T(8,128)S(1)}, u32[]{:S(2)}, u32[]{:S(2)}) %collective-permute-start.3) | collective-permute-done | bytes 49184 | tf_op jit(solution)/shard_map/ppermute | solution.py:542
  27.2 0.3 shard_map.80
  27.5 2.2 %collective-permute-start.7 = (f32[98,8,128]{2,1,0:T(8,128)S(1)}, f32[98,8,128]{2,1,0:T(8,128)S(1)}, u32[]{:S(2)}, u32[]{:S(2)}) collective-permute-start(f32[98,8,128]{2,1,0:T(8,128)S(1)} %get-tuple-element.56), channel_id=1, source_target_pairs={{0,1},{1,0},{2,3},{3,2},{4,5},{5,4},{6,7},{7,6},{8,9},{9,8},{10,11... | collective-permute-start | bytes 1204232 | tf_op jit(solution)/shard_map/ppermute | solution.py:547
  29.6 1.4 %collective-permute-done.7.edge_side = f32[98,8,128]{2,1,0:T(8,128)S(1)} collective-permute-done((f32[98,8,128]{2,1,0:T(8,128)S(1)}, f32[98,8,128]{2,1,0:T(8,128)S(1)}, u32[]{:S(2)}, u32[]{:S(2)}) %collective-permute-start.7) | collective-permute-done | bytes 401440 | tf_op jit(solution)/shard_map/ppermute | solution.py:547
  31.0 4.5 %shard_map.81 = (f32[3,13,8,384]{3,2,1,0:T(8,128)S(1)}, f32[117,384]{1,0:T(8,128)S(1)}, f32[117,384]{1,0:T(8,128)S(1)}, f32[16,8,128]{2,1,0:T(8,128)S(1)}) custom-call(f32[8,8,256]{2,1,0:T(8,128)S(1)} %copy-done.2, s32[8,8,256]{2,1,0:T(8,128)S(1)} %copy-done.3, f32[2,3,8,256]{3,2,1,0:T(8,128)S(1)} %collective-permute-done.2.d_first, ...), custom_call_target="tpu_custom_call" | custom-call | flops 10000000 | bytes 1000000 | tf_op jit(solution)/shard_map/pallas_call | solution.py:526
  35.5 11.3 %all_to_all.10.part_ref = f32[16,8,128]{2,1,0:T(8,128)S(1)} all-to-all(f32[16,8,128]{2,1,0:T(8,128)S(1)} %get-tuple-element.61), channel_id=1, replica_groups=mesh['gx'=16,'gy'=8,'gz'=2] {'gy','gz'}, dimensions={0} | all-to-all | bytes 131072 | tf_op jit(solution)/shard_map/all_to_all | solution.py:604
  46.8 0.2 collective-permute-start.8
  47.0 0.4 collective-permute-start.9
  47.4 11.0 %all_to_all.11.part_ref = f32[16,8,128]{2,1,0:T(8,128)S(1)} all-to-all(f32[16,8,128]{2,1,0:T(8,128)S(1)} %shard_map.82), channel_id=1, replica_groups=mesh['gx'=16,'gy'=8,'gz'=2] {'gx'}, dimensions={0} | all-to-all | bytes 131072 | tf_op jit(solution)/shard_map/all_to_all | solution.py:608
  58.4 0.0 collective-permute-done.8.y_first
  58.4 0.0 collective-permute-done.9.y_second
  58.4 1.6 %shard_map.83 = (f32[8,8,256]{2,1,0:T(8,128)}, f32[8,8,256]{2,1,0:T(8,128)}, f32[6,8,8,256]{3,2,1,0:T(8,128)}) custom-call(f32[16,8,128]{2,1,0:T(8,128)S(1)} %all_to_all.11.part_ref, f32[3,13,8,384]{3,2,1,0:T(8,128)S(1)} %get-tuple-element.63.own_ref, f32[117,384]{1,0:T(8,128)S(1)} %collective-permute-done.8.y_first, ...), custom_call_target="tpu_custom_call" | custom-call | flops 10000000 | bytes 1000000 | tf_op jit(solution)/shard_map/pallas_call | solution.py:526
  (3 shorter events, 0.0 us)
Async XLA Ops:
  0.6 7.0 %copy-start.3 = (s32[8,8,256]{2,1,0:T(8,128)S(1)}, s32[8,8,256]{2,1,0:T(8,128)}, u32[]{:S(2)}) copy-start(s32[8,8,256]{2,1,0:T(8,128)} %passive_ref.3) | copy-start | bytes 196612
  1.8 8.7 %collective-permute-start.1 = (f32[4,5,8,256]{3,2,1,0:T(8,128)S(1)}, f32[4,5,8,256]{3,2,1,0:T(8,128)S(1)}, u32[]{:S(2)}, u32[]{:S(2)}) collective-permute-start(f32[4,5,8,256]{3,2,1,0:T(8,128)S(1)} %get-tuple-element.67), channel_id=1, source_target_pairs={{16,32},{48,64},{80,96},{112,128},{144,160},{176,192},{208,224},{2... | collective-permute-start | bytes 491528 | tf_op jit(solution)/shard_map/ppermute | solution.py:542
  7.7 0.7 %copy-start.4 = (s32[1024]{0:T(1024)S(1)}, s32[1024]{0:T(1024)}, u32[]{:S(2)}) copy-start(s32[1024]{0:T(1024)} %param.9) | copy-start | bytes 12292
  7.7 1.8 %copy-start.2 = (f32[8,8,256]{2,1,0:T(8,128)S(1)}, f32[8,8,256]{2,1,0:T(8,128)}, u32[]{:S(2)}) copy-start(f32[8,8,256]{2,1,0:T(8,128)} %design_ref.3) | copy-start | bytes 196612
  7.7 4.8 %copy-start = (f32[3,8,8,256]{3,2,1,0:T(8,128)S(1)}, f32[3,8,8,256]{3,2,1,0:T(8,128)}, u32[]{:S(2)}) copy-start(f32[3,8,8,256]{3,2,1,0:T(8,128)} %shift_ref.7) | copy-start | bytes 589828
  7.7 4.7 %collective-permute-start = (f32[4,5,8,256]{3,2,1,0:T(8,128)S(1)}, f32[4,5,8,256]{3,2,1,0:T(8,128)S(1)}, u32[]{:S(2)}, u32[]{:S(2)}) collective-permute-start(f32[4,5,8,256]{3,2,1,0:T(8,128)S(1)} %get-tuple-element.68), channel_id=1, source_target_pairs={{0,16},{32,48},{64,80},{96,112},{128,144},{160,176},{192,208},{224... | collective-permute-start | bytes 491528 | tf_op jit(solution)/shard_map/ppermute | solution.py:542
  9.5 2.9 %copy-start.1 = (f32[8,8,256]{2,1,0:T(8,128)S(1)}, f32[8,8,256]{2,1,0:T(8,128)}, u32[]{:S(2)}) copy-start(f32[8,8,256]{2,1,0:T(8,128)} %physical_ref.7) | copy-start | bytes 196612
  12.6 11.6 %collective-permute-start.6 = (f32[72,8,128]{2,1,0:T(8,128)S(1)}, f32[72,8,128]{2,1,0:T(8,128)S(1)}, u32[]{:S(2)}, u32[]{:S(2)}) collective-permute-start(f32[72,8,128]{2,1,0:T(8,128)S(1)} %shard_map.78), channel_id=1, source_target_pairs={{0,1},{1,0},{2,3},{3,2},{4,5},{5,4},{6,7},{7,6},{8,9},{9,8},{10,11... | collective-permute-start | bytes 884744 | tf_op jit(solution)/shard_map/ppermute | solution.py:547
  14.6 10.6 %collective-permute-start.4 = (f32[198,256]{1,0:T(8,128)S(1)}, f32[198,256]{1,0:T(8,128)S(1)}, u32[]{:S(2)}, u32[]{:S(2)}) collective-permute-start(f32[198,256]{1,0:T(8,128)S(1)} %get-tuple-element.47), channel_id=1, source_target_pairs={{0,2},{4,6},{8,10},{12,14},{2,0},{6,4},{10,8},{14,12},{1,3},{5,7},... | collective-permute-start | bytes 608264 | tf_op jit(solution)/shard_map/ppermute | solution.py:542
  16.3 9.8 %collective-permute-start.5 = (f32[198,256]{1,0:T(8,128)S(1)}, f32[198,256]{1,0:T(8,128)S(1)}, u32[]{:S(2)}, u32[]{:S(2)}) collective-permute-start(f32[198,256]{1,0:T(8,128)S(1)} %get-tuple-element.48), channel_id=1, source_target_pairs={{2,4},{6,8},{10,12},{14,0},{4,2},{8,6},{12,10},{0,14},{3,5},{7,9},... | collective-permute-start | bytes 608264 | tf_op jit(solution)/shard_map/ppermute | solution.py:542
  20.9 5.2 %collective-permute-start.2 = (f32[2,3,8,256]{3,2,1,0:T(8,128)S(1)}, f32[2,3,8,256]{3,2,1,0:T(8,128)S(1)}, u32[]{:S(2)}, u32[]{:S(2)}) collective-permute-start(f32[2,3,8,256]{3,2,1,0:T(8,128)S(1)} %get-tuple-element.45), channel_id=1, source_target_pairs={{0,16},{32,48},{64,80},{96,112},{128,144},{160,176},{192,208},{224... | collective-permute-start | bytes 147464 | tf_op jit(solution)/shard_map/ppermute | solution.py:542
  20.9 6.3 %collective-permute-start.3 = (f32[2,3,8,256]{3,2,1,0:T(8,128)S(1)}, f32[2,3,8,256]{3,2,1,0:T(8,128)S(1)}, u32[]{:S(2)}, u32[]{:S(2)}) collective-permute-start(f32[2,3,8,256]{3,2,1,0:T(8,128)S(1)} %get-tuple-element.46), channel_id=1, source_target_pairs={{16,32},{48,64},{80,96},{112,128},{144,160},{176,192},{208,224},{2... | collective-permute-start | bytes 147464 | tf_op jit(solution)/shard_map/ppermute | solution.py:542
  27.5 3.5 %collective-permute-start.7 = (f32[98,8,128]{2,1,0:T(8,128)S(1)}, f32[98,8,128]{2,1,0:T(8,128)S(1)}, u32[]{:S(2)}, u32[]{:S(2)}) collective-permute-start(f32[98,8,128]{2,1,0:T(8,128)S(1)} %get-tuple-element.56), channel_id=1, source_target_pairs={{0,1},{1,0},{2,3},{3,2},{4,5},{5,4},{6,7},{7,6},{8,9},{9,8},{10,11... | collective-permute-start | bytes 1204232 | tf_op jit(solution)/shard_map/ppermute | solution.py:547
  46.8 11.6 %collective-permute-start.8 = (f32[117,384]{1,0:T(8,128)S(1)}, f32[117,384]{1,0:T(8,128)S(1)}, u32[]{:S(2)}, u32[]{:S(2)}) collective-permute-start(f32[117,384]{1,0:T(8,128)S(1)} %get-tuple-element.64), channel_id=1, source_target_pairs={{0,2},{4,6},{8,10},{12,14},{2,0},{6,4},{10,8},{14,12},{1,3},{5,7},... | collective-permute-start | bytes 539144 | tf_op jit(solution)/shard_map/ppermute | solution.py:542
  47.0 11.4 %collective-permute-start.9 = (f32[117,384]{1,0:T(8,128)S(1)}, f32[117,384]{1,0:T(8,128)S(1)}, u32[]{:S(2)}, u32[]{:S(2)}) collective-permute-start(f32[117,384]{1,0:T(8,128)S(1)} %get-tuple-element.65), channel_id=1, source_target_pairs={{2,4},{6,8},{10,12},{14,0},{4,2},{8,6},{12,10},{0,14},{3,5},{7,9},... | collective-permute-start | bytes 539144 | tf_op jit(solution)/shard_map/ppermute | solution.py:542

commit v13 on v12

--- a/solution.py
+++ b/solution.py
@@ -270,7 +270,7 @@
     return jnp.concatenate([plane[7:8], high, *filler, low[low.shape[0] - 2 :], plane[0:2]], axis=0)
 
 
-def faces_y_kernel(shift_ref, physical_ref, x_first, x_second, first_ref, second_ref):
+def faces_y_kernel(shift_ref, physical_ref, x_first, x_second, first_ref, second_ref, side_ref):
     even = is_even("gy")
     read = plane_reader(shift_ref, physical_ref, x_first, x_second)
     for index in range(4 * NODES):
@@ -278,12 +278,7 @@
         rows = row_place(index)
         depth = rows.stop - rows.start
         place_pair(even, first_ref, second_ref, plane[SY - depth :], plane[0:depth], rows)
-
-
-def faces_side_kernel(shift_ref, physical_ref, x_first, x_second, side_ref):
-    read = plane_reader(shift_ref, physical_ref, x_first, x_second)
-    for index in range(4 * NODES):
-        side_ref[index] = near_half(read(index))
+        side_ref[index] = near_half(plane)
 
 
 def faces_edge_kernel(
@@ -574,11 +569,12 @@
     faces = (11 * NODES, SZ)
     tiles = (4 * NODES, SY, SZ)
     ext = (4, NODES, SY, LANES)
-    y_faces = call(faces_y_kernel, (displacement, physical, *x_faces), [faces, faces], [], 10**6)
-    y_faces, x_faces, design_faces = lax.optimization_barrier((y_faces, x_faces, design_faces))
+    *y_faces, side = call(
+        faces_y_kernel, (displacement, physical, *x_faces), [faces, faces, (4 * NODES, SY, SIDE)], [], 10**6
+    )
+    y_faces, side, design_faces = lax.optimization_barrier((y_faces, side, design_faces))
     y_faces = exchange(*y_faces, "gy")
     design_faces = exchange(*design_faces, "gx")
-    (side,) = call(faces_side_kernel, (displacement, physical, *x_faces), [(4 * NODES, SY, SIDE)], [], 1)
     (inner_part,) = call(
         functools.partial(inner_kernel, groups=groups),
         (displacement, physical, *x_faces, other_core(side), inverse), [own_frame], [ext], 1,

time: 60.2 us -> 60.1 us (level)
    pallas_call x8 -> x7, Pallas kernels: 8.74 us -> 8.7 us  [call(): pl.pallas_call(kernel, out_shape=outs, in_specs=[pl.BlockSpec(memory_spac...]
where the time goes in v13:
time: 60.1 us; the launch traced here: 59.9 us
  blocking collectives  22.3 us (37%)
  starting transfers between devices  20.2 us (34%)
  Pallas kernels  8.7 us (14%)
  waiting for transfers between devices  6.18 us (10%)
  other arithmetic  1.18 us (2%)
  between operations  0.75 us (1%)
  local copies, waits for them, and re-layouts  0.67 us (1%)
    ppermute x8, starting transfers between devices, exchange(): lax.ppermute(faces, axis, pairs + [(j, i) for i, j in pairs])  16.1 us
    all_to_all x1, blocking collectives, body(): part = lax.all_to_all(part, ('gy', 'gz'), 0, 0, tiled=True)  11.3 us
    all_to_all x1, blocking collectives, body(): part = lax.all_to_all(part, 'gx', 0, 0, tiled=True)  11 us
    pallas_call x7, Pallas kernels, call(): pl.pallas_call(kernel, out_shape=outs, in_specs=[pl.BlockSpec(memory_spac...  8.7 us
    ppermute x8, waiting for transfers between devices, exchange(): lax.ppermute(faces, axis, pairs + [(j, i) for i, j in pairs])  4.82 us
    ppermute x2, starting transfers between devices, other_core(): return lax.ppermute(values, 'gz', [(0, 1), (1, 0)])  4.11 us
    ppermute x2, waiting for transfers between devices, other_core(): return lax.ppermute(values, 'gz', [(0, 1), (1, 0)])  1.36 us
  transfers between devices with their start and end apart: 10, of which 5 were waited for; matrix products, arithmetic and copies ran while one was open for 0% of the time, Pallas kernels for 4%

profile of v13, /device:TPU:1, one launch (start us, length us, event | category | flops | bytes accessed | tf_op | source)
XLA Modules:
  0.0 59.9 jit_solution(17605041541441237019)
XLA Ops:
  0.6 0.0 copy-start.3
  0.7 1.2 %fusion.2 = (f32[4,5,8,256]{3,2,1,0:T(8,128)S(1)}, f32[4,5,8,256]{3,2,1,0:T(8,128)S(1)}) fusion(f32[1,8,8,256]{3,2,1,0:T(8,128)} %bitcast.5, f32[3,8,8,256]{3,2,1,0:T(8,128)} %shift_ref.5, pred[]{:T(512)S(6)} %eq.5), kind=kLoop, calls=%fused_computation.5 | loop fusion | flops 204800 | bytes 589825 | tf_op jit(solution)/shard_map/jit(_where)/select_n | solution.py:554
  1.8 5.8 %collective-permute-start.1 = (f32[4,5,8,256]{3,2,1,0:T(8,128)S(1)}, f32[4,5,8,256]{3,2,1,0:T(8,128)S(1)}, u32[]{:S(2)}, u32[]{:S(2)}) collective-permute-start(f32[4,5,8,256]{3,2,1,0:T(8,128)S(1)} %get-tuple-element.67), channel_id=1, source_target_pairs={{16,32},{48,64},{80,96},{112,128},{144,160},{176,192},{208,224},{2... | collective-permute-start | bytes 491528 | tf_op jit(solution)/shard_map/ppermute | solution.py:537
  7.7 0.0 copy-start.4
  7.7 0.0 copy-start.2
  7.7 0.0 copy-start
  7.7 0.0 collective-permute-start
  7.7 0.0 copy-done.3
  7.7 0.6 %copy-done.4 = s32[1024]{0:T(1024)S(1)} copy-done((s32[1024]{0:T(1024)S(1)}, s32[1024]{0:T(1024)}, u32[]{:S(2)}) %copy-start.4) | copy-done | bytes 4120
  8.3 1.2 %shard_map.76 = (f32[17,16,384]{2,1,0:T(8,128)S(1)}, f32[17,8,384]{2,1,0:T(8,128)S(1)}, f32[13,8,384]{2,1,0:T(8,128)S(1)}, f32[8,8,256]{2,1,0:T(8,128)S(1)}) custom-call(s32[1,1024]{1,0:T(1,128)S(1)} %bitcast.7), custom_call_target="tpu_custom_call" | custom-call | flops 10000000 | bytes 1000000 | tf_op jit(solution)/shard_map/pallas_call | solution.py:521
  9.5 0.0 copy-done.2
  9.5 0.0 copy-start.1
  9.5 1.0 %collective-permute-done.1.x_second = f32[4,5,8,256]{3,2,1,0:T(8,128)S(1)} collective-permute-done((f32[4,5,8,256]{3,2,1,0:T(8,128)S(1)}, f32[4,5,8,256]{3,2,1,0:T(8,128)S(1)}, u32[]{:S(2)}, u32[]{:S(2)}) %collective-permute-start.1) | collective-permute-done | bytes 163872 | tf_op jit(solution)/shard_map/ppermute | solution.py:537
  10.5 1.9 %collective-permute-done.x_first = f32[4,5,8,256]{3,2,1,0:T(8,128)S(1)} collective-permute-done((f32[4,5,8,256]{3,2,1,0:T(8,128)S(1)}, f32[4,5,8,256]{3,2,1,0:T(8,128)S(1)}, u32[]{:S(2)}, u32[]{:S(2)}) %collective-permute-start) | collective-permute-done | bytes 163872 | tf_op jit(solution)/shard_map/ppermute | solution.py:537
  12.4 0.0 copy-done
  12.4 0.0 copy-done.1
  12.4 0.2 shard_map.77
  12.6 2.0 %collective-permute-start.6 = (f32[72,8,128]{2,1,0:T(8,128)S(1)}, f32[72,8,128]{2,1,0:T(8,128)S(1)}, u32[]{:S(2)}, u32[]{:S(2)}) collective-permute-start(f32[72,8,128]{2,1,0:T(8,128)S(1)} %get-tuple-element.50), channel_id=1, source_target_pairs={{0,1},{1,0},{2,3},{3,2},{4,5},{5,4},{6,7},{7,6},{8,9},{9,8},{10,11... | collective-permute-start | bytes 884744 | tf_op jit(solution)/shard_map/ppermute | solution.py:542
  14.5 1.7 %collective-permute-start.4 = (f32[198,256]{1,0:T(8,128)S(1)}, f32[198,256]{1,0:T(8,128)S(1)}, u32[]{:S(2)}, u32[]{:S(2)}) collective-permute-start(f32[198,256]{1,0:T(8,128)S(1)} %get-tuple-element.48), channel_id=1, source_target_pairs={{0,2},{4,6},{8,10},{12,14},{2,0},{6,4},{10,8},{14,12},{1,3},{5,7},... | collective-permute-start | bytes 608264 | tf_op jit(solution)/shard_map/ppermute | solution.py:537
  16.2 4.7 %collective-permute-start.5 = (f32[198,256]{1,0:T(8,128)S(1)}, f32[198,256]{1,0:T(8,128)S(1)}, u32[]{:S(2)}, u32[]{:S(2)}) collective-permute-start(f32[198,256]{1,0:T(8,128)S(1)} %get-tuple-element.49), channel_id=1, source_target_pairs={{2,4},{6,8},{10,12},{14,0},{4,2},{8,6},{12,10},{0,14},{3,5},{7,9},... | collective-permute-start | bytes 608264 | tf_op jit(solution)/shard_map/ppermute | solution.py:537
  20.9 0.0 collective-permute-start.2
  20.9 3.3 %collective-permute-start.3 = (f32[2,3,8,256]{3,2,1,0:T(8,128)S(1)}, f32[2,3,8,256]{3,2,1,0:T(8,128)S(1)}, u32[]{:S(2)}, u32[]{:S(2)}) collective-permute-start(f32[2,3,8,256]{3,2,1,0:T(8,128)S(1)} %get-tuple-element.47), channel_id=1, source_target_pairs={{16,32},{48,64},{80,96},{112,128},{144,160},{176,192},{208,224},{2... | collective-permute-start | bytes 147464 | tf_op jit(solution)/shard_map/ppermute | solution.py:537
  24.2 0.0 collective-permute-done.6.side
  24.2 1.0 %shard_map.78.inner_ref = f32[17,8,384]{2,1,0:T(8,128)S(1)} custom-call(f32[3,8,8,256]{3,2,1,0:T(8,128)S(1)} %copy-done, f32[8,8,256]{2,1,0:T(8,128)S(1)} %copy-done.1, f32[4,5,8,256]{3,2,1,0:T(8,128)S(1)} %collective-permute-done.x_first, f32[4,5,8,256]{3,2,1,0:T(8,128)S(1)} %collective-permute-done.1.x_second, ...), custom_call_target="tpu_custom_call" | custom-call | flops 1 | bytes 1 | tf_op jit(solution)/shard_map/pallas_call | solution.py:521
  25.2 0.0 collective-permute-done.4.y_first
  25.2 0.8 %collective-permute-done.5.y_second = f32[198,256]{1,0:T(8,128)S(1)} collective-permute-done((f32[198,256]{1,0:T(8,128)S(1)}, f32[198,256]{1,0:T(8,128)S(1)}, u32[]{:S(2)}, u32[]{:S(2)}) %collective-permute-start.5) | collective-permute-done | bytes 202784 | tf_op jit(solution)/shard_map/ppermute | solution.py:537
  26.0 0.0 collective-permute-done.2.d_first
  26.0 1.1 %collective-permute-done.3.d_second = f32[2,3,8,256]{3,2,1,0:T(8,128)S(1)} collective-permute-done((f32[2,3,8,256]{3,2,1,0:T(8,128)S(1)}, f32[2,3,8,256]{3,2,1,0:T(8,128)S(1)}, u32[]{:S(2)}, u32[]{:S(2)}) %collective-permute-start.3) | collective-permute-done | bytes 49184 | tf_op jit(solution)/shard_map/ppermute | solution.py:537
  27.1 0.3 shard_map.79
  27.4 2.2 %collective-permute-start.7 = (f32[98,8,128]{2,1,0:T(8,128)S(1)}, f32[98,8,128]{2,1,0:T(8,128)S(1)}, u32[]{:S(2)}, u32[]{:S(2)}) collective-permute-start(f32[98,8,128]{2,1,0:T(8,128)S(1)} %get-tuple-element.56), channel_id=1, source_target_pairs={{0,1},{1,0},{2,3},{3,2},{4,5},{5,4},{6,7},{7,6},{8,9},{9,8},{10,11... | collective-permute-start | bytes 1204232 | tf_op jit(solution)/shard_map/ppermute | solution.py:542
  29.6 1.4 %collective-permute-done.7.edge_side = f32[98,8,128]{2,1,0:T(8,128)S(1)} collective-permute-done((f32[98,8,128]{2,1,0:T(8,128)S(1)}, f32[98,8,128]{2,1,0:T(8,128)S(1)}, u32[]{:S(2)}, u32[]{:S(2)}) %collective-permute-start.7) | collective-permute-done | bytes 401440 | tf_op jit(solution)/shard_map/ppermute | solution.py:542
  30.9 4.5 %shard_map.80 = (f32[3,13,8,384]{3,2,1,0:T(8,128)S(1)}, f32[117,384]{1,0:T(8,128)S(1)}, f32[117,384]{1,0:T(8,128)S(1)}, f32[16,8,128]{2,1,0:T(8,128)S(1)}) custom-call(f32[8,8,256]{2,1,0:T(8,128)S(1)} %copy-done.2, s32[8,8,256]{2,1,0:T(8,128)S(1)} %copy-done.3, f32[2,3,8,256]{3,2,1,0:T(8,128)S(1)} %collective-permute-done.2.d_first, ...), custom_call_target="tpu_custom_call" | custom-call | flops 10000000 | bytes 1000000 | tf_op jit(solution)/shard_map/pallas_call | solution.py:521
  35.5 11.3 %all_to_all.10.part_ref = f32[16,8,128]{2,1,0:T(8,128)S(1)} all-to-all(f32[16,8,128]{2,1,0:T(8,128)S(1)} %get-tuple-element.61), channel_id=1, replica_groups=mesh['gx'=16,'gy'=8,'gz'=2] {'gy','gz'}, dimensions={0} | all-to-all | bytes 131072 | tf_op jit(solution)/shard_map/all_to_all | solution.py:600
  46.7 0.2 collective-permute-start.8
  46.9 0.4 collective-permute-start.9
  47.3 11.0 %all_to_all.11.part_ref = f32[16,8,128]{2,1,0:T(8,128)S(1)} all-to-all(f32[16,8,128]{2,1,0:T(8,128)S(1)} %shard_map.81), channel_id=1, replica_groups=mesh['gx'=16,'gy'=8,'gz'=2] {'gx'}, dimensions={0} | all-to-all | bytes 131072 | tf_op jit(solution)/shard_map/all_to_all | solution.py:604
  58.3 0.0 collective-permute-done.8.y_first
  58.3 0.0 collective-permute-done.9.y_second
  58.3 1.6 %shard_map.82 = (f32[8,8,256]{2,1,0:T(8,128)}, f32[8,8,256]{2,1,0:T(8,128)}, f32[6,8,8,256]{3,2,1,0:T(8,128)}) custom-call(f32[16,8,128]{2,1,0:T(8,128)S(1)} %all_to_all.11.part_ref, f32[3,13,8,384]{3,2,1,0:T(8,128)S(1)} %get-tuple-element.63.own_ref, f32[117,384]{1,0:T(8,128)S(1)} %collective-permute-done.8.y_first, ...), custom_call_target="tpu_custom_call" | custom-call | flops 10000000 | bytes 1000000 | tf_op jit(solution)/shard_map/pallas_call | solution.py:521
  (3 shorter events, 0.0 us)
Async XLA Ops:
  0.6 7.0 %copy-start.3 = (s32[8,8,256]{2,1,0:T(8,128)S(1)}, s32[8,8,256]{2,1,0:T(8,128)}, u32[]{:S(2)}) copy-start(s32[8,8,256]{2,1,0:T(8,128)} %passive_ref.3) | copy-start | bytes 196612
  1.8 8.7 %collective-permute-start.1 = (f32[4,5,8,256]{3,2,1,0:T(8,128)S(1)}, f32[4,5,8,256]{3,2,1,0:T(8,128)S(1)}, u32[]{:S(2)}, u32[]{:S(2)}) collective-permute-start(f32[4,5,8,256]{3,2,1,0:T(8,128)S(1)} %get-tuple-element.67), channel_id=1, source_target_pairs={{16,32},{48,64},{80,96},{112,128},{144,160},{176,192},{208,224},{2... | collective-permute-start | bytes 491528 | tf_op jit(solution)/shard_map/ppermute | solution.py:537
  7.7 0.7 %copy-start.4 = (s32[1024]{0:T(1024)S(1)}, s32[1024]{0:T(1024)}, u32[]{:S(2)}) copy-start(s32[1024]{0:T(1024)} %param.9) | copy-start | bytes 12292
  7.7 1.8 %copy-start.2 = (f32[8,8,256]{2,1,0:T(8,128)S(1)}, f32[8,8,256]{2,1,0:T(8,128)}, u32[]{:S(2)}) copy-start(f32[8,8,256]{2,1,0:T(8,128)} %design_ref.3) | copy-start | bytes 196612
  7.7 4.8 %copy-start = (f32[3,8,8,256]{3,2,1,0:T(8,128)S(1)}, f32[3,8,8,256]{3,2,1,0:T(8,128)}, u32[]{:S(2)}) copy-start(f32[3,8,8,256]{3,2,1,0:T(8,128)} %shift_ref.5) | copy-start | bytes 589828
  7.7 4.7 %collective-permute-start = (f32[4,5,8,256]{3,2,1,0:T(8,128)S(1)}, f32[4,5,8,256]{3,2,1,0:T(8,128)S(1)}, u32[]{:S(2)}, u32[]{:S(2)}) collective-permute-start(f32[4,5,8,256]{3,2,1,0:T(8,128)S(1)} %get-tuple-element.68), channel_id=1, source_target_pairs={{0,16},{32,48},{64,80},{96,112},{128,144},{160,176},{192,208},{224... | collective-permute-start | bytes 491528 | tf_op jit(solution)/shard_map/ppermute | solution.py:537
  9.5 2.9 %copy-start.1 = (f32[8,8,256]{2,1,0:T(8,128)S(1)}, f32[8,8,256]{2,1,0:T(8,128)}, u32[]{:S(2)}) copy-start(f32[8,8,256]{2,1,0:T(8,128)} %physical_ref.5) | copy-start | bytes 196612
  12.6 11.6 %collective-permute-start.6 = (f32[72,8,128]{2,1,0:T(8,128)S(1)}, f32[72,8,128]{2,1,0:T(8,128)S(1)}, u32[]{:S(2)}, u32[]{:S(2)}) collective-permute-start(f32[72,8,128]{2,1,0:T(8,128)S(1)} %get-tuple-element.50), channel_id=1, source_target_pairs={{0,1},{1,0},{2,3},{3,2},{4,5},{5,4},{6,7},{7,6},{8,9},{9,8},{10,11... | collective-permute-start | bytes 884744 | tf_op jit(solution)/shard_map/ppermute | solution.py:542
  14.5 10.6 %collective-permute-start.4 = (f32[198,256]{1,0:T(8,128)S(1)}, f32[198,256]{1,0:T(8,128)S(1)}, u32[]{:S(2)}, u32[]{:S(2)}) collective-permute-start(f32[198,256]{1,0:T(8,128)S(1)} %get-tuple-element.48), channel_id=1, source_target_pairs={{0,2},{4,6},{8,10},{12,14},{2,0},{6,4},{10,8},{14,12},{1,3},{5,7},... | collective-permute-start | bytes 608264 | tf_op jit(solution)/shard_map/ppermute | solution.py:537
  16.2 9.8 %collective-permute-start.5 = (f32[198,256]{1,0:T(8,128)S(1)}, f32[198,256]{1,0:T(8,128)S(1)}, u32[]{:S(2)}, u32[]{:S(2)}) collective-permute-start(f32[198,256]{1,0:T(8,128)S(1)} %get-tuple-element.49), channel_id=1, source_target_pairs={{2,4},{6,8},{10,12},{14,0},{4,2},{8,6},{12,10},{0,14},{3,5},{7,9},... | collective-permute-start | bytes 608264 | tf_op jit(solution)/shard_map/ppermute | solution.py:537
  20.9 5.2 %collective-permute-start.2 = (f32[2,3,8,256]{3,2,1,0:T(8,128)S(1)}, f32[2,3,8,256]{3,2,1,0:T(8,128)S(1)}, u32[]{:S(2)}, u32[]{:S(2)}) collective-permute-start(f32[2,3,8,256]{3,2,1,0:T(8,128)S(1)} %get-tuple-element.46), channel_id=1, source_target_pairs={{0,16},{32,48},{64,80},{96,112},{128,144},{160,176},{192,208},{224... | collective-permute-start | bytes 147464 | tf_op jit(solution)/shard_map/ppermute | solution.py:537
  20.9 6.3 %collective-permute-start.3 = (f32[2,3,8,256]{3,2,1,0:T(8,128)S(1)}, f32[2,3,8,256]{3,2,1,0:T(8,128)S(1)}, u32[]{:S(2)}, u32[]{:S(2)}) collective-permute-start(f32[2,3,8,256]{3,2,1,0:T(8,128)S(1)} %get-tuple-element.47), channel_id=1, source_target_pairs={{16,32},{48,64},{80,96},{112,128},{144,160},{176,192},{208,224},{2... | collective-permute-start | bytes 147464 | tf_op jit(solution)/shard_map/ppermute | solution.py:537
  27.4 3.5 %collective-permute-start.7 = (f32[98,8,128]{2,1,0:T(8,128)S(1)}, f32[98,8,128]{2,1,0:T(8,128)S(1)}, u32[]{:S(2)}, u32[]{:S(2)}) collective-permute-start(f32[98,8,128]{2,1,0:T(8,128)S(1)} %get-tuple-element.56), channel_id=1, source_target_pairs={{0,1},{1,0},{2,3},{3,2},{4,5},{5,4},{6,7},{7,6},{8,9},{9,8},{10,11... | collective-permute-start | bytes 1204232 | tf_op jit(solution)/shard_map/ppermute | solution.py:542
  46.7 11.6 %collective-permute-start.8 = (f32[117,384]{1,0:T(8,128)S(1)}, f32[117,384]{1,0:T(8,128)S(1)}, u32[]{:S(2)}, u32[]{:S(2)}) collective-permute-start(f32[117,384]{1,0:T(8,128)S(1)} %get-tuple-element.64), channel_id=1, source_target_pairs={{0,2},{4,6},{8,10},{12,14},{2,0},{6,4},{10,8},{14,12},{1,3},{5,7},... | collective-permute-start | bytes 539144 | tf_op jit(solution)/shard_map/ppermute | solution.py:537
  46.9 11.4 %collective-permute-start.9 = (f32[117,384]{1,0:T(8,128)S(1)}, f32[117,384]{1,0:T(8,128)S(1)}, u32[]{:S(2)}, u32[]{:S(2)}) collective-permute-start(f32[117,384]{1,0:T(8,128)S(1)} %get-tuple-element.65), channel_id=1, source_target_pairs={{2,4},{6,8},{10,12},{14,0},{4,2},{8,6},{12,10},{0,14},{3,5},{7,9},... | collective-permute-start | bytes 539144 | tf_op jit(solution)/shard_map/ppermute | solution.py:537
